TPU v7x, 32 devices: a whole 2x2x4 slice. The times are simulated.
32 devices in a mesh: row: 4 (over y, x), col: 8 (over z, core).
Axes of the slice: x: 2, y: 2, z: 4, core: 2. Of those that a mesh axis runs over, the one named last changes fastest.
Arguments:
- blocks: bfloat16 [32, 48, 128, 128], P('row', 'col'), as said below
- col_index: int32 [32, 48], P('row', 'col'), may hold values from -1 to 31, as said below
- vectors: float32 [4096, 256], P(('col', 'row')), may hold values from -6 to 6
Outputs:
- orbitals: float32 [4096, 256], P(('col', 'row'))
Inputs may be any that keep to these rules, and one draw needn't show every extreme that they name: `col_index`: entry [I, c * 6 + t] is the global index of a nonzero block of block row I that lies in column group c (block columns c * 4 to (c + 1) * 4 - 1), or -1 for an empty slot; within one row and group the listed blocks come first and are distinct. The pattern is symmetric (J is listed in row I exactly when I is listed in row J) and every row lists its diagonal block. At most 4 blocks of one row lie in one column group, and some rows have exactly 4 there. `blocks`: H is symmetric: the block listed for (J, I) is the transpose of the block listed for (I, J). Blocks in empty slots are not part of H.
All inputs are finite; a program needn't handle non-finite values.
Results may differ from a plain program's by a relative error of at most 0.006.
Values may be sent and summed in bfloat16 or wider, within the bound.
No kernel may reach another device: no remote copies, remote signals or barrier semaphores. Data moves between devices by JAX's collectives and lax.ppermute only.
A program may use at most 128 MiB of HBM per device.

v0:
```python
import math

import jax
import jax.numpy as jnp
from jax import lax
from jax.sharding import PartitionSpec as P

DEGREE = 4


LOWER = -2.0
CUTOFF = 0.0
UPPER = 2.0


def filter_coefs(degree):
    half_width = (UPPER - CUTOFF) / 2.0
    center = (UPPER + CUTOFF) / 2.0
    sigma_now = half_width / (LOWER - center)
    tau_value = 2.0 / sigma_now
    scales = [sigma_now / half_width]
    carries = [0.0]
    for number in range(1, degree):
        sigma_next = 1.0 / (tau_value - sigma_now)
        scales.append(2.0 * sigma_next / half_width)
        carries.append(sigma_now * sigma_next)
        sigma_now = sigma_next
    return (center, scales, carries)


def on_device(blocks, col_index, vectors):
    center, scales, carries = filter_coefs(DEGREE)
    row_count = lax.axis_size("row")
    col_count = lax.axis_size("col")
    row_rank = lax.axis_index("row")
    col_rank = lax.axis_index("col")
    group_rows = blocks.shape[0]
    block_width = blocks.shape[2]
    states = vectors.shape[1]
    piece_rows = vectors.shape[0]
    tile_blocks = piece_rows // block_width * row_count
    first_row = row_rank * group_rows
    first_col = col_rank * tile_blocks
    is_live = col_index >= 0
    local_col = jnp.where(is_live, col_index - first_col, 0)
    columns = jnp.arange(tile_blocks, dtype=jnp.int32)
    global_rows = first_row + jnp.arange(group_rows, dtype=jnp.int32)
    diagonal = ((global_rows - first_col)[:, None] == columns[None, :]).astype(jnp.bfloat16)
    weights = ((local_col[:, :, None] == columns) & is_live[:, :, None]).astype(jnp.float32)
    nothing = jnp.zeros((), jnp.bfloat16)
    previous = vectors
    current = vectors
    for number in range(DEGREE):
        lowered = current.astype(jnp.bfloat16)
        if number % 2 == 0:
            gathered = lax.all_gather(lowered, "row", axis=0, tiled=True)
            forward_blocked = gathered.reshape(tile_blocks, block_width, states)
            forward_shifted = jnp.einsum(
                "ij,jbk->ibk", diagonal, forward_blocked, preferred_element_type=jnp.float32
            )
            picked = jnp.where(is_live[:, :, None, None], forward_blocked[local_col], nothing)
            forward_summed = jnp.einsum(
                "isab,isbk->iak", blocks, picked, preferred_element_type=jnp.float32
            )
            summed_image = lax.psum_scatter(
                (forward_summed - center * forward_shifted).reshape(
                    group_rows * block_width, states
                ),
                "col",
                scatter_dimension=0,
                tiled=True,
            )
        else:
            gathered = lax.all_gather(lowered, "col", axis=0, tiled=True)
            blocked = gathered.reshape(group_rows, block_width, states)
            shifted = jnp.einsum(
                "ij,ibk->jbk", diagonal, blocked, preferred_element_type=jnp.float32
            )
            products = jnp.einsum(
                "isab,iak->isbk", blocks, blocked, preferred_element_type=jnp.float32
            )
            summed = jnp.einsum(
                "isj,isbk->jbk",
                weights,
                products,
                precision=lax.Precision.HIGHEST,
                preferred_element_type=jnp.float32,
            )
            summed_image = lax.psum_scatter(
                (summed - center * shifted).reshape(tile_blocks * block_width, states),
                "row",
                scatter_dimension=0,
                tiled=True,
            )
        if number == 0:
            following = scales[0] * summed_image
        else:
            following = scales[number] * summed_image - carries[number] * previous
        previous, current = (current, following)
    filtered = current
    local_gram = jnp.dot(
        filtered.T, filtered, precision=lax.Precision.HIGHEST, preferred_element_type=jnp.float32
    )
    gram_sum = lax.psum(local_gram, ("row", "col"))
    factor = jnp.linalg.cholesky(gram_sum)
    inverse = jax.scipy.linalg.solve_triangular(
        factor, jnp.eye(states, dtype=jnp.float32), lower=True
    )
    filtered = jnp.dot(
        filtered, inverse.T, precision=lax.Precision.HIGHEST, preferred_element_type=jnp.float32
    )
    orbital_count = piece_rows * row_count * col_count
    return math.sqrt(orbital_count) * filtered


def solution(mesh):
    return jax.shard_map(
        on_device,
        mesh=mesh,
        in_specs=(P("row", "col", None, None), P("row", "col"), P(("col", "row"), None)),
        out_specs=P(("col", "row"), None),
        check_vma=False,
    )
```

profile of v0, /device:TPU:0, one launch (start us, length us, event | category | flops | bytes accessed | tf_op | source)
XLA Modules:
  0.0 421.4 jit_solution(2115944967044561802)
XLA Ops:
  9.0 10.4 %all_gather.12 = bf16[512,256]{1,0:T(8,128)(2,1)S(1)} all-gather(bf16[128,256]{1,0:T(8,128)(2,1)S(1)} %convert_element_type.15), channel_id=1, replica_groups=mesh['row'=4,'col'=8] {'row'}, dimensions={0}, use_global_device_ids=true | all-gather | bytes 327680 | tf_op jit(solution)/shard_map/all_gather | solution.py:56
  19.9 2.5 gather_fusion
  22.4 3.7 fusion.21
  26.4 32.5 %reduce-scatter.5.cloned.1.call-done = f32[128,256]{1,0:T(8,128)} async-done(((f32[1024,256]{1,0:T(8,128)}), f32[128,256]{1,0:T(8,128)}) %reduce-scatter.5.cloned.1.call-update) | async-done | bytes 131088 | tf_op jit(solution)/shard_map/reduce_scatter | solution.py:65
  59.8 15.0 %all_gather.13 = bf16[1024,256]{1,0:T(8,128)(2,1)S(1)} all-gather(bf16[128,256]{1,0:T(8,128)(2,1)S(1)} %multiply_convert_fusion), channel_id=1, replica_groups=mesh['row'=4,'col'=8] {'col'}, dimensions={0}, use_global_device_ids=true | all-gather | bytes 589824 | tf_op jit(solution)/shard_map/all_gather | solution.py:74
  74.8 3.7 fusion.62
  78.5 6.7 %copy.26 = f32[8,256,6,128]{1,0,2,3:T(8,128)} copy(f32[8,256,6,128]{3,1,2,0:T(8,128)} %fusion.62) | data formatting | bytes 12582912 | tf_op jit(solution)/shard_map/isab,iak->isbk/dot_general | solution.py:79
  85.2 5.6 %fusion.24 = f32[4,128,256]{2,0,1:T(4,128)S(1)} fusion(f32[8,256,6,128]{1,0,2,3:T(8,128)} %copy.26, s32[8,6]{0,1:T(8,128)S(1)} %copy.12, pred[8,6]{0,1:T(8,128)(4,1)S(1)} %copy.13), kind=kOutput, calls=%fused_computation.22 | convolution fusion | flops 75497856 | bytes 6815984 | tf_op jit(solution)/shard_map/isj,isbk->jbk/dot_general | solution.py:82
  92.1 23.4 %reduce-scatter.7.cloned.1.call-done = f32[128,256]{1,0:T(8,128)} async-done(((f32[512,256]{1,0:T(8,128)}), f32[128,256]{1,0:T(8,128)}) %reduce-scatter.7.cloned.1.call-update) | async-done | bytes 131088 | tf_op jit(solution)/shard_map/reduce_scatter | solution.py:89
  116.5 8.9 %all_gather.14 = bf16[512,256]{1,0:T(8,128)(2,1)S(1)} all-gather(bf16[128,256]{1,0:T(8,128)(2,1)S(1)} %fusion.47), channel_id=1, replica_groups=mesh['row'=4,'col'=8] {'row'}, dimensions={0}, use_global_device_ids=true | all-gather | bytes 327680 | tf_op jit(solution)/shard_map/all_gather | solution.py:56
  125.7 2.5 gather_fusion.1
  128.3 3.8 fusion.18
  132.1 32.6 %reduce-scatter.9.cloned.1.call-done = f32[128,256]{1,0:T(8,128)} async-done(((f32[1024,256]{1,0:T(8,128)}), f32[128,256]{1,0:T(8,128)}) %reduce-scatter.9.cloned.1.call-update) | async-done | bytes 131088 | tf_op jit(solution)/shard_map/reduce_scatter | solution.py:65
  165.6 15.2 %all_gather.15 = bf16[1024,256]{1,0:T(8,128)(2,1)S(1)} all-gather(bf16[128,256]{1,0:T(8,128)(2,1)S(1)} %subtract_convert_fusion), channel_id=1, replica_groups=mesh['row'=4,'col'=8] {'col'}, dimensions={0}, use_global_device_ids=true | all-gather | bytes 589824 | tf_op jit(solution)/shard_map/all_gather | solution.py:74
  180.8 3.7 fusion.63
  184.5 6.7 %copy.30 = f32[8,256,6,128]{1,0,2,3:T(8,128)} copy(f32[8,256,6,128]{3,1,2,0:T(8,128)} %fusion.63) | data formatting | bytes 12582912 | tf_op jit(solution)/shard_map/isab,iak->isbk/dot_general | solution.py:79
  191.2 5.6 %fusion.27 = f32[4,128,256]{2,0,1:T(4,128)S(1)} fusion(f32[8,256,6,128]{1,0,2,3:T(8,128)} %copy.30, s32[8,6]{0,1:T(8,128)S(1)} %copy.12, pred[8,6]{0,1:T(8,128)(4,1)S(1)} %copy.13), kind=kOutput, calls=%fused_computation.23 | convolution fusion | flops 75497856 | bytes 6815984 | tf_op jit(solution)/shard_map/isj,isbk->jbk/dot_general | solution.py:82
  198.1 22.9 %reduce-scatter.11.cloned.1.call-done = f32[128,256]{1,0:T(8,128)} async-done(((f32[512,256]{1,0:T(8,128)}), f32[128,256]{1,0:T(8,128)}) %reduce-scatter.11.cloned.1.call-update) | async-done | bytes 131088 | tf_op jit(solution)/shard_map/reduce_scatter | solution.py:89
  223.3 128.1 %all-reduce.3.cloned.1.call-done = f32[256,256]{0,1:T(8,128)} async-done(((f32[256,256]{0,1:T(8,128)}), f32[256,256]{0,1:T(8,128)}) %all-reduce.3.cloned.1.call-update) | async-done | bytes 262160 | tf_op jit(solution)/shard_map/psum | solution.py:104
  353.5 11.7 %cholesky.50 = f32[128,128]{1,0:T(8,128)S(1)} custom-call(f32[128,128]{1,0:T(8,128)S(1)} %cholesky.118), custom_call_target="Cholesky" | custom-call | tf_op jit(solution)/shard_map/jit(cholesky)/cholesky | solution.py:105
  365.3 9.8 %custom-call.15 = f32[1,128,128]{1,2,0:T(8,128)S(1)} custom-call(f32[1,128,128]{2,1,0:T(8,128)S(1)} %get-tuple-element.28), custom_call_target="InvertDiagBlocksLowerTriangular" | custom-call | tf_op jit(solution)/shard_map/jit(cholesky)/cholesky | solution.py:105
  375.6 11.7 %cholesky.105 = f32[128,128]{1,0:T(8,128)S(1)} custom-call(f32[128,128]{1,0:T(8,128)S(1)} %convolution_subtract_fusion.3), custom_call_target="Cholesky" | custom-call | tf_op jit(solution)/shard_map/jit(cholesky)/cholesky | solution.py:105
  389.3 4.0 while.1
  393.3 19.7 %custom-call.16 = f32[2,128,128]{1,2,0:T(8,128)S(1)} custom-call(f32[2,128,128]{2,1,0:T(8,128)S(1)} %get-tuple-element.12), custom_call_target="InvertDiagBlocksLowerTriangular" | custom-call | tf_op jit(solution)/shard_map/jit(_solve_triangular)/triangular_solve | solution.py:106
  (62 shorter events, 20.3 us)
Async XLA Ops:
  6.5 15.8 %copy-start = (bf16[8,6,128,128]{3,2,1,0:T(8,128)(2,1)S(1)}, bf16[8,6,128,128]{3,2,1,0:T(8,128)(2,1)}, u32[]{:S(2)}) copy-start(bf16[8,6,128,128]{3,2,1,0:T(8,128)(2,1)} %param.3) | copy-start | bytes 4718596
  6.5 52.3 %reduce-scatter.5.cloned.1.call-start = ((), (), s32[]{:S(2)}) async-start(), calls=%async_computation.4 | async-start | bytes 1179648 | tf_op jit(solution)/shard_map/reduce_scatter | solution.py:65
  26.1 89.4 %reduce-scatter.7.cloned.1.call-start = ((), (), s32[]{:S(2)}) async-start(), calls=%async_computation.5 | async-start | bytes 655360 | tf_op jit(solution)/shard_map/reduce_scatter | solution.py:89
  90.8 24.8 %copy-start.1 = (f32[128,256]{1,0:T(8,128)S(1)}, f32[128,256]{1,0:T(8,128)}, u32[]{:S(2)}) copy-start(f32[128,256]{1,0:T(8,128)} %param.5) | copy-start | bytes 393220
  92.1 72.6 %reduce-scatter.9.cloned.1.call-start = ((), (), s32[]{:S(2)}) async-start(), calls=%async_computation.6 | async-start | bytes 1179648 | tf_op jit(solution)/shard_map/reduce_scatter | solution.py:65
  128.3 36.4 %copy-start.4 = (f32[128,256]{1,0:T(8,128)S(1)}, f32[128,256]{1,0:T(8,128)}, u32[]{:S(2)}) copy-start(f32[128,256]{1,0:T(8,128)} %reduce-scatter.5.cloned.1.call-done) | copy-start | bytes 393220
  132.0 89.0 %reduce-scatter.11.cloned.1.call-start = ((), (), s32[]{:S(2)}) async-start(), calls=%async_computation.7 | async-start | bytes 655360 | tf_op jit(solution)/shard_map/reduce_scatter | solution.py:89
  196.8 24.3 %copy-start.2 = (f32[128,256]{1,0:T(8,128)S(1)}, f32[128,256]{1,0:T(8,128)}, u32[]{:S(2)}) copy-start(f32[128,256]{1,0:T(8,128)} %reduce-scatter.7.cloned.1.call-done) | copy-start | bytes 393220
  198.1 153.3 %all-reduce.3.cloned.1.call-start = ((), (), s32[]{:S(2)}) async-start(), calls=%async_computation.8 | async-start | bytes 524288 | tf_op jit(solution)/shard_map/psum | solution.py:104
  221.1 192.7 %copy-start.3 = (f32[128,256]{1,0:T(8,128)S(1)}, f32[128,256]{1,0:T(8,128)}, u32[]{:S(2)}) copy-start(f32[128,256]{1,0:T(8,128)} %reduce-scatter.11.cloned.1.call-done) | copy-start | bytes 393220
Sparse Core Ops, SparseCore 0:
  26.2 32.5 reduce-scatter.4
  92.2 23.2 reduce-scatter.6
  132.2 32.4 reduce-scatter.8
  198.2 22.8 reduce-scatter.10
  226.4 124.9 all-reduce.2
where the time goes:
time: 422 us; the launch traced here: 421 us
  waiting for transfers between devices  240 us (57%)
  other arithmetic  59.9 us (14%)
  blocking collectives  49.6 us (12%)
  matrix products  32.1 us (8%)
  local copies, waits for them, and re-layouts  25.4 us (6%)
  between operations  14.5 us (3%)
    psum x1, waiting for transfers between devices, on_device(): gram_sum = lax.psum(local_gram, ('row', 'col'))  128 us
    reduce_scatter x2, waiting for transfers between devices, on_device(): lax.psum_scatter((forward_summed - center * forward_shifted).reshape(grou...  65.1 us
    reduce_scatter x2, waiting for transfers between devices, on_device(): lax.psum_scatter((summed - center * shifted).reshape(tile_blocks * block_...  46.3 us
    another operation x6, other arithmetic, on_device(): factor = jnp.linalg.cholesky(gram_sum)  34 us
    all_gather x2, blocking collectives, on_device(): gathered = lax.all_gather(lowered, 'col', axis=0, tiled=True)  30.2 us
    another operation x3, other arithmetic, on_device(): jax.scipy.linalg.solve_triangular(factor, jnp.eye(states, dtype=jnp.float...  19.7 us
    all_gather x2, blocking collectives, on_device(): gathered = lax.all_gather(lowered, 'row', axis=0, tiled=True)  19.4 us
    dot_general x2, local copies, waits for them, and re-layouts, on_device(): jnp.einsum('isab,iak->isbk', blocks, blocked, preferred_element_type=jnp....  13.4 us
  transfers between devices with their start and end apart: 5, of which 5 were waited for; matrix products, arithmetic and copies ran while one was open for 0% of the time, Pallas kernels for 0%

commit v1 on v0

v1 whole, which is shorter than its diff:
```python
import math

import jax
import jax.numpy as jnp
from jax import lax
from jax.experimental import pallas as pl
from jax.experimental.pallas import tpu as pltpu
from jax.sharding import PartitionSpec as P

DEGREE = 4


LOWER = -2.0
CUTOFF = 0.0
UPPER = 2.0


def filter_coefs(degree):
    half_width = (UPPER - CUTOFF) / 2.0
    center = (UPPER + CUTOFF) / 2.0
    sigma_now = half_width / (LOWER - center)
    tau_value = 2.0 / sigma_now
    scales = [sigma_now / half_width]
    carries = [0.0]
    for number in range(1, degree):
        sigma_next = 1.0 / (tau_value - sigma_now)
        scales.append(2.0 * sigma_next / half_width)
        carries.append(sigma_now * sigma_next)
        sigma_now = sigma_next
    return (center, scales, carries)


def swap(value, axis, distance):
    count = lax.axis_size(axis)
    return lax.ppermute(value, axis, [(i, i ^ distance) for i in range(count)])


def bits_below(count):
    return [1 << n for n in range(count.bit_length() - 1)]


def densify(blocks, col_index, tile_blocks):
    group_rows, slots, width, _ = blocks.shape

    def kernel(index_ref, blocks_ref, tile_ref):
        row = pl.program_id(0)
        tile_ref[...] = jnp.zeros_like(tile_ref)
        for slot in range(slots):
            place = index_ref[row, slot]

            @pl.when(place >= 0)
            def _():
                start = pl.multiple_of(lax.rem(place, tile_blocks) * width, width)
                tile_ref[:, pl.ds(start, width)] = blocks_ref[0, slot]

    return pl.pallas_call(
        kernel,
        grid_spec=pltpu.PrefetchScalarGridSpec(
            num_scalar_prefetch=1,
            grid=(group_rows,),
            in_specs=[pl.BlockSpec((1, slots, width, width), lambda i, index: (i, 0, 0, 0))],
            out_specs=pl.BlockSpec((width, tile_blocks * width), lambda i, index: (i, 0)),
        ),
        out_shape=jax.ShapeDtypeStruct((group_rows * width, tile_blocks * width), blocks.dtype),
    )(col_index, blocks)


def exact_dot(a, b, dims):
    return lax.dot_general(
        a, b, (dims, ((), ())), precision=lax.Precision.HIGHEST, preferred_element_type=jnp.float32
    )


def factor_in_place(ref, size):
    rows = lax.broadcasted_iota(jnp.int32, (size, size), 0)
    lanes = lax.broadcasted_iota(jnp.int32, (size, size), 1)
    lane_row = lax.broadcasted_iota(jnp.int32, (1, size), 1)

    def pivot(j, unused):
        row = ref[pl.ds(j, 1), :]
        here = lane_row == j
        d = jnp.sum(jnp.where(here, row, 0.0), axis=1, keepdims=True)
        inv_root = lax.rsqrt(d)
        inv = 1.0 / d
        matrix = ref[...]
        below = rows > j
        column = jnp.sum(jnp.where(lanes == j, matrix, 0.0), axis=1, keepdims=True)
        pivot_row = jnp.where(here, 1.0, row)
        scaled = pivot_row * inv
        kept = jnp.where((lanes == j) & below, 0.0, matrix)
        ref[...] = kept - jnp.where(below, column * scaled, 0.0)
        ref[pl.ds(j, 1), :] = pivot_row * inv_root
        return unused

    lax.fori_loop(0, size, pivot, 0)


def inverse_factor(cross, packed):
    size = cross.shape[0]

    def kernel(cross_ref, packed_ref, out_ref, work):
        rows = lax.broadcasted_iota(jnp.int32, (size, size), 0)
        lanes = lax.broadcasted_iota(jnp.int32, (size, size), 1)
        both = packed_ref[:size, :]
        mirrored = both.T
        work[...] = jnp.where(rows >= lanes, both, mirrored)
        factor_in_place(work, size)
        first = jnp.where(rows >= lanes, work[...], 0.0)
        below = exact_dot(cross_ref[...], first, ((1,), (1,)))
        second = jnp.where(lanes > rows, both, mirrored)
        second = jnp.where(lanes == rows, packed_ref[size : size + 1, :], second)
        work[...] = second - exact_dot(below, below, ((1,), (1,)))
        factor_in_place(work, size)
        last = jnp.where(rows >= lanes, work[...], 0.0)
        out_ref[:size, :size] = first
        out_ref[:size, size:] = jnp.zeros((size, size), jnp.float32)
        out_ref[size:, :size] = -exact_dot(
            last, exact_dot(below, first, ((1,), (0,))), ((1,), (0,))
        )
        out_ref[size:, size:] = last

    return pl.pallas_call(
        kernel,
        out_shape=jax.ShapeDtypeStruct((2 * size, 2 * size), jnp.float32),
        scratch_shapes=[pltpu.VMEM((size, size), jnp.float32)],
    )(cross, packed)


def on_device(blocks, col_index, vectors):
    center, scales, carries = filter_coefs(DEGREE)
    row_count = lax.axis_size("row")
    col_count = lax.axis_size("col")
    row_rank = lax.axis_index("row")
    col_rank = lax.axis_index("col")
    core = col_rank % 2
    group_rows, _, width, _ = blocks.shape
    piece_rows, states = vectors.shape
    half = states // 2
    tile_blocks = piece_rows // width * row_count
    tile_rows = tile_blocks * width
    row_bits = bits_below(row_count)
    z_bits = [2 * bit for bit in bits_below(col_count // 2)]
    narrow = jnp.bfloat16

    mine_first = core == 0
    left, right = vectors[:, :half], vectors[:, half:]
    own_start = jnp.where(mine_first, left, right)
    other_start = swap(jnp.where(mine_first, right, left), "col", 1)
    start = jnp.stack([own_start, other_start])
    low_start = start.astype(narrow)

    arrived = [low_start] + [swap(low_start, "row", k) for k in range(1, row_count)]
    arrived = jnp.stack(arrived)
    ordered = jnp.stack([lax.dynamic_index_in_dim(arrived, row_rank ^ k, 0, False) for k in range(row_count)])
    low_own = ordered[:, 0].reshape(tile_rows, half)
    low_other = ordered[:, 1].reshape(tile_rows, half)

    own = densify(blocks, col_index, tile_blocks)
    other = swap(own, "col", 1)

    first_row = row_rank * group_rows
    own_offset = first_row - col_rank * tile_blocks
    other_offset = first_row - (col_rank ^ 1) * tile_blocks

    def rows_from(value, offset, value_blocks, wanted_blocks):
        edge = jnp.zeros((wanted_blocks * width, value.shape[1]), value.dtype)
        padded = jnp.concatenate([edge, value, edge])
        begin = jnp.clip(offset + wanted_blocks, 0, value_blocks + wanted_blocks)
        return lax.dynamic_slice_in_dim(padded, begin * width, wanted_blocks * width, 0)

    def forward(low_own, low_other):
        product = jnp.dot(own, low_own, preferred_element_type=jnp.float32)
        product = product + jnp.dot(other, low_other, preferred_element_type=jnp.float32)
        diagonal = rows_from(low_own, own_offset, tile_blocks, group_rows).astype(jnp.float32)
        diagonal += rows_from(low_other, other_offset, tile_blocks, group_rows).astype(jnp.float32)
        return product - center * diagonal

    def backward(low):
        def part(tile, offset):
            product = lax.dot_general(tile, low, (((0,), (0,)), ((), ())), preferred_element_type=jnp.float32)
            diagonal = rows_from(low, -offset, group_rows, tile_blocks).astype(jnp.float32)
            return product - center * diagonal

        return part(own, own_offset), part(other, other_offset)

    def halves_of(value, bit):
        rows = value.shape[0] // 2
        upper = (col_rank & bit) != 0
        first, second = value[:rows], value[rows:]
        return jnp.where(upper, second, first), jnp.where(upper, first, second)

    def sum_over_z(value):
        for bit in z_bits[:-1]:
            kept, sent = halves_of(value, bit)
            value = kept + swap(sent.astype(narrow), "col", bit).astype(jnp.float32)
        for bit in z_bits[-1:]:
            sent = value.astype(narrow)
            value = sent.astype(jnp.float32) + swap(sent, "col", bit).astype(jnp.float32)
        return value

    def gather_over_z(value):
        for bit in reversed(z_bits[:-1]):
            partner = swap(value, "col", bit)
            upper = (col_rank & bit) != 0
            value = jnp.concatenate(
                [jnp.where(upper, partner, value), jnp.where(upper, value, partner)]
            )
        return value

    def sum_over_row(one, two):
        for bit_one, bit_two in zip(row_bits, reversed(row_bits)):
            one, two = one + swap(one, "row", bit_one), two + swap(two, "row", bit_two)
        return one, two

    def placed(piece):
        here = jnp.arange(row_count)[:, None, None] == row_rank
        return jnp.where(here, piece[None], 0.0).reshape(tile_rows, half)

    y1 = scales[0] * sum_over_z(forward(low_own, low_other))
    low = gather_over_z(y1.astype(narrow))
    part_own, part_other = backward(low)
    y2_own, y2_other = sum_over_row(
        scales[1] * part_own - carries[1] * placed(start[0]),
        scales[1] * part_other - carries[1] * placed(start[1]),
    )
    y3 = scales[2] * sum_over_z(forward(y2_own.astype(narrow), y2_other.astype(narrow))) - carries[2] * y1
    low = gather_over_z(y3.astype(narrow))
    part_own, part_other = backward(low)
    image_own, image_other = sum_over_row(part_own, part_other)
    y4_own = scales[3] * image_own - carries[3] * y2_own
    y4_other = scales[3] * image_other - carries[3] * y2_other

    partner = swap(y4_other, "col", 1)
    filtered = jnp.concatenate(
        [jnp.where(mine_first, y4_own, partner), jnp.where(mine_first, partner, y4_own)], axis=1
    )
    gram = exact_dot(filtered, filtered, ((0,), (0,)))
    rows = lax.broadcasted_iota(jnp.int32, (half, half), 0)
    lanes = lax.broadcasted_iota(jnp.int32, (half, half), 1)
    corner = gram[half:, half:]
    cross = gram[half:, :half]
    packed = jnp.where(rows >= lanes, gram[:half, :half], corner)
    diagonal = jnp.sum(jnp.where(rows == lanes, corner, 0.0), axis=0, keepdims=True)
    cross = jnp.pad(cross, ((0, 8), (0, 0)))
    packed = jnp.concatenate([packed, diagonal, jnp.zeros((7, half), jnp.float32)])
    total = jnp.where(mine_first, cross, packed) + swap(jnp.where(mine_first, packed, cross), "col", 1)
    for bit in z_bits:
        total = total + swap(total, "col", bit)
    partner = swap(total, "col", 1)
    cross = jnp.where(mine_first, total, partner)[:half]
    packed = jnp.where(mine_first, partner, total)
    inverse = inverse_factor(cross, packed)

    mine = lax.dynamic_slice_in_dim(filtered, row_rank * piece_rows, piece_rows, 0)
    orbital_count = piece_rows * row_count * col_count
    return math.sqrt(orbital_count) * exact_dot(mine, inverse, ((1,), (1,)))


def solution(mesh):
    return jax.shard_map(
        on_device,
        mesh=mesh,
        in_specs=(P("row", "col", None, None), P("row", "col"), P(("col", "row"), None)),
        out_specs=P(("col", "row"), None),
        check_vma=False,
    )
```

time: 422 us -> 138 us (0.33)
  waiting for transfers between devices: 240 us -> 54.6 us
  other arithmetic: 59.9 us -> 3.34 us
  blocking collectives: 49.6 us -> 0 us
  Pallas kernels: 0 us -> 34.9 us
  starting transfers between devices: 0.17 us -> 31.7 us
  local copies, waits for them, and re-layouts: 25.4 us -> 0.26 us
  matrix products: 32.1 us -> 12.2 us
  between operations: 14.5 us -> 0.31 us
    psum x1 -> x0, waiting for transfers between devices: 128 us -> none  [on_device(): gram_sum = lax.psum(local_gram, ('row', 'col'))]
    reduce_scatter x4 -> x0, waiting for transfers between devices: 111 us -> none  [the longest x2 65.1 us: on_device(): lax.psum_scatter((forward_summed - center * forward_shifted).reshape(grou...]
    ppermute x0 -> x24, waiting for transfers between devices: none -> 54.6 us  [swap(): return lax.ppermute(value, axis, [(i, i ^ distance) for i in range(count)])]
    another operation x9 -> x6, other arithmetic: 53.7 us -> 0.98 us  [the longest x4 0.91 us: on_device(): start = jnp.stack([own_start, other_start])]
    all_gather x4 -> x0, blocking collectives: 49.6 us -> none  [the longest x2 30.2 us: on_device(): gathered = lax.all_gather(lowered, 'col', axis=0, tiled=True)]
    pallas_call x0 -> x2, Pallas kernels: none -> 34.9 us  [the longest x1 28.8 us: inverse_factor(): pl.pallas_call(kernel, out_shape=jax.ShapeDtypeStruct((2 * size, 2 * size...]
    ppermute x0 -> x24, starting transfers between devices: none -> 31.7 us  [swap(): return lax.ppermute(value, axis, [(i, i ^ distance) for i in range(count)])]
    dot_general x12 -> x10, matrix products: 30.8 us -> 12.2 us  [the longest x2 3.65 us: forward(): product = jnp.dot(own, low_own, preferred_element_type=jnp.float32)]
  transfers between devices with their start and end apart: 5 -> 24, of which waited for: 5 -> 20; matrix products, arithmetic and copies ran while one was open for 0% -> 1% of each run, Pallas kernels for 0% -> 5%
where the time goes in v1:
time: 138 us; the launch traced here: 137 us
  waiting for transfers between devices  54.6 us (40%)
  Pallas kernels  34.9 us (25%)
  starting transfers between devices  31.7 us (23%)
  matrix products  12.2 us (9%)
  other arithmetic  3.34 us (2%)
    ppermute x24, waiting for transfers between devices, swap(): return lax.ppermute(value, axis, [(i, i ^ distance) for i in range(count)])  54.6 us
    ppermute x24, starting transfers between devices, swap(): return lax.ppermute(value, axis, [(i, i ^ distance) for i in range(count)])  31.7 us
    pallas_call x1, Pallas kernels, inverse_factor(): pl.pallas_call(kernel, out_shape=jax.ShapeDtypeStruct((2 * size, 2 * size...  28.8 us
    pallas_call x1, Pallas kernels, densify(): pl.pallas_call(kernel, grid_spec=pltpu.PrefetchScalarGridSpec(num_scalar_...  6.19 us
    dot_general x2, matrix products, forward(): product = jnp.dot(own, low_own, preferred_element_type=jnp.float32)  3.65 us
    dot_general x2, matrix products, forward(): jnp.dot(other, low_other, preferred_element_type=jnp.float32)  3.65 us
    dot_general x2, matrix products, exact_dot(): lax.dot_general(a, b, (dims, ((), ())), precision=lax.Precision.HIGHEST,...  3.03 us
  transfers between devices with their start and end apart: 24, of which 20 were waited for; matrix products, arithmetic and copies ran while one was open for 1% of the time, Pallas kernels for 5%

profile of v1, /device:TPU:0, one launch (start us, length us, event | category | flops | bytes accessed | tf_op | source)
XLA Modules:
  0.0 137.4 jit_solution(450081262419117685)
XLA Ops:
  1.4 6.2 %shard_map.37 = bf16[1024,512]{1,0:T(8,128)(2,1)} custom-call(s32[8,6]{1,0:T(8,128)} %index_ref.1, bf16[8,6,128,128]{3,2,1,0:T(8,128)(2,1)} %blocks_ref.1), custom_call_target="tpu_custom_call" | custom-call | tf_op jit(solution)/shard_map/pallas_call | solution.py:56
  7.7 4.0 %collective-permute-start.3 = (bf16[2,128,128]{2,1,0:T(8,128)(2,1)S(1)}, bf16[2,128,128]{2,1,0:T(8,128)(2,1)S(1)}, u32[]{:S(2)}, u32[]{:S(2)}) collective-permute-start(bf16[2,128,128]{2,1,0:T(8,128)(2,1)S(1)} %pad_maximum_fusion.14), channel_id=1, source_target_pairs={{0,24},{8,16},{16,8},{24,0},{1,25},{9,17},{17,9},{25,1},{2,26},{10... | collective-permute-start | bytes 196616 | tf_op jit(solution)/shard_map/ppermute | solution.py:35
  14.0 2.0 %collective-permute-done.2 = bf16[2,128,128]{2,1,0:T(8,128)(2,1)S(1)} collective-permute-done((bf16[2,128,128]{2,1,0:T(8,128)(2,1)S(1)}, bf16[2,128,128]{2,1,0:T(8,128)(2,1)S(1)}, u32[]{:S(2)}, u32[]{:S(2)}) %collective-permute-start.2) | collective-permute-done | bytes 65568 | tf_op jit(solution)/shard_map/ppermute | solution.py:35
  17.1 3.2 %fusion = f32[1024,128]{1,0:T(8,128)S(1)} fusion(f32[1024,128]{1,0:T(8,128)S(1)} %fusion.29, bf16[1024,512]{1,0:T(8,128)(2,1)S(1)} %collective-permute-done.4, bf16[512,128]{1,0:T(8,128)(2,1)S(1)} %bitcast.39, s32[]{:T(128)S(6)} %select_n.147, bf16[1024,128]{1,0:T(8,128)(2,1)S(1)} %broadcast.37, s32[]{:T(128)S(6)} %select_n.146, ...), kind=kOutput, calls=%fused_computation.2 | convolution fusion | flops 136183808 | bytes 2752520 | tf_op jit(solution)/shard_map/dot_general | solution.py:173
  22.0 3.4 %collective-permute-done.5 = bf16[512,128]{1,0:T(8,128)(2,1)S(1)} collective-permute-done((bf16[512,128]{1,0:T(8,128)(2,1)S(1)}, bf16[512,128]{1,0:T(8,128)(2,1)S(1)}, u32[]{:S(2)}, u32[]{:S(2)}) %collective-permute-start.5) | collective-permute-done | bytes 131104 | tf_op jit(solution)/shard_map/ppermute | solution.py:35
  25.5 2.6 %collective-permute-start.6 = (bf16[512,128]{1,0:T(8,128)(2,1)S(1)}, bf16[512,128]{1,0:T(8,128)(2,1)S(1)}, u32[]{:S(2)}, u32[]{:S(2)}) collective-permute-start(bf16[512,128]{1,0:T(8,128)(2,1)S(1)} %add_convert_fusion.1), channel_id=1, source_target_pairs={{0,4},{1,5},{2,6},{3,7},{4,0},{5,1},{6,2},{7,3},{8,12},{9,13},{10,... | collective-permute-start | bytes 393224 | tf_op jit(solution)/shard_map/ppermute | solution.py:35
  28.1 4.8 %collective-permute-done.6 = bf16[512,128]{1,0:T(8,128)(2,1)S(1)} collective-permute-done((bf16[512,128]{1,0:T(8,128)(2,1)S(1)}, bf16[512,128]{1,0:T(8,128)(2,1)S(1)}, u32[]{:S(2)}, u32[]{:S(2)}) %collective-permute-start.6) | collective-permute-done | bytes 131104 | tf_op jit(solution)/shard_map/ppermute | solution.py:35
  33.8 4.2 %collective-permute-done.7 = bf16[512,128]{1,0:T(8,128)(2,1)S(1)} collective-permute-done((bf16[512,128]{1,0:T(8,128)(2,1)S(1)}, bf16[512,128]{1,0:T(8,128)(2,1)S(1)}, u32[]{:S(2)}, u32[]{:S(2)}) %collective-permute-start.7) | collective-permute-done | bytes 131104 | tf_op jit(solution)/shard_map/ppermute | solution.py:35
  41.2 3.8 %collective-permute-done.8 = f32[512,128]{1,0:T(8,128)S(1)} collective-permute-done((f32[512,128]{1,0:T(8,128)S(1)}, f32[512,128]{1,0:T(8,128)S(1)}, u32[]{:S(2)}, u32[]{:S(2)}) %collective-permute-start.8) | collective-permute-done | bytes 262176 | tf_op jit(solution)/shard_map/ppermute | solution.py:35
  45.1 2.5 %collective-permute-start.9 = (f32[512,128]{1,0:T(8,128)S(1)}, f32[512,128]{1,0:T(8,128)S(1)}, u32[]{:S(2)}, u32[]{:S(2)}) collective-permute-start(f32[512,128]{1,0:T(8,128)S(1)} %add.126), channel_id=1, source_target_pairs={{0,16},{8,24},{16,0},{24,8},{1,17},{9,25},{17,1},{25,9},{2,18},{10... | collective-permute-start | bytes 786440 | tf_op jit(solution)/shard_map/ppermute | solution.py:35
  52.0 3.4 %collective-permute-done.11 = f32[512,128]{1,0:T(8,128)S(1)} collective-permute-done((f32[512,128]{1,0:T(8,128)S(1)}, f32[512,128]{1,0:T(8,128)S(1)}, u32[]{:S(2)}, u32[]{:S(2)}) %collective-permute-start.11) | collective-permute-done | bytes 262176 | tf_op jit(solution)/shard_map/ppermute | solution.py:35
  55.8 3.2 %fusion.1 = f32[1024,128]{1,0:T(8,128)S(1)} fusion(f32[1024,128]{1,0:T(8,128)S(1)} %fusion.30, bf16[1024,512]{1,0:T(8,128)(2,1)S(1)} %copy-done, bf16[512,128]{1,0:T(8,128)(2,1)S(1)} %add_convert_fusion.3, s32[]{:T(128)S(6)} %select_n.147, bf16[1024,128]{1,0:T(8,128)(2,1)S(1)} %broadcast.37, s32[]{:T(128)S(6)} %select_n.146, ...), kind=kOutput, calls=%fused_computation.3 | convolution fusion | flops 136183808 | bytes 2752520 | tf_op jit(solution)/shard_map/dot_general | solution.py:172
  60.6 3.7 %collective-permute-done.12 = bf16[512,128]{1,0:T(8,128)(2,1)S(1)} collective-permute-done((bf16[512,128]{1,0:T(8,128)(2,1)S(1)}, bf16[512,128]{1,0:T(8,128)(2,1)S(1)}, u32[]{:S(2)}, u32[]{:S(2)}) %collective-permute-start.12) | collective-permute-done | bytes 131104 | tf_op jit(solution)/shard_map/ppermute | solution.py:35
  64.3 2.7 %collective-permute-start.13 = (bf16[512,128]{1,0:T(8,128)(2,1)S(1)}, bf16[512,128]{1,0:T(8,128)(2,1)S(1)}, u32[]{:S(2)}, u32[]{:S(2)}) collective-permute-start(bf16[512,128]{1,0:T(8,128)(2,1)S(1)} %add_convert_fusion), channel_id=1, source_target_pairs={{0,4},{1,5},{2,6},{3,7},{4,0},{5,1},{6,2},{7,3},{8,12},{9,13},{10,... | collective-permute-start | bytes 393224 | tf_op jit(solution)/shard_map/ppermute | solution.py:35
  67.0 3.2 %collective-permute-done.13 = bf16[512,128]{1,0:T(8,128)(2,1)S(1)} collective-permute-done((bf16[512,128]{1,0:T(8,128)(2,1)S(1)}, bf16[512,128]{1,0:T(8,128)(2,1)S(1)}, u32[]{:S(2)}, u32[]{:S(2)}) %collective-permute-start.13) | collective-permute-done | bytes 131104 | tf_op jit(solution)/shard_map/ppermute | solution.py:35
  70.3 2.2 %collective-permute-start.14 = (bf16[512,128]{1,0:T(8,128)(2,1)S(1)}, bf16[512,128]{1,0:T(8,128)(2,1)S(1)}, u32[]{:S(2)}, u32[]{:S(2)}) collective-permute-start(bf16[512,128]{1,0:T(8,128)(2,1)S(1)} %subtract_convert_fusion), channel_id=1, source_target_pairs={{0,2},{1,3},{2,0},{3,1},{4,6},{5,7},{6,4},{7,5},{8,10},{9,11},{10,... | collective-permute-start | bytes 393224 | tf_op jit(solution)/shard_map/ppermute | solution.py:35
  72.5 2.9 %collective-permute-done.14 = bf16[512,128]{1,0:T(8,128)(2,1)S(1)} collective-permute-done((bf16[512,128]{1,0:T(8,128)(2,1)S(1)}, bf16[512,128]{1,0:T(8,128)(2,1)S(1)}, u32[]{:S(2)}, u32[]{:S(2)}) %collective-permute-start.14) | collective-permute-done | bytes 131104 | tf_op jit(solution)/shard_map/ppermute | solution.py:35
  79.2 3.9 %collective-permute-done.17 = f32[512,128]{1,0:T(8,128)S(1)} collective-permute-done((f32[512,128]{1,0:T(8,128)S(1)}, f32[512,128]{1,0:T(8,128)S(1)}, u32[]{:S(2)}, u32[]{:S(2)}) %collective-permute-start.17) | collective-permute-done | bytes 262176 | tf_op jit(solution)/shard_map/ppermute | solution.py:35
  85.7 3.9 %collective-permute-done.18 = f32[512,128]{1,0:T(8,128)S(1)} collective-permute-done((f32[512,128]{1,0:T(8,128)S(1)}, f32[512,128]{1,0:T(8,128)S(1)}, u32[]{:S(2)}, u32[]{:S(2)}) %collective-permute-start.18) | collective-permute-done | bytes 262176 | tf_op jit(solution)/shard_map/ppermute | solution.py:35
  95.4 3.3 %collective-permute-done.21 = f32[136,128]{1,0:T(8,128)S(1)} collective-permute-done((f32[136,128]{1,0:T(8,128)S(1)}, f32[136,128]{1,0:T(8,128)S(1)}, u32[]{:S(2)}, u32[]{:S(2)}) %collective-permute-start.21) | collective-permute-done | bytes 69664 | tf_op jit(solution)/shard_map/ppermute | solution.py:35
  98.7 2.6 %collective-permute-start.22 = (f32[136,128]{1,0:T(8,128)S(1)}, f32[136,128]{1,0:T(8,128)S(1)}, u32[]{:S(2)}, u32[]{:S(2)}) collective-permute-start(f32[136,128]{1,0:T(8,128)S(1)} %add.142), channel_id=1, source_target_pairs={{0,4},{1,5},{2,6},{3,7},{4,0},{5,1},{6,2},{7,3},{8,12},{9,13},{10,... | collective-permute-start | bytes 208904 | tf_op jit(solution)/shard_map/ppermute | solution.py:35
  101.3 2.7 %collective-permute-done.22 = f32[136,128]{1,0:T(8,128)S(1)} collective-permute-done((f32[136,128]{1,0:T(8,128)S(1)}, f32[136,128]{1,0:T(8,128)S(1)}, u32[]{:S(2)}, u32[]{:S(2)}) %collective-permute-start.22) | collective-permute-done | bytes 69664 | tf_op jit(solution)/shard_map/ppermute | solution.py:35
  106.7 28.8 %shard_map.38 = f32[256,256]{1,0:T(8,128)} custom-call(f32[128,128]{1,0:T(8,128)} %slice_select_fusion.cross_ref, f32[136,128]{1,0:T(8,128)} %broadcast_select_fusion.6.packed_ref), custom_call_target="tpu_custom_call" | custom-call | tf_op jit(solution)/shard_map/pallas_call | solution.py:122
  135.4 2.0 %convolution_multiply_fusion = f32[128,256]{1,0:T(8,128)} fusion(f32[256,256]{1,0:T(8,128)} %shard_map.38, s32[]{:T(128)S(6)} %select_n.162, f32[512,128]{1,0:T(8,128)S(1)} %get-tuple-element.5, f32[512,128]{1,0:T(8,128)S(1)} %broadcast_select_fusion.4), kind=kOutput, calls=%fused_computation.12 | convolution fusion | flops 100728832 | bytes 917508 | tf_op jit(solution)/shard_map/dot_general | solution.py:69
  (79 shorter events, 31.8 us)
Async XLA Ops:
  0.9 6.8 %collective-permute-start = (f32[128,128]{1,0:T(8,128)S(1)}, f32[128,128]{1,0:T(8,128)S(1)}, u32[]{:S(2)}, u32[]{:S(2)}) collective-permute-start(f32[128,128]{1,0:T(8,128)S(1)} %get-tuple-element.22), channel_id=1, source_target_pairs={{0,1},{1,0},{2,3},{3,2},{4,5},{5,4},{6,7},{7,6},{8,9},{9,8},{10,11... | collective-permute-start | bytes 196616 | tf_op jit(solution)/shard_map/ppermute | solution.py:35
  7.6 9.5 %collective-permute-start.4 = (bf16[1024,512]{1,0:T(8,128)(2,1)}, bf16[1024,512]{1,0:T(8,128)(2,1)S(1)}, u32[]{:S(2)}, u32[]{:S(2)}) collective-permute-start(bf16[1024,512]{1,0:T(8,128)(2,1)} %shard_map.37), channel_id=1, source_target_pairs={{0,1},{1,0},{2,3},{3,2},{4,5},{5,4},{6,7},{7,6},{8,9},{9,8},{10,11... | collective-permute-start | bytes 3145736 | tf_op jit(solution)/shard_map/ppermute | solution.py:35
  7.7 6.3 %collective-permute-start.3 = (bf16[2,128,128]{2,1,0:T(8,128)(2,1)S(1)}, bf16[2,128,128]{2,1,0:T(8,128)(2,1)S(1)}, u32[]{:S(2)}, u32[]{:S(2)}) collective-permute-start(bf16[2,128,128]{2,1,0:T(8,128)(2,1)S(1)} %pad_maximum_fusion.14), channel_id=1, source_target_pairs={{0,24},{8,16},{16,8},{24,0},{1,25},{9,17},{17,9},{25,1},{2,26},{10... | collective-permute-start | bytes 196616 | tf_op jit(solution)/shard_map/ppermute | solution.py:35
  11.7 4.3 %collective-permute-start.2 = (bf16[2,128,128]{2,1,0:T(8,128)(2,1)S(1)}, bf16[2,128,128]{2,1,0:T(8,128)(2,1)S(1)}, u32[]{:S(2)}, u32[]{:S(2)}) collective-permute-start(bf16[2,128,128]{2,1,0:T(8,128)(2,1)S(1)} %pad_maximum_fusion.14), channel_id=1, source_target_pairs={{0,16},{8,24},{16,0},{24,8},{1,17},{9,25},{17,1},{25,9},{2,18},{10... | collective-permute-start | bytes 196616 | tf_op jit(solution)/shard_map/ppermute | solution.py:35
  12.2 4.3 %collective-permute-start.1 = (bf16[2,128,128]{2,1,0:T(8,128)(2,1)S(1)}, bf16[2,128,128]{2,1,0:T(8,128)(2,1)S(1)}, u32[]{:S(2)}, u32[]{:S(2)}) collective-permute-start(bf16[2,128,128]{2,1,0:T(8,128)(2,1)S(1)} %pad_maximum_fusion.14), channel_id=1, source_target_pairs={{0,8},{8,0},{16,24},{24,16},{1,9},{9,1},{17,25},{25,17},{2,10},{10... | collective-permute-start | bytes 196616 | tf_op jit(solution)/shard_map/ppermute | solution.py:35
  20.4 5.0 %collective-permute-start.5 = (bf16[512,128]{1,0:T(8,128)(2,1)S(1)}, bf16[512,128]{1,0:T(8,128)(2,1)S(1)}, u32[]{:S(2)}, u32[]{:S(2)}) collective-permute-start(bf16[512,128]{1,0:T(8,128)(2,1)S(1)} %select_convert_fusion.1), channel_id=1, source_target_pairs={{0,2},{1,3},{2,0},{3,1},{4,6},{5,7},{6,4},{7,5},{8,10},{9,11},{10,... | collective-permute-start | bytes 393224 | tf_op jit(solution)/shard_map/ppermute | solution.py:35
  25.5 7.4 %collective-permute-start.6 = (bf16[512,128]{1,0:T(8,128)(2,1)S(1)}, bf16[512,128]{1,0:T(8,128)(2,1)S(1)}, u32[]{:S(2)}, u32[]{:S(2)}) collective-permute-start(bf16[512,128]{1,0:T(8,128)(2,1)S(1)} %add_convert_fusion.1), channel_id=1, source_target_pairs={{0,4},{1,5},{2,6},{3,7},{4,0},{5,1},{6,2},{7,3},{8,12},{9,13},{10,... | collective-permute-start | bytes 393224 | tf_op jit(solution)/shard_map/ppermute | solution.py:35
  33.0 5.0 %collective-permute-start.7 = (bf16[512,128]{1,0:T(8,128)(2,1)S(1)}, bf16[512,128]{1,0:T(8,128)(2,1)S(1)}, u32[]{:S(2)}, u32[]{:S(2)}) collective-permute-start(bf16[512,128]{1,0:T(8,128)(2,1)S(1)} %multiply_convert_fusion), channel_id=1, source_target_pairs={{0,2},{1,3},{2,0},{3,1},{4,6},{5,7},{6,4},{7,5},{8,10},{9,11},{10,... | collective-permute-start | bytes 393224 | tf_op jit(solution)/shard_map/ppermute | solution.py:35
  38.6 6.4 %collective-permute-start.8 = (f32[512,128]{1,0:T(8,128)S(1)}, f32[512,128]{1,0:T(8,128)S(1)}, u32[]{:S(2)}, u32[]{:S(2)}) collective-permute-start(f32[512,128]{1,0:T(8,128)S(1)} %fusion.5), channel_id=1, source_target_pairs={{0,8},{8,0},{16,24},{24,16},{1,9},{9,1},{17,25},{25,17},{2,10},{10... | collective-permute-start | bytes 786440 | tf_op jit(solution)/shard_map/ppermute | solution.py:35
  40.5 8.4 %collective-permute-start.10 = (f32[512,128]{1,0:T(8,128)S(1)}, f32[512,128]{1,0:T(8,128)S(1)}, u32[]{:S(2)}, u32[]{:S(2)}) collective-permute-start(f32[512,128]{1,0:T(8,128)S(1)} %fusion.3), channel_id=1, source_target_pairs={{0,16},{8,24},{16,0},{24,8},{1,17},{9,25},{17,1},{25,9},{2,18},{10... | collective-permute-start | bytes 786440 | tf_op jit(solution)/shard_map/ppermute | solution.py:35
  45.1 6.9 %collective-permute-start.9 = (f32[512,128]{1,0:T(8,128)S(1)}, f32[512,128]{1,0:T(8,128)S(1)}, u32[]{:S(2)}, u32[]{:S(2)}) collective-permute-start(f32[512,128]{1,0:T(8,128)S(1)} %add.126), channel_id=1, source_target_pairs={{0,16},{8,24},{16,0},{24,8},{1,17},{9,25},{17,1},{25,9},{2,18},{10... | collective-permute-start | bytes 786440 | tf_op jit(solution)/shard_map/ppermute | solution.py:35
  48.9 6.4 %collective-permute-start.11 = (f32[512,128]{1,0:T(8,128)S(1)}, f32[512,128]{1,0:T(8,128)S(1)}, u32[]{:S(2)}, u32[]{:S(2)}) collective-permute-start(f32[512,128]{1,0:T(8,128)S(1)} %add.130), channel_id=1, source_target_pairs={{0,8},{8,0},{16,24},{24,16},{1,9},{9,1},{17,25},{25,17},{2,10},{10... | collective-permute-start | bytes 786440 | tf_op jit(solution)/shard_map/ppermute | solution.py:35
  59.1 5.2 %collective-permute-start.12 = (bf16[512,128]{1,0:T(8,128)(2,1)S(1)}, bf16[512,128]{1,0:T(8,128)(2,1)S(1)}, u32[]{:S(2)}, u32[]{:S(2)}) collective-permute-start(bf16[512,128]{1,0:T(8,128)(2,1)S(1)} %select_convert_fusion), channel_id=1, source_target_pairs={{0,2},{1,3},{2,0},{3,1},{4,6},{5,7},{6,4},{7,5},{8,10},{9,11},{10,... | collective-permute-start | bytes 393224 | tf_op jit(solution)/shard_map/ppermute | solution.py:35
  64.3 5.9 %collective-permute-start.13 = (bf16[512,128]{1,0:T(8,128)(2,1)S(1)}, bf16[512,128]{1,0:T(8,128)(2,1)S(1)}, u32[]{:S(2)}, u32[]{:S(2)}) collective-permute-start(bf16[512,128]{1,0:T(8,128)(2,1)S(1)} %add_convert_fusion), channel_id=1, source_target_pairs={{0,4},{1,5},{2,6},{3,7},{4,0},{5,1},{6,2},{7,3},{8,12},{9,13},{10,... | collective-permute-start | bytes 393224 | tf_op jit(solution)/shard_map/ppermute | solution.py:35
  70.3 5.2 %collective-permute-start.14 = (bf16[512,128]{1,0:T(8,128)(2,1)S(1)}, bf16[512,128]{1,0:T(8,128)(2,1)S(1)}, u32[]{:S(2)}, u32[]{:S(2)}) collective-permute-start(bf16[512,128]{1,0:T(8,128)(2,1)S(1)} %subtract_convert_fusion), channel_id=1, source_target_pairs={{0,2},{1,3},{2,0},{3,1},{4,6},{5,7},{6,4},{7,5},{8,10},{9,11},{10,... | collective-permute-start | bytes 393224 | tf_op jit(solution)/shard_map/ppermute | solution.py:35
  76.0 7.1 %collective-permute-start.17 = (f32[512,128]{1,0:T(8,128)S(1)}, f32[512,128]{1,0:T(8,128)S(1)}, u32[]{:S(2)}, u32[]{:S(2)}) collective-permute-start(f32[512,128]{1,0:T(8,128)S(1)} %convolution_subtract_fusion), channel_id=1, source_target_pairs={{0,16},{8,24},{16,0},{24,8},{1,17},{9,25},{17,1},{25,9},{2,18},{10... | collective-permute-start | bytes 786440 | tf_op jit(solution)/shard_map/ppermute | solution.py:35
  78.5 6.6 %collective-permute-start.15 = (f32[512,128]{1,0:T(8,128)S(1)}, f32[512,128]{1,0:T(8,128)S(1)}, u32[]{:S(2)}, u32[]{:S(2)}) collective-permute-start(f32[512,128]{1,0:T(8,128)S(1)} %convolution_subtract_fusion.1), channel_id=1, source_target_pairs={{0,8},{8,0},{16,24},{24,16},{1,9},{9,1},{17,25},{25,17},{2,10},{10... | collective-permute-start | bytes 786440 | tf_op jit(solution)/shard_map/ppermute | solution.py:35
  83.1 6.4 %collective-permute-start.18 = (f32[512,128]{1,0:T(8,128)S(1)}, f32[512,128]{1,0:T(8,128)S(1)}, u32[]{:S(2)}, u32[]{:S(2)}) collective-permute-start(f32[512,128]{1,0:T(8,128)S(1)} %add.138), channel_id=1, source_target_pairs={{0,8},{8,0},{16,24},{24,16},{1,9},{9,1},{17,25},{25,17},{2,10},{10... | collective-permute-start | bytes 786440 | tf_op jit(solution)/shard_map/ppermute | solution.py:35
  85.2 6.4 %collective-permute-start.16 = (f32[512,128]{1,0:T(8,128)S(1)}, f32[512,128]{1,0:T(8,128)S(1)}, u32[]{:S(2)}, u32[]{:S(2)}) collective-permute-start(f32[512,128]{1,0:T(8,128)S(1)} %add.136), channel_id=1, source_target_pairs={{0,16},{8,24},{16,0},{24,8},{1,17},{9,25},{17,1},{25,9},{2,18},{10... | collective-permute-start | bytes 786440 | tf_op jit(solution)/shard_map/ppermute | solution.py:35
  89.6 2.0 %collective-permute-start.19 = (f32[512,128]{1,0:T(8,128)S(1)}, f32[512,128]{1,0:T(8,128)S(1)}, u32[]{:S(2)}, u32[]{:S(2)}) collective-permute-start(f32[512,128]{1,0:T(8,128)S(1)} %multiply_subtract_fusion), channel_id=1, source_target_pairs={{0,1},{1,0},{2,3},{3,2},{4,5},{5,4},{6,7},{7,6},{8,9},{9,8},{10,11... | collective-permute-start | bytes 786440 | tf_op jit(solution)/shard_map/ppermute | solution.py:35
  92.9 1.3 collective-permute-start.20
  94.3 4.4 %collective-permute-start.21 = (f32[136,128]{1,0:T(8,128)S(1)}, f32[136,128]{1,0:T(8,128)S(1)}, u32[]{:S(2)}, u32[]{:S(2)}) collective-permute-start(f32[136,128]{1,0:T(8,128)S(1)} %select_add_fusion), channel_id=1, source_target_pairs={{0,2},{1,3},{2,0},{3,1},{4,6},{5,7},{6,4},{7,5},{8,10},{9,11},{10,... | collective-permute-start | bytes 208904 | tf_op jit(solution)/shard_map/ppermute | solution.py:35
  98.7 5.4 %collective-permute-start.22 = (f32[136,128]{1,0:T(8,128)S(1)}, f32[136,128]{1,0:T(8,128)S(1)}, u32[]{:S(2)}, u32[]{:S(2)}) collective-permute-start(f32[136,128]{1,0:T(8,128)S(1)} %add.142), channel_id=1, source_target_pairs={{0,4},{1,5},{2,6},{3,7},{4,0},{5,1},{6,2},{7,3},{8,12},{9,13},{10,... | collective-permute-start | bytes 208904 | tf_op jit(solution)/shard_map/ppermute | solution.py:35
  104.1 1.3 collective-permute-start.23
  (1 other events, 9.0 us)

commit v2 on v1

--- a/solution.py
+++ b/solution.py
@@ -41,25 +41,27 @@
 
 def densify(blocks, col_index, tile_blocks):
     group_rows, slots, width, _ = blocks.shape
+    slots = min(slots, tile_blocks)
+    step = 2
 
     def kernel(index_ref, blocks_ref, tile_ref):
-        row = pl.program_id(0)
-        tile_ref[...] = jnp.zeros_like(tile_ref)
-        for slot in range(slots):
-            place = index_ref[row, slot]
-
-            @pl.when(place >= 0)
-            def _():
-                start = pl.multiple_of(lax.rem(place, tile_blocks) * width, width)
-                tile_ref[:, pl.ds(start, width)] = blocks_ref[0, slot]
+        nothing = jnp.zeros((width, width), blocks.dtype)
+        for inner in range(step):
+            places = [index_ref[pl.program_id(0) * step + inner, slot] for slot in range(slots)]
+            places = [jnp.where(place >= 0, lax.rem(place, tile_blocks), -1) for place in places]
+            for column in range(tile_blocks):
+                value = nothing
+                for slot in range(slots):
+                    value = jnp.where(places[slot] == column, blocks_ref[inner, slot], value)
+                tile_ref[inner * width : (inner + 1) * width, column * width : (column + 1) * width] = value
 
     return pl.pallas_call(
         kernel,
         grid_spec=pltpu.PrefetchScalarGridSpec(
             num_scalar_prefetch=1,
-            grid=(group_rows,),
-            in_specs=[pl.BlockSpec((1, slots, width, width), lambda i, index: (i, 0, 0, 0))],
-            out_specs=pl.BlockSpec((width, tile_blocks * width), lambda i, index: (i, 0)),
+            grid=(group_rows // step,),
+            in_specs=[pl.BlockSpec((step, slots, width, width), lambda i, index: (i, 0, 0, 0))],
+            out_specs=pl.BlockSpec((step * width, tile_blocks * width), lambda i, index: (i, 0)),
         ),
         out_shape=jax.ShapeDtypeStruct((group_rows * width, tile_blocks * width), blocks.dtype),
     )(col_index, blocks)
@@ -71,59 +73,75 @@
     )
 
 
-def factor_in_place(ref, size):
-    rows = lax.broadcasted_iota(jnp.int32, (size, size), 0)
-    lanes = lax.broadcasted_iota(jnp.int32, (size, size), 1)
-    lane_row = lax.broadcasted_iota(jnp.int32, (1, size), 1)
-
-    def pivot(j, unused):
-        row = ref[pl.ds(j, 1), :]
-        here = lane_row == j
-        d = jnp.sum(jnp.where(here, row, 0.0), axis=1, keepdims=True)
-        inv_root = lax.rsqrt(d)
-        inv = 1.0 / d
-        matrix = ref[...]
-        below = rows > j
-        column = jnp.sum(jnp.where(lanes == j, matrix, 0.0), axis=1, keepdims=True)
-        pivot_row = jnp.where(here, 1.0, row)
-        scaled = pivot_row * inv
-        kept = jnp.where((lanes == j) & below, 0.0, matrix)
-        ref[...] = kept - jnp.where(below, column * scaled, 0.0)
-        ref[pl.ds(j, 1), :] = pivot_row * inv_root
-        return unused
-
-    lax.fori_loop(0, size, pivot, 0)
-
-
-def inverse_factor(cross, packed):
-    size = cross.shape[0]
-
-    def kernel(cross_ref, packed_ref, out_ref, work):
+def factor(matrix, tall):
+    size = matrix.shape[1]
+    groups = [matrix[first : first + tall] for first in range(0, size, tall)]
+    sub = lax.broadcasted_iota(jnp.int32, (tall, size), 0)
+    lane = lax.broadcasted_iota(jnp.int32, (tall, size), 1)
+    for number, head in enumerate(groups):
+        first = tall * number
+        block = (lane >= first) & (lane < first + tall)
+        columns = [jnp.broadcast_to(head[:, first + q : first + q + 1], head.shape) for q in range(tall)]
+        x = jnp.where(block, jnp.where(lane - first == sub, 1.0, 0.0), head)
+        z = x
+        pivots = jnp.ones_like(x)
+        inverses = jnp.ones_like(x)
+        for p in range(tall):
+            pivot = columns[p][p : p + 1, :]
+            inverse = 1.0 / pivot
+            ratio = columns[p] * inverse
+            below = jnp.where(sub > p, ratio, 0.0)
+            others = jnp.where(sub == p, 0.0, ratio)
+            for q in range(p + 1, tall):
+                columns[q] = columns[q] - others * columns[q][p : p + 1, :]
+            x = x - below * x[p : p + 1, :]
+            z = z - others * z[p : p + 1, :]
+            pivots = jnp.where(sub == p, pivot, pivots)
+            inverses = jnp.where(sub == p, inverse, inverses)
+        z = z * inverses
+        for later in range(number + 1, len(groups)):
+            value = jnp.where(block, 0.0, groups[later])
+            for p in range(tall):
+                value = value - groups[later][:, first + p : first + p + 1] * z[p : p + 1, :]
+            groups[later] = value
+        groups[number] = x * lax.rsqrt(pivots)
+    return jnp.concatenate(groups)
+
+
+def orthonormal(total, partner, filtered, mine_first, scale):
+    size = total.shape[1]
+    tall = 16
+
+    def kernel(first_ref, total_ref, partner_ref, filtered_ref, out_ref):
         rows = lax.broadcasted_iota(jnp.int32, (size, size), 0)
         lanes = lax.broadcasted_iota(jnp.int32, (size, size), 1)
-        both = packed_ref[:size, :]
+        is_first = first_ref[0] != 0
+        cross = jnp.where(is_first, total_ref[:size, :], partner_ref[:size, :])
+        both = jnp.where(is_first, partner_ref[:size, :], total_ref[:size, :])
+        diagonal = jnp.where(is_first, partner_ref[size : size + 1, :], total_ref[size : size + 1, :])
         mirrored = both.T
-        work[...] = jnp.where(rows >= lanes, both, mirrored)
-        factor_in_place(work, size)
-        first = jnp.where(rows >= lanes, work[...], 0.0)
-        below = exact_dot(cross_ref[...], first, ((1,), (1,)))
+        first = factor(jnp.where(rows >= lanes, both, mirrored), tall)
+        first = jnp.where(rows >= lanes, first, 0.0)
+        below = exact_dot(cross, first, ((1,), (1,)))
         second = jnp.where(lanes > rows, both, mirrored)
-        second = jnp.where(lanes == rows, packed_ref[size : size + 1, :], second)
-        work[...] = second - exact_dot(below, below, ((1,), (1,)))
-        factor_in_place(work, size)
-        last = jnp.where(rows >= lanes, work[...], 0.0)
-        out_ref[:size, :size] = first
-        out_ref[:size, size:] = jnp.zeros((size, size), jnp.float32)
-        out_ref[size:, :size] = -exact_dot(
-            last, exact_dot(below, first, ((1,), (0,))), ((1,), (0,))
-        )
-        out_ref[size:, size:] = last
+        second = jnp.where(lanes == rows, diagonal, second)
+        last = factor(second - exact_dot(below, below, ((1,), (1,))), tall)
+        last = jnp.where(rows >= lanes, last, 0.0)
+        left = exact_dot(filtered_ref[:, :size], first, ((1,), (1,)))
+        out_ref[:, :size] = scale * left
+        right = filtered_ref[:, size:] - exact_dot(left, below, ((1,), (1,)))
+        out_ref[:, size:] = scale * exact_dot(right, last, ((1,), (1,)))
 
     return pl.pallas_call(
         kernel,
-        out_shape=jax.ShapeDtypeStruct((2 * size, 2 * size), jnp.float32),
-        scratch_shapes=[pltpu.VMEM((size, size), jnp.float32)],
-    )(cross, packed)
+        grid_spec=pltpu.PrefetchScalarGridSpec(
+            num_scalar_prefetch=1,
+            grid=(1,),
+            in_specs=[pl.BlockSpec(a.shape, lambda i, first: (0, 0)) for a in (total, partner, filtered)],
+            out_specs=pl.BlockSpec(filtered.shape, lambda i, first: (0, 0)),
+        ),
+        out_shape=jax.ShapeDtypeStruct(filtered.shape, jnp.float32),
+    )(mine_first.astype(jnp.int32).reshape(1), total, partner, filtered)
 
 
 def on_device(blocks, col_index, vectors):
@@ -162,24 +180,28 @@
     own_offset = first_row - col_rank * tile_blocks
     other_offset = first_row - (col_rank ^ 1) * tile_blocks
 
-    def rows_from(value, offset, value_blocks, wanted_blocks):
-        edge = jnp.zeros((wanted_blocks * width, value.shape[1]), value.dtype)
-        padded = jnp.concatenate([edge, value, edge])
-        begin = jnp.clip(offset + wanted_blocks, 0, value_blocks + wanted_blocks)
-        return lax.dynamic_slice_in_dim(padded, begin * width, wanted_blocks * width, 0)
+    segments = group_rows // tile_blocks
+
+    def spread(low, offset):
+        value = low.astype(jnp.float32)
+        return jnp.concatenate(
+            [jnp.where(offset == -k * tile_blocks, value, 0.0) for k in range(segments)]
+        )
+
+    def picked(low, offset):
+        value = low.astype(jnp.float32).reshape(segments, tile_rows, half)
+        parts = [jnp.where(offset == -k * tile_blocks, value[k], 0.0) for k in range(segments)]
+        return sum(parts[1:], parts[0])
 
     def forward(low_own, low_other):
         product = jnp.dot(own, low_own, preferred_element_type=jnp.float32)
         product = product + jnp.dot(other, low_other, preferred_element_type=jnp.float32)
-        diagonal = rows_from(low_own, own_offset, tile_blocks, group_rows).astype(jnp.float32)
-        diagonal += rows_from(low_other, other_offset, tile_blocks, group_rows).astype(jnp.float32)
-        return product - center * diagonal
+        return product - center * (spread(low_own, own_offset) + spread(low_other, other_offset))
 
     def backward(low):
         def part(tile, offset):
             product = lax.dot_general(tile, low, (((0,), (0,)), ((), ())), preferred_element_type=jnp.float32)
-            diagonal = rows_from(low, -offset, group_rows, tile_blocks).astype(jnp.float32)
-            return product - center * diagonal
+            return product - center * picked(low, offset)
 
         return part(own, own_offset), part(other, other_offset)
 
@@ -247,13 +269,9 @@
     for bit in z_bits:
         total = total + swap(total, "col", bit)
     partner = swap(total, "col", 1)
-    cross = jnp.where(mine_first, total, partner)[:half]
-    packed = jnp.where(mine_first, partner, total)
-    inverse = inverse_factor(cross, packed)
-
     mine = lax.dynamic_slice_in_dim(filtered, row_rank * piece_rows, piece_rows, 0)
     orbital_count = piece_rows * row_count * col_count
-    return math.sqrt(orbital_count) * exact_dot(mine, inverse, ((1,), (1,)))
+    return orthonormal(total, partner, mine, mine_first, math.sqrt(orbital_count))
 
 
 def solution(mesh):

time: 138 us -> 111 us (0.80)
  Pallas kernels: 34.9 us -> 13.6 us
  waiting for transfers between devices: 54.6 us -> 62.6 us
  matrix products: 12.2 us -> 4.65 us
  starting transfers between devices: 31.7 us -> 24.8 us
  local copies, waits for them, and re-layouts: 0.26 us -> 1.84 us
    pallas_call x1, Pallas kernels: 28.8 us -> 9.33 us  [orthonormal(): pl.pallas_call(kernel, grid_spec=pltpu.PrefetchScalarGridSpec(num_scalar_...]
    ppermute x24, waiting for transfers between devices: 54.6 us -> 62.6 us  [swap(): return lax.ppermute(value, axis, [(i, i ^ distance) for i in range(count)])]
    ppermute x24, starting transfers between devices: 31.7 us -> 24.8 us  [swap(): return lax.ppermute(value, axis, [(i, i ^ distance) for i in range(count)])]
    dot_general x2, matrix products: 3.65 us -> 0.86 us  [forward(): product = jnp.dot(own, low_own, preferred_element_type=jnp.float32)]
    dot_general x2, matrix products: 3.65 us -> 0.86 us  [forward(): jnp.dot(other, low_other, preferred_element_type=jnp.float32)]
    dot_general x2 -> x1, matrix products: 3.03 us -> 1.02 us  [exact_dot(): lax.dot_general(a, b, (dims, ((), ())), precision=lax.Precision.HIGHEST,...]
    pallas_call x1, Pallas kernels: 6.19 us -> 4.27 us  [densify(): pl.pallas_call(kernel, grid_spec=pltpu.PrefetchScalarGridSpec(num_scalar_...]
    unnamed x2 -> x6, local copies, waits for them, and re-layouts: 0.01 us -> 1.65 us
  transfers between devices with their start and end apart: 24 -> 24, of which waited for: 20 -> 22; matrix products, arithmetic and copies ran while one was open for 1% -> 3% of each run, Pallas kernels for 5% -> 4%
where the time goes in v2:
time: 111 us
  waiting for transfers between devices  62.6 us (56%)
  starting transfers between devices  24.8 us (22%)
  Pallas kernels  13.6 us (12%)
  matrix products  4.65 us (4%)
  other arithmetic  2.89 us (3%)
  local copies, waits for them, and re-layouts  1.84 us (2%)
    ppermute x24, waiting for transfers between devices, swap(): return lax.ppermute(value, axis, [(i, i ^ distance) for i in range(count)])  62.6 us
    ppermute x24, starting transfers between devices, swap(): return lax.ppermute(value, axis, [(i, i ^ distance) for i in range(count)])  24.8 us
    pallas_call x1, Pallas kernels, orthonormal(): pl.pallas_call(kernel, grid_spec=pltpu.PrefetchScalarGridSpec(num_scalar_...  9.33 us
    pallas_call x1, Pallas kernels, densify(): pl.pallas_call(kernel, grid_spec=pltpu.PrefetchScalarGridSpec(num_scalar_...  4.27 us
  transfers between devices with their start and end apart: 24, of which 22 were waited for; matrix products, arithmetic and copies ran while one was open for 3% of the time, Pallas kernels for 4%

profile of v2, /device:TPU:0, one launch (start us, length us, event | category | flops | bytes accessed | tf_op | source)
XLA Modules:
  0.0 110.7 jit_solution(12515095955077711564)
XLA Ops:
  2.3 2.9 %collective-permute-start.1 = (bf16[2,128,128]{2,1,0:T(8,128)(2,1)S(1)}, bf16[2,128,128]{2,1,0:T(8,128)(2,1)S(1)}, u32[]{:S(2)}, u32[]{:S(2)}) collective-permute-start(bf16[2,128,128]{2,1,0:T(8,128)(2,1)S(1)} %pad_maximum_fusion.10), channel_id=1, source_target_pairs={{0,8},{8,0},{16,24},{24,16},{1,9},{9,1},{17,25},{25,17},{2,10},{10... | collective-permute-start | bytes 196616 | tf_op jit(solution)/shard_map/ppermute | solution.py:35
  5.2 1.5 %collective-permute-start.2 = (bf16[2,128,128]{2,1,0:T(8,128)(2,1)S(1)}, bf16[2,128,128]{2,1,0:T(8,128)(2,1)S(1)}, u32[]{:S(2)}, u32[]{:S(2)}) collective-permute-start(bf16[2,128,128]{2,1,0:T(8,128)(2,1)S(1)} %pad_maximum_fusion.10), channel_id=1, source_target_pairs={{0,16},{8,24},{16,0},{24,8},{1,17},{9,25},{17,1},{25,9},{2,18},{10... | collective-permute-start | bytes 196616 | tf_op jit(solution)/shard_map/ppermute | solution.py:35
  6.8 4.3 %shard_map.37 = bf16[1024,512]{1,0:T(8,128)(2,1)} custom-call(s32[8,6]{1,0:T(8,128)} %index_ref.1, bf16[8,6,128,128]{3,2,1,0:T(8,128)(2,1)} %blocks_ref.1), custom_call_target="tpu_custom_call" | custom-call | tf_op jit(solution)/shard_map/pallas_call | solution.py:58
  14.4 2.1 %collective-permute-start.5 = (bf16[512,128]{1,0:T(8,128)(2,1)S(1)}, bf16[512,128]{1,0:T(8,128)(2,1)S(1)}, u32[]{:S(2)}, u32[]{:S(2)}) collective-permute-start(bf16[512,128]{1,0:T(8,128)(2,1)S(1)} %select_convert_fusion.1), channel_id=1, source_target_pairs={{0,2},{1,3},{2,0},{3,1},{4,6},{5,7},{6,4},{7,5},{8,10},{9,11},{10,... | collective-permute-start | bytes 393224 | tf_op jit(solution)/shard_map/ppermute | solution.py:35
  16.5 3.8 %collective-permute-done.5 = bf16[512,128]{1,0:T(8,128)(2,1)S(1)} collective-permute-done((bf16[512,128]{1,0:T(8,128)(2,1)S(1)}, bf16[512,128]{1,0:T(8,128)(2,1)S(1)}, u32[]{:S(2)}, u32[]{:S(2)}) %collective-permute-start.5) | collective-permute-done | bytes 131104 | tf_op jit(solution)/shard_map/ppermute | solution.py:35
  20.3 2.8 %collective-permute-start.6 = (bf16[512,128]{1,0:T(8,128)(2,1)S(1)}, bf16[512,128]{1,0:T(8,128)(2,1)S(1)}, u32[]{:S(2)}, u32[]{:S(2)}) collective-permute-start(bf16[512,128]{1,0:T(8,128)(2,1)S(1)} %add_convert_fusion.1), channel_id=1, source_target_pairs={{0,4},{1,5},{2,6},{3,7},{4,0},{5,1},{6,2},{7,3},{8,12},{9,13},{10,... | collective-permute-start | bytes 393224 | tf_op jit(solution)/shard_map/ppermute | solution.py:35
  23.2 6.0 %collective-permute-done.6 = bf16[512,128]{1,0:T(8,128)(2,1)S(1)} collective-permute-done((bf16[512,128]{1,0:T(8,128)(2,1)S(1)}, bf16[512,128]{1,0:T(8,128)(2,1)S(1)}, u32[]{:S(2)}, u32[]{:S(2)}) %collective-permute-start.6) | collective-permute-done | bytes 131104 | tf_op jit(solution)/shard_map/ppermute | solution.py:35
  30.0 4.2 %collective-permute-done.7 = bf16[512,128]{1,0:T(8,128)(2,1)S(1)} collective-permute-done((bf16[512,128]{1,0:T(8,128)(2,1)S(1)}, bf16[512,128]{1,0:T(8,128)(2,1)S(1)}, u32[]{:S(2)}, u32[]{:S(2)}) %collective-permute-start.7) | collective-permute-done | bytes 131104 | tf_op jit(solution)/shard_map/ppermute | solution.py:35
  36.7 1.6 %collective-permute-start.10 = (f32[512,128]{1,0:T(8,128)S(1)}, f32[512,128]{1,0:T(8,128)S(1)}, u32[]{:S(2)}, u32[]{:S(2)}) collective-permute-start(f32[512,128]{1,0:T(8,128)S(1)} %fusion.3), channel_id=1, source_target_pairs={{0,16},{8,24},{16,0},{24,8},{1,17},{9,25},{17,1},{25,9},{2,18},{10... | collective-permute-start | bytes 786440 | tf_op jit(solution)/shard_map/ppermute | solution.py:35
  38.2 3.0 %collective-permute-done.8 = f32[512,128]{1,0:T(8,128)S(1)} collective-permute-done((f32[512,128]{1,0:T(8,128)S(1)}, f32[512,128]{1,0:T(8,128)S(1)}, u32[]{:S(2)}, u32[]{:S(2)}) %collective-permute-start.8) | collective-permute-done | bytes 262176 | tf_op jit(solution)/shard_map/ppermute | solution.py:35
  42.7 2.9 %collective-permute-done.10 = f32[512,128]{1,0:T(8,128)S(1)} collective-permute-done((f32[512,128]{1,0:T(8,128)S(1)}, f32[512,128]{1,0:T(8,128)S(1)}, u32[]{:S(2)}, u32[]{:S(2)}) %collective-permute-start.10) | collective-permute-done | bytes 262176 | tf_op jit(solution)/shard_map/ppermute | solution.py:35
  45.8 3.0 %collective-permute-done.9 = f32[512,128]{1,0:T(8,128)S(1)} collective-permute-done((f32[512,128]{1,0:T(8,128)S(1)}, f32[512,128]{1,0:T(8,128)S(1)}, u32[]{:S(2)}, u32[]{:S(2)}) %collective-permute-start.9) | collective-permute-done | bytes 262176 | tf_op jit(solution)/shard_map/ppermute | solution.py:35
  48.8 3.3 %collective-permute-done.11 = f32[512,128]{1,0:T(8,128)S(1)} collective-permute-done((f32[512,128]{1,0:T(8,128)S(1)}, f32[512,128]{1,0:T(8,128)S(1)}, u32[]{:S(2)}, u32[]{:S(2)}) %collective-permute-start.11) | collective-permute-done | bytes 262176 | tf_op jit(solution)/shard_map/ppermute | solution.py:35
  53.1 5.9 %collective-permute-done.12 = bf16[512,128]{1,0:T(8,128)(2,1)S(1)} collective-permute-done((bf16[512,128]{1,0:T(8,128)(2,1)S(1)}, bf16[512,128]{1,0:T(8,128)(2,1)S(1)}, u32[]{:S(2)}, u32[]{:S(2)}) %collective-permute-start.12) | collective-permute-done | bytes 131104 | tf_op jit(solution)/shard_map/ppermute | solution.py:35
  59.0 1.5 %collective-permute-start.13 = (bf16[512,128]{1,0:T(8,128)(2,1)S(1)}, bf16[512,128]{1,0:T(8,128)(2,1)S(1)}, u32[]{:S(2)}, u32[]{:S(2)}) collective-permute-start(bf16[512,128]{1,0:T(8,128)(2,1)S(1)} %add_convert_fusion), channel_id=1, source_target_pairs={{0,4},{1,5},{2,6},{3,7},{4,0},{5,1},{6,2},{7,3},{8,12},{9,13},{10,... | collective-permute-start | bytes 393224 | tf_op jit(solution)/shard_map/ppermute | solution.py:35
  60.5 5.2 %collective-permute-done.13 = bf16[512,128]{1,0:T(8,128)(2,1)S(1)} collective-permute-done((bf16[512,128]{1,0:T(8,128)(2,1)S(1)}, bf16[512,128]{1,0:T(8,128)(2,1)S(1)}, u32[]{:S(2)}, u32[]{:S(2)}) %collective-permute-start.13) | collective-permute-done | bytes 131104 | tf_op jit(solution)/shard_map/ppermute | solution.py:35
  65.8 5.0 %collective-permute-done.14 = bf16[512,128]{1,0:T(8,128)(2,1)S(1)} collective-permute-done((bf16[512,128]{1,0:T(8,128)(2,1)S(1)}, bf16[512,128]{1,0:T(8,128)(2,1)S(1)}, u32[]{:S(2)}, u32[]{:S(2)}) %collective-permute-start.14) | collective-permute-done | bytes 131104 | tf_op jit(solution)/shard_map/ppermute | solution.py:35
  71.3 1.9 %collective-permute-start.17 = (f32[512,128]{1,0:T(8,128)S(1)}, f32[512,128]{1,0:T(8,128)S(1)}, u32[]{:S(2)}, u32[]{:S(2)}) collective-permute-start(f32[512,128]{1,0:T(8,128)S(1)} %convolution_subtract_fusion), channel_id=1, source_target_pairs={{0,16},{8,24},{16,0},{24,8},{1,17},{9,25},{17,1},{25,9},{2,18},{10... | collective-permute-start | bytes 786440 | tf_op jit(solution)/shard_map/ppermute | solution.py:35
  73.9 4.9 %collective-permute-done.17 = f32[512,128]{1,0:T(8,128)S(1)} collective-permute-done((f32[512,128]{1,0:T(8,128)S(1)}, f32[512,128]{1,0:T(8,128)S(1)}, u32[]{:S(2)}, u32[]{:S(2)}) %collective-permute-start.17) | collective-permute-done | bytes 262176 | tf_op jit(solution)/shard_map/ppermute | solution.py:35
  81.2 4.1 %collective-permute-done.18 = f32[512,128]{1,0:T(8,128)S(1)} collective-permute-done((f32[512,128]{1,0:T(8,128)S(1)}, f32[512,128]{1,0:T(8,128)S(1)}, u32[]{:S(2)}, u32[]{:S(2)}) %collective-permute-start.18) | collective-permute-done | bytes 262176 | tf_op jit(solution)/shard_map/ppermute | solution.py:35
  91.0 3.1 %collective-permute-done.21 = f32[136,128]{1,0:T(8,128)S(1)} collective-permute-done((f32[136,128]{1,0:T(8,128)S(1)}, f32[136,128]{1,0:T(8,128)S(1)}, u32[]{:S(2)}, u32[]{:S(2)}) %collective-permute-start.21) | collective-permute-done | bytes 69664 | tf_op jit(solution)/shard_map/ppermute | solution.py:35
  94.0 2.7 %collective-permute-start.22 = (f32[136,128]{1,0:T(8,128)S(1)}, f32[136,128]{1,0:T(8,128)S(1)}, u32[]{:S(2)}, u32[]{:S(2)}) collective-permute-start(f32[136,128]{1,0:T(8,128)S(1)} %add.117), channel_id=1, source_target_pairs={{0,4},{1,5},{2,6},{3,7},{4,0},{5,1},{6,2},{7,3},{8,12},{9,13},{10,... | collective-permute-start | bytes 208904 | tf_op jit(solution)/shard_map/ppermute | solution.py:35
  96.8 2.6 %collective-permute-done.22 = f32[136,128]{1,0:T(8,128)S(1)} collective-permute-done((f32[136,128]{1,0:T(8,128)S(1)}, f32[136,128]{1,0:T(8,128)S(1)}, u32[]{:S(2)}, u32[]{:S(2)}) %collective-permute-start.22) | collective-permute-done | bytes 69664 | tf_op jit(solution)/shard_map/ppermute | solution.py:35
  101.4 9.3 %shard_map.38 = f32[128,256]{1,0:T(8,128)} custom-call(s32[1]{0:T(128)} %bitcast.first_ref, f32[136,128]{1,0:T(8,128)} %copy-done.1, f32[136,128]{1,0:T(8,128)} %copy-done.2, f32[128,256]{1,0:T(8,128)} %fusion.9.filtered_ref), custom_call_target="tpu_custom_call" | custom-call | tf_op jit(solution)/shard_map/pallas_call | solution.py:135
  (82 shorter events, 23.0 us)
Async XLA Ops:
  0.9 1.4 %collective-permute-start = (f32[128,128]{1,0:T(8,128)S(1)}, f32[128,128]{1,0:T(8,128)S(1)}, u32[]{:S(2)}, u32[]{:S(2)}) collective-permute-start(f32[128,128]{1,0:T(8,128)S(1)} %get-tuple-element.30), channel_id=1, source_target_pairs={{0,1},{1,0},{2,3},{3,2},{4,5},{5,4},{6,7},{7,6},{8,9},{9,8},{10,11... | collective-permute-start | bytes 196616 | tf_op jit(solution)/shard_map/ppermute | solution.py:35
  2.3 8.7 %collective-permute-start.1 = (bf16[2,128,128]{2,1,0:T(8,128)(2,1)S(1)}, bf16[2,128,128]{2,1,0:T(8,128)(2,1)S(1)}, u32[]{:S(2)}, u32[]{:S(2)}) collective-permute-start(bf16[2,128,128]{2,1,0:T(8,128)(2,1)S(1)} %pad_maximum_fusion.10), channel_id=1, source_target_pairs={{0,8},{8,0},{16,24},{24,16},{1,9},{9,1},{17,25},{25,17},{2,10},{10... | collective-permute-start | bytes 196616 | tf_op jit(solution)/shard_map/ppermute | solution.py:35
  5.2 5.8 %collective-permute-start.2 = (bf16[2,128,128]{2,1,0:T(8,128)(2,1)S(1)}, bf16[2,128,128]{2,1,0:T(8,128)(2,1)S(1)}, u32[]{:S(2)}, u32[]{:S(2)}) collective-permute-start(bf16[2,128,128]{2,1,0:T(8,128)(2,1)S(1)} %pad_maximum_fusion.10), channel_id=1, source_target_pairs={{0,16},{8,24},{16,0},{24,8},{1,17},{9,25},{17,1},{25,9},{2,18},{10... | collective-permute-start | bytes 196616 | tf_op jit(solution)/shard_map/ppermute | solution.py:35
  6.8 5.2 %collective-permute-start.3 = (bf16[2,128,128]{2,1,0:T(8,128)(2,1)S(1)}, bf16[2,128,128]{2,1,0:T(8,128)(2,1)S(1)}, u32[]{:S(2)}, u32[]{:S(2)}) collective-permute-start(bf16[2,128,128]{2,1,0:T(8,128)(2,1)S(1)} %pad_maximum_fusion.10), channel_id=1, source_target_pairs={{0,24},{8,16},{16,8},{24,0},{1,25},{9,17},{17,9},{25,1},{2,26},{10... | collective-permute-start | bytes 196616 | tf_op jit(solution)/shard_map/ppermute | solution.py:35
  11.1 2.9 %collective-permute-start.4 = (bf16[1024,512]{1,0:T(8,128)(2,1)}, bf16[1024,512]{1,0:T(8,128)(2,1)S(1)}, u32[]{:S(2)}, u32[]{:S(2)}) collective-permute-start(bf16[1024,512]{1,0:T(8,128)(2,1)} %shard_map.37), channel_id=1, source_target_pairs={{0,1},{1,0},{2,3},{3,2},{4,5},{5,4},{6,7},{7,6},{8,9},{9,8},{10,11... | collective-permute-start | bytes 3145736 | tf_op jit(solution)/shard_map/ppermute | solution.py:35
  14.4 5.9 %collective-permute-start.5 = (bf16[512,128]{1,0:T(8,128)(2,1)S(1)}, bf16[512,128]{1,0:T(8,128)(2,1)S(1)}, u32[]{:S(2)}, u32[]{:S(2)}) collective-permute-start(bf16[512,128]{1,0:T(8,128)(2,1)S(1)} %select_convert_fusion.1), channel_id=1, source_target_pairs={{0,2},{1,3},{2,0},{3,1},{4,6},{5,7},{6,4},{7,5},{8,10},{9,11},{10,... | collective-permute-start | bytes 393224 | tf_op jit(solution)/shard_map/ppermute | solution.py:35
  20.3 8.8 %collective-permute-start.6 = (bf16[512,128]{1,0:T(8,128)(2,1)S(1)}, bf16[512,128]{1,0:T(8,128)(2,1)S(1)}, u32[]{:S(2)}, u32[]{:S(2)}) collective-permute-start(bf16[512,128]{1,0:T(8,128)(2,1)S(1)} %add_convert_fusion.1), channel_id=1, source_target_pairs={{0,4},{1,5},{2,6},{3,7},{4,0},{5,1},{6,2},{7,3},{8,12},{9,13},{10,... | collective-permute-start | bytes 393224 | tf_op jit(solution)/shard_map/ppermute | solution.py:35
  29.2 5.0 %collective-permute-start.7 = (bf16[512,128]{1,0:T(8,128)(2,1)S(1)}, bf16[512,128]{1,0:T(8,128)(2,1)S(1)}, u32[]{:S(2)}, u32[]{:S(2)}) collective-permute-start(bf16[512,128]{1,0:T(8,128)(2,1)S(1)} %multiply_convert_fusion), channel_id=1, source_target_pairs={{0,2},{1,3},{2,0},{3,1},{4,6},{5,7},{6,4},{7,5},{8,10},{9,11},{10,... | collective-permute-start | bytes 393224 | tf_op jit(solution)/shard_map/ppermute | solution.py:35
  34.8 6.4 %collective-permute-start.8 = (f32[512,128]{1,0:T(8,128)S(1)}, f32[512,128]{1,0:T(8,128)S(1)}, u32[]{:S(2)}, u32[]{:S(2)}) collective-permute-start(f32[512,128]{1,0:T(8,128)S(1)} %fusion.5), channel_id=1, source_target_pairs={{0,8},{8,0},{16,24},{24,16},{1,9},{9,1},{17,25},{25,17},{2,10},{10... | collective-permute-start | bytes 786440 | tf_op jit(solution)/shard_map/ppermute | solution.py:35
  36.7 8.9 %collective-permute-start.10 = (f32[512,128]{1,0:T(8,128)S(1)}, f32[512,128]{1,0:T(8,128)S(1)}, u32[]{:S(2)}, u32[]{:S(2)}) collective-permute-start(f32[512,128]{1,0:T(8,128)S(1)} %fusion.3), channel_id=1, source_target_pairs={{0,16},{8,24},{16,0},{24,8},{1,17},{9,25},{17,1},{25,9},{2,18},{10... | collective-permute-start | bytes 786440 | tf_op jit(solution)/shard_map/ppermute | solution.py:35
  41.2 7.5 %collective-permute-start.9 = (f32[512,128]{1,0:T(8,128)S(1)}, f32[512,128]{1,0:T(8,128)S(1)}, u32[]{:S(2)}, u32[]{:S(2)}) collective-permute-start(f32[512,128]{1,0:T(8,128)S(1)} %add.101), channel_id=1, source_target_pairs={{0,16},{8,24},{16,0},{24,8},{1,17},{9,25},{17,1},{25,9},{2,18},{10... | collective-permute-start | bytes 786440 | tf_op jit(solution)/shard_map/ppermute | solution.py:35
  45.6 6.4 %collective-permute-start.11 = (f32[512,128]{1,0:T(8,128)S(1)}, f32[512,128]{1,0:T(8,128)S(1)}, u32[]{:S(2)}, u32[]{:S(2)}) collective-permute-start(f32[512,128]{1,0:T(8,128)S(1)} %add.104), channel_id=1, source_target_pairs={{0,8},{8,0},{16,24},{24,16},{1,9},{9,1},{17,25},{25,17},{2,10},{10... | collective-permute-start | bytes 786440 | tf_op jit(solution)/shard_map/ppermute | solution.py:35
  53.0 5.9 %collective-permute-start.12 = (bf16[512,128]{1,0:T(8,128)(2,1)S(1)}, bf16[512,128]{1,0:T(8,128)(2,1)S(1)}, u32[]{:S(2)}, u32[]{:S(2)}) collective-permute-start(bf16[512,128]{1,0:T(8,128)(2,1)S(1)} %select_convert_fusion), channel_id=1, source_target_pairs={{0,2},{1,3},{2,0},{3,1},{4,6},{5,7},{6,4},{7,5},{8,10},{9,11},{10,... | collective-permute-start | bytes 393224 | tf_op jit(solution)/shard_map/ppermute | solution.py:35
  59.0 6.7 %collective-permute-start.13 = (bf16[512,128]{1,0:T(8,128)(2,1)S(1)}, bf16[512,128]{1,0:T(8,128)(2,1)S(1)}, u32[]{:S(2)}, u32[]{:S(2)}) collective-permute-start(bf16[512,128]{1,0:T(8,128)(2,1)S(1)} %add_convert_fusion), channel_id=1, source_target_pairs={{0,4},{1,5},{2,6},{3,7},{4,0},{5,1},{6,2},{7,3},{8,12},{9,13},{10,... | collective-permute-start | bytes 393224 | tf_op jit(solution)/shard_map/ppermute | solution.py:35
  65.8 5.0 %collective-permute-start.14 = (bf16[512,128]{1,0:T(8,128)(2,1)S(1)}, bf16[512,128]{1,0:T(8,128)(2,1)S(1)}, u32[]{:S(2)}, u32[]{:S(2)}) collective-permute-start(bf16[512,128]{1,0:T(8,128)(2,1)S(1)} %subtract_convert_fusion), channel_id=1, source_target_pairs={{0,2},{1,3},{2,0},{3,1},{4,6},{5,7},{6,4},{7,5},{8,10},{9,11},{10,... | collective-permute-start | bytes 393224 | tf_op jit(solution)/shard_map/ppermute | solution.py:35
  71.3 7.5 %collective-permute-start.17 = (f32[512,128]{1,0:T(8,128)S(1)}, f32[512,128]{1,0:T(8,128)S(1)}, u32[]{:S(2)}, u32[]{:S(2)}) collective-permute-start(f32[512,128]{1,0:T(8,128)S(1)} %convolution_subtract_fusion), channel_id=1, source_target_pairs={{0,16},{8,24},{16,0},{24,8},{1,17},{9,25},{17,1},{25,9},{2,18},{10... | collective-permute-start | bytes 786440 | tf_op jit(solution)/shard_map/ppermute | solution.py:35
  73.7 6.4 %collective-permute-start.15 = (f32[512,128]{1,0:T(8,128)S(1)}, f32[512,128]{1,0:T(8,128)S(1)}, u32[]{:S(2)}, u32[]{:S(2)}) collective-permute-start(f32[512,128]{1,0:T(8,128)S(1)} %convolution_subtract_fusion.1), channel_id=1, source_target_pairs={{0,8},{8,0},{16,24},{24,16},{1,9},{9,1},{17,25},{25,17},{2,10},{10... | collective-permute-start | bytes 786440 | tf_op jit(solution)/shard_map/ppermute | solution.py:35
  78.9 6.4 %collective-permute-start.18 = (f32[512,128]{1,0:T(8,128)S(1)}, f32[512,128]{1,0:T(8,128)S(1)}, u32[]{:S(2)}, u32[]{:S(2)}) collective-permute-start(f32[512,128]{1,0:T(8,128)S(1)} %add.114), channel_id=1, source_target_pairs={{0,8},{8,0},{16,24},{24,16},{1,9},{9,1},{17,25},{25,17},{2,10},{10... | collective-permute-start | bytes 786440 | tf_op jit(solution)/shard_map/ppermute | solution.py:35
  80.2 6.4 %collective-permute-start.16 = (f32[512,128]{1,0:T(8,128)S(1)}, f32[512,128]{1,0:T(8,128)S(1)}, u32[]{:S(2)}, u32[]{:S(2)}) collective-permute-start(f32[512,128]{1,0:T(8,128)S(1)} %add.111), channel_id=1, source_target_pairs={{0,16},{8,24},{16,0},{24,8},{1,17},{9,25},{17,1},{25,9},{2,18},{10... | collective-permute-start | bytes 786440 | tf_op jit(solution)/shard_map/ppermute | solution.py:35
  85.4 1.6 %collective-permute-start.19 = (f32[512,128]{1,0:T(8,128)S(1)}, f32[512,128]{1,0:T(8,128)S(1)}, u32[]{:S(2)}, u32[]{:S(2)}) collective-permute-start(f32[512,128]{1,0:T(8,128)S(1)} %multiply_subtract_fusion), channel_id=1, source_target_pairs={{0,1},{1,0},{2,3},{3,2},{4,5},{5,4},{6,7},{7,6},{8,9},{9,8},{10,11... | collective-permute-start | bytes 786440 | tf_op jit(solution)/shard_map/ppermute | solution.py:35
  88.2 1.3 %collective-permute-start.20 = (f32[136,128]{1,0:T(8,128)S(1)}, f32[136,128]{1,0:T(8,128)S(1)}, u32[]{:S(2)}, u32[]{:S(2)}) collective-permute-start(f32[136,128]{1,0:T(8,128)S(1)} %pad_select_fusion), channel_id=1, source_target_pairs={{0,1},{1,0},{2,3},{3,2},{4,5},{5,4},{6,7},{7,6},{8,9},{9,8},{10,11... | collective-permute-start | bytes 208904 | tf_op jit(solution)/shard_map/ppermute | solution.py:35
  89.7 4.4 %collective-permute-start.21 = (f32[136,128]{1,0:T(8,128)S(1)}, f32[136,128]{1,0:T(8,128)S(1)}, u32[]{:S(2)}, u32[]{:S(2)}) collective-permute-start(f32[136,128]{1,0:T(8,128)S(1)} %select_add_fusion), channel_id=1, source_target_pairs={{0,2},{1,3},{2,0},{3,1},{4,6},{5,7},{6,4},{7,5},{8,10},{9,11},{10,... | collective-permute-start | bytes 208904 | tf_op jit(solution)/shard_map/ppermute | solution.py:35
  94.0 5.3 %collective-permute-start.22 = (f32[136,128]{1,0:T(8,128)S(1)}, f32[136,128]{1,0:T(8,128)S(1)}, u32[]{:S(2)}, u32[]{:S(2)}) collective-permute-start(f32[136,128]{1,0:T(8,128)S(1)} %add.117), channel_id=1, source_target_pairs={{0,4},{1,5},{2,6},{3,7},{4,0},{5,1},{6,2},{7,3},{8,12},{9,13},{10,... | collective-permute-start | bytes 208904 | tf_op jit(solution)/shard_map/ppermute | solution.py:35
  99.4 1.3 %collective-permute-start.23 = (f32[136,128]{1,0:T(8,128)S(1)}, f32[136,128]{1,0:T(8,128)S(1)}, u32[]{:S(2)}, u32[]{:S(2)}) collective-permute-start(f32[136,128]{1,0:T(8,128)S(1)} %add.118.total_ref), channel_id=1, source_target_pairs={{0,1},{1,0},{2,3},{3,2},{4,5},{5,4},{6,7},{7,6},{8,9},{9,8},{10,11... | collective-permute-start | bytes 208904 | tf_op jit(solution)/shard_map/ppermute | solution.py:35
  (3 other events, 3.2 us)

commit v3 on v2

--- a/solution.py
+++ b/solution.py
@@ -39,10 +39,17 @@
     return [1 << n for n in range(count.bit_length() - 1)]
 
 
+def in_order(values, rank):
+    stacked = jnp.stack(values)
+    return jnp.concatenate(
+        [lax.dynamic_index_in_dim(stacked, rank ^ k, 0, False) for k in range(len(values))]
+    )
+
+
 def densify(blocks, col_index, tile_blocks):
     group_rows, slots, width, _ = blocks.shape
     slots = min(slots, tile_blocks)
-    step = 2
+    step = max(group_rows // 2, 1)
 
     def kernel(index_ref, blocks_ref, tile_ref):
         nothing = jnp.zeros((width, width), blocks.dtype)
@@ -157,7 +164,9 @@
     tile_blocks = piece_rows // width * row_count
     tile_rows = tile_blocks * width
     row_bits = bits_below(row_count)
-    z_bits = [2 * bit for bit in bits_below(col_count // 2)]
+    z_count = col_count // 2
+    z_rank = col_rank // 2
+    z_bits = [2 * bit for bit in bits_below(z_count)]
     narrow = jnp.bfloat16
 
     mine_first = core == 0
@@ -168,10 +177,8 @@
     low_start = start.astype(narrow)
 
     arrived = [low_start] + [swap(low_start, "row", k) for k in range(1, row_count)]
-    arrived = jnp.stack(arrived)
-    ordered = jnp.stack([lax.dynamic_index_in_dim(arrived, row_rank ^ k, 0, False) for k in range(row_count)])
-    low_own = ordered[:, 0].reshape(tile_rows, half)
-    low_other = ordered[:, 1].reshape(tile_rows, half)
+    low_own = in_order([value[0] for value in arrived], row_rank)
+    low_other = in_order([value[1] for value in arrived], row_rank)
 
     own = densify(blocks, col_index, tile_blocks)
     other = swap(own, "col", 1)
@@ -205,33 +212,26 @@
 
         return part(own, own_offset), part(other, other_offset)
 
-    def halves_of(value, bit):
-        rows = value.shape[0] // 2
-        upper = (col_rank & bit) != 0
-        first, second = value[:rows], value[rows:]
-        return jnp.where(upper, second, first), jnp.where(upper, first, second)
+    def piece_of(value, index):
+        rows = value.shape[0] // z_count
+        return lax.dynamic_slice_in_dim(value, index * rows, rows, 0)
 
     def sum_over_z(value):
-        for bit in z_bits[:-1]:
-            kept, sent = halves_of(value, bit)
-            value = kept + swap(sent.astype(narrow), "col", bit).astype(jnp.float32)
-        for bit in z_bits[-1:]:
-            sent = value.astype(narrow)
-            value = sent.astype(jnp.float32) + swap(sent, "col", bit).astype(jnp.float32)
-        return value
+        sent = value.astype(narrow)
+        total = piece_of(value, z_rank)
+        for k in range(1, z_count):
+            total = total + swap(piece_of(sent, z_rank ^ k), "col", 2 * k).astype(jnp.float32)
+        return total
 
     def gather_over_z(value):
-        for bit in reversed(z_bits[:-1]):
-            partner = swap(value, "col", bit)
-            upper = (col_rank & bit) != 0
-            value = jnp.concatenate(
-                [jnp.where(upper, partner, value), jnp.where(upper, value, partner)]
-            )
-        return value
+        return in_order([value] + [swap(value, "col", 2 * k) for k in range(1, z_count)], z_rank)
 
     def sum_over_row(one, two):
-        for bit_one, bit_two in zip(row_bits, reversed(row_bits)):
-            one, two = one + swap(one, "row", bit_one), two + swap(two, "row", bit_two)
+        for level, (bit_one, bit_two) in enumerate(zip(row_bits, reversed(row_bits))):
+            sent = narrow if level < 2 else jnp.float32
+            low_one, low_two = one.astype(sent), two.astype(sent)
+            one = low_one.astype(jnp.float32) + swap(low_one, "row", bit_one).astype(jnp.float32)
+            two = low_two.astype(jnp.float32) + swap(low_two, "row", bit_two).astype(jnp.float32)
         return one, two
 
     def placed(piece):

time: 111 us -> 108 us (0.973)
  waiting for transfers between devices: 62.6 us -> 54.9 us
  starting transfers between devices: 24.8 us -> 31.9 us
  Pallas kernels: 13.6 us -> 12.3 us
    ppermute x24 -> x30, waiting for transfers between devices: 62.6 us -> 54.9 us  [swap(): return lax.ppermute(value, axis, [(i, i ^ distance) for i in range(count)])]
    ppermute x24 -> x30, starting transfers between devices: 24.8 us -> 31.9 us  [swap(): return lax.ppermute(value, axis, [(i, i ^ distance) for i in range(count)])]
    pallas_call x1, Pallas kernels: 4.27 us -> 3.01 us  [densify(): pl.pallas_call(kernel, grid_spec=pltpu.PrefetchScalarGridSpec(num_scalar_...]
  transfers between devices with their start and end apart: 24 -> 30, of which waited for: 22 -> 22; matrix products, arithmetic and copies ran while one was open for 3% -> 3% of each run, Pallas kernels for 4% -> 3%
where the time goes in v3:
time: 108 us
  waiting for transfers between devices  54.9 us (51%)
  starting transfers between devices  31.9 us (30%)
  Pallas kernels  12.3 us (11%)
  matrix products  4.72 us (4%)
  other arithmetic  2.74 us (3%)
    ppermute x30, waiting for transfers between devices, swap(): return lax.ppermute(value, axis, [(i, i ^ distance) for i in range(count)])  54.9 us
    ppermute x30, starting transfers between devices, swap(): return lax.ppermute(value, axis, [(i, i ^ distance) for i in range(count)])  31.9 us
    pallas_call x1, Pallas kernels, orthonormal(): pl.pallas_call(kernel, grid_spec=pltpu.PrefetchScalarGridSpec(num_scalar_...  9.33 us
    pallas_call x1, Pallas kernels, densify(): pl.pallas_call(kernel, grid_spec=pltpu.PrefetchScalarGridSpec(num_scalar_...  3.01 us
  transfers between devices with their start and end apart: 30, of which 22 were waited for; matrix products, arithmetic and copies ran while one was open for 3% of the time, Pallas kernels for 3%

profile of v3, /device:TPU:0, one launch (start us, length us, event | category | flops | bytes accessed | tf_op | source)
XLA Modules:
  0.0 107.9 jit_solution(11050660119047599095)
XLA Ops:
  2.3 2.9 %collective-permute-start.1 = (bf16[2,128,128]{2,1,0:T(8,128)(2,1)S(1)}, bf16[2,128,128]{2,1,0:T(8,128)(2,1)S(1)}, u32[]{:S(2)}, u32[]{:S(2)}) collective-permute-start(bf16[2,128,128]{2,1,0:T(8,128)(2,1)S(1)} %pad_maximum_fusion.10), channel_id=1, source_target_pairs={{0,8},{8,0},{16,24},{24,16},{1,9},{9,1},{17,25},{25,17},{2,10},{10... | collective-permute-start | bytes 196616 | tf_op jit(solution)/shard_map/ppermute | solution.py:35
  5.2 3.0 %shard_map.37 = bf16[1024,512]{1,0:T(8,128)(2,1)} custom-call(s32[8,6]{1,0:T(8,128)} %index_ref.1, bf16[8,6,128,128]{3,2,1,0:T(8,128)(2,1)} %blocks_ref.1), custom_call_target="tpu_custom_call" | custom-call | tf_op jit(solution)/shard_map/pallas_call | solution.py:65
  9.9 2.8 %collective-permute-done.2 = bf16[2,128,128]{2,1,0:T(8,128)(2,1)S(1)} collective-permute-done((bf16[2,128,128]{2,1,0:T(8,128)(2,1)S(1)}, bf16[2,128,128]{2,1,0:T(8,128)(2,1)S(1)}, u32[]{:S(2)}, u32[]{:S(2)}) %collective-permute-start.2) | collective-permute-done | bytes 65568 | tf_op jit(solution)/shard_map/ppermute | solution.py:35
  12.8 2.2 %collective-permute-done.3 = bf16[2,128,128]{2,1,0:T(8,128)(2,1)S(1)} collective-permute-done((bf16[2,128,128]{2,1,0:T(8,128)(2,1)S(1)}, bf16[2,128,128]{2,1,0:T(8,128)(2,1)S(1)}, u32[]{:S(2)}, u32[]{:S(2)}) %collective-permute-start.3) | collective-permute-done | bytes 65568 | tf_op jit(solution)/shard_map/ppermute | solution.py:35
  16.1 1.6 %collective-permute-start.5 = (bf16[256,128]{1,0:T(8,128)(2,1)S(1)}, bf16[256,128]{1,0:T(8,128)(2,1)S(1)}, u32[]{:S(2)}, u32[]{:S(2)}) collective-permute-start(bf16[256,128]{1,0:T(8,128)(2,1)S(1)} %get-tuple-element.27), channel_id=1, source_target_pairs={{0,2},{1,3},{2,0},{3,1},{4,6},{5,7},{6,4},{7,5},{8,10},{9,11},{10,... | collective-permute-start | bytes 196616 | tf_op jit(solution)/shard_map/ppermute | solution.py:35
  17.7 2.6 %collective-permute-start.6 = (bf16[256,128]{1,0:T(8,128)(2,1)S(1)}, bf16[256,128]{1,0:T(8,128)(2,1)S(1)}, u32[]{:S(2)}, u32[]{:S(2)}) collective-permute-start(bf16[256,128]{1,0:T(8,128)(2,1)S(1)} %get-tuple-element.29), channel_id=1, source_target_pairs={{0,4},{1,5},{2,6},{3,7},{4,0},{5,1},{6,2},{7,3},{8,12},{9,13},{10,... | collective-permute-start | bytes 196616 | tf_op jit(solution)/shard_map/ppermute | solution.py:35
  21.0 3.2 %collective-permute-done.6 = bf16[256,128]{1,0:T(8,128)(2,1)S(1)} collective-permute-done((bf16[256,128]{1,0:T(8,128)(2,1)S(1)}, bf16[256,128]{1,0:T(8,128)(2,1)S(1)}, u32[]{:S(2)}, u32[]{:S(2)}) %collective-permute-start.6) | collective-permute-done | bytes 65568 | tf_op jit(solution)/shard_map/ppermute | solution.py:35
  24.3 2.2 %collective-permute-done.7 = bf16[256,128]{1,0:T(8,128)(2,1)S(1)} collective-permute-done((bf16[256,128]{1,0:T(8,128)(2,1)S(1)}, bf16[256,128]{1,0:T(8,128)(2,1)S(1)}, u32[]{:S(2)}, u32[]{:S(2)}) %collective-permute-start.7) | collective-permute-done | bytes 65568 | tf_op jit(solution)/shard_map/ppermute | solution.py:35
  28.1 2.9 %collective-permute-start.10 = (bf16[256,128]{1,0:T(8,128)(2,1)S(1)}, bf16[256,128]{1,0:T(8,128)(2,1)S(1)}, u32[]{:S(2)}, u32[]{:S(2)}) collective-permute-start(bf16[256,128]{1,0:T(8,128)(2,1)S(1)} %multiply_convert_fusion), channel_id=1, source_target_pairs={{0,6},{1,7},{2,4},{3,5},{4,2},{5,3},{6,0},{7,1},{8,14},{9,15},{10,... | collective-permute-start | bytes 196616 | tf_op jit(solution)/shard_map/ppermute | solution.py:35
  31.8 2.4 %collective-permute-done.10 = bf16[256,128]{1,0:T(8,128)(2,1)S(1)} collective-permute-done((bf16[256,128]{1,0:T(8,128)(2,1)S(1)}, bf16[256,128]{1,0:T(8,128)(2,1)S(1)}, u32[]{:S(2)}, u32[]{:S(2)}) %collective-permute-start.10) | collective-permute-done | bytes 65568 | tf_op jit(solution)/shard_map/ppermute | solution.py:35
  36.9 4.4 %collective-permute-done.13 = bf16[512,128]{1,0:T(8,128)(2,1)S(1)} collective-permute-done((bf16[512,128]{1,0:T(8,128)(2,1)S(1)}, bf16[512,128]{1,0:T(8,128)(2,1)S(1)}, u32[]{:S(2)}, u32[]{:S(2)}) %collective-permute-start.13) | collective-permute-done | bytes 131104 | tf_op jit(solution)/shard_map/ppermute | solution.py:35
  42.6 3.6 %collective-permute-done.14 = bf16[512,128]{1,0:T(8,128)(2,1)S(1)} collective-permute-done((bf16[512,128]{1,0:T(8,128)(2,1)S(1)}, bf16[512,128]{1,0:T(8,128)(2,1)S(1)}, u32[]{:S(2)}, u32[]{:S(2)}) %collective-permute-start.14) | collective-permute-done | bytes 131104 | tf_op jit(solution)/shard_map/ppermute | solution.py:35
  47.9 2.8 %collective-permute-start.16 = (bf16[256,128]{1,0:T(8,128)(2,1)S(1)}, bf16[256,128]{1,0:T(8,128)(2,1)S(1)}, u32[]{:S(2)}, u32[]{:S(2)}) collective-permute-start(bf16[256,128]{1,0:T(8,128)(2,1)S(1)} %get-tuple-element.18), channel_id=1, source_target_pairs={{0,4},{1,5},{2,6},{3,7},{4,0},{5,1},{6,2},{7,3},{8,12},{9,13},{10,... | collective-permute-start | bytes 196616 | tf_op jit(solution)/shard_map/ppermute | solution.py:35
  53.1 3.7 %collective-permute-done.17 = bf16[256,128]{1,0:T(8,128)(2,1)S(1)} collective-permute-done((bf16[256,128]{1,0:T(8,128)(2,1)S(1)}, bf16[256,128]{1,0:T(8,128)(2,1)S(1)}, u32[]{:S(2)}, u32[]{:S(2)}) %collective-permute-start.17) | collective-permute-done | bytes 65568 | tf_op jit(solution)/shard_map/ppermute | solution.py:35
  59.4 1.9 %collective-permute-start.20 = (bf16[256,128]{1,0:T(8,128)(2,1)S(1)}, bf16[256,128]{1,0:T(8,128)(2,1)S(1)}, u32[]{:S(2)}, u32[]{:S(2)}) collective-permute-start(bf16[256,128]{1,0:T(8,128)(2,1)S(1)} %subtract_convert_fusion), channel_id=1, source_target_pairs={{0,6},{1,7},{2,4},{3,5},{4,2},{5,3},{6,0},{7,1},{8,14},{9,15},{10,... | collective-permute-start | bytes 196616 | tf_op jit(solution)/shard_map/ppermute | solution.py:35
  61.3 2.9 %collective-permute-done.19 = bf16[256,128]{1,0:T(8,128)(2,1)S(1)} collective-permute-done((bf16[256,128]{1,0:T(8,128)(2,1)S(1)}, bf16[256,128]{1,0:T(8,128)(2,1)S(1)}, u32[]{:S(2)}, u32[]{:S(2)}) %collective-permute-start.19) | collective-permute-done | bytes 65568 | tf_op jit(solution)/shard_map/ppermute | solution.py:35
  67.3 3.9 %collective-permute-done.23 = bf16[512,128]{1,0:T(8,128)(2,1)S(1)} collective-permute-done((bf16[512,128]{1,0:T(8,128)(2,1)S(1)}, bf16[512,128]{1,0:T(8,128)(2,1)S(1)}, u32[]{:S(2)}, u32[]{:S(2)}) %collective-permute-start.23) | collective-permute-done | bytes 131104 | tf_op jit(solution)/shard_map/ppermute | solution.py:35
  71.2 1.7 %collective-permute-start.24 = (bf16[512,128]{1,0:T(8,128)(2,1)S(1)}, bf16[512,128]{1,0:T(8,128)(2,1)S(1)}, u32[]{:S(2)}, u32[]{:S(2)}) collective-permute-start(bf16[512,128]{1,0:T(8,128)(2,1)S(1)} %add_convert_fusion), channel_id=1, source_target_pairs={{0,8},{8,0},{16,24},{24,16},{1,9},{9,1},{17,25},{25,17},{2,10},{10... | collective-permute-start | bytes 393224 | tf_op jit(solution)/shard_map/ppermute | solution.py:35
  73.9 2.4 %collective-permute-done.24 = bf16[512,128]{1,0:T(8,128)(2,1)S(1)} collective-permute-done((bf16[512,128]{1,0:T(8,128)(2,1)S(1)}, bf16[512,128]{1,0:T(8,128)(2,1)S(1)}, u32[]{:S(2)}, u32[]{:S(2)}) %collective-permute-start.24) | collective-permute-done | bytes 131104 | tf_op jit(solution)/shard_map/ppermute | solution.py:35
  76.4 2.0 %collective-permute-done.21 = bf16[512,128]{1,0:T(8,128)(2,1)S(1)} collective-permute-done((bf16[512,128]{1,0:T(8,128)(2,1)S(1)}, bf16[512,128]{1,0:T(8,128)(2,1)S(1)}, u32[]{:S(2)}, u32[]{:S(2)}) %collective-permute-start.21) | collective-permute-done | bytes 131104 | tf_op jit(solution)/shard_map/ppermute | solution.py:35
  79.7 3.9 %collective-permute-done.22 = bf16[512,128]{1,0:T(8,128)(2,1)S(1)} collective-permute-done((bf16[512,128]{1,0:T(8,128)(2,1)S(1)}, bf16[512,128]{1,0:T(8,128)(2,1)S(1)}, u32[]{:S(2)}, u32[]{:S(2)}) %collective-permute-start.22) | collective-permute-done | bytes 131104 | tf_op jit(solution)/shard_map/ppermute | solution.py:35
  87.0 3.6 %collective-permute-done.27 = f32[136,128]{1,0:T(8,128)S(1)} collective-permute-done((f32[136,128]{1,0:T(8,128)S(1)}, f32[136,128]{1,0:T(8,128)S(1)}, u32[]{:S(2)}, u32[]{:S(2)}) %collective-permute-start.27) | collective-permute-done | bytes 69664 | tf_op jit(solution)/shard_map/ppermute | solution.py:35
  91.3 5.3 %collective-permute-done.28 = f32[136,128]{1,0:T(8,128)S(1)} collective-permute-done((f32[136,128]{1,0:T(8,128)S(1)}, f32[136,128]{1,0:T(8,128)S(1)}, u32[]{:S(2)}, u32[]{:S(2)}) %collective-permute-start.28) | collective-permute-done | bytes 69664 | tf_op jit(solution)/shard_map/ppermute | solution.py:35
  98.6 9.3 %shard_map.38 = f32[128,256]{1,0:T(8,128)} custom-call(s32[1]{0:T(128)} %bitcast.first_ref, f32[136,128]{1,0:T(8,128)} %copy-done.1, f32[136,128]{1,0:T(8,128)} %copy-done.2, f32[128,256]{1,0:T(8,128)} %fusion.15.filtered_ref), custom_call_target="tpu_custom_call" | custom-call | tf_op jit(solution)/shard_map/pallas_call | solution.py:142
  (93 shorter events, 30.5 us)
Async XLA Ops:
  2.3 7.6 %collective-permute-start.1 = (bf16[2,128,128]{2,1,0:T(8,128)(2,1)S(1)}, bf16[2,128,128]{2,1,0:T(8,128)(2,1)S(1)}, u32[]{:S(2)}, u32[]{:S(2)}) collective-permute-start(bf16[2,128,128]{2,1,0:T(8,128)(2,1)S(1)} %pad_maximum_fusion.10), channel_id=1, source_target_pairs={{0,8},{8,0},{16,24},{24,16},{1,9},{9,1},{17,25},{25,17},{2,10},{10... | collective-permute-start | bytes 196616 | tf_op jit(solution)/shard_map/ppermute | solution.py:35
  8.2 7.3 %collective-permute-start.4 = (bf16[1024,512]{1,0:T(8,128)(2,1)}, bf16[1024,512]{1,0:T(8,128)(2,1)S(1)}, u32[]{:S(2)}, u32[]{:S(2)}) collective-permute-start(bf16[1024,512]{1,0:T(8,128)(2,1)} %shard_map.37), channel_id=1, source_target_pairs={{0,1},{1,0},{2,3},{3,2},{4,5},{5,4},{6,7},{7,6},{8,9},{9,8},{10,11... | collective-permute-start | bytes 3145736 | tf_op jit(solution)/shard_map/ppermute | solution.py:35
  8.3 4.5 %collective-permute-start.2 = (bf16[2,128,128]{2,1,0:T(8,128)(2,1)S(1)}, bf16[2,128,128]{2,1,0:T(8,128)(2,1)S(1)}, u32[]{:S(2)}, u32[]{:S(2)}) collective-permute-start(bf16[2,128,128]{2,1,0:T(8,128)(2,1)S(1)} %pad_maximum_fusion.10), channel_id=1, source_target_pairs={{0,16},{8,24},{16,0},{24,8},{1,17},{9,25},{17,1},{25,9},{2,18},{10... | collective-permute-start | bytes 196616 | tf_op jit(solution)/shard_map/ppermute | solution.py:35
  9.8 5.2 %collective-permute-start.3 = (bf16[2,128,128]{2,1,0:T(8,128)(2,1)S(1)}, bf16[2,128,128]{2,1,0:T(8,128)(2,1)S(1)}, u32[]{:S(2)}, u32[]{:S(2)}) collective-permute-start(bf16[2,128,128]{2,1,0:T(8,128)(2,1)S(1)} %pad_maximum_fusion.10), channel_id=1, source_target_pairs={{0,24},{8,16},{16,8},{24,0},{1,25},{9,17},{17,9},{25,1},{2,26},{10... | collective-permute-start | bytes 196616 | tf_op jit(solution)/shard_map/ppermute | solution.py:35
  16.1 5.0 %collective-permute-start.5 = (bf16[256,128]{1,0:T(8,128)(2,1)S(1)}, bf16[256,128]{1,0:T(8,128)(2,1)S(1)}, u32[]{:S(2)}, u32[]{:S(2)}) collective-permute-start(bf16[256,128]{1,0:T(8,128)(2,1)S(1)} %get-tuple-element.27), channel_id=1, source_target_pairs={{0,2},{1,3},{2,0},{3,1},{4,6},{5,7},{6,4},{7,5},{8,10},{9,11},{10,... | collective-permute-start | bytes 196616 | tf_op jit(solution)/shard_map/ppermute | solution.py:35
  17.7 6.6 %collective-permute-start.6 = (bf16[256,128]{1,0:T(8,128)(2,1)S(1)}, bf16[256,128]{1,0:T(8,128)(2,1)S(1)}, u32[]{:S(2)}, u32[]{:S(2)}) collective-permute-start(bf16[256,128]{1,0:T(8,128)(2,1)S(1)} %get-tuple-element.29), channel_id=1, source_target_pairs={{0,4},{1,5},{2,6},{3,7},{4,0},{5,1},{6,2},{7,3},{8,12},{9,13},{10,... | collective-permute-start | bytes 196616 | tf_op jit(solution)/shard_map/ppermute | solution.py:35
  20.3 6.1 %collective-permute-start.7 = (bf16[256,128]{1,0:T(8,128)(2,1)S(1)}, bf16[256,128]{1,0:T(8,128)(2,1)S(1)}, u32[]{:S(2)}, u32[]{:S(2)}) collective-permute-start(bf16[256,128]{1,0:T(8,128)(2,1)S(1)} %get-tuple-element.28), channel_id=1, source_target_pairs={{0,6},{1,7},{2,4},{3,5},{4,2},{5,3},{6,0},{7,1},{8,14},{9,15},{10,... | collective-permute-start | bytes 196616 | tf_op jit(solution)/shard_map/ppermute | solution.py:35
  26.5 4.7 %collective-permute-start.8 = (bf16[256,128]{1,0:T(8,128)(2,1)S(1)}, bf16[256,128]{1,0:T(8,128)(2,1)S(1)}, u32[]{:S(2)}, u32[]{:S(2)}) collective-permute-start(bf16[256,128]{1,0:T(8,128)(2,1)S(1)} %multiply_convert_fusion), channel_id=1, source_target_pairs={{0,2},{1,3},{2,0},{3,1},{4,6},{5,7},{6,4},{7,5},{8,10},{9,11},{10,... | collective-permute-start | bytes 196616 | tf_op jit(solution)/shard_map/ppermute | solution.py:35
  26.5 5.2 %collective-permute-start.9 = (bf16[256,128]{1,0:T(8,128)(2,1)S(1)}, bf16[256,128]{1,0:T(8,128)(2,1)S(1)}, u32[]{:S(2)}, u32[]{:S(2)}) collective-permute-start(bf16[256,128]{1,0:T(8,128)(2,1)S(1)} %multiply_convert_fusion), channel_id=1, source_target_pairs={{0,4},{1,5},{2,6},{3,7},{4,0},{5,1},{6,2},{7,3},{8,12},{9,13},{10,... | collective-permute-start | bytes 196616 | tf_op jit(solution)/shard_map/ppermute | solution.py:35
  28.1 6.1 %collective-permute-start.10 = (bf16[256,128]{1,0:T(8,128)(2,1)S(1)}, bf16[256,128]{1,0:T(8,128)(2,1)S(1)}, u32[]{:S(2)}, u32[]{:S(2)}) collective-permute-start(bf16[256,128]{1,0:T(8,128)(2,1)S(1)} %multiply_convert_fusion), channel_id=1, source_target_pairs={{0,6},{1,7},{2,4},{3,5},{4,2},{5,3},{6,0},{7,1},{8,14},{9,15},{10,... | collective-permute-start | bytes 196616 | tf_op jit(solution)/shard_map/ppermute | solution.py:35
  34.8 6.4 %collective-permute-start.13 = (bf16[512,128]{1,0:T(8,128)(2,1)S(1)}, bf16[512,128]{1,0:T(8,128)(2,1)S(1)}, u32[]{:S(2)}, u32[]{:S(2)}) collective-permute-start(bf16[512,128]{1,0:T(8,128)(2,1)S(1)} %fusion.7), channel_id=1, source_target_pairs={{0,16},{8,24},{16,0},{24,8},{1,17},{9,25},{17,1},{25,9},{2,18},{10... | collective-permute-start | bytes 393224 | tf_op jit(solution)/shard_map/ppermute | solution.py:35
  36.3 5.4 %collective-permute-start.11 = (bf16[512,128]{1,0:T(8,128)(2,1)S(1)}, bf16[512,128]{1,0:T(8,128)(2,1)S(1)}, u32[]{:S(2)}, u32[]{:S(2)}) collective-permute-start(bf16[512,128]{1,0:T(8,128)(2,1)S(1)} %fusion.6), channel_id=1, source_target_pairs={{0,8},{8,0},{16,24},{24,16},{1,9},{9,1},{17,25},{25,17},{2,10},{10... | collective-permute-start | bytes 393224 | tf_op jit(solution)/shard_map/ppermute | solution.py:35
  41.2 5.0 %collective-permute-start.14 = (bf16[512,128]{1,0:T(8,128)(2,1)S(1)}, bf16[512,128]{1,0:T(8,128)(2,1)S(1)}, u32[]{:S(2)}, u32[]{:S(2)}) collective-permute-start(bf16[512,128]{1,0:T(8,128)(2,1)S(1)} %add_convert_fusion.2), channel_id=1, source_target_pairs={{0,8},{8,0},{16,24},{24,16},{1,9},{9,1},{17,25},{25,17},{2,10},{10... | collective-permute-start | bytes 393224 | tf_op jit(solution)/shard_map/ppermute | solution.py:35
  41.8 5.0 %collective-permute-start.12 = (bf16[512,128]{1,0:T(8,128)(2,1)S(1)}, bf16[512,128]{1,0:T(8,128)(2,1)S(1)}, u32[]{:S(2)}, u32[]{:S(2)}) collective-permute-start(bf16[512,128]{1,0:T(8,128)(2,1)S(1)} %add_convert_fusion.3), channel_id=1, source_target_pairs={{0,16},{8,24},{16,0},{24,8},{1,17},{9,25},{17,1},{25,9},{2,18},{10... | collective-permute-start | bytes 393224 | tf_op jit(solution)/shard_map/ppermute | solution.py:35
  47.9 5.2 %collective-permute-start.16 = (bf16[256,128]{1,0:T(8,128)(2,1)S(1)}, bf16[256,128]{1,0:T(8,128)(2,1)S(1)}, u32[]{:S(2)}, u32[]{:S(2)}) collective-permute-start(bf16[256,128]{1,0:T(8,128)(2,1)S(1)} %get-tuple-element.18), channel_id=1, source_target_pairs={{0,4},{1,5},{2,6},{3,7},{4,0},{5,1},{6,2},{7,3},{8,12},{9,13},{10,... | collective-permute-start | bytes 196616 | tf_op jit(solution)/shard_map/ppermute | solution.py:35
  50.7 6.1 %collective-permute-start.17 = (bf16[256,128]{1,0:T(8,128)(2,1)S(1)}, bf16[256,128]{1,0:T(8,128)(2,1)S(1)}, u32[]{:S(2)}, u32[]{:S(2)}) collective-permute-start(bf16[256,128]{1,0:T(8,128)(2,1)S(1)} %get-tuple-element.17), channel_id=1, source_target_pairs={{0,6},{1,7},{2,4},{3,5},{4,2},{5,3},{6,0},{7,1},{8,14},{9,15},{10,... | collective-permute-start | bytes 196616 | tf_op jit(solution)/shard_map/ppermute | solution.py:35
  58.3 5.9 %collective-permute-start.19 = (bf16[256,128]{1,0:T(8,128)(2,1)S(1)}, bf16[256,128]{1,0:T(8,128)(2,1)S(1)}, u32[]{:S(2)}, u32[]{:S(2)}) collective-permute-start(bf16[256,128]{1,0:T(8,128)(2,1)S(1)} %subtract_convert_fusion), channel_id=1, source_target_pairs={{0,4},{1,5},{2,6},{3,7},{4,0},{5,1},{6,2},{7,3},{8,12},{9,13},{10,... | collective-permute-start | bytes 196616 | tf_op jit(solution)/shard_map/ppermute | solution.py:35
  59.4 6.2 %collective-permute-start.20 = (bf16[256,128]{1,0:T(8,128)(2,1)S(1)}, bf16[256,128]{1,0:T(8,128)(2,1)S(1)}, u32[]{:S(2)}, u32[]{:S(2)}) collective-permute-start(bf16[256,128]{1,0:T(8,128)(2,1)S(1)} %subtract_convert_fusion), channel_id=1, source_target_pairs={{0,6},{1,7},{2,4},{3,5},{4,2},{5,3},{6,0},{7,1},{8,14},{9,15},{10,... | collective-permute-start | bytes 196616 | tf_op jit(solution)/shard_map/ppermute | solution.py:35
  66.2 5.0 %collective-permute-start.23 = (bf16[512,128]{1,0:T(8,128)(2,1)S(1)}, bf16[512,128]{1,0:T(8,128)(2,1)S(1)}, u32[]{:S(2)}, u32[]{:S(2)}) collective-permute-start(bf16[512,128]{1,0:T(8,128)(2,1)S(1)} %fusion.9), channel_id=1, source_target_pairs={{0,16},{8,24},{16,0},{24,8},{1,17},{9,25},{17,1},{25,9},{2,18},{10... | collective-permute-start | bytes 393224 | tf_op jit(solution)/shard_map/ppermute | solution.py:35
  71.2 5.0 %collective-permute-start.24 = (bf16[512,128]{1,0:T(8,128)(2,1)S(1)}, bf16[512,128]{1,0:T(8,128)(2,1)S(1)}, u32[]{:S(2)}, u32[]{:S(2)}) collective-permute-start(bf16[512,128]{1,0:T(8,128)(2,1)S(1)} %add_convert_fusion), channel_id=1, source_target_pairs={{0,8},{8,0},{16,24},{24,16},{1,9},{9,1},{17,25},{25,17},{2,10},{10... | collective-permute-start | bytes 393224 | tf_op jit(solution)/shard_map/ppermute | solution.py:35
  73.4 5.0 %collective-permute-start.21 = (bf16[512,128]{1,0:T(8,128)(2,1)S(1)}, bf16[512,128]{1,0:T(8,128)(2,1)S(1)}, u32[]{:S(2)}, u32[]{:S(2)}) collective-permute-start(bf16[512,128]{1,0:T(8,128)(2,1)S(1)} %fusion.8), channel_id=1, source_target_pairs={{0,8},{8,0},{16,24},{24,16},{1,9},{9,1},{17,25},{25,17},{2,10},{10... | collective-permute-start | bytes 393224 | tf_op jit(solution)/shard_map/ppermute | solution.py:35
  76.4 7.2 %collective-permute-start.25 = (f32[512,128]{1,0:T(8,128)S(1)}, f32[512,128]{1,0:T(8,128)S(1)}, u32[]{:S(2)}, u32[]{:S(2)}) collective-permute-start(f32[512,128]{1,0:T(8,128)S(1)} %multiply_subtract_fusion), channel_id=1, source_target_pairs={{0,1},{1,0},{2,3},{3,2},{4,5},{5,4},{6,7},{7,6},{8,9},{9,8},{10,11... | collective-permute-start | bytes 786440 | tf_op jit(solution)/shard_map/ppermute | solution.py:35
  78.5 5.0 %collective-permute-start.22 = (bf16[512,128]{1,0:T(8,128)(2,1)S(1)}, bf16[512,128]{1,0:T(8,128)(2,1)S(1)}, u32[]{:S(2)}, u32[]{:S(2)}) collective-permute-start(bf16[512,128]{1,0:T(8,128)(2,1)S(1)} %add_convert_fusion.1), channel_id=1, source_target_pairs={{0,16},{8,24},{16,0},{24,8},{1,17},{9,25},{17,1},{25,9},{2,18},{10... | collective-permute-start | bytes 393224 | tf_op jit(solution)/shard_map/ppermute | solution.py:35
  90.6 6.0 %collective-permute-start.28 = (f32[136,128]{1,0:T(8,128)S(1)}, f32[136,128]{1,0:T(8,128)S(1)}, u32[]{:S(2)}, u32[]{:S(2)}) collective-permute-start(f32[136,128]{1,0:T(8,128)S(1)} %add.171), channel_id=1, source_target_pairs={{0,4},{1,5},{2,6},{3,7},{4,0},{5,1},{6,2},{7,3},{8,12},{9,13},{10,... | collective-permute-start | bytes 208904 | tf_op jit(solution)/shard_map/ppermute | solution.py:35
  (9 other events, 26.2 us)

commit v4 on v3

--- a/solution.py
+++ b/solution.py
@@ -115,14 +115,15 @@
     return jnp.concatenate(groups)
 
 
-def orthonormal(total, partner, filtered, mine_first, scale):
+def orthonormal(total, partner, filtered, mine_first, rank, piece_rows, scale):
     size = total.shape[1]
     tall = 16
 
-    def kernel(first_ref, total_ref, partner_ref, filtered_ref, out_ref):
+    def kernel(flags_ref, total_ref, partner_ref, filtered_ref, out_ref):
         rows = lax.broadcasted_iota(jnp.int32, (size, size), 0)
         lanes = lax.broadcasted_iota(jnp.int32, (size, size), 1)
-        is_first = first_ref[0] != 0
+        is_first = flags_ref[0] != 0
+        start = pl.multiple_of(flags_ref[1] * piece_rows, piece_rows)
         cross = jnp.where(is_first, total_ref[:size, :], partner_ref[:size, :])
         both = jnp.where(is_first, partner_ref[:size, :], total_ref[:size, :])
         diagonal = jnp.where(is_first, partner_ref[size : size + 1, :], total_ref[size : size + 1, :])
@@ -134,21 +135,18 @@
         second = jnp.where(lanes == rows, diagonal, second)
         last = factor(second - exact_dot(below, below, ((1,), (1,))), tall)
         last = jnp.where(rows >= lanes, last, 0.0)
-        left = exact_dot(filtered_ref[:, :size], first, ((1,), (1,)))
+        left = exact_dot(filtered_ref[pl.ds(start, piece_rows), :size], first, ((1,), (1,)))
         out_ref[:, :size] = scale * left
-        right = filtered_ref[:, size:] - exact_dot(left, below, ((1,), (1,)))
+        right = filtered_ref[pl.ds(start, piece_rows), size:] - exact_dot(left, below, ((1,), (1,)))
         out_ref[:, size:] = scale * exact_dot(right, last, ((1,), (1,)))
 
+    vmem = pl.BlockSpec(memory_space=pltpu.VMEM)
     return pl.pallas_call(
         kernel,
-        grid_spec=pltpu.PrefetchScalarGridSpec(
-            num_scalar_prefetch=1,
-            grid=(1,),
-            in_specs=[pl.BlockSpec(a.shape, lambda i, first: (0, 0)) for a in (total, partner, filtered)],
-            out_specs=pl.BlockSpec(filtered.shape, lambda i, first: (0, 0)),
-        ),
-        out_shape=jax.ShapeDtypeStruct(filtered.shape, jnp.float32),
-    )(mine_first.astype(jnp.int32).reshape(1), total, partner, filtered)
+        in_specs=[pl.BlockSpec(memory_space=pltpu.SMEM), vmem, vmem, vmem],
+        out_specs=vmem,
+        out_shape=jax.ShapeDtypeStruct((piece_rows, 2 * size), jnp.float32),
+    )(jnp.stack([mine_first.astype(jnp.int32), rank]), total, partner, filtered)
 
 
 def on_device(blocks, col_index, vectors):
@@ -170,15 +168,17 @@
     narrow = jnp.bfloat16
 
     mine_first = core == 0
-    left, right = vectors[:, :half], vectors[:, half:]
-    own_start = jnp.where(mine_first, left, right)
-    other_start = swap(jnp.where(mine_first, right, left), "col", 1)
-    start = jnp.stack([own_start, other_start])
-    low_start = start.astype(narrow)
-
+
+    def kept_and_sent(value):
+        left, right = value[:, :half], value[:, half:]
+        return jnp.where(mine_first, left, right), jnp.where(mine_first, right, left)
+
+    low_start = vectors.astype(narrow)
     arrived = [low_start] + [swap(low_start, "row", k) for k in range(1, row_count)]
-    low_own = in_order([value[0] for value in arrived], row_rank)
-    low_other = in_order([value[1] for value in arrived], row_rank)
+    low_own, sent = kept_and_sent(in_order(arrived, row_rank))
+    low_other = swap(sent, "col", 1)
+    own_start, sent = kept_and_sent(vectors)
+    other_start = swap(sent, "col", 1)
 
     own = densify(blocks, col_index, tile_blocks)
     other = swap(own, "col", 1)
@@ -229,9 +229,12 @@
     def sum_over_row(one, two):
         for level, (bit_one, bit_two) in enumerate(zip(row_bits, reversed(row_bits))):
             sent = narrow if level < 2 else jnp.float32
-            low_one, low_two = one.astype(sent), two.astype(sent)
-            one = low_one.astype(jnp.float32) + swap(low_one, "row", bit_one).astype(jnp.float32)
-            two = low_two.astype(jnp.float32) + swap(low_two, "row", bit_two).astype(jnp.float32)
+            low_one, low_two = lax.optimization_barrier((one.astype(sent), two.astype(sent)))
+            from_one, from_two = lax.optimization_barrier(
+                (swap(low_one, "row", bit_one), swap(low_two, "row", bit_two))
+            )
+            one = low_one.astype(jnp.float32) + from_one.astype(jnp.float32)
+            two = low_two.astype(jnp.float32) + from_two.astype(jnp.float32)
         return one, two
 
     def placed(piece):
@@ -242,8 +245,8 @@
     low = gather_over_z(y1.astype(narrow))
     part_own, part_other = backward(low)
     y2_own, y2_other = sum_over_row(
-        scales[1] * part_own - carries[1] * placed(start[0]),
-        scales[1] * part_other - carries[1] * placed(start[1]),
+        scales[1] * part_own - carries[1] * placed(own_start),
+        scales[1] * part_other - carries[1] * placed(other_start),
     )
     y3 = scales[2] * sum_over_z(forward(y2_own.astype(narrow), y2_other.astype(narrow))) - carries[2] * y1
     low = gather_over_z(y3.astype(narrow))
@@ -269,9 +272,8 @@
     for bit in z_bits:
         total = total + swap(total, "col", bit)
     partner = swap(total, "col", 1)
-    mine = lax.dynamic_slice_in_dim(filtered, row_rank * piece_rows, piece_rows, 0)
     orbital_count = piece_rows * row_count * col_count
-    return orthonormal(total, partner, mine, mine_first, math.sqrt(orbital_count))
+    return orthonormal(total, partner, filtered, mine_first, row_rank, piece_rows, math.sqrt(orbital_count))
 
 
 def solution(mesh):

time: 108 us -> 105 us (0.972)
  waiting for transfers between devices: 54.9 us -> 48.5 us
  starting transfers between devices: 31.9 us -> 34.3 us
    ppermute x30 -> x31, waiting for transfers between devices: 54.9 us -> 48.5 us  [swap(): return lax.ppermute(value, axis, [(i, i ^ distance) for i in range(count)])]
    ppermute x30 -> x31, starting transfers between devices: 31.9 us -> 34.3 us  [swap(): return lax.ppermute(value, axis, [(i, i ^ distance) for i in range(count)])]
  transfers between devices with their start and end apart: 30 -> 31, of which waited for: 22 -> 23; matrix products, arithmetic and copies ran while one was open for 3% -> 3% of each run, Pallas kernels for 3% -> 3%
where the time goes in v4:
time: 105 us
  waiting for transfers between devices  48.5 us (46%)
  starting transfers between devices  34.3 us (33%)
  Pallas kernels  12.5 us (12%)
  matrix products  4.72 us (4%)
  other arithmetic  3.72 us (4%)
    ppermute x31, waiting for transfers between devices, swap(): return lax.ppermute(value, axis, [(i, i ^ distance) for i in range(count)])  48.5 us
    ppermute x31, starting transfers between devices, swap(): return lax.ppermute(value, axis, [(i, i ^ distance) for i in range(count)])  34.3 us
    pallas_call x1, Pallas kernels, orthonormal(): pl.pallas_call(kernel, in_specs=[pl.BlockSpec(memory_space=pltpu.SMEM), v...  9.48 us
    pallas_call x1, Pallas kernels, densify(): pl.pallas_call(kernel, grid_spec=pltpu.PrefetchScalarGridSpec(num_scalar_...  3.02 us
  transfers between devices with their start and end apart: 31, of which 23 were waited for; matrix products, arithmetic and copies ran while one was open for 3% of the time, Pallas kernels for 3%

profile of v4, /device:TPU:0, one launch (start us, length us, event | category | flops | bytes accessed | tf_op | source)
XLA Modules:
  0.0 105.1 jit_solution(1427654621986965449)
XLA Ops:
  1.0 3.0 %collective-permute-start = (bf16[128,256]{1,0:T(8,128)(2,1)S(1)}, bf16[128,256]{1,0:T(8,128)(2,1)S(1)}, u32[]{:S(2)}, u32[]{:S(2)}) collective-permute-start(bf16[128,256]{1,0:T(8,128)(2,1)S(1)} %convert_element_type.134), channel_id=1, source_target_pairs={{0,8},{8,0},{16,24},{24,16},{1,9},{9,1},{17,25},{25,17},{2,10},{10... | collective-permute-start | bytes 196616 | tf_op jit(solution)/shard_map/ppermute | solution.py:35
  4.0 1.5 %collective-permute-start.1 = (bf16[128,256]{1,0:T(8,128)(2,1)S(1)}, bf16[128,256]{1,0:T(8,128)(2,1)S(1)}, u32[]{:S(2)}, u32[]{:S(2)}) collective-permute-start(bf16[128,256]{1,0:T(8,128)(2,1)S(1)} %convert_element_type.134), channel_id=1, source_target_pairs={{0,16},{8,24},{16,0},{24,8},{1,17},{9,25},{17,1},{25,9},{2,18},{10... | collective-permute-start | bytes 196616 | tf_op jit(solution)/shard_map/ppermute | solution.py:35
  5.5 3.0 %shard_map.37 = bf16[1024,512]{1,0:T(8,128)(2,1)} custom-call(s32[8,6]{1,0:T(8,128)} %index_ref.1, bf16[8,6,128,128]{3,2,1,0:T(8,128)(2,1)} %blocks_ref.1), custom_call_target="tpu_custom_call" | custom-call | tf_op jit(solution)/shard_map/pallas_call | solution.py:65
  12.7 1.6 %collective-permute-start.5 = (bf16[256,128]{1,0:T(8,128)(2,1)S(1)}, bf16[256,128]{1,0:T(8,128)(2,1)S(1)}, u32[]{:S(2)}, u32[]{:S(2)}) collective-permute-start(bf16[256,128]{1,0:T(8,128)(2,1)S(1)} %get-tuple-element.59), channel_id=1, source_target_pairs={{0,2},{1,3},{2,0},{3,1},{4,6},{5,7},{6,4},{7,5},{8,10},{9,11},{10,... | collective-permute-start | bytes 196616 | tf_op jit(solution)/shard_map/ppermute | solution.py:35
  14.4 2.6 %collective-permute-start.6 = (bf16[256,128]{1,0:T(8,128)(2,1)S(1)}, bf16[256,128]{1,0:T(8,128)(2,1)S(1)}, u32[]{:S(2)}, u32[]{:S(2)}) collective-permute-start(bf16[256,128]{1,0:T(8,128)(2,1)S(1)} %get-tuple-element.61), channel_id=1, source_target_pairs={{0,4},{1,5},{2,6},{3,7},{4,0},{5,1},{6,2},{7,3},{8,12},{9,13},{10,... | collective-permute-start | bytes 196616 | tf_op jit(solution)/shard_map/ppermute | solution.py:35
  17.2 4.7 %collective-permute-done.6 = bf16[256,128]{1,0:T(8,128)(2,1)S(1)} collective-permute-done((bf16[256,128]{1,0:T(8,128)(2,1)S(1)}, bf16[256,128]{1,0:T(8,128)(2,1)S(1)}, u32[]{:S(2)}, u32[]{:S(2)}) %collective-permute-start.6) | collective-permute-done | bytes 65568 | tf_op jit(solution)/shard_map/ppermute | solution.py:35
  24.1 1.7 %collective-permute-start.9 = (bf16[256,128]{1,0:T(8,128)(2,1)S(1)}, bf16[256,128]{1,0:T(8,128)(2,1)S(1)}, u32[]{:S(2)}, u32[]{:S(2)}) collective-permute-start(bf16[256,128]{1,0:T(8,128)(2,1)S(1)} %multiply_convert_fusion), channel_id=1, source_target_pairs={{0,4},{1,5},{2,6},{3,7},{4,0},{5,1},{6,2},{7,3},{8,12},{9,13},{10,... | collective-permute-start | bytes 196616 | tf_op jit(solution)/shard_map/ppermute | solution.py:35
  25.8 1.8 %collective-permute-start.10 = (bf16[256,128]{1,0:T(8,128)(2,1)S(1)}, bf16[256,128]{1,0:T(8,128)(2,1)S(1)}, u32[]{:S(2)}, u32[]{:S(2)}) collective-permute-start(bf16[256,128]{1,0:T(8,128)(2,1)S(1)} %multiply_convert_fusion), channel_id=1, source_target_pairs={{0,6},{1,7},{2,4},{3,5},{4,2},{5,3},{6,0},{7,1},{8,14},{9,15},{10,... | collective-permute-start | bytes 196616 | tf_op jit(solution)/shard_map/ppermute | solution.py:35
  27.9 2.5 %collective-permute-done.9 = bf16[256,128]{1,0:T(8,128)(2,1)S(1)} collective-permute-done((bf16[256,128]{1,0:T(8,128)(2,1)S(1)}, bf16[256,128]{1,0:T(8,128)(2,1)S(1)}, u32[]{:S(2)}, u32[]{:S(2)}) %collective-permute-start.9) | collective-permute-done | bytes 65568 | tf_op jit(solution)/shard_map/ppermute | solution.py:35
  30.3 1.5 %collective-permute-done.10 = bf16[256,128]{1,0:T(8,128)(2,1)S(1)} collective-permute-done((bf16[256,128]{1,0:T(8,128)(2,1)S(1)}, bf16[256,128]{1,0:T(8,128)(2,1)S(1)}, u32[]{:S(2)}, u32[]{:S(2)}) %collective-permute-start.10) | collective-permute-done | bytes 65568 | tf_op jit(solution)/shard_map/ppermute | solution.py:35
  35.9 2.1 %collective-permute-done.12 = bf16[512,128]{1,0:T(8,128)(2,1)S(1)} collective-permute-done((bf16[512,128]{1,0:T(8,128)(2,1)S(1)}, bf16[512,128]{1,0:T(8,128)(2,1)S(1)}, u32[]{:S(2)}, u32[]{:S(2)}) %collective-permute-start.12) | collective-permute-done | bytes 131104 | tf_op jit(solution)/shard_map/ppermute | solution.py:35
  38.0 2.7 %collective-permute-done.13 = bf16[512,128]{1,0:T(8,128)(2,1)S(1)} collective-permute-done((bf16[512,128]{1,0:T(8,128)(2,1)S(1)}, bf16[512,128]{1,0:T(8,128)(2,1)S(1)}, u32[]{:S(2)}, u32[]{:S(2)}) %collective-permute-start.13) | collective-permute-done | bytes 131104 | tf_op jit(solution)/shard_map/ppermute | solution.py:35
  40.8 1.6 %collective-permute-start.14 = (bf16[512,128]{1,0:T(8,128)(2,1)S(1)}, bf16[512,128]{1,0:T(8,128)(2,1)S(1)}, u32[]{:S(2)}, u32[]{:S(2)}) collective-permute-start(bf16[512,128]{1,0:T(8,128)(2,1)S(1)} %get-tuple-element.25), channel_id=1, source_target_pairs={{0,16},{8,24},{16,0},{24,8},{1,17},{9,25},{17,1},{25,9},{2,18},{10... | collective-permute-start | bytes 393224 | tf_op jit(solution)/shard_map/ppermute | solution.py:35
  42.9 2.9 %collective-permute-done.14 = bf16[512,128]{1,0:T(8,128)(2,1)S(1)} collective-permute-done((bf16[512,128]{1,0:T(8,128)(2,1)S(1)}, bf16[512,128]{1,0:T(8,128)(2,1)S(1)}, u32[]{:S(2)}, u32[]{:S(2)}) %collective-permute-start.14) | collective-permute-done | bytes 131104 | tf_op jit(solution)/shard_map/ppermute | solution.py:35
  48.4 2.2 %collective-permute-start.17 = (bf16[256,128]{1,0:T(8,128)(2,1)S(1)}, bf16[256,128]{1,0:T(8,128)(2,1)S(1)}, u32[]{:S(2)}, u32[]{:S(2)}) collective-permute-start(bf16[256,128]{1,0:T(8,128)(2,1)S(1)} %get-tuple-element.50), channel_id=1, source_target_pairs={{0,4},{1,5},{2,6},{3,7},{4,0},{5,1},{6,2},{7,3},{8,12},{9,13},{10,... | collective-permute-start | bytes 196616 | tf_op jit(solution)/shard_map/ppermute | solution.py:35
  50.6 2.2 %collective-permute-start.18 = (bf16[256,128]{1,0:T(8,128)(2,1)S(1)}, bf16[256,128]{1,0:T(8,128)(2,1)S(1)}, u32[]{:S(2)}, u32[]{:S(2)}) collective-permute-start(bf16[256,128]{1,0:T(8,128)(2,1)S(1)} %get-tuple-element.49), channel_id=1, source_target_pairs={{0,6},{1,7},{2,4},{3,5},{4,2},{5,3},{6,0},{7,1},{8,14},{9,15},{10,... | collective-permute-start | bytes 196616 | tf_op jit(solution)/shard_map/ppermute | solution.py:35
  53.6 3.4 %collective-permute-done.17 = bf16[256,128]{1,0:T(8,128)(2,1)S(1)} collective-permute-done((bf16[256,128]{1,0:T(8,128)(2,1)S(1)}, bf16[256,128]{1,0:T(8,128)(2,1)S(1)}, u32[]{:S(2)}, u32[]{:S(2)}) %collective-permute-start.17) | collective-permute-done | bytes 65568 | tf_op jit(solution)/shard_map/ppermute | solution.py:35
  59.9 1.7 %collective-permute-start.21 = (bf16[256,128]{1,0:T(8,128)(2,1)S(1)}, bf16[256,128]{1,0:T(8,128)(2,1)S(1)}, u32[]{:S(2)}, u32[]{:S(2)}) collective-permute-start(bf16[256,128]{1,0:T(8,128)(2,1)S(1)} %subtract_convert_fusion), channel_id=1, source_target_pairs={{0,6},{1,7},{2,4},{3,5},{4,2},{5,3},{6,0},{7,1},{8,14},{9,15},{10,... | collective-permute-start | bytes 196616 | tf_op jit(solution)/shard_map/ppermute | solution.py:35
  61.6 2.9 %collective-permute-done.20 = bf16[256,128]{1,0:T(8,128)(2,1)S(1)} collective-permute-done((bf16[256,128]{1,0:T(8,128)(2,1)S(1)}, bf16[256,128]{1,0:T(8,128)(2,1)S(1)}, u32[]{:S(2)}, u32[]{:S(2)}) %collective-permute-start.20) | collective-permute-done | bytes 65568 | tf_op jit(solution)/shard_map/ppermute | solution.py:35
  68.8 3.3 %collective-permute-done.22 = bf16[512,128]{1,0:T(8,128)(2,1)S(1)} collective-permute-done((bf16[512,128]{1,0:T(8,128)(2,1)S(1)}, bf16[512,128]{1,0:T(8,128)(2,1)S(1)}, u32[]{:S(2)}, u32[]{:S(2)}) %collective-permute-start.22) | collective-permute-done | bytes 131104 | tf_op jit(solution)/shard_map/ppermute | solution.py:35
  75.2 2.7 %collective-permute-done.24 = bf16[512,128]{1,0:T(8,128)(2,1)S(1)} collective-permute-done((bf16[512,128]{1,0:T(8,128)(2,1)S(1)}, bf16[512,128]{1,0:T(8,128)(2,1)S(1)}, u32[]{:S(2)}, u32[]{:S(2)}) %collective-permute-start.24) | collective-permute-done | bytes 131104 | tf_op jit(solution)/shard_map/ppermute | solution.py:35
  83.9 3.6 %collective-permute-done.28 = f32[136,128]{1,0:T(8,128)S(1)} collective-permute-done((f32[136,128]{1,0:T(8,128)S(1)}, f32[136,128]{1,0:T(8,128)S(1)}, u32[]{:S(2)}, u32[]{:S(2)}) %collective-permute-start.28) | collective-permute-done | bytes 69664 | tf_op jit(solution)/shard_map/ppermute | solution.py:35
  89.4 4.2 %collective-permute-done.29 = f32[136,128]{1,0:T(8,128)S(1)} collective-permute-done((f32[136,128]{1,0:T(8,128)S(1)}, f32[136,128]{1,0:T(8,128)S(1)}, u32[]{:S(2)}, u32[]{:S(2)}) %collective-permute-start.29) | collective-permute-done | bytes 69664 | tf_op jit(solution)/shard_map/ppermute | solution.py:35
  95.6 9.5 %shard_map.38 = f32[128,256]{1,0:T(8,128)} custom-call(s32[2]{0:T(128)} %pad_add_fusion.flags_ref, f32[136,128]{1,0:T(8,128)} %copy-done.2, f32[136,128]{1,0:T(8,128)} %copy-done.3, f32[512,256]{1,0:T(8,128)} %pad_maximum_fusion.filtered_ref), custom_call_target="tpu_custom_call" | custom-call | tf_op jit(solution)/shard_map/pallas_call | solution.py:144
  (96 shorter events, 35.6 us)
Async XLA Ops:
  1.0 8.2 %collective-permute-start = (bf16[128,256]{1,0:T(8,128)(2,1)S(1)}, bf16[128,256]{1,0:T(8,128)(2,1)S(1)}, u32[]{:S(2)}, u32[]{:S(2)}) collective-permute-start(bf16[128,256]{1,0:T(8,128)(2,1)S(1)} %convert_element_type.134), channel_id=1, source_target_pairs={{0,8},{8,0},{16,24},{24,16},{1,9},{9,1},{17,25},{25,17},{2,10},{10... | collective-permute-start | bytes 196616 | tf_op jit(solution)/shard_map/ppermute | solution.py:35
  4.0 5.3 %collective-permute-start.1 = (bf16[128,256]{1,0:T(8,128)(2,1)S(1)}, bf16[128,256]{1,0:T(8,128)(2,1)S(1)}, u32[]{:S(2)}, u32[]{:S(2)}) collective-permute-start(bf16[128,256]{1,0:T(8,128)(2,1)S(1)} %convert_element_type.134), channel_id=1, source_target_pairs={{0,16},{8,24},{16,0},{24,8},{1,17},{9,25},{17,1},{25,9},{2,18},{10... | collective-permute-start | bytes 196616 | tf_op jit(solution)/shard_map/ppermute | solution.py:35
  5.5 5.2 %collective-permute-start.2 = (bf16[128,256]{1,0:T(8,128)(2,1)S(1)}, bf16[128,256]{1,0:T(8,128)(2,1)S(1)}, u32[]{:S(2)}, u32[]{:S(2)}) collective-permute-start(bf16[128,256]{1,0:T(8,128)(2,1)S(1)} %convert_element_type.134), channel_id=1, source_target_pairs={{0,24},{8,16},{16,8},{24,0},{1,25},{9,17},{17,9},{25,1},{2,26},{10... | collective-permute-start | bytes 196616 | tf_op jit(solution)/shard_map/ppermute | solution.py:35
  8.6 19.1 %collective-permute-start.11 = (f32[128,128]{1,0:T(8,128)S(1)}, f32[128,128]{1,0:T(8,128)S(1)}, u32[]{:S(2)}, u32[]{:S(2)}) collective-permute-start(f32[128,128]{1,0:T(8,128)S(1)} %get-tuple-element.66), channel_id=1, source_target_pairs={{0,1},{1,0},{2,3},{3,2},{4,5},{5,4},{6,7},{7,6},{8,9},{9,8},{10,11... | collective-permute-start | bytes 196616 | tf_op jit(solution)/shard_map/ppermute | solution.py:35
  12.7 4.5 %collective-permute-start.5 = (bf16[256,128]{1,0:T(8,128)(2,1)S(1)}, bf16[256,128]{1,0:T(8,128)(2,1)S(1)}, u32[]{:S(2)}, u32[]{:S(2)}) collective-permute-start(bf16[256,128]{1,0:T(8,128)(2,1)S(1)} %get-tuple-element.59), channel_id=1, source_target_pairs={{0,2},{1,3},{2,0},{3,1},{4,6},{5,7},{6,4},{7,5},{8,10},{9,11},{10,... | collective-permute-start | bytes 196616 | tf_op jit(solution)/shard_map/ppermute | solution.py:35
  14.4 7.5 %collective-permute-start.6 = (bf16[256,128]{1,0:T(8,128)(2,1)S(1)}, bf16[256,128]{1,0:T(8,128)(2,1)S(1)}, u32[]{:S(2)}, u32[]{:S(2)}) collective-permute-start(bf16[256,128]{1,0:T(8,128)(2,1)S(1)} %get-tuple-element.61), channel_id=1, source_target_pairs={{0,4},{1,5},{2,6},{3,7},{4,0},{5,1},{6,2},{7,3},{8,12},{9,13},{10,... | collective-permute-start | bytes 196616 | tf_op jit(solution)/shard_map/ppermute | solution.py:35
  17.0 6.2 %collective-permute-start.7 = (bf16[256,128]{1,0:T(8,128)(2,1)S(1)}, bf16[256,128]{1,0:T(8,128)(2,1)S(1)}, u32[]{:S(2)}, u32[]{:S(2)}) collective-permute-start(bf16[256,128]{1,0:T(8,128)(2,1)S(1)} %get-tuple-element.60), channel_id=1, source_target_pairs={{0,6},{1,7},{2,4},{3,5},{4,2},{5,3},{6,0},{7,1},{8,14},{9,15},{10,... | collective-permute-start | bytes 196616 | tf_op jit(solution)/shard_map/ppermute | solution.py:35
  23.2 4.7 %collective-permute-start.8 = (bf16[256,128]{1,0:T(8,128)(2,1)S(1)}, bf16[256,128]{1,0:T(8,128)(2,1)S(1)}, u32[]{:S(2)}, u32[]{:S(2)}) collective-permute-start(bf16[256,128]{1,0:T(8,128)(2,1)S(1)} %multiply_convert_fusion), channel_id=1, source_target_pairs={{0,2},{1,3},{2,0},{3,1},{4,6},{5,7},{6,4},{7,5},{8,10},{9,11},{10,... | collective-permute-start | bytes 196616 | tf_op jit(solution)/shard_map/ppermute | solution.py:35
  24.1 6.2 %collective-permute-start.9 = (bf16[256,128]{1,0:T(8,128)(2,1)S(1)}, bf16[256,128]{1,0:T(8,128)(2,1)S(1)}, u32[]{:S(2)}, u32[]{:S(2)}) collective-permute-start(bf16[256,128]{1,0:T(8,128)(2,1)S(1)} %multiply_convert_fusion), channel_id=1, source_target_pairs={{0,4},{1,5},{2,6},{3,7},{4,0},{5,1},{6,2},{7,3},{8,12},{9,13},{10,... | collective-permute-start | bytes 196616 | tf_op jit(solution)/shard_map/ppermute | solution.py:35
  25.8 6.1 %collective-permute-start.10 = (bf16[256,128]{1,0:T(8,128)(2,1)S(1)}, bf16[256,128]{1,0:T(8,128)(2,1)S(1)}, u32[]{:S(2)}, u32[]{:S(2)}) collective-permute-start(bf16[256,128]{1,0:T(8,128)(2,1)S(1)} %multiply_convert_fusion), channel_id=1, source_target_pairs={{0,6},{1,7},{2,4},{3,5},{4,2},{5,3},{6,0},{7,1},{8,14},{9,15},{10,... | collective-permute-start | bytes 196616 | tf_op jit(solution)/shard_map/ppermute | solution.py:35
  33.0 5.0 %collective-permute-start.12 = (bf16[512,128]{1,0:T(8,128)(2,1)S(1)}, bf16[512,128]{1,0:T(8,128)(2,1)S(1)}, u32[]{:S(2)}, u32[]{:S(2)}) collective-permute-start(bf16[512,128]{1,0:T(8,128)(2,1)S(1)} %fusion.6), channel_id=1, source_target_pairs={{0,8},{8,0},{16,24},{24,16},{1,9},{9,1},{17,25},{25,17},{2,10},{10... | collective-permute-start | bytes 393224 | tf_op jit(solution)/shard_map/ppermute | solution.py:35
  34.4 6.3 %collective-permute-start.13 = (bf16[512,128]{1,0:T(8,128)(2,1)S(1)}, bf16[512,128]{1,0:T(8,128)(2,1)S(1)}, u32[]{:S(2)}, u32[]{:S(2)}) collective-permute-start(bf16[512,128]{1,0:T(8,128)(2,1)S(1)} %fusion.7), channel_id=1, source_target_pairs={{0,16},{8,24},{16,0},{24,8},{1,17},{9,25},{17,1},{25,9},{2,18},{10... | collective-permute-start | bytes 393224 | tf_op jit(solution)/shard_map/ppermute | solution.py:35
  40.8 5.0 %collective-permute-start.14 = (bf16[512,128]{1,0:T(8,128)(2,1)S(1)}, bf16[512,128]{1,0:T(8,128)(2,1)S(1)}, u32[]{:S(2)}, u32[]{:S(2)}) collective-permute-start(bf16[512,128]{1,0:T(8,128)(2,1)S(1)} %get-tuple-element.25), channel_id=1, source_target_pairs={{0,16},{8,24},{16,0},{24,8},{1,17},{9,25},{17,1},{25,9},{2,18},{10... | collective-permute-start | bytes 393224 | tf_op jit(solution)/shard_map/ppermute | solution.py:35
  42.3 5.0 %collective-permute-start.15 = (bf16[512,128]{1,0:T(8,128)(2,1)S(1)}, bf16[512,128]{1,0:T(8,128)(2,1)S(1)}, u32[]{:S(2)}, u32[]{:S(2)}) collective-permute-start(bf16[512,128]{1,0:T(8,128)(2,1)S(1)} %get-tuple-element.26), channel_id=1, source_target_pairs={{0,8},{8,0},{16,24},{24,16},{1,9},{9,1},{17,25},{25,17},{2,10},{10... | collective-permute-start | bytes 393224 | tf_op jit(solution)/shard_map/ppermute | solution.py:35
  48.3 5.2 %collective-permute-start.16 = (bf16[256,128]{1,0:T(8,128)(2,1)S(1)}, bf16[256,128]{1,0:T(8,128)(2,1)S(1)}, u32[]{:S(2)}, u32[]{:S(2)}) collective-permute-start(bf16[256,128]{1,0:T(8,128)(2,1)S(1)} %get-tuple-element.48), channel_id=1, source_target_pairs={{0,2},{1,3},{2,0},{3,1},{4,6},{5,7},{6,4},{7,5},{8,10},{9,11},{10,... | collective-permute-start | bytes 196616 | tf_op jit(solution)/shard_map/ppermute | solution.py:35
  48.4 8.6 %collective-permute-start.17 = (bf16[256,128]{1,0:T(8,128)(2,1)S(1)}, bf16[256,128]{1,0:T(8,128)(2,1)S(1)}, u32[]{:S(2)}, u32[]{:S(2)}) collective-permute-start(bf16[256,128]{1,0:T(8,128)(2,1)S(1)} %get-tuple-element.50), channel_id=1, source_target_pairs={{0,4},{1,5},{2,6},{3,7},{4,0},{5,1},{6,2},{7,3},{8,12},{9,13},{10,... | collective-permute-start | bytes 196616 | tf_op jit(solution)/shard_map/ppermute | solution.py:35
  50.6 6.4 %collective-permute-start.18 = (bf16[256,128]{1,0:T(8,128)(2,1)S(1)}, bf16[256,128]{1,0:T(8,128)(2,1)S(1)}, u32[]{:S(2)}, u32[]{:S(2)}) collective-permute-start(bf16[256,128]{1,0:T(8,128)(2,1)S(1)} %get-tuple-element.49), channel_id=1, source_target_pairs={{0,6},{1,7},{2,4},{3,5},{4,2},{5,3},{6,0},{7,1},{8,14},{9,15},{10,... | collective-permute-start | bytes 196616 | tf_op jit(solution)/shard_map/ppermute | solution.py:35
  58.6 5.9 %collective-permute-start.20 = (bf16[256,128]{1,0:T(8,128)(2,1)S(1)}, bf16[256,128]{1,0:T(8,128)(2,1)S(1)}, u32[]{:S(2)}, u32[]{:S(2)}) collective-permute-start(bf16[256,128]{1,0:T(8,128)(2,1)S(1)} %subtract_convert_fusion), channel_id=1, source_target_pairs={{0,4},{1,5},{2,6},{3,7},{4,0},{5,1},{6,2},{7,3},{8,12},{9,13},{10,... | collective-permute-start | bytes 196616 | tf_op jit(solution)/shard_map/ppermute | solution.py:35
  59.9 6.1 %collective-permute-start.21 = (bf16[256,128]{1,0:T(8,128)(2,1)S(1)}, bf16[256,128]{1,0:T(8,128)(2,1)S(1)}, u32[]{:S(2)}, u32[]{:S(2)}) collective-permute-start(bf16[256,128]{1,0:T(8,128)(2,1)S(1)} %subtract_convert_fusion), channel_id=1, source_target_pairs={{0,6},{1,7},{2,4},{3,5},{4,2},{5,3},{6,0},{7,1},{8,14},{9,15},{10,... | collective-permute-start | bytes 196616 | tf_op jit(solution)/shard_map/ppermute | solution.py:35
  67.1 5.0 %collective-permute-start.22 = (bf16[512,128]{1,0:T(8,128)(2,1)S(1)}, bf16[512,128]{1,0:T(8,128)(2,1)S(1)}, u32[]{:S(2)}, u32[]{:S(2)}) collective-permute-start(bf16[512,128]{1,0:T(8,128)(2,1)S(1)} %fusion.8), channel_id=1, source_target_pairs={{0,8},{8,0},{16,24},{24,16},{1,9},{9,1},{17,25},{25,17},{2,10},{10... | collective-permute-start | bytes 393224 | tf_op jit(solution)/shard_map/ppermute | solution.py:35
  67.8 5.0 %collective-permute-start.23 = (bf16[512,128]{1,0:T(8,128)(2,1)S(1)}, bf16[512,128]{1,0:T(8,128)(2,1)S(1)}, u32[]{:S(2)}, u32[]{:S(2)}) collective-permute-start(bf16[512,128]{1,0:T(8,128)(2,1)S(1)} %fusion.9), channel_id=1, source_target_pairs={{0,16},{8,24},{16,0},{24,8},{1,17},{9,25},{17,1},{25,9},{2,18},{10... | collective-permute-start | bytes 393224 | tf_op jit(solution)/shard_map/ppermute | solution.py:35
  72.9 5.0 %collective-permute-start.24 = (bf16[512,128]{1,0:T(8,128)(2,1)S(1)}, bf16[512,128]{1,0:T(8,128)(2,1)S(1)}, u32[]{:S(2)}, u32[]{:S(2)}) collective-permute-start(bf16[512,128]{1,0:T(8,128)(2,1)S(1)} %add_convert_fusion.1), channel_id=1, source_target_pairs={{0,16},{8,24},{16,0},{24,8},{1,17},{9,25},{17,1},{25,9},{2,18},{10... | collective-permute-start | bytes 393224 | tf_op jit(solution)/shard_map/ppermute | solution.py:35
  73.9 5.0 %collective-permute-start.25 = (bf16[512,128]{1,0:T(8,128)(2,1)S(1)}, bf16[512,128]{1,0:T(8,128)(2,1)S(1)}, u32[]{:S(2)}, u32[]{:S(2)}) collective-permute-start(bf16[512,128]{1,0:T(8,128)(2,1)S(1)} %add_convert_fusion), channel_id=1, source_target_pairs={{0,8},{8,0},{16,24},{24,16},{1,9},{9,1},{17,25},{25,17},{2,10},{10... | collective-permute-start | bytes 393224 | tf_op jit(solution)/shard_map/ppermute | solution.py:35
  87.6 6.0 %collective-permute-start.29 = (f32[136,128]{1,0:T(8,128)S(1)}, f32[136,128]{1,0:T(8,128)S(1)}, u32[]{:S(2)}, u32[]{:S(2)}) collective-permute-start(f32[136,128]{1,0:T(8,128)S(1)} %add.164), channel_id=1, source_target_pairs={{0,4},{1,5},{2,6},{3,7},{4,0},{5,1},{6,2},{7,3},{8,12},{9,13},{10,... | collective-permute-start | bytes 208904 | tf_op jit(solution)/shard_map/ppermute | solution.py:35
  (11 other events, 31.1 us)

commit v5 on v4

--- a/solution.py
+++ b/solution.py
@@ -39,11 +39,20 @@
     return [1 << n for n in range(count.bit_length() - 1)]
 
 
+def partners(count):
+    return [1, *range(count - 1, 1, -1)]
+
+
 def in_order(values, rank):
-    stacked = jnp.stack(values)
-    return jnp.concatenate(
-        [lax.dynamic_index_in_dim(stacked, rank ^ k, 0, False) for k in range(len(values))]
-    )
+    stacked = jnp.stack(list(values.values()))
+    distances = jnp.array(list(values), jnp.int32)
+    places = jnp.arange(len(values), dtype=jnp.int32)
+
+    def value_of(index):
+        place = jnp.sum(jnp.where(distances == (rank ^ index), places, 0))
+        return lax.dynamic_index_in_dim(stacked, place, 0, False)
+
+    return jnp.concatenate([value_of(index) for index in range(len(values))])
 
 
 def densify(blocks, col_index, tile_blocks):
@@ -71,6 +80,7 @@
             out_specs=pl.BlockSpec((step * width, tile_blocks * width), lambda i, index: (i, 0)),
         ),
         out_shape=jax.ShapeDtypeStruct((group_rows * width, tile_blocks * width), blocks.dtype),
+        compiler_params=pltpu.CompilerParams(vmem_limit_bytes=24 << 20),
     )(col_index, blocks)
 
 
@@ -146,6 +156,7 @@
         in_specs=[pl.BlockSpec(memory_space=pltpu.SMEM), vmem, vmem, vmem],
         out_specs=vmem,
         out_shape=jax.ShapeDtypeStruct((piece_rows, 2 * size), jnp.float32),
+        compiler_params=pltpu.CompilerParams(vmem_limit_bytes=8 << 20),
     )(jnp.stack([mine_first.astype(jnp.int32), rank]), total, partner, filtered)
 
 
@@ -164,7 +175,6 @@
     row_bits = bits_below(row_count)
     z_count = col_count // 2
     z_rank = col_rank // 2
-    z_bits = [2 * bit for bit in bits_below(z_count)]
     narrow = jnp.bfloat16
 
     mine_first = core == 0
@@ -174,7 +184,7 @@
         return jnp.where(mine_first, left, right), jnp.where(mine_first, right, left)
 
     low_start = vectors.astype(narrow)
-    arrived = [low_start] + [swap(low_start, "row", k) for k in range(1, row_count)]
+    arrived = {0: low_start, **{k: swap(low_start, "row", k) for k in partners(row_count)}}
     low_own, sent = kept_and_sent(in_order(arrived, row_rank))
     low_other = swap(sent, "col", 1)
     own_start, sent = kept_and_sent(vectors)
@@ -219,12 +229,12 @@
     def sum_over_z(value):
         sent = value.astype(narrow)
         total = piece_of(value, z_rank)
-        for k in range(1, z_count):
+        for k in partners(z_count):
             total = total + swap(piece_of(sent, z_rank ^ k), "col", 2 * k).astype(jnp.float32)
         return total
 
     def gather_over_z(value):
-        return in_order([value] + [swap(value, "col", 2 * k) for k in range(1, z_count)], z_rank)
+        return in_order({0: value, **{k: swap(value, "col", 2 * k) for k in partners(z_count)}}, z_rank)
 
     def sum_over_row(one, two):
         for level, (bit_one, bit_two) in enumerate(zip(row_bits, reversed(row_bits))):
@@ -269,8 +279,7 @@
     cross = jnp.pad(cross, ((0, 8), (0, 0)))
     packed = jnp.concatenate([packed, diagonal, jnp.zeros((7, half), jnp.float32)])
     total = jnp.where(mine_first, cross, packed) + swap(jnp.where(mine_first, packed, cross), "col", 1)
-    for bit in z_bits:
-        total = total + swap(total, "col", bit)
+    total = sum([swap(total, "col", 2 * k) for k in partners(z_count)], total)
     partner = swap(total, "col", 1)
     orbital_count = piece_rows * row_count * col_count
     return orthonormal(total, partner, filtered, mine_first, row_rank, piece_rows, math.sqrt(orbital_count))

time: 105 us -> 115 us (1.095)
  between operations: 0.43 us -> 15.7 us
  waiting for transfers between devices: 48.5 us -> 45.3 us
  Pallas kernels: 12.5 us -> 10 us
  local copies, waits for them, and re-layouts: 0.93 us -> 2.39 us
    ppermute x31 -> x32, waiting for transfers between devices: 48.5 us -> 45.3 us  [swap(): return lax.ppermute(value, axis, [(i, i ^ distance) for i in range(count)])]
    pallas_call x1, Pallas kernels: 3.02 us -> 1.14 us  [densify(): pl.pallas_call(kernel, grid_spec=pltpu.PrefetchScalarGridSpec(num_scalar_...]
    unnamed x8, local copies, waits for them, and re-layouts: 0.64 us -> 2.1 us
    ppermute x31 -> x32, starting transfers between devices: 34.3 us -> 33.2 us  [swap(): return lax.ppermute(value, axis, [(i, i ^ distance) for i in range(count)])]
  transfers between devices with their start and end apart: 31 -> 32, of which waited for: 23 -> 23; matrix products, arithmetic and copies ran while one was open for 3% -> 2% of each run, Pallas kernels for 3% -> 1%
where the time goes in v5:
time: 115 us
  waiting for transfers between devices  45.3 us (39%)
  starting transfers between devices  33.2 us (29%)
  between operations  15.7 us (14%)
  Pallas kernels  10 us (9%)
  matrix products  4.72 us (4%)
  other arithmetic  3.17 us (3%)
  local copies, waits for them, and re-layouts  2.39 us (2%)
    ppermute x32, waiting for transfers between devices, swap(): return lax.ppermute(value, axis, [(i, i ^ distance) for i in range(count)])  45.3 us
    ppermute x32, starting transfers between devices, swap(): return lax.ppermute(value, axis, [(i, i ^ distance) for i in range(count)])  33.2 us
    pallas_call x1, Pallas kernels, orthonormal(): pl.pallas_call(kernel, in_specs=[pl.BlockSpec(memory_space=pltpu.SMEM), v...  8.9 us
  transfers between devices with their start and end apart: 32, of which 23 were waited for; matrix products, arithmetic and copies ran while one was open for 2% of the time, Pallas kernels for 1%

profile of v5, /device:TPU:0, one launch (start us, length us, event | category | flops | bytes accessed | tf_op | source)
XLA Modules:
  0.0 114.5 jit_solution(15941383946763329568)
XLA Ops:
  1.0 3.0 %collective-permute-start = (bf16[128,256]{1,0:T(8,128)(2,1)S(1)}, bf16[128,256]{1,0:T(8,128)(2,1)S(1)}, u32[]{:S(2)}, u32[]{:S(2)}) collective-permute-start(bf16[128,256]{1,0:T(8,128)(2,1)S(1)} %convert_element_type.134), channel_id=1, source_target_pairs={{0,8},{8,0},{16,24},{24,16},{1,9},{9,1},{17,25},{25,17},{2,10},{10... | collective-permute-start | bytes 196616 | tf_op jit(solution)/shard_map/ppermute | solution.py:35
  20.3 2.1 %collective-permute-start.5 = (bf16[256,128]{1,0:T(8,128)(2,1)S(1)}, bf16[256,128]{1,0:T(8,128)(2,1)S(1)}, u32[]{:S(2)}, u32[]{:S(2)}) collective-permute-start(bf16[256,128]{1,0:T(8,128)(2,1)S(1)} %get-tuple-element.67), channel_id=1, source_target_pairs={{0,2},{1,3},{2,0},{3,1},{4,6},{5,7},{6,4},{7,5},{8,10},{9,11},{10,... | collective-permute-start | bytes 196616 | tf_op jit(solution)/shard_map/ppermute | solution.py:35
  22.4 2.5 %collective-permute-start.6 = (bf16[256,128]{1,0:T(8,128)(2,1)S(1)}, bf16[256,128]{1,0:T(8,128)(2,1)S(1)}, u32[]{:S(2)}, u32[]{:S(2)}) collective-permute-start(bf16[256,128]{1,0:T(8,128)(2,1)S(1)} %get-tuple-element.69), channel_id=1, source_target_pairs={{0,6},{1,7},{2,4},{3,5},{4,2},{5,3},{6,0},{7,1},{8,14},{9,15},{10,... | collective-permute-start | bytes 196616 | tf_op jit(solution)/shard_map/ppermute | solution.py:35
  25.0 4.1 %collective-permute-done.6 = bf16[256,128]{1,0:T(8,128)(2,1)S(1)} collective-permute-done((bf16[256,128]{1,0:T(8,128)(2,1)S(1)}, bf16[256,128]{1,0:T(8,128)(2,1)S(1)}, u32[]{:S(2)}, u32[]{:S(2)}) %collective-permute-start.6) | collective-permute-done | bytes 65568 | tf_op jit(solution)/shard_map/ppermute | solution.py:35
  29.0 2.3 %collective-permute-done.7 = bf16[256,128]{1,0:T(8,128)(2,1)S(1)} collective-permute-done((bf16[256,128]{1,0:T(8,128)(2,1)S(1)}, bf16[256,128]{1,0:T(8,128)(2,1)S(1)}, u32[]{:S(2)}, u32[]{:S(2)}) %collective-permute-start.7) | collective-permute-done | bytes 65568 | tf_op jit(solution)/shard_map/ppermute | solution.py:35
  31.5 2.7 %collective-permute-start.9 = (bf16[256,128]{1,0:T(8,128)(2,1)S(1)}, bf16[256,128]{1,0:T(8,128)(2,1)S(1)}, u32[]{:S(2)}, u32[]{:S(2)}) collective-permute-start(bf16[256,128]{1,0:T(8,128)(2,1)S(1)} %multiply_convert_fusion), channel_id=1, source_target_pairs={{0,6},{1,7},{2,4},{3,5},{4,2},{5,3},{6,0},{7,1},{8,14},{9,15},{10,... | collective-permute-start | bytes 196616 | tf_op jit(solution)/shard_map/ppermute | solution.py:35
  43.7 1.6 %collective-permute-start.12 = (bf16[512,128]{1,0:T(8,128)(2,1)S(1)}, bf16[512,128]{1,0:T(8,128)(2,1)S(1)}, u32[]{:S(2)}, u32[]{:S(2)}) collective-permute-start(bf16[512,128]{1,0:T(8,128)(2,1)S(1)} %fusion.6), channel_id=1, source_target_pairs={{0,8},{8,0},{16,24},{24,16},{1,9},{9,1},{17,25},{25,17},{2,10},{10... | collective-permute-start | bytes 393224 | tf_op jit(solution)/shard_map/ppermute | solution.py:35
  45.3 1.5 %collective-permute-start.13 = (bf16[512,128]{1,0:T(8,128)(2,1)S(1)}, bf16[512,128]{1,0:T(8,128)(2,1)S(1)}, u32[]{:S(2)}, u32[]{:S(2)}) collective-permute-start(bf16[512,128]{1,0:T(8,128)(2,1)S(1)} %fusion.7), channel_id=1, source_target_pairs={{0,16},{8,24},{16,0},{24,8},{1,17},{9,25},{17,1},{25,9},{2,18},{10... | collective-permute-start | bytes 393224 | tf_op jit(solution)/shard_map/ppermute | solution.py:35
  46.8 2.0 %collective-permute-done.12 = bf16[512,128]{1,0:T(8,128)(2,1)S(1)} collective-permute-done((bf16[512,128]{1,0:T(8,128)(2,1)S(1)}, bf16[512,128]{1,0:T(8,128)(2,1)S(1)}, u32[]{:S(2)}, u32[]{:S(2)}) %collective-permute-start.12) | collective-permute-done | bytes 131104 | tf_op jit(solution)/shard_map/ppermute | solution.py:35
  50.3 1.6 %collective-permute-start.14 = (bf16[512,128]{1,0:T(8,128)(2,1)S(1)}, bf16[512,128]{1,0:T(8,128)(2,1)S(1)}, u32[]{:S(2)}, u32[]{:S(2)}) collective-permute-start(bf16[512,128]{1,0:T(8,128)(2,1)S(1)} %get-tuple-element.25), channel_id=1, source_target_pairs={{0,16},{8,24},{16,0},{24,8},{1,17},{9,25},{17,1},{25,9},{2,18},{10... | collective-permute-start | bytes 393224 | tf_op jit(solution)/shard_map/ppermute | solution.py:35
  52.4 2.9 %collective-permute-done.14 = bf16[512,128]{1,0:T(8,128)(2,1)S(1)} collective-permute-done((bf16[512,128]{1,0:T(8,128)(2,1)S(1)}, bf16[512,128]{1,0:T(8,128)(2,1)S(1)}, u32[]{:S(2)}, u32[]{:S(2)}) %collective-permute-start.14) | collective-permute-done | bytes 131104 | tf_op jit(solution)/shard_map/ppermute | solution.py:35
  58.9 2.6 %collective-permute-start.17 = (bf16[256,128]{1,0:T(8,128)(2,1)S(1)}, bf16[256,128]{1,0:T(8,128)(2,1)S(1)}, u32[]{:S(2)}, u32[]{:S(2)}) collective-permute-start(bf16[256,128]{1,0:T(8,128)(2,1)S(1)} %get-tuple-element.58), channel_id=1, source_target_pairs={{0,6},{1,7},{2,4},{3,5},{4,2},{5,3},{6,0},{7,1},{8,14},{9,15},{10,... | collective-permute-start | bytes 196616 | tf_op jit(solution)/shard_map/ppermute | solution.py:35
  62.8 2.6 %collective-permute-done.17 = bf16[256,128]{1,0:T(8,128)(2,1)S(1)} collective-permute-done((bf16[256,128]{1,0:T(8,128)(2,1)S(1)}, bf16[256,128]{1,0:T(8,128)(2,1)S(1)}, u32[]{:S(2)}, u32[]{:S(2)}) %collective-permute-start.17) | collective-permute-done | bytes 65568 | tf_op jit(solution)/shard_map/ppermute | solution.py:35
  65.4 4.0 %collective-permute-done.18 = bf16[256,128]{1,0:T(8,128)(2,1)S(1)} collective-permute-done((bf16[256,128]{1,0:T(8,128)(2,1)S(1)}, bf16[256,128]{1,0:T(8,128)(2,1)S(1)}, u32[]{:S(2)}, u32[]{:S(2)}) %collective-permute-start.18) | collective-permute-done | bytes 65568 | tf_op jit(solution)/shard_map/ppermute | solution.py:35
  69.6 1.6 %collective-permute-start.20 = (bf16[256,128]{1,0:T(8,128)(2,1)S(1)}, bf16[256,128]{1,0:T(8,128)(2,1)S(1)}, u32[]{:S(2)}, u32[]{:S(2)}) collective-permute-start(bf16[256,128]{1,0:T(8,128)(2,1)S(1)} %subtract_convert_fusion), channel_id=1, source_target_pairs={{0,6},{1,7},{2,4},{3,5},{4,2},{5,3},{6,0},{7,1},{8,14},{9,15},{10,... | collective-permute-start | bytes 196616 | tf_op jit(solution)/shard_map/ppermute | solution.py:35
  71.2 1.8 %collective-permute-start.21 = (bf16[256,128]{1,0:T(8,128)(2,1)S(1)}, bf16[256,128]{1,0:T(8,128)(2,1)S(1)}, u32[]{:S(2)}, u32[]{:S(2)}) collective-permute-start(bf16[256,128]{1,0:T(8,128)(2,1)S(1)} %subtract_convert_fusion), channel_id=1, source_target_pairs={{0,4},{1,5},{2,6},{3,7},{4,0},{5,1},{6,2},{7,3},{8,12},{9,13},{10,... | collective-permute-start | bytes 196616 | tf_op jit(solution)/shard_map/ppermute | solution.py:35
  73.8 2.0 %collective-permute-done.20 = bf16[256,128]{1,0:T(8,128)(2,1)S(1)} collective-permute-done((bf16[256,128]{1,0:T(8,128)(2,1)S(1)}, bf16[256,128]{1,0:T(8,128)(2,1)S(1)}, u32[]{:S(2)}, u32[]{:S(2)}) %collective-permute-start.20) | collective-permute-done | bytes 65568 | tf_op jit(solution)/shard_map/ppermute | solution.py:35
  75.8 1.6 %collective-permute-done.21 = bf16[256,128]{1,0:T(8,128)(2,1)S(1)} collective-permute-done((bf16[256,128]{1,0:T(8,128)(2,1)S(1)}, bf16[256,128]{1,0:T(8,128)(2,1)S(1)}, u32[]{:S(2)}, u32[]{:S(2)}) %collective-permute-start.21) | collective-permute-done | bytes 65568 | tf_op jit(solution)/shard_map/ppermute | solution.py:35
  79.8 3.7 %collective-permute-done.22 = bf16[512,128]{1,0:T(8,128)(2,1)S(1)} collective-permute-done((bf16[512,128]{1,0:T(8,128)(2,1)S(1)}, bf16[512,128]{1,0:T(8,128)(2,1)S(1)}, u32[]{:S(2)}, u32[]{:S(2)}) %collective-permute-start.22) | collective-permute-done | bytes 131104 | tf_op jit(solution)/shard_map/ppermute | solution.py:35
  86.4 3.0 %collective-permute-done.24 = bf16[512,128]{1,0:T(8,128)(2,1)S(1)} collective-permute-done((bf16[512,128]{1,0:T(8,128)(2,1)S(1)}, bf16[512,128]{1,0:T(8,128)(2,1)S(1)}, u32[]{:S(2)}, u32[]{:S(2)}) %collective-permute-start.24) | collective-permute-done | bytes 131104 | tf_op jit(solution)/shard_map/ppermute | solution.py:35
  94.6 2.2 %collective-permute-start.29 = (f32[136,128]{1,0:T(8,128)S(1)}, f32[136,128]{1,0:T(8,128)S(1)}, u32[]{:S(2)}, u32[]{:S(2)}) collective-permute-start(f32[136,128]{1,0:T(8,128)S(1)} %select_add_fusion), channel_id=1, source_target_pairs={{0,6},{1,7},{2,4},{3,5},{4,2},{5,3},{6,0},{7,1},{8,14},{9,15},{10,... | collective-permute-start | bytes 208904 | tf_op jit(solution)/shard_map/ppermute | solution.py:35
  98.7 2.8 %collective-permute-done.29 = f32[136,128]{1,0:T(8,128)S(1)} collective-permute-done((f32[136,128]{1,0:T(8,128)S(1)}, f32[136,128]{1,0:T(8,128)S(1)}, u32[]{:S(2)}, u32[]{:S(2)}) %collective-permute-start.29) | collective-permute-done | bytes 69664 | tf_op jit(solution)/shard_map/ppermute | solution.py:35
  101.5 2.8 %collective-permute-done.30 = f32[136,128]{1,0:T(8,128)S(1)} collective-permute-done((f32[136,128]{1,0:T(8,128)S(1)}, f32[136,128]{1,0:T(8,128)S(1)}, u32[]{:S(2)}, u32[]{:S(2)}) %collective-permute-start.30) | collective-permute-done | bytes 69664 | tf_op jit(solution)/shard_map/ppermute | solution.py:35
  105.6 8.9 %shard_map.65 = f32[128,256]{1,0:T(8,128)} custom-call(s32[2]{0:T(128)S(1)} %pad_add_fusion.flags_ref, f32[136,128]{1,0:T(8,128)S(1)} %add_add_fusion.total_ref, f32[136,128]{1,0:T(8,128)S(1)} %collective-permute-done.31.partner_ref, f32[512,256]{1,0:T(8,128)S(1)} %pad_maximum_fusion.filtered_ref), custom_call_target="tpu_custom_call" | custom-call | tf_op jit(solution)/shard_map/pallas_call | solution.py:154
  (98 shorter events, 33.0 us)
Async XLA Ops:
  1.0 17.2 %collective-permute-start = (bf16[128,256]{1,0:T(8,128)(2,1)S(1)}, bf16[128,256]{1,0:T(8,128)(2,1)S(1)}, u32[]{:S(2)}, u32[]{:S(2)}) collective-permute-start(bf16[128,256]{1,0:T(8,128)(2,1)S(1)} %convert_element_type.134), channel_id=1, source_target_pairs={{0,8},{8,0},{16,24},{24,16},{1,9},{9,1},{17,25},{25,17},{2,10},{10... | collective-permute-start | bytes 196616 | tf_op jit(solution)/shard_map/ppermute | solution.py:35
  4.0 14.2 %collective-permute-start.1 = (bf16[128,256]{1,0:T(8,128)(2,1)S(1)}, bf16[128,256]{1,0:T(8,128)(2,1)S(1)}, u32[]{:S(2)}, u32[]{:S(2)}) collective-permute-start(bf16[128,256]{1,0:T(8,128)(2,1)S(1)} %convert_element_type.134), channel_id=1, source_target_pairs={{0,24},{8,16},{16,8},{24,0},{1,25},{9,17},{17,9},{25,1},{2,26},{10... | collective-permute-start | bytes 196616 | tf_op jit(solution)/shard_map/ppermute | solution.py:35
  5.5 12.7 %collective-permute-start.2 = (bf16[128,256]{1,0:T(8,128)(2,1)S(1)}, bf16[128,256]{1,0:T(8,128)(2,1)S(1)}, u32[]{:S(2)}, u32[]{:S(2)}) collective-permute-start(bf16[128,256]{1,0:T(8,128)(2,1)S(1)} %convert_element_type.134), channel_id=1, source_target_pairs={{0,16},{8,24},{16,0},{24,8},{1,17},{9,25},{17,1},{25,9},{2,18},{10... | collective-permute-start | bytes 196616 | tf_op jit(solution)/shard_map/ppermute | solution.py:35
  8.8 11.0 %collective-permute-start.3 = (bf16[1024,512]{1,0:T(8,128)(2,1)S(1)}, bf16[1024,512]{1,0:T(8,128)(2,1)S(1)}, u32[]{:S(2)}, u32[]{:S(2)}) collective-permute-start(bf16[1024,512]{1,0:T(8,128)(2,1)S(1)} %shard_map.64), channel_id=1, source_target_pairs={{0,1},{1,0},{2,3},{3,2},{4,5},{5,4},{6,7},{7,6},{8,9},{9,8},{10,11... | collective-permute-start | bytes 3145736 | tf_op jit(solution)/shard_map/ppermute | solution.py:35
  8.9 33.5 %collective-permute-start.11 = (f32[128,128]{1,0:T(8,128)S(1)}, f32[128,128]{1,0:T(8,128)S(1)}, u32[]{:S(2)}, u32[]{:S(2)}) collective-permute-start(f32[128,128]{1,0:T(8,128)S(1)} %get-tuple-element.74), channel_id=1, source_target_pairs={{0,1},{1,0},{2,3},{3,2},{4,5},{5,4},{6,7},{7,6},{8,9},{9,8},{10,11... | collective-permute-start | bytes 196616 | tf_op jit(solution)/shard_map/ppermute | solution.py:35
  22.4 6.7 %collective-permute-start.6 = (bf16[256,128]{1,0:T(8,128)(2,1)S(1)}, bf16[256,128]{1,0:T(8,128)(2,1)S(1)}, u32[]{:S(2)}, u32[]{:S(2)}) collective-permute-start(bf16[256,128]{1,0:T(8,128)(2,1)S(1)} %get-tuple-element.69), channel_id=1, source_target_pairs={{0,6},{1,7},{2,4},{3,5},{4,2},{5,3},{6,0},{7,1},{8,14},{9,15},{10,... | collective-permute-start | bytes 196616 | tf_op jit(solution)/shard_map/ppermute | solution.py:35
  24.9 6.5 %collective-permute-start.7 = (bf16[256,128]{1,0:T(8,128)(2,1)S(1)}, bf16[256,128]{1,0:T(8,128)(2,1)S(1)}, u32[]{:S(2)}, u32[]{:S(2)}) collective-permute-start(bf16[256,128]{1,0:T(8,128)(2,1)S(1)} %get-tuple-element.68), channel_id=1, source_target_pairs={{0,4},{1,5},{2,6},{3,7},{4,0},{5,1},{6,2},{7,3},{8,12},{9,13},{10,... | collective-permute-start | bytes 196616 | tf_op jit(solution)/shard_map/ppermute | solution.py:35
  31.4 11.1 %collective-permute-start.8 = (bf16[256,128]{1,0:T(8,128)(2,1)S(1)}, bf16[256,128]{1,0:T(8,128)(2,1)S(1)}, u32[]{:S(2)}, u32[]{:S(2)}) collective-permute-start(bf16[256,128]{1,0:T(8,128)(2,1)S(1)} %multiply_convert_fusion), channel_id=1, source_target_pairs={{0,2},{1,3},{2,0},{3,1},{4,6},{5,7},{6,4},{7,5},{8,10},{9,11},{10,... | collective-permute-start | bytes 196616 | tf_op jit(solution)/shard_map/ppermute | solution.py:35
  31.5 11.1 %collective-permute-start.9 = (bf16[256,128]{1,0:T(8,128)(2,1)S(1)}, bf16[256,128]{1,0:T(8,128)(2,1)S(1)}, u32[]{:S(2)}, u32[]{:S(2)}) collective-permute-start(bf16[256,128]{1,0:T(8,128)(2,1)S(1)} %multiply_convert_fusion), channel_id=1, source_target_pairs={{0,6},{1,7},{2,4},{3,5},{4,2},{5,3},{6,0},{7,1},{8,14},{9,15},{10,... | collective-permute-start | bytes 196616 | tf_op jit(solution)/shard_map/ppermute | solution.py:35
  34.2 8.4 %collective-permute-start.10 = (bf16[256,128]{1,0:T(8,128)(2,1)S(1)}, bf16[256,128]{1,0:T(8,128)(2,1)S(1)}, u32[]{:S(2)}, u32[]{:S(2)}) collective-permute-start(bf16[256,128]{1,0:T(8,128)(2,1)S(1)} %multiply_convert_fusion), channel_id=1, source_target_pairs={{0,4},{1,5},{2,6},{3,7},{4,0},{5,1},{6,2},{7,3},{8,12},{9,13},{10,... | collective-permute-start | bytes 196616 | tf_op jit(solution)/shard_map/ppermute | solution.py:35
  43.7 5.0 %collective-permute-start.12 = (bf16[512,128]{1,0:T(8,128)(2,1)S(1)}, bf16[512,128]{1,0:T(8,128)(2,1)S(1)}, u32[]{:S(2)}, u32[]{:S(2)}) collective-permute-start(bf16[512,128]{1,0:T(8,128)(2,1)S(1)} %fusion.6), channel_id=1, source_target_pairs={{0,8},{8,0},{16,24},{24,16},{1,9},{9,1},{17,25},{25,17},{2,10},{10... | collective-permute-start | bytes 393224 | tf_op jit(solution)/shard_map/ppermute | solution.py:35
  45.3 5.0 %collective-permute-start.13 = (bf16[512,128]{1,0:T(8,128)(2,1)S(1)}, bf16[512,128]{1,0:T(8,128)(2,1)S(1)}, u32[]{:S(2)}, u32[]{:S(2)}) collective-permute-start(bf16[512,128]{1,0:T(8,128)(2,1)S(1)} %fusion.7), channel_id=1, source_target_pairs={{0,16},{8,24},{16,0},{24,8},{1,17},{9,25},{17,1},{25,9},{2,18},{10... | collective-permute-start | bytes 393224 | tf_op jit(solution)/shard_map/ppermute | solution.py:35
  50.3 5.0 %collective-permute-start.14 = (bf16[512,128]{1,0:T(8,128)(2,1)S(1)}, bf16[512,128]{1,0:T(8,128)(2,1)S(1)}, u32[]{:S(2)}, u32[]{:S(2)}) collective-permute-start(bf16[512,128]{1,0:T(8,128)(2,1)S(1)} %get-tuple-element.25), channel_id=1, source_target_pairs={{0,16},{8,24},{16,0},{24,8},{1,17},{9,25},{17,1},{25,9},{2,18},{10... | collective-permute-start | bytes 393224 | tf_op jit(solution)/shard_map/ppermute | solution.py:35
  51.9 5.0 %collective-permute-start.15 = (bf16[512,128]{1,0:T(8,128)(2,1)S(1)}, bf16[512,128]{1,0:T(8,128)(2,1)S(1)}, u32[]{:S(2)}, u32[]{:S(2)}) collective-permute-start(bf16[512,128]{1,0:T(8,128)(2,1)S(1)} %get-tuple-element.26), channel_id=1, source_target_pairs={{0,8},{8,0},{16,24},{24,16},{1,9},{9,1},{17,25},{25,17},{2,10},{10... | collective-permute-start | bytes 393224 | tf_op jit(solution)/shard_map/ppermute | solution.py:35
  58.9 6.5 %collective-permute-start.17 = (bf16[256,128]{1,0:T(8,128)(2,1)S(1)}, bf16[256,128]{1,0:T(8,128)(2,1)S(1)}, u32[]{:S(2)}, u32[]{:S(2)}) collective-permute-start(bf16[256,128]{1,0:T(8,128)(2,1)S(1)} %get-tuple-element.58), channel_id=1, source_target_pairs={{0,6},{1,7},{2,4},{3,5},{4,2},{5,3},{6,0},{7,1},{8,14},{9,15},{10,... | collective-permute-start | bytes 196616 | tf_op jit(solution)/shard_map/ppermute | solution.py:35
  61.6 7.9 %collective-permute-start.18 = (bf16[256,128]{1,0:T(8,128)(2,1)S(1)}, bf16[256,128]{1,0:T(8,128)(2,1)S(1)}, u32[]{:S(2)}, u32[]{:S(2)}) collective-permute-start(bf16[256,128]{1,0:T(8,128)(2,1)S(1)} %get-tuple-element.57), channel_id=1, source_target_pairs={{0,4},{1,5},{2,6},{3,7},{4,0},{5,1},{6,2},{7,3},{8,12},{9,13},{10,... | collective-permute-start | bytes 196616 | tf_op jit(solution)/shard_map/ppermute | solution.py:35
  69.6 6.2 %collective-permute-start.20 = (bf16[256,128]{1,0:T(8,128)(2,1)S(1)}, bf16[256,128]{1,0:T(8,128)(2,1)S(1)}, u32[]{:S(2)}, u32[]{:S(2)}) collective-permute-start(bf16[256,128]{1,0:T(8,128)(2,1)S(1)} %subtract_convert_fusion), channel_id=1, source_target_pairs={{0,6},{1,7},{2,4},{3,5},{4,2},{5,3},{6,0},{7,1},{8,14},{9,15},{10,... | collective-permute-start | bytes 196616 | tf_op jit(solution)/shard_map/ppermute | solution.py:35
  71.2 6.2 %collective-permute-start.21 = (bf16[256,128]{1,0:T(8,128)(2,1)S(1)}, bf16[256,128]{1,0:T(8,128)(2,1)S(1)}, u32[]{:S(2)}, u32[]{:S(2)}) collective-permute-start(bf16[256,128]{1,0:T(8,128)(2,1)S(1)} %subtract_convert_fusion), channel_id=1, source_target_pairs={{0,4},{1,5},{2,6},{3,7},{4,0},{5,1},{6,2},{7,3},{8,12},{9,13},{10,... | collective-permute-start | bytes 196616 | tf_op jit(solution)/shard_map/ppermute | solution.py:35
  78.5 5.0 %collective-permute-start.22 = (bf16[512,128]{1,0:T(8,128)(2,1)S(1)}, bf16[512,128]{1,0:T(8,128)(2,1)S(1)}, u32[]{:S(2)}, u32[]{:S(2)}) collective-permute-start(bf16[512,128]{1,0:T(8,128)(2,1)S(1)} %fusion.8), channel_id=1, source_target_pairs={{0,8},{8,0},{16,24},{24,16},{1,9},{9,1},{17,25},{25,17},{2,10},{10... | collective-permute-start | bytes 393224 | tf_op jit(solution)/shard_map/ppermute | solution.py:35
  79.2 5.0 %collective-permute-start.23 = (bf16[512,128]{1,0:T(8,128)(2,1)S(1)}, bf16[512,128]{1,0:T(8,128)(2,1)S(1)}, u32[]{:S(2)}, u32[]{:S(2)}) collective-permute-start(bf16[512,128]{1,0:T(8,128)(2,1)S(1)} %fusion.9), channel_id=1, source_target_pairs={{0,16},{8,24},{16,0},{24,8},{1,17},{9,25},{17,1},{25,9},{2,18},{10... | collective-permute-start | bytes 393224 | tf_op jit(solution)/shard_map/ppermute | solution.py:35
  84.3 5.0 %collective-permute-start.24 = (bf16[512,128]{1,0:T(8,128)(2,1)S(1)}, bf16[512,128]{1,0:T(8,128)(2,1)S(1)}, u32[]{:S(2)}, u32[]{:S(2)}) collective-permute-start(bf16[512,128]{1,0:T(8,128)(2,1)S(1)} %add_convert_fusion.1), channel_id=1, source_target_pairs={{0,16},{8,24},{16,0},{24,8},{1,17},{9,25},{17,1},{25,9},{2,18},{10... | collective-permute-start | bytes 393224 | tf_op jit(solution)/shard_map/ppermute | solution.py:35
  85.0 5.0 %collective-permute-start.25 = (bf16[512,128]{1,0:T(8,128)(2,1)S(1)}, bf16[512,128]{1,0:T(8,128)(2,1)S(1)}, u32[]{:S(2)}, u32[]{:S(2)}) collective-permute-start(bf16[512,128]{1,0:T(8,128)(2,1)S(1)} %add_convert_fusion), channel_id=1, source_target_pairs={{0,8},{8,0},{16,24},{24,16},{1,9},{9,1},{17,25},{25,17},{2,10},{10... | collective-permute-start | bytes 393224 | tf_op jit(solution)/shard_map/ppermute | solution.py:35
  94.6 6.9 %collective-permute-start.29 = (f32[136,128]{1,0:T(8,128)S(1)}, f32[136,128]{1,0:T(8,128)S(1)}, u32[]{:S(2)}, u32[]{:S(2)}) collective-permute-start(f32[136,128]{1,0:T(8,128)S(1)} %select_add_fusion), channel_id=1, source_target_pairs={{0,6},{1,7},{2,4},{3,5},{4,2},{5,3},{6,0},{7,1},{8,14},{9,15},{10,... | collective-permute-start | bytes 208904 | tf_op jit(solution)/shard_map/ppermute | solution.py:35
  96.8 7.5 %collective-permute-start.30 = (f32[136,128]{1,0:T(8,128)S(1)}, f32[136,128]{1,0:T(8,128)S(1)}, u32[]{:S(2)}, u32[]{:S(2)}) collective-permute-start(f32[136,128]{1,0:T(8,128)S(1)} %select_add_fusion), channel_id=1, source_target_pairs={{0,4},{1,5},{2,6},{3,7},{4,0},{5,1},{6,2},{7,3},{8,12},{9,13},{10,... | collective-permute-start | bytes 208904 | tf_op jit(solution)/shard_map/ppermute | solution.py:35
  (12 other events, 44.4 us)

commit v6 on v5

--- a/solution.py
+++ b/solution.py
@@ -45,11 +45,12 @@
 
 def in_order(values, rank):
     stacked = jnp.stack(list(values.values()))
-    distances = jnp.array(list(values), jnp.int32)
-    places = jnp.arange(len(values), dtype=jnp.int32)
 
     def value_of(index):
-        place = jnp.sum(jnp.where(distances == (rank ^ index), places, 0))
+        place = rank ^ index
+        for number, distance in enumerate(values):
+            if number != distance:
+                place = jnp.where((rank ^ index) == distance, number, place)
         return lax.dynamic_index_in_dim(stacked, place, 0, False)
 
     return jnp.concatenate([value_of(index) for index in range(len(values))])

time: 115 us -> 104 us (0.904)
  between operations: 15.7 us -> 0.48 us
  waiting for transfers between devices: 45.3 us -> 51.1 us
    ppermute x32, waiting for transfers between devices: 45.3 us -> 51.1 us  [swap(): return lax.ppermute(value, axis, [(i, i ^ distance) for i in range(count)])]
  transfers between devices with their start and end apart: 32 -> 32, of which waited for: 23 -> 27; matrix products, arithmetic and copies ran while one was open for 2% -> 2% of each run, Pallas kernels for 1% -> 1%
where the time goes in v6:
time: 104 us
  waiting for transfers between devices  51.1 us (49%)
  starting transfers between devices  32.8 us (32%)
  Pallas kernels  10 us (10%)
  matrix products  4.72 us (5%)
  local copies, waits for them, and re-layouts  2.39 us (2%)
  other arithmetic  2.35 us (2%)
    ppermute x32, waiting for transfers between devices, swap(): return lax.ppermute(value, axis, [(i, i ^ distance) for i in range(count)])  51.1 us
    ppermute x32, starting transfers between devices, swap(): return lax.ppermute(value, axis, [(i, i ^ distance) for i in range(count)])  32.8 us
    pallas_call x1, Pallas kernels, orthonormal(): pl.pallas_call(kernel, in_specs=[pl.BlockSpec(memory_space=pltpu.SMEM), v...  8.9 us
    unnamed x6, local copies, waits for them, and re-layouts  2.1 us
  transfers between devices with their start and end apart: 32, of which 27 were waited for; matrix products, arithmetic and copies ran while one was open for 2% of the time, Pallas kernels for 1%

profile of v6, /device:TPU:0, one launch (start us, length us, event | category | flops | bytes accessed | tf_op | source)
XLA Modules:
  0.0 103.9 jit_solution(11684552740625392071)
XLA Ops:
  1.0 3.0 %collective-permute-start = (bf16[128,256]{1,0:T(8,128)(2,1)S(1)}, bf16[128,256]{1,0:T(8,128)(2,1)S(1)}, u32[]{:S(2)}, u32[]{:S(2)}) collective-permute-start(bf16[128,256]{1,0:T(8,128)(2,1)S(1)} %convert_element_type.134), channel_id=1, source_target_pairs={{0,8},{8,0},{16,24},{24,16},{1,9},{9,1},{17,25},{25,17},{2,10},{10... | collective-permute-start | bytes 196616 | tf_op jit(solution)/shard_map/ppermute | solution.py:35
  12.3 2.1 %collective-permute-start.5 = (bf16[256,128]{1,0:T(8,128)(2,1)S(1)}, bf16[256,128]{1,0:T(8,128)(2,1)S(1)}, u32[]{:S(2)}, u32[]{:S(2)}) collective-permute-start(bf16[256,128]{1,0:T(8,128)(2,1)S(1)} %get-tuple-element.59), channel_id=1, source_target_pairs={{0,2},{1,3},{2,0},{3,1},{4,6},{5,7},{6,4},{7,5},{8,10},{9,11},{10,... | collective-permute-start | bytes 196616 | tf_op jit(solution)/shard_map/ppermute | solution.py:35
  14.4 2.5 %collective-permute-start.6 = (bf16[256,128]{1,0:T(8,128)(2,1)S(1)}, bf16[256,128]{1,0:T(8,128)(2,1)S(1)}, u32[]{:S(2)}, u32[]{:S(2)}) collective-permute-start(bf16[256,128]{1,0:T(8,128)(2,1)S(1)} %get-tuple-element.61), channel_id=1, source_target_pairs={{0,6},{1,7},{2,4},{3,5},{4,2},{5,3},{6,0},{7,1},{8,14},{9,15},{10,... | collective-permute-start | bytes 196616 | tf_op jit(solution)/shard_map/ppermute | solution.py:35
  17.0 4.1 %collective-permute-done.6 = bf16[256,128]{1,0:T(8,128)(2,1)S(1)} collective-permute-done((bf16[256,128]{1,0:T(8,128)(2,1)S(1)}, bf16[256,128]{1,0:T(8,128)(2,1)S(1)}, u32[]{:S(2)}, u32[]{:S(2)}) %collective-permute-start.6) | collective-permute-done | bytes 65568 | tf_op jit(solution)/shard_map/ppermute | solution.py:35
  21.1 2.3 %collective-permute-done.7 = bf16[256,128]{1,0:T(8,128)(2,1)S(1)} collective-permute-done((bf16[256,128]{1,0:T(8,128)(2,1)S(1)}, bf16[256,128]{1,0:T(8,128)(2,1)S(1)}, u32[]{:S(2)}, u32[]{:S(2)}) %collective-permute-start.7) | collective-permute-done | bytes 65568 | tf_op jit(solution)/shard_map/ppermute | solution.py:35
  23.5 2.7 %collective-permute-start.9 = (bf16[256,128]{1,0:T(8,128)(2,1)S(1)}, bf16[256,128]{1,0:T(8,128)(2,1)S(1)}, u32[]{:S(2)}, u32[]{:S(2)}) collective-permute-start(bf16[256,128]{1,0:T(8,128)(2,1)S(1)} %multiply_convert_fusion), channel_id=1, source_target_pairs={{0,6},{1,7},{2,4},{3,5},{4,2},{5,3},{6,0},{7,1},{8,14},{9,15},{10,... | collective-permute-start | bytes 196616 | tf_op jit(solution)/shard_map/ppermute | solution.py:35
  27.8 2.7 %collective-permute-done.9 = bf16[256,128]{1,0:T(8,128)(2,1)S(1)} collective-permute-done((bf16[256,128]{1,0:T(8,128)(2,1)S(1)}, bf16[256,128]{1,0:T(8,128)(2,1)S(1)}, u32[]{:S(2)}, u32[]{:S(2)}) %collective-permute-start.9) | collective-permute-done | bytes 65568 | tf_op jit(solution)/shard_map/ppermute | solution.py:35
  30.4 2.8 %collective-permute-done.10 = bf16[256,128]{1,0:T(8,128)(2,1)S(1)} collective-permute-done((bf16[256,128]{1,0:T(8,128)(2,1)S(1)}, bf16[256,128]{1,0:T(8,128)(2,1)S(1)}, u32[]{:S(2)}, u32[]{:S(2)}) %collective-permute-start.10) | collective-permute-done | bytes 65568 | tf_op jit(solution)/shard_map/ppermute | solution.py:35
  34.3 1.6 %collective-permute-start.12 = (bf16[512,128]{1,0:T(8,128)(2,1)S(1)}, bf16[512,128]{1,0:T(8,128)(2,1)S(1)}, u32[]{:S(2)}, u32[]{:S(2)}) collective-permute-start(bf16[512,128]{1,0:T(8,128)(2,1)S(1)} %fusion.6), channel_id=1, source_target_pairs={{0,8},{8,0},{16,24},{24,16},{1,9},{9,1},{17,25},{25,17},{2,10},{10... | collective-permute-start | bytes 393224 | tf_op jit(solution)/shard_map/ppermute | solution.py:35
  37.4 2.0 %collective-permute-done.12 = bf16[512,128]{1,0:T(8,128)(2,1)S(1)} collective-permute-done((bf16[512,128]{1,0:T(8,128)(2,1)S(1)}, bf16[512,128]{1,0:T(8,128)(2,1)S(1)}, u32[]{:S(2)}, u32[]{:S(2)}) %collective-permute-start.12) | collective-permute-done | bytes 131104 | tf_op jit(solution)/shard_map/ppermute | solution.py:35
  40.9 1.6 %collective-permute-start.14 = (bf16[512,128]{1,0:T(8,128)(2,1)S(1)}, bf16[512,128]{1,0:T(8,128)(2,1)S(1)}, u32[]{:S(2)}, u32[]{:S(2)}) collective-permute-start(bf16[512,128]{1,0:T(8,128)(2,1)S(1)} %get-tuple-element.25), channel_id=1, source_target_pairs={{0,16},{8,24},{16,0},{24,8},{1,17},{9,25},{17,1},{25,9},{2,18},{10... | collective-permute-start | bytes 393224 | tf_op jit(solution)/shard_map/ppermute | solution.py:35
  43.0 2.9 %collective-permute-done.14 = bf16[512,128]{1,0:T(8,128)(2,1)S(1)} collective-permute-done((bf16[512,128]{1,0:T(8,128)(2,1)S(1)}, bf16[512,128]{1,0:T(8,128)(2,1)S(1)}, u32[]{:S(2)}, u32[]{:S(2)}) %collective-permute-start.14) | collective-permute-done | bytes 131104 | tf_op jit(solution)/shard_map/ppermute | solution.py:35
  50.4 1.6 %collective-permute-start.18 = (bf16[256,128]{1,0:T(8,128)(2,1)S(1)}, bf16[256,128]{1,0:T(8,128)(2,1)S(1)}, u32[]{:S(2)}, u32[]{:S(2)}) collective-permute-start(bf16[256,128]{1,0:T(8,128)(2,1)S(1)} %get-tuple-element.49), channel_id=1, source_target_pairs={{0,4},{1,5},{2,6},{3,7},{4,0},{5,1},{6,2},{7,3},{8,12},{9,13},{10,... | collective-permute-start | bytes 196616 | tf_op jit(solution)/shard_map/ppermute | solution.py:35
  52.8 3.1 %collective-permute-done.17 = bf16[256,128]{1,0:T(8,128)(2,1)S(1)} collective-permute-done((bf16[256,128]{1,0:T(8,128)(2,1)S(1)}, bf16[256,128]{1,0:T(8,128)(2,1)S(1)}, u32[]{:S(2)}, u32[]{:S(2)}) %collective-permute-start.17) | collective-permute-done | bytes 65568 | tf_op jit(solution)/shard_map/ppermute | solution.py:35
  55.9 2.6 %collective-permute-done.18 = bf16[256,128]{1,0:T(8,128)(2,1)S(1)} collective-permute-done((bf16[256,128]{1,0:T(8,128)(2,1)S(1)}, bf16[256,128]{1,0:T(8,128)(2,1)S(1)}, u32[]{:S(2)}, u32[]{:S(2)}) %collective-permute-start.18) | collective-permute-done | bytes 65568 | tf_op jit(solution)/shard_map/ppermute | solution.py:35
  58.7 2.4 %collective-permute-start.20 = (bf16[256,128]{1,0:T(8,128)(2,1)S(1)}, bf16[256,128]{1,0:T(8,128)(2,1)S(1)}, u32[]{:S(2)}, u32[]{:S(2)}) collective-permute-start(bf16[256,128]{1,0:T(8,128)(2,1)S(1)} %subtract_convert_fusion), channel_id=1, source_target_pairs={{0,6},{1,7},{2,4},{3,5},{4,2},{5,3},{6,0},{7,1},{8,14},{9,15},{10,... | collective-permute-start | bytes 196616 | tf_op jit(solution)/shard_map/ppermute | solution.py:35
  63.0 2.0 %collective-permute-done.20 = bf16[256,128]{1,0:T(8,128)(2,1)S(1)} collective-permute-done((bf16[256,128]{1,0:T(8,128)(2,1)S(1)}, bf16[256,128]{1,0:T(8,128)(2,1)S(1)}, u32[]{:S(2)}, u32[]{:S(2)}) %collective-permute-start.20) | collective-permute-done | bytes 65568 | tf_op jit(solution)/shard_map/ppermute | solution.py:35
  65.0 2.0 %collective-permute-done.21 = bf16[256,128]{1,0:T(8,128)(2,1)S(1)} collective-permute-done((bf16[256,128]{1,0:T(8,128)(2,1)S(1)}, bf16[256,128]{1,0:T(8,128)(2,1)S(1)}, u32[]{:S(2)}, u32[]{:S(2)}) %collective-permute-start.21) | collective-permute-done | bytes 65568 | tf_op jit(solution)/shard_map/ppermute | solution.py:35
  69.2 3.9 %collective-permute-done.22 = bf16[512,128]{1,0:T(8,128)(2,1)S(1)} collective-permute-done((bf16[512,128]{1,0:T(8,128)(2,1)S(1)}, bf16[512,128]{1,0:T(8,128)(2,1)S(1)}, u32[]{:S(2)}, u32[]{:S(2)}) %collective-permute-start.22) | collective-permute-done | bytes 131104 | tf_op jit(solution)/shard_map/ppermute | solution.py:35
  75.8 3.0 %collective-permute-done.24 = bf16[512,128]{1,0:T(8,128)(2,1)S(1)} collective-permute-done((bf16[512,128]{1,0:T(8,128)(2,1)S(1)}, bf16[512,128]{1,0:T(8,128)(2,1)S(1)}, u32[]{:S(2)}, u32[]{:S(2)}) %collective-permute-start.24) | collective-permute-done | bytes 131104 | tf_op jit(solution)/shard_map/ppermute | solution.py:35
  84.2 1.5 %collective-permute-start.29 = (f32[136,128]{1,0:T(8,128)S(1)}, f32[136,128]{1,0:T(8,128)S(1)}, u32[]{:S(2)}, u32[]{:S(2)}) collective-permute-start(f32[136,128]{1,0:T(8,128)S(1)} %select_add_fusion), channel_id=1, source_target_pairs={{0,6},{1,7},{2,4},{3,5},{4,2},{5,3},{6,0},{7,1},{8,14},{9,15},{10,... | collective-permute-start | bytes 208904 | tf_op jit(solution)/shard_map/ppermute | solution.py:35
  88.0 2.7 %collective-permute-done.29 = f32[136,128]{1,0:T(8,128)S(1)} collective-permute-done((f32[136,128]{1,0:T(8,128)S(1)}, f32[136,128]{1,0:T(8,128)S(1)}, u32[]{:S(2)}, u32[]{:S(2)}) %collective-permute-start.29) | collective-permute-done | bytes 69664 | tf_op jit(solution)/shard_map/ppermute | solution.py:35
  90.8 2.9 %collective-permute-done.30 = f32[136,128]{1,0:T(8,128)S(1)} collective-permute-done((f32[136,128]{1,0:T(8,128)S(1)}, f32[136,128]{1,0:T(8,128)S(1)}, u32[]{:S(2)}, u32[]{:S(2)}) %collective-permute-start.30) | collective-permute-done | bytes 69664 | tf_op jit(solution)/shard_map/ppermute | solution.py:35
  95.0 8.9 %shard_map.38 = f32[128,256]{1,0:T(8,128)} custom-call(s32[2]{0:T(128)S(1)} %pad_add_fusion.flags_ref, f32[136,128]{1,0:T(8,128)S(1)} %add_add_fusion.total_ref, f32[136,128]{1,0:T(8,128)S(1)} %collective-permute-done.31.partner_ref, f32[512,256]{1,0:T(8,128)S(1)} %pad_maximum_fusion.filtered_ref), custom_call_target="tpu_custom_call" | custom-call | tf_op jit(solution)/shard_map/pallas_call | solution.py:155
  (95 shorter events, 36.7 us)
Async XLA Ops:
  1.0 8.6 %collective-permute-start = (bf16[128,256]{1,0:T(8,128)(2,1)S(1)}, bf16[128,256]{1,0:T(8,128)(2,1)S(1)}, u32[]{:S(2)}, u32[]{:S(2)}) collective-permute-start(bf16[128,256]{1,0:T(8,128)(2,1)S(1)} %convert_element_type.134), channel_id=1, source_target_pairs={{0,8},{8,0},{16,24},{24,16},{1,9},{9,1},{17,25},{25,17},{2,10},{10... | collective-permute-start | bytes 196616 | tf_op jit(solution)/shard_map/ppermute | solution.py:35
  4.0 5.6 %collective-permute-start.1 = (bf16[128,256]{1,0:T(8,128)(2,1)S(1)}, bf16[128,256]{1,0:T(8,128)(2,1)S(1)}, u32[]{:S(2)}, u32[]{:S(2)}) collective-permute-start(bf16[128,256]{1,0:T(8,128)(2,1)S(1)} %convert_element_type.134), channel_id=1, source_target_pairs={{0,24},{8,16},{16,8},{24,0},{1,25},{9,17},{17,9},{25,1},{2,26},{10... | collective-permute-start | bytes 196616 | tf_op jit(solution)/shard_map/ppermute | solution.py:35
  5.5 4.5 %collective-permute-start.2 = (bf16[128,256]{1,0:T(8,128)(2,1)S(1)}, bf16[128,256]{1,0:T(8,128)(2,1)S(1)}, u32[]{:S(2)}, u32[]{:S(2)}) collective-permute-start(bf16[128,256]{1,0:T(8,128)(2,1)S(1)} %convert_element_type.134), channel_id=1, source_target_pairs={{0,16},{8,24},{16,0},{24,8},{1,17},{9,25},{17,1},{25,9},{2,18},{10... | collective-permute-start | bytes 196616 | tf_op jit(solution)/shard_map/ppermute | solution.py:35
  8.9 18.2 %collective-permute-start.11 = (f32[128,128]{1,0:T(8,128)S(1)}, f32[128,128]{1,0:T(8,128)S(1)}, u32[]{:S(2)}, u32[]{:S(2)}) collective-permute-start(f32[128,128]{1,0:T(8,128)S(1)} %get-tuple-element.66), channel_id=1, source_target_pairs={{0,1},{1,0},{2,3},{3,2},{4,5},{5,4},{6,7},{7,6},{8,9},{9,8},{10,11... | collective-permute-start | bytes 196616 | tf_op jit(solution)/shard_map/ppermute | solution.py:35
  12.3 4.7 %collective-permute-start.5 = (bf16[256,128]{1,0:T(8,128)(2,1)S(1)}, bf16[256,128]{1,0:T(8,128)(2,1)S(1)}, u32[]{:S(2)}, u32[]{:S(2)}) collective-permute-start(bf16[256,128]{1,0:T(8,128)(2,1)S(1)} %get-tuple-element.59), channel_id=1, source_target_pairs={{0,2},{1,3},{2,0},{3,1},{4,6},{5,7},{6,4},{7,5},{8,10},{9,11},{10,... | collective-permute-start | bytes 196616 | tf_op jit(solution)/shard_map/ppermute | solution.py:35
  14.4 6.7 %collective-permute-start.6 = (bf16[256,128]{1,0:T(8,128)(2,1)S(1)}, bf16[256,128]{1,0:T(8,128)(2,1)S(1)}, u32[]{:S(2)}, u32[]{:S(2)}) collective-permute-start(bf16[256,128]{1,0:T(8,128)(2,1)S(1)} %get-tuple-element.61), channel_id=1, source_target_pairs={{0,6},{1,7},{2,4},{3,5},{4,2},{5,3},{6,0},{7,1},{8,14},{9,15},{10,... | collective-permute-start | bytes 196616 | tf_op jit(solution)/shard_map/ppermute | solution.py:35
  16.9 6.5 %collective-permute-start.7 = (bf16[256,128]{1,0:T(8,128)(2,1)S(1)}, bf16[256,128]{1,0:T(8,128)(2,1)S(1)}, u32[]{:S(2)}, u32[]{:S(2)}) collective-permute-start(bf16[256,128]{1,0:T(8,128)(2,1)S(1)} %get-tuple-element.60), channel_id=1, source_target_pairs={{0,4},{1,5},{2,6},{3,7},{4,0},{5,1},{6,2},{7,3},{8,12},{9,13},{10,... | collective-permute-start | bytes 196616 | tf_op jit(solution)/shard_map/ppermute | solution.py:35
  23.5 6.9 %collective-permute-start.9 = (bf16[256,128]{1,0:T(8,128)(2,1)S(1)}, bf16[256,128]{1,0:T(8,128)(2,1)S(1)}, u32[]{:S(2)}, u32[]{:S(2)}) collective-permute-start(bf16[256,128]{1,0:T(8,128)(2,1)S(1)} %multiply_convert_fusion), channel_id=1, source_target_pairs={{0,6},{1,7},{2,4},{3,5},{4,2},{5,3},{6,0},{7,1},{8,14},{9,15},{10,... | collective-permute-start | bytes 196616 | tf_op jit(solution)/shard_map/ppermute | solution.py:35
  26.2 7.0 %collective-permute-start.10 = (bf16[256,128]{1,0:T(8,128)(2,1)S(1)}, bf16[256,128]{1,0:T(8,128)(2,1)S(1)}, u32[]{:S(2)}, u32[]{:S(2)}) collective-permute-start(bf16[256,128]{1,0:T(8,128)(2,1)S(1)} %multiply_convert_fusion), channel_id=1, source_target_pairs={{0,4},{1,5},{2,6},{3,7},{4,0},{5,1},{6,2},{7,3},{8,12},{9,13},{10,... | collective-permute-start | bytes 196616 | tf_op jit(solution)/shard_map/ppermute | solution.py:35
  34.3 5.0 %collective-permute-start.12 = (bf16[512,128]{1,0:T(8,128)(2,1)S(1)}, bf16[512,128]{1,0:T(8,128)(2,1)S(1)}, u32[]{:S(2)}, u32[]{:S(2)}) collective-permute-start(bf16[512,128]{1,0:T(8,128)(2,1)S(1)} %fusion.6), channel_id=1, source_target_pairs={{0,8},{8,0},{16,24},{24,16},{1,9},{9,1},{17,25},{25,17},{2,10},{10... | collective-permute-start | bytes 393224 | tf_op jit(solution)/shard_map/ppermute | solution.py:35
  35.9 5.0 %collective-permute-start.13 = (bf16[512,128]{1,0:T(8,128)(2,1)S(1)}, bf16[512,128]{1,0:T(8,128)(2,1)S(1)}, u32[]{:S(2)}, u32[]{:S(2)}) collective-permute-start(bf16[512,128]{1,0:T(8,128)(2,1)S(1)} %fusion.7), channel_id=1, source_target_pairs={{0,16},{8,24},{16,0},{24,8},{1,17},{9,25},{17,1},{25,9},{2,18},{10... | collective-permute-start | bytes 393224 | tf_op jit(solution)/shard_map/ppermute | solution.py:35
  40.9 5.0 %collective-permute-start.14 = (bf16[512,128]{1,0:T(8,128)(2,1)S(1)}, bf16[512,128]{1,0:T(8,128)(2,1)S(1)}, u32[]{:S(2)}, u32[]{:S(2)}) collective-permute-start(bf16[512,128]{1,0:T(8,128)(2,1)S(1)} %get-tuple-element.25), channel_id=1, source_target_pairs={{0,16},{8,24},{16,0},{24,8},{1,17},{9,25},{17,1},{25,9},{2,18},{10... | collective-permute-start | bytes 393224 | tf_op jit(solution)/shard_map/ppermute | solution.py:35
  42.5 5.0 %collective-permute-start.15 = (bf16[512,128]{1,0:T(8,128)(2,1)S(1)}, bf16[512,128]{1,0:T(8,128)(2,1)S(1)}, u32[]{:S(2)}, u32[]{:S(2)}) collective-permute-start(bf16[512,128]{1,0:T(8,128)(2,1)S(1)} %get-tuple-element.26), channel_id=1, source_target_pairs={{0,8},{8,0},{16,24},{24,16},{1,9},{9,1},{17,25},{25,17},{2,10},{10... | collective-permute-start | bytes 393224 | tf_op jit(solution)/shard_map/ppermute | solution.py:35
  49.1 6.9 %collective-permute-start.17 = (bf16[256,128]{1,0:T(8,128)(2,1)S(1)}, bf16[256,128]{1,0:T(8,128)(2,1)S(1)}, u32[]{:S(2)}, u32[]{:S(2)}) collective-permute-start(bf16[256,128]{1,0:T(8,128)(2,1)S(1)} %get-tuple-element.50), channel_id=1, source_target_pairs={{0,6},{1,7},{2,4},{3,5},{4,2},{5,3},{6,0},{7,1},{8,14},{9,15},{10,... | collective-permute-start | bytes 196616 | tf_op jit(solution)/shard_map/ppermute | solution.py:35
  50.4 8.2 %collective-permute-start.18 = (bf16[256,128]{1,0:T(8,128)(2,1)S(1)}, bf16[256,128]{1,0:T(8,128)(2,1)S(1)}, u32[]{:S(2)}, u32[]{:S(2)}) collective-permute-start(bf16[256,128]{1,0:T(8,128)(2,1)S(1)} %get-tuple-element.49), channel_id=1, source_target_pairs={{0,4},{1,5},{2,6},{3,7},{4,0},{5,1},{6,2},{7,3},{8,12},{9,13},{10,... | collective-permute-start | bytes 196616 | tf_op jit(solution)/shard_map/ppermute | solution.py:35
  58.7 6.2 %collective-permute-start.20 = (bf16[256,128]{1,0:T(8,128)(2,1)S(1)}, bf16[256,128]{1,0:T(8,128)(2,1)S(1)}, u32[]{:S(2)}, u32[]{:S(2)}) collective-permute-start(bf16[256,128]{1,0:T(8,128)(2,1)S(1)} %subtract_convert_fusion), channel_id=1, source_target_pairs={{0,6},{1,7},{2,4},{3,5},{4,2},{5,3},{6,0},{7,1},{8,14},{9,15},{10,... | collective-permute-start | bytes 196616 | tf_op jit(solution)/shard_map/ppermute | solution.py:35
  61.1 5.9 %collective-permute-start.21 = (bf16[256,128]{1,0:T(8,128)(2,1)S(1)}, bf16[256,128]{1,0:T(8,128)(2,1)S(1)}, u32[]{:S(2)}, u32[]{:S(2)}) collective-permute-start(bf16[256,128]{1,0:T(8,128)(2,1)S(1)} %subtract_convert_fusion), channel_id=1, source_target_pairs={{0,4},{1,5},{2,6},{3,7},{4,0},{5,1},{6,2},{7,3},{8,12},{9,13},{10,... | collective-permute-start | bytes 196616 | tf_op jit(solution)/shard_map/ppermute | solution.py:35
  68.1 5.0 %collective-permute-start.22 = (bf16[512,128]{1,0:T(8,128)(2,1)S(1)}, bf16[512,128]{1,0:T(8,128)(2,1)S(1)}, u32[]{:S(2)}, u32[]{:S(2)}) collective-permute-start(bf16[512,128]{1,0:T(8,128)(2,1)S(1)} %fusion.8), channel_id=1, source_target_pairs={{0,8},{8,0},{16,24},{24,16},{1,9},{9,1},{17,25},{25,17},{2,10},{10... | collective-permute-start | bytes 393224 | tf_op jit(solution)/shard_map/ppermute | solution.py:35
  68.7 5.0 %collective-permute-start.23 = (bf16[512,128]{1,0:T(8,128)(2,1)S(1)}, bf16[512,128]{1,0:T(8,128)(2,1)S(1)}, u32[]{:S(2)}, u32[]{:S(2)}) collective-permute-start(bf16[512,128]{1,0:T(8,128)(2,1)S(1)} %fusion.9), channel_id=1, source_target_pairs={{0,16},{8,24},{16,0},{24,8},{1,17},{9,25},{17,1},{25,9},{2,18},{10... | collective-permute-start | bytes 393224 | tf_op jit(solution)/shard_map/ppermute | solution.py:35
  73.7 5.0 %collective-permute-start.24 = (bf16[512,128]{1,0:T(8,128)(2,1)S(1)}, bf16[512,128]{1,0:T(8,128)(2,1)S(1)}, u32[]{:S(2)}, u32[]{:S(2)}) collective-permute-start(bf16[512,128]{1,0:T(8,128)(2,1)S(1)} %add_convert_fusion.1), channel_id=1, source_target_pairs={{0,16},{8,24},{16,0},{24,8},{1,17},{9,25},{17,1},{25,9},{2,18},{10... | collective-permute-start | bytes 393224 | tf_op jit(solution)/shard_map/ppermute | solution.py:35
  74.3 5.0 %collective-permute-start.25 = (bf16[512,128]{1,0:T(8,128)(2,1)S(1)}, bf16[512,128]{1,0:T(8,128)(2,1)S(1)}, u32[]{:S(2)}, u32[]{:S(2)}) collective-permute-start(bf16[512,128]{1,0:T(8,128)(2,1)S(1)} %add_convert_fusion), channel_id=1, source_target_pairs={{0,8},{8,0},{16,24},{24,16},{1,9},{9,1},{17,25},{25,17},{2,10},{10... | collective-permute-start | bytes 393224 | tf_op jit(solution)/shard_map/ppermute | solution.py:35
  83.7 4.4 %collective-permute-start.28 = (f32[136,128]{1,0:T(8,128)S(1)}, f32[136,128]{1,0:T(8,128)S(1)}, u32[]{:S(2)}, u32[]{:S(2)}) collective-permute-start(f32[136,128]{1,0:T(8,128)S(1)} %select_add_fusion), channel_id=1, source_target_pairs={{0,2},{1,3},{2,0},{3,1},{4,6},{5,7},{6,4},{7,5},{8,10},{9,11},{10,... | collective-permute-start | bytes 208904 | tf_op jit(solution)/shard_map/ppermute | solution.py:35
  84.2 6.6 %collective-permute-start.29 = (f32[136,128]{1,0:T(8,128)S(1)}, f32[136,128]{1,0:T(8,128)S(1)}, u32[]{:S(2)}, u32[]{:S(2)}) collective-permute-start(f32[136,128]{1,0:T(8,128)S(1)} %select_add_fusion), channel_id=1, source_target_pairs={{0,6},{1,7},{2,4},{3,5},{4,2},{5,3},{6,0},{7,1},{8,14},{9,15},{10,... | collective-permute-start | bytes 208904 | tf_op jit(solution)/shard_map/ppermute | solution.py:35
  85.7 8.0 %collective-permute-start.30 = (f32[136,128]{1,0:T(8,128)S(1)}, f32[136,128]{1,0:T(8,128)S(1)}, u32[]{:S(2)}, u32[]{:S(2)}) collective-permute-start(f32[136,128]{1,0:T(8,128)S(1)} %select_add_fusion), channel_id=1, source_target_pairs={{0,4},{1,5},{2,6},{3,7},{4,0},{5,1},{6,2},{7,3},{8,12},{9,13},{10,... | collective-permute-start | bytes 208904 | tf_op jit(solution)/shard_map/ppermute | solution.py:35
  (11 other events, 32.9 us)

commit v7 on v6

--- a/solution.py
+++ b/solution.py
@@ -89,6 +89,12 @@
     return lax.dot_general(
         a, b, (dims, ((), ())), precision=lax.Precision.HIGHEST, preferred_element_type=jnp.float32
     )
+
+
+def tree_sum(terms):
+    while len(terms) > 1:
+        terms = [sum(terms[n + 1 : n + 2], terms[n]) for n in range(0, len(terms), 2)]
+    return terms[0]
 
 
 def factor(matrix, tall):
@@ -107,34 +113,43 @@
         for p in range(tall):
             pivot = columns[p][p : p + 1, :]
             inverse = 1.0 / pivot
-            ratio = columns[p] * inverse
-            below = jnp.where(sub > p, ratio, 0.0)
-            others = jnp.where(sub == p, 0.0, ratio)
+            masked = jnp.where(sub == p, 0.0, columns[p])
+            others = masked * inverse
+            below = jnp.where(sub > p, others, 0.0)
             for q in range(p + 1, tall):
-                columns[q] = columns[q] - others * columns[q][p : p + 1, :]
+                if q == p + 1:
+                    columns[q] = columns[q] - (masked * columns[q][p : p + 1, :]) * inverse
+                else:
+                    columns[q] = columns[q] - others * columns[q][p : p + 1, :]
             x = x - below * x[p : p + 1, :]
             z = z - others * z[p : p + 1, :]
             pivots = jnp.where(sub == p, pivot, pivots)
             inverses = jnp.where(sub == p, inverse, inverses)
         z = z * inverses
-        for later in range(number + 1, len(groups)):
-            value = jnp.where(block, 0.0, groups[later])
-            for p in range(tall):
-                value = value - groups[later][:, first + p : first + p + 1] * z[p : p + 1, :]
-            groups[later] = value
+        if number + 1 < len(groups):
+            following = groups[number + 1]
+            terms = [following[:, first + p : first + p + 1] * z[p : p + 1, :] for p in range(tall)]
+            groups[number + 1] = jnp.where(block, 0.0, following) - tree_sum(terms)
+        if number + 2 < len(groups):
+            rest = jnp.concatenate(groups[number + 2 :])
+            lanes = lax.broadcasted_iota(jnp.int32, rest.shape, 1)
+            gone = (lanes >= first) & (lanes < first + tall)
+            placed = [jnp.zeros((first, size), jnp.float32)] if first else []
+            placed = jnp.concatenate([*placed, z, jnp.zeros((size - first - tall, size), jnp.float32)])
+            rest = jnp.where(gone, 0.0, rest) - exact_dot(rest, placed, ((1,), (0,)))
+            groups[number + 2 :] = [rest[n : n + tall] for n in range(0, rest.shape[0], tall)]
         groups[number] = x * lax.rsqrt(pivots)
     return jnp.concatenate(groups)
 
 
-def orthonormal(total, partner, filtered, mine_first, rank, piece_rows, scale):
+def orthonormal(total, partner, mine, theirs, mine_first, scale):
     size = total.shape[1]
     tall = 16
 
-    def kernel(flags_ref, total_ref, partner_ref, filtered_ref, out_ref):
+    def kernel(first_ref, total_ref, partner_ref, mine_ref, theirs_ref, out_ref):
         rows = lax.broadcasted_iota(jnp.int32, (size, size), 0)
         lanes = lax.broadcasted_iota(jnp.int32, (size, size), 1)
-        is_first = flags_ref[0] != 0
-        start = pl.multiple_of(flags_ref[1] * piece_rows, piece_rows)
+        is_first = first_ref[0] != 0
         cross = jnp.where(is_first, total_ref[:size, :], partner_ref[:size, :])
         both = jnp.where(is_first, partner_ref[:size, :], total_ref[:size, :])
         diagonal = jnp.where(is_first, partner_ref[size : size + 1, :], total_ref[size : size + 1, :])
@@ -146,19 +161,20 @@
         second = jnp.where(lanes == rows, diagonal, second)
         last = factor(second - exact_dot(below, below, ((1,), (1,))), tall)
         last = jnp.where(rows >= lanes, last, 0.0)
-        left = exact_dot(filtered_ref[pl.ds(start, piece_rows), :size], first, ((1,), (1,)))
+        left = jnp.where(is_first, mine_ref[...], theirs_ref[...])
+        left = exact_dot(left, first, ((1,), (1,)))
         out_ref[:, :size] = scale * left
-        right = filtered_ref[pl.ds(start, piece_rows), size:] - exact_dot(left, below, ((1,), (1,)))
+        right = jnp.where(is_first, theirs_ref[...], mine_ref[...]) - exact_dot(left, below, ((1,), (1,)))
         out_ref[:, size:] = scale * exact_dot(right, last, ((1,), (1,)))
 
     vmem = pl.BlockSpec(memory_space=pltpu.VMEM)
     return pl.pallas_call(
         kernel,
-        in_specs=[pl.BlockSpec(memory_space=pltpu.SMEM), vmem, vmem, vmem],
+        in_specs=[pl.BlockSpec(memory_space=pltpu.SMEM), vmem, vmem, vmem, vmem],
         out_specs=vmem,
-        out_shape=jax.ShapeDtypeStruct((piece_rows, 2 * size), jnp.float32),
+        out_shape=jax.ShapeDtypeStruct((mine.shape[0], 2 * size), jnp.float32),
         compiler_params=pltpu.CompilerParams(vmem_limit_bytes=8 << 20),
-    )(jnp.stack([mine_first.astype(jnp.int32), rank]), total, partner, filtered)
+    )(mine_first.astype(jnp.int32).reshape(1), total, partner, mine, theirs)
 
 
 def on_device(blocks, col_index, vectors):
@@ -175,7 +191,7 @@
     tile_rows = tile_blocks * width
     row_bits = bits_below(row_count)
     z_count = col_count // 2
-    z_rank = col_rank // 2
+    z_bits = [2 * bit for bit in bits_below(z_count)]
     narrow = jnp.bfloat16
 
     mine_first = core == 0
@@ -214,7 +230,9 @@
     def forward(low_own, low_other):
         product = jnp.dot(own, low_own, preferred_element_type=jnp.float32)
         product = product + jnp.dot(other, low_other, preferred_element_type=jnp.float32)
-        return product - center * (spread(low_own, own_offset) + spread(low_other, other_offset))
+        product = product - center * (spread(low_own, own_offset) + spread(low_other, other_offset))
+        middle = product.shape[0] // 2
+        return product[:middle], product[middle:]
 
     def backward(low):
         def part(tile, offset):
@@ -223,67 +241,54 @@
 
         return part(own, own_offset), part(other, other_offset)
 
-    def piece_of(value, index):
-        rows = value.shape[0] // z_count
-        return lax.dynamic_slice_in_dim(value, index * rows, rows, 0)
-
-    def sum_over_z(value):
-        sent = value.astype(narrow)
-        total = piece_of(value, z_rank)
-        for k in partners(z_count):
-            total = total + swap(piece_of(sent, z_rank ^ k), "col", 2 * k).astype(jnp.float32)
-        return total
-
-    def gather_over_z(value):
-        return in_order({0: value, **{k: swap(value, "col", 2 * k) for k in partners(z_count)}}, z_rank)
-
-    def sum_over_row(one, two):
-        for level, (bit_one, bit_two) in enumerate(zip(row_bits, reversed(row_bits))):
-            sent = narrow if level < 2 else jnp.float32
-            low_one, low_two = lax.optimization_barrier((one.astype(sent), two.astype(sent)))
+    def sum_over(axis, bits, one, two):
+        for bit_one, bit_two in zip(bits, reversed(bits)):
             from_one, from_two = lax.optimization_barrier(
-                (swap(low_one, "row", bit_one), swap(low_two, "row", bit_two))
+                (swap(one.astype(narrow), axis, bit_one), swap(two.astype(narrow), axis, bit_two))
             )
-            one = low_one.astype(jnp.float32) + from_one.astype(jnp.float32)
-            two = low_two.astype(jnp.float32) + from_two.astype(jnp.float32)
+            one, two = one + from_one.astype(jnp.float32), two + from_two.astype(jnp.float32)
         return one, two
 
     def placed(piece):
         here = jnp.arange(row_count)[:, None, None] == row_rank
         return jnp.where(here, piece[None], 0.0).reshape(tile_rows, half)
 
-    y1 = scales[0] * sum_over_z(forward(low_own, low_other))
-    low = gather_over_z(y1.astype(narrow))
-    part_own, part_other = backward(low)
-    y2_own, y2_other = sum_over_row(
+    y1_one, y1_two = [
+        scales[0] * image for image in sum_over("col", z_bits, *forward(low_own, low_other))
+    ]
+    part_own, part_other = backward(jnp.concatenate([y1_one.astype(narrow), y1_two.astype(narrow)]))
+    y2_own, y2_other = sum_over(
+        "row",
+        row_bits,
         scales[1] * part_own - carries[1] * placed(own_start),
         scales[1] * part_other - carries[1] * placed(other_start),
     )
-    y3 = scales[2] * sum_over_z(forward(y2_own.astype(narrow), y2_other.astype(narrow))) - carries[2] * y1
-    low = gather_over_z(y3.astype(narrow))
-    part_own, part_other = backward(low)
-    image_own, image_other = sum_over_row(part_own, part_other)
+    image_one, image_two = sum_over(
+        "col", z_bits, *forward(y2_own.astype(narrow), y2_other.astype(narrow))
+    )
+    low_one = (scales[2] * image_one - carries[2] * y1_one).astype(narrow)
+    low_two = (scales[2] * image_two - carries[2] * y1_two).astype(narrow)
+    part_own, part_other = backward(jnp.concatenate([low_one, low_two]))
+    image_own, image_other = sum_over("row", row_bits, part_own, part_other)
     y4_own = scales[3] * image_own - carries[3] * y2_own
     y4_other = scales[3] * image_other - carries[3] * y2_other
 
-    partner = swap(y4_other, "col", 1)
-    filtered = jnp.concatenate(
-        [jnp.where(mine_first, y4_own, partner), jnp.where(mine_first, partner, y4_own)], axis=1
-    )
-    gram = exact_dot(filtered, filtered, ((0,), (0,)))
+    mine = jnp.concatenate([y4_own, y4_other])
+    theirs = swap(jnp.concatenate([y4_other, y4_own]), "col", 1)
+    corner = exact_dot(mine, mine, ((0,), (0,)))
+    cross = exact_dot(theirs, jnp.where(mine_first, mine, theirs), ((0,), (0,)))
     rows = lax.broadcasted_iota(jnp.int32, (half, half), 0)
     lanes = lax.broadcasted_iota(jnp.int32, (half, half), 1)
-    corner = gram[half:, half:]
-    cross = gram[half:, :half]
-    packed = jnp.where(rows >= lanes, gram[:half, :half], corner)
+    packed = jnp.where(mine_first | (rows >= lanes), cross, corner)
     diagonal = jnp.sum(jnp.where(rows == lanes, corner, 0.0), axis=0, keepdims=True)
-    cross = jnp.pad(cross, ((0, 8), (0, 0)))
-    packed = jnp.concatenate([packed, diagonal, jnp.zeros((7, half), jnp.float32)])
-    total = jnp.where(mine_first, cross, packed) + swap(jnp.where(mine_first, packed, cross), "col", 1)
+    total = jnp.concatenate([packed, jnp.pad(diagonal, ((0, 7), (0, 0)))])
     total = sum([swap(total, "col", 2 * k) for k in partners(z_count)], total)
     partner = swap(total, "col", 1)
     orbital_count = piece_rows * row_count * col_count
-    return orthonormal(total, partner, filtered, mine_first, row_rank, piece_rows, math.sqrt(orbital_count))
+    here = row_rank * piece_rows
+    mine = lax.dynamic_slice_in_dim(mine, here, piece_rows, 0)
+    theirs = lax.dynamic_slice_in_dim(theirs, here, piece_rows, 0)
+    return orthonormal(total, partner, mine, theirs, mine_first, math.sqrt(orbital_count))
 
 
 def solution(mesh):

time: 104 us -> 97.5 us (0.938)
  starting transfers between devices: 32.8 us -> 28.1 us
  Pallas kernels: 10 us -> 8.06 us
    ppermute x32 -> x27, starting transfers between devices: 32.8 us -> 28.1 us  [swap(): return lax.ppermute(value, axis, [(i, i ^ distance) for i in range(count)])]
    pallas_call x1, Pallas kernels: 8.9 us -> 6.92 us  [orthonormal(): pl.pallas_call(kernel, in_specs=[pl.BlockSpec(memory_space=pltpu.SMEM), v...]
    ppermute x32 -> x27, waiting for transfers between devices: 51.1 us -> 50.3 us  [swap(): return lax.ppermute(value, axis, [(i, i ^ distance) for i in range(count)])]
  transfers between devices with their start and end apart: 32 -> 27, of which waited for: 27 -> 21; matrix products, arithmetic and copies ran while one was open for 2% -> 3% of each run, Pallas kernels for 1% -> 1%
where the time goes in v7:
time: 97.5 us; the launch traced here: 97.3 us
  waiting for transfers between devices  50.3 us (52%)
  starting transfers between devices  28.1 us (29%)
  Pallas kernels  8.06 us (8%)
  matrix products  5.68 us (6%)
  other arithmetic  2.42 us (2%)
  local copies, waits for them, and re-layouts  2.29 us (2%)
    ppermute x27, waiting for transfers between devices, swap(): return lax.ppermute(value, axis, [(i, i ^ distance) for i in range(count)])  50.3 us
    ppermute x27, starting transfers between devices, swap(): return lax.ppermute(value, axis, [(i, i ^ distance) for i in range(count)])  28.1 us
    pallas_call x1, Pallas kernels, orthonormal(): pl.pallas_call(kernel, in_specs=[pl.BlockSpec(memory_space=pltpu.SMEM), v...  6.92 us
    unnamed x6, local copies, waits for them, and re-layouts  2.1 us
    dot_general x2, matrix products, exact_dot(): lax.dot_general(a, b, (dims, ((), ())), precision=lax.Precision.HIGHEST,...  2.02 us
  transfers between devices with their start and end apart: 27, of which 21 were waited for; matrix products, arithmetic and copies ran while one was open for 3% of the time, Pallas kernels for 1%

profile of v7, /device:TPU:0, one launch (start us, length us, event | category | flops | bytes accessed | tf_op | source)
XLA Modules:
  0.0 97.3 jit_solution(8483957912360177615)
XLA Ops:
  1.0 3.0 %collective-permute-start.3 = (bf16[128,256]{1,0:T(8,128)(2,1)S(1)}, bf16[128,256]{1,0:T(8,128)(2,1)S(1)}, u32[]{:S(2)}, u32[]{:S(2)}) collective-permute-start(bf16[128,256]{1,0:T(8,128)(2,1)S(1)} %convert_element_type.140), channel_id=1, source_target_pairs={{0,16},{8,24},{16,0},{24,8},{1,17},{9,25},{17,1},{25,9},{2,18},{10... | collective-permute-start | bytes 196616 | tf_op jit(solution)/shard_map/ppermute | solution.py:35
  4.0 1.4 %collective-permute-start.2 = (bf16[128,256]{1,0:T(8,128)(2,1)S(1)}, bf16[128,256]{1,0:T(8,128)(2,1)S(1)}, u32[]{:S(2)}, u32[]{:S(2)}) collective-permute-start(bf16[128,256]{1,0:T(8,128)(2,1)S(1)} %convert_element_type.140), channel_id=1, source_target_pairs={{0,24},{8,16},{16,8},{24,0},{1,25},{9,17},{17,9},{25,1},{2,26},{10... | collective-permute-start | bytes 196616 | tf_op jit(solution)/shard_map/ppermute | solution.py:35
  12.2 2.1 %collective-permute-start.5 = (bf16[512,128]{1,0:T(8,128)(2,1)S(1)}, bf16[512,128]{1,0:T(8,128)(2,1)S(1)}, u32[]{:S(2)}, u32[]{:S(2)}) collective-permute-start(bf16[512,128]{1,0:T(8,128)(2,1)S(1)} %get-tuple-element.54), channel_id=1, source_target_pairs={{0,2},{1,3},{2,0},{3,1},{4,6},{5,7},{6,4},{7,5},{8,10},{9,11},{10,... | collective-permute-start | bytes 393224 | tf_op jit(solution)/shard_map/ppermute | solution.py:35
  14.3 2.6 %collective-permute-start.6 = (bf16[512,128]{1,0:T(8,128)(2,1)S(1)}, bf16[512,128]{1,0:T(8,128)(2,1)S(1)}, u32[]{:S(2)}, u32[]{:S(2)}) collective-permute-start(bf16[512,128]{1,0:T(8,128)(2,1)S(1)} %get-tuple-element.53), channel_id=1, source_target_pairs={{0,4},{1,5},{2,6},{3,7},{4,0},{5,1},{6,2},{7,3},{8,12},{9,13},{10,... | collective-permute-start | bytes 393224 | tf_op jit(solution)/shard_map/ppermute | solution.py:35
  17.0 3.3 %collective-permute-done.5 = bf16[512,128]{1,0:T(8,128)(2,1)S(1)} collective-permute-done((bf16[512,128]{1,0:T(8,128)(2,1)S(1)}, bf16[512,128]{1,0:T(8,128)(2,1)S(1)}, u32[]{:S(2)}, u32[]{:S(2)}) %collective-permute-start.5) | collective-permute-done | bytes 131104 | tf_op jit(solution)/shard_map/ppermute | solution.py:35
  20.3 3.0 %collective-permute-done.6 = bf16[512,128]{1,0:T(8,128)(2,1)S(1)} collective-permute-done((bf16[512,128]{1,0:T(8,128)(2,1)S(1)}, bf16[512,128]{1,0:T(8,128)(2,1)S(1)}, u32[]{:S(2)}, u32[]{:S(2)}) %collective-permute-start.6) | collective-permute-done | bytes 131104 | tf_op jit(solution)/shard_map/ppermute | solution.py:35
  23.8 2.7 %collective-permute-start.8 = (bf16[512,128]{1,0:T(8,128)(2,1)S(1)}, bf16[512,128]{1,0:T(8,128)(2,1)S(1)}, u32[]{:S(2)}, u32[]{:S(2)}) collective-permute-start(bf16[512,128]{1,0:T(8,128)(2,1)S(1)} %get-tuple-element.51), channel_id=1, source_target_pairs={{0,2},{1,3},{2,0},{3,1},{4,6},{5,7},{6,4},{7,5},{8,10},{9,11},{10,... | collective-permute-start | bytes 393224 | tf_op jit(solution)/shard_map/ppermute | solution.py:35
  26.7 4.0 %collective-permute-done.7 = bf16[512,128]{1,0:T(8,128)(2,1)S(1)} collective-permute-done((bf16[512,128]{1,0:T(8,128)(2,1)S(1)}, bf16[512,128]{1,0:T(8,128)(2,1)S(1)}, u32[]{:S(2)}, u32[]{:S(2)}) %collective-permute-start.7) | collective-permute-done | bytes 131104 | tf_op jit(solution)/shard_map/ppermute | solution.py:35
  31.4 1.6 %collective-permute-start.9 = (bf16[512,128]{1,0:T(8,128)(2,1)S(1)}, bf16[512,128]{1,0:T(8,128)(2,1)S(1)}, u32[]{:S(2)}, u32[]{:S(2)}) collective-permute-start(bf16[512,128]{1,0:T(8,128)(2,1)S(1)} %get-tuple-element.65), channel_id=1, source_target_pairs={{0,8},{8,0},{16,24},{24,16},{1,9},{9,1},{17,25},{25,17},{2,10},{10... | collective-permute-start | bytes 393224 | tf_op jit(solution)/shard_map/ppermute | solution.py:35
  33.5 1.6 %collective-permute-start.11 = (bf16[512,128]{1,0:T(8,128)(2,1)S(1)}, bf16[512,128]{1,0:T(8,128)(2,1)S(1)}, u32[]{:S(2)}, u32[]{:S(2)}) collective-permute-start(bf16[512,128]{1,0:T(8,128)(2,1)S(1)} %get-tuple-element.67), channel_id=1, source_target_pairs={{0,16},{8,24},{16,0},{24,8},{1,17},{9,25},{17,1},{25,9},{2,18},{10... | collective-permute-start | bytes 393224 | tf_op jit(solution)/shard_map/ppermute | solution.py:35
  36.5 3.1 %collective-permute-done.11 = bf16[512,128]{1,0:T(8,128)(2,1)S(1)} collective-permute-done((bf16[512,128]{1,0:T(8,128)(2,1)S(1)}, bf16[512,128]{1,0:T(8,128)(2,1)S(1)}, u32[]{:S(2)}, u32[]{:S(2)}) %collective-permute-start.11) | collective-permute-done | bytes 131104 | tf_op jit(solution)/shard_map/ppermute | solution.py:35
  39.6 1.6 %collective-permute-start.12 = (bf16[512,128]{1,0:T(8,128)(2,1)S(1)}, bf16[512,128]{1,0:T(8,128)(2,1)S(1)}, u32[]{:S(2)}, u32[]{:S(2)}) collective-permute-start(bf16[512,128]{1,0:T(8,128)(2,1)S(1)} %fusion.11), channel_id=1, source_target_pairs={{0,16},{8,24},{16,0},{24,8},{1,17},{9,25},{17,1},{25,9},{2,18},{10... | collective-permute-start | bytes 393224 | tf_op jit(solution)/shard_map/ppermute | solution.py:35
  41.8 2.8 %collective-permute-done.12 = bf16[512,128]{1,0:T(8,128)(2,1)S(1)} collective-permute-done((bf16[512,128]{1,0:T(8,128)(2,1)S(1)}, bf16[512,128]{1,0:T(8,128)(2,1)S(1)}, u32[]{:S(2)}, u32[]{:S(2)}) %collective-permute-start.12) | collective-permute-done | bytes 131104 | tf_op jit(solution)/shard_map/ppermute | solution.py:35
  44.7 1.6 %collective-permute-done.13 = bf16[512,128]{1,0:T(8,128)(2,1)S(1)} collective-permute-done((bf16[512,128]{1,0:T(8,128)(2,1)S(1)}, bf16[512,128]{1,0:T(8,128)(2,1)S(1)}, u32[]{:S(2)}, u32[]{:S(2)}) %collective-permute-start.13) | collective-permute-done | bytes 131104 | tf_op jit(solution)/shard_map/ppermute | solution.py:35
  47.5 2.5 %collective-permute-start.15 = (bf16[512,128]{1,0:T(8,128)(2,1)S(1)}, bf16[512,128]{1,0:T(8,128)(2,1)S(1)}, u32[]{:S(2)}, u32[]{:S(2)}) collective-permute-start(bf16[512,128]{1,0:T(8,128)(2,1)S(1)} %get-tuple-element.47), channel_id=1, source_target_pairs={{0,4},{1,5},{2,6},{3,7},{4,0},{5,1},{6,2},{7,3},{8,12},{9,13},{10,... | collective-permute-start | bytes 393224 | tf_op jit(solution)/shard_map/ppermute | solution.py:35
  49.9 3.7 %collective-permute-done.14 = bf16[512,128]{1,0:T(8,128)(2,1)S(1)} collective-permute-done((bf16[512,128]{1,0:T(8,128)(2,1)S(1)}, bf16[512,128]{1,0:T(8,128)(2,1)S(1)}, u32[]{:S(2)}, u32[]{:S(2)}) %collective-permute-start.14) | collective-permute-done | bytes 131104 | tf_op jit(solution)/shard_map/ppermute | solution.py:35
  53.6 2.9 %collective-permute-done.15 = bf16[512,128]{1,0:T(8,128)(2,1)S(1)} collective-permute-done((bf16[512,128]{1,0:T(8,128)(2,1)S(1)}, bf16[512,128]{1,0:T(8,128)(2,1)S(1)}, u32[]{:S(2)}, u32[]{:S(2)}) %collective-permute-start.15) | collective-permute-done | bytes 131104 | tf_op jit(solution)/shard_map/ppermute | solution.py:35
  57.3 6.3 %collective-permute-done.16 = bf16[512,128]{1,0:T(8,128)(2,1)S(1)} collective-permute-done((bf16[512,128]{1,0:T(8,128)(2,1)S(1)}, bf16[512,128]{1,0:T(8,128)(2,1)S(1)}, u32[]{:S(2)}, u32[]{:S(2)}) %collective-permute-start.16) | collective-permute-done | bytes 131104 | tf_op jit(solution)/shard_map/ppermute | solution.py:35
  66.1 3.4 %collective-permute-done.18 = bf16[512,128]{1,0:T(8,128)(2,1)S(1)} collective-permute-done((bf16[512,128]{1,0:T(8,128)(2,1)S(1)}, bf16[512,128]{1,0:T(8,128)(2,1)S(1)}, u32[]{:S(2)}, u32[]{:S(2)}) %collective-permute-start.18) | collective-permute-done | bytes 131104 | tf_op jit(solution)/shard_map/ppermute | solution.py:35
  71.2 1.6 %collective-permute-start.21 = (bf16[512,128]{1,0:T(8,128)(2,1)S(1)}, bf16[512,128]{1,0:T(8,128)(2,1)S(1)}, u32[]{:S(2)}, u32[]{:S(2)}) collective-permute-start(bf16[512,128]{1,0:T(8,128)(2,1)S(1)} %fusion.13), channel_id=1, source_target_pairs={{0,8},{8,0},{16,24},{24,16},{1,9},{9,1},{17,25},{25,17},{2,10},{10... | collective-permute-start | bytes 393224 | tf_op jit(solution)/shard_map/ppermute | solution.py:35
  72.8 2.9 %collective-permute-done.20 = bf16[512,128]{1,0:T(8,128)(2,1)S(1)} collective-permute-done((bf16[512,128]{1,0:T(8,128)(2,1)S(1)}, bf16[512,128]{1,0:T(8,128)(2,1)S(1)}, u32[]{:S(2)}, u32[]{:S(2)}) %collective-permute-start.20) | collective-permute-done | bytes 131104 | tf_op jit(solution)/shard_map/ppermute | solution.py:35
  80.4 2.1 %collective-permute-start.24 = (f32[136,128]{1,0:T(8,128)S(1)}, f32[136,128]{1,0:T(8,128)S(1)}, u32[]{:S(2)}, u32[]{:S(2)}) collective-permute-start(f32[136,128]{1,0:T(8,128)S(1)} %select_maximum_fusion), channel_id=1, source_target_pairs={{0,6},{1,7},{2,4},{3,5},{4,2},{5,3},{6,0},{7,1},{8,14},{9,15},{10,... | collective-permute-start | bytes 208904 | tf_op jit(solution)/shard_map/ppermute | solution.py:35
  83.1 4.7 %collective-permute-done.25 = f32[136,128]{1,0:T(8,128)S(1)} collective-permute-done((f32[136,128]{1,0:T(8,128)S(1)}, f32[136,128]{1,0:T(8,128)S(1)}, u32[]{:S(2)}, u32[]{:S(2)}) %collective-permute-start.25) | collective-permute-done | bytes 69664 | tf_op jit(solution)/shard_map/ppermute | solution.py:35
  90.4 6.9 %shard_map.38 = f32[128,256]{1,0:T(8,128)} custom-call(s32[1]{0:T(128)} %bitcast.first_ref, f32[136,128]{1,0:T(8,128)S(1)} %add_add_fusion.total_ref, f32[136,128]{1,0:T(8,128)S(1)} %collective-permute-done.26.partner_ref, f32[128,128]{1,0:T(8,128)S(1)} %fusion.23.mine_ref, f32[128,128]{1,0:T(8,128)S(1)} %constant_dynamic-slice_fusion.theirs_ref), custom_call_target="tpu_custom_call" | custom-call | tf_op jit(solution)/shard_map/pallas_call | solution.py:171
  (83 shorter events, 25.5 us)
Async XLA Ops:
  1.0 8.0 %collective-permute-start.3 = (bf16[128,256]{1,0:T(8,128)(2,1)S(1)}, bf16[128,256]{1,0:T(8,128)(2,1)S(1)}, u32[]{:S(2)}, u32[]{:S(2)}) collective-permute-start(bf16[128,256]{1,0:T(8,128)(2,1)S(1)} %convert_element_type.140), channel_id=1, source_target_pairs={{0,16},{8,24},{16,0},{24,8},{1,17},{9,25},{17,1},{25,9},{2,18},{10... | collective-permute-start | bytes 196616 | tf_op jit(solution)/shard_map/ppermute | solution.py:35
  4.0 5.7 %collective-permute-start.2 = (bf16[128,256]{1,0:T(8,128)(2,1)S(1)}, bf16[128,256]{1,0:T(8,128)(2,1)S(1)}, u32[]{:S(2)}, u32[]{:S(2)}) collective-permute-start(bf16[128,256]{1,0:T(8,128)(2,1)S(1)} %convert_element_type.140), channel_id=1, source_target_pairs={{0,24},{8,16},{16,8},{24,0},{1,25},{9,17},{17,9},{25,1},{2,26},{10... | collective-permute-start | bytes 196616 | tf_op jit(solution)/shard_map/ppermute | solution.py:35
  5.4 4.3 %collective-permute-start.1 = (bf16[128,256]{1,0:T(8,128)(2,1)S(1)}, bf16[128,256]{1,0:T(8,128)(2,1)S(1)}, u32[]{:S(2)}, u32[]{:S(2)}) collective-permute-start(bf16[128,256]{1,0:T(8,128)(2,1)S(1)} %convert_element_type.140), channel_id=1, source_target_pairs={{0,8},{8,0},{16,24},{24,16},{1,9},{9,1},{17,25},{25,17},{2,10},{10... | collective-permute-start | bytes 196616 | tf_op jit(solution)/shard_map/ppermute | solution.py:35
  8.8 3.0 %collective-permute-start = (bf16[1024,512]{1,0:T(8,128)(2,1)S(1)}, bf16[1024,512]{1,0:T(8,128)(2,1)S(1)}, u32[]{:S(2)}, u32[]{:S(2)}) collective-permute-start(bf16[1024,512]{1,0:T(8,128)(2,1)S(1)} %shard_map.37), channel_id=1, source_target_pairs={{0,1},{1,0},{2,3},{3,2},{4,5},{5,4},{6,7},{7,6},{8,9},{9,8},{10,11... | collective-permute-start | bytes 3145736 | tf_op jit(solution)/shard_map/ppermute | solution.py:35
  12.2 8.0 %collective-permute-start.5 = (bf16[512,128]{1,0:T(8,128)(2,1)S(1)}, bf16[512,128]{1,0:T(8,128)(2,1)S(1)}, u32[]{:S(2)}, u32[]{:S(2)}) collective-permute-start(bf16[512,128]{1,0:T(8,128)(2,1)S(1)} %get-tuple-element.54), channel_id=1, source_target_pairs={{0,2},{1,3},{2,0},{3,1},{4,6},{5,7},{6,4},{7,5},{8,10},{9,11},{10,... | collective-permute-start | bytes 393224 | tf_op jit(solution)/shard_map/ppermute | solution.py:35
  14.3 9.0 %collective-permute-start.6 = (bf16[512,128]{1,0:T(8,128)(2,1)S(1)}, bf16[512,128]{1,0:T(8,128)(2,1)S(1)}, u32[]{:S(2)}, u32[]{:S(2)}) collective-permute-start(bf16[512,128]{1,0:T(8,128)(2,1)S(1)} %get-tuple-element.53), channel_id=1, source_target_pairs={{0,4},{1,5},{2,6},{3,7},{4,0},{5,1},{6,2},{7,3},{8,12},{9,13},{10,... | collective-permute-start | bytes 393224 | tf_op jit(solution)/shard_map/ppermute | solution.py:35
  16.9 9.6 %collective-permute-start.10 = (f32[128,128]{1,0:T(8,128)S(1)}, f32[128,128]{1,0:T(8,128)S(1)}, u32[]{:S(2)}, u32[]{:S(2)}) collective-permute-start(f32[128,128]{1,0:T(8,128)S(1)} %get-tuple-element.59), channel_id=1, source_target_pairs={{0,1},{1,0},{2,3},{3,2},{4,5},{5,4},{6,7},{7,6},{8,9},{9,8},{10,11... | collective-permute-start | bytes 196616 | tf_op jit(solution)/shard_map/ppermute | solution.py:35
  23.4 7.3 %collective-permute-start.7 = (bf16[512,128]{1,0:T(8,128)(2,1)S(1)}, bf16[512,128]{1,0:T(8,128)(2,1)S(1)}, u32[]{:S(2)}, u32[]{:S(2)}) collective-permute-start(bf16[512,128]{1,0:T(8,128)(2,1)S(1)} %get-tuple-element.52), channel_id=1, source_target_pairs={{0,4},{1,5},{2,6},{3,7},{4,0},{5,1},{6,2},{7,3},{8,12},{9,13},{10,... | collective-permute-start | bytes 393224 | tf_op jit(solution)/shard_map/ppermute | solution.py:35
  23.8 7.0 %collective-permute-start.8 = (bf16[512,128]{1,0:T(8,128)(2,1)S(1)}, bf16[512,128]{1,0:T(8,128)(2,1)S(1)}, u32[]{:S(2)}, u32[]{:S(2)}) collective-permute-start(bf16[512,128]{1,0:T(8,128)(2,1)S(1)} %get-tuple-element.51), channel_id=1, source_target_pairs={{0,2},{1,3},{2,0},{3,1},{4,6},{5,7},{6,4},{7,5},{8,10},{9,11},{10,... | collective-permute-start | bytes 393224 | tf_op jit(solution)/shard_map/ppermute | solution.py:35
  31.4 5.0 %collective-permute-start.9 = (bf16[512,128]{1,0:T(8,128)(2,1)S(1)}, bf16[512,128]{1,0:T(8,128)(2,1)S(1)}, u32[]{:S(2)}, u32[]{:S(2)}) collective-permute-start(bf16[512,128]{1,0:T(8,128)(2,1)S(1)} %get-tuple-element.65), channel_id=1, source_target_pairs={{0,8},{8,0},{16,24},{24,16},{1,9},{9,1},{17,25},{25,17},{2,10},{10... | collective-permute-start | bytes 393224 | tf_op jit(solution)/shard_map/ppermute | solution.py:35
  33.5 6.1 %collective-permute-start.11 = (bf16[512,128]{1,0:T(8,128)(2,1)S(1)}, bf16[512,128]{1,0:T(8,128)(2,1)S(1)}, u32[]{:S(2)}, u32[]{:S(2)}) collective-permute-start(bf16[512,128]{1,0:T(8,128)(2,1)S(1)} %get-tuple-element.67), channel_id=1, source_target_pairs={{0,16},{8,24},{16,0},{24,8},{1,17},{9,25},{17,1},{25,9},{2,18},{10... | collective-permute-start | bytes 393224 | tf_op jit(solution)/shard_map/ppermute | solution.py:35
  39.6 5.0 %collective-permute-start.12 = (bf16[512,128]{1,0:T(8,128)(2,1)S(1)}, bf16[512,128]{1,0:T(8,128)(2,1)S(1)}, u32[]{:S(2)}, u32[]{:S(2)}) collective-permute-start(bf16[512,128]{1,0:T(8,128)(2,1)S(1)} %fusion.11), channel_id=1, source_target_pairs={{0,16},{8,24},{16,0},{24,8},{1,17},{9,25},{17,1},{25,9},{2,18},{10... | collective-permute-start | bytes 393224 | tf_op jit(solution)/shard_map/ppermute | solution.py:35
  41.3 5.0 %collective-permute-start.13 = (bf16[512,128]{1,0:T(8,128)(2,1)S(1)}, bf16[512,128]{1,0:T(8,128)(2,1)S(1)}, u32[]{:S(2)}, u32[]{:S(2)}) collective-permute-start(bf16[512,128]{1,0:T(8,128)(2,1)S(1)} %fusion.12), channel_id=1, source_target_pairs={{0,8},{8,0},{16,24},{24,16},{1,9},{9,1},{17,25},{25,17},{2,10},{10... | collective-permute-start | bytes 393224 | tf_op jit(solution)/shard_map/ppermute | solution.py:35
  47.4 6.2 %collective-permute-start.14 = (bf16[512,128]{1,0:T(8,128)(2,1)S(1)}, bf16[512,128]{1,0:T(8,128)(2,1)S(1)}, u32[]{:S(2)}, u32[]{:S(2)}) collective-permute-start(bf16[512,128]{1,0:T(8,128)(2,1)S(1)} %get-tuple-element.48), channel_id=1, source_target_pairs={{0,2},{1,3},{2,0},{3,1},{4,6},{5,7},{6,4},{7,5},{8,10},{9,11},{10,... | collective-permute-start | bytes 393224 | tf_op jit(solution)/shard_map/ppermute | solution.py:35
  47.5 9.1 %collective-permute-start.15 = (bf16[512,128]{1,0:T(8,128)(2,1)S(1)}, bf16[512,128]{1,0:T(8,128)(2,1)S(1)}, u32[]{:S(2)}, u32[]{:S(2)}) collective-permute-start(bf16[512,128]{1,0:T(8,128)(2,1)S(1)} %get-tuple-element.47), channel_id=1, source_target_pairs={{0,4},{1,5},{2,6},{3,7},{4,0},{5,1},{6,2},{7,3},{8,12},{9,13},{10,... | collective-permute-start | bytes 393224 | tf_op jit(solution)/shard_map/ppermute | solution.py:35
  56.6 7.0 %collective-permute-start.16 = (bf16[512,128]{1,0:T(8,128)(2,1)S(1)}, bf16[512,128]{1,0:T(8,128)(2,1)S(1)}, u32[]{:S(2)}, u32[]{:S(2)}) collective-permute-start(bf16[512,128]{1,0:T(8,128)(2,1)S(1)} %get-tuple-element.46), channel_id=1, source_target_pairs={{0,4},{1,5},{2,6},{3,7},{4,0},{5,1},{6,2},{7,3},{8,12},{9,13},{10,... | collective-permute-start | bytes 393224 | tf_op jit(solution)/shard_map/ppermute | solution.py:35
  57.3 6.4 %collective-permute-start.17 = (bf16[512,128]{1,0:T(8,128)(2,1)S(1)}, bf16[512,128]{1,0:T(8,128)(2,1)S(1)}, u32[]{:S(2)}, u32[]{:S(2)}) collective-permute-start(bf16[512,128]{1,0:T(8,128)(2,1)S(1)} %get-tuple-element.45), channel_id=1, source_target_pairs={{0,2},{1,3},{2,0},{3,1},{4,6},{5,7},{6,4},{7,5},{8,10},{9,11},{10,... | collective-permute-start | bytes 393224 | tf_op jit(solution)/shard_map/ppermute | solution.py:35
  64.4 5.0 %collective-permute-start.18 = (bf16[512,128]{1,0:T(8,128)(2,1)S(1)}, bf16[512,128]{1,0:T(8,128)(2,1)S(1)}, u32[]{:S(2)}, u32[]{:S(2)}) collective-permute-start(bf16[512,128]{1,0:T(8,128)(2,1)S(1)} %get-tuple-element.69), channel_id=1, source_target_pairs={{0,8},{8,0},{16,24},{24,16},{1,9},{9,1},{17,25},{25,17},{2,10},{10... | collective-permute-start | bytes 393224 | tf_op jit(solution)/shard_map/ppermute | solution.py:35
  65.5 5.0 %collective-permute-start.19 = (bf16[512,128]{1,0:T(8,128)(2,1)S(1)}, bf16[512,128]{1,0:T(8,128)(2,1)S(1)}, u32[]{:S(2)}, u32[]{:S(2)}) collective-permute-start(bf16[512,128]{1,0:T(8,128)(2,1)S(1)} %get-tuple-element.71), channel_id=1, source_target_pairs={{0,16},{8,24},{16,0},{24,8},{1,17},{9,25},{17,1},{25,9},{2,18},{10... | collective-permute-start | bytes 393224 | tf_op jit(solution)/shard_map/ppermute | solution.py:35
  70.6 5.0 %collective-permute-start.20 = (bf16[512,128]{1,0:T(8,128)(2,1)S(1)}, bf16[512,128]{1,0:T(8,128)(2,1)S(1)}, u32[]{:S(2)}, u32[]{:S(2)}) collective-permute-start(bf16[512,128]{1,0:T(8,128)(2,1)S(1)} %fusion.14), channel_id=1, source_target_pairs={{0,16},{8,24},{16,0},{24,8},{1,17},{9,25},{17,1},{25,9},{2,18},{10... | collective-permute-start | bytes 393224 | tf_op jit(solution)/shard_map/ppermute | solution.py:35
  71.2 5.0 %collective-permute-start.21 = (bf16[512,128]{1,0:T(8,128)(2,1)S(1)}, bf16[512,128]{1,0:T(8,128)(2,1)S(1)}, u32[]{:S(2)}, u32[]{:S(2)}) collective-permute-start(bf16[512,128]{1,0:T(8,128)(2,1)S(1)} %fusion.13), channel_id=1, source_target_pairs={{0,8},{8,0},{16,24},{24,16},{1,9},{9,1},{17,25},{25,17},{2,10},{10... | collective-permute-start | bytes 393224 | tf_op jit(solution)/shard_map/ppermute | solution.py:35
  79.5 8.3 %collective-permute-start.25 = (f32[136,128]{1,0:T(8,128)S(1)}, f32[136,128]{1,0:T(8,128)S(1)}, u32[]{:S(2)}, u32[]{:S(2)}) collective-permute-start(f32[136,128]{1,0:T(8,128)S(1)} %select_maximum_fusion), channel_id=1, source_target_pairs={{0,4},{1,5},{2,6},{3,7},{4,0},{5,1},{6,2},{7,3},{8,12},{9,13},{10,... | collective-permute-start | bytes 208904 | tf_op jit(solution)/shard_map/ppermute | solution.py:35
  80.4 7.4 %collective-permute-start.24 = (f32[136,128]{1,0:T(8,128)S(1)}, f32[136,128]{1,0:T(8,128)S(1)}, u32[]{:S(2)}, u32[]{:S(2)}) collective-permute-start(f32[136,128]{1,0:T(8,128)S(1)} %select_maximum_fusion), channel_id=1, source_target_pairs={{0,6},{1,7},{2,4},{3,5},{4,2},{5,3},{6,0},{7,1},{8,14},{9,15},{10,... | collective-permute-start | bytes 208904 | tf_op jit(solution)/shard_map/ppermute | solution.py:35
  82.5 6.5 %collective-permute-start.23 = (f32[136,128]{1,0:T(8,128)S(1)}, f32[136,128]{1,0:T(8,128)S(1)}, u32[]{:S(2)}, u32[]{:S(2)}) collective-permute-start(f32[136,128]{1,0:T(8,128)S(1)} %select_maximum_fusion), channel_id=1, source_target_pairs={{0,2},{1,3},{2,0},{3,1},{4,6},{5,7},{6,4},{7,5},{8,10},{9,11},{10,... | collective-permute-start | bytes 208904 | tf_op jit(solution)/shard_map/ppermute | solution.py:35
  (6 other events, 16.1 us)

commit v8 on v7

--- a/solution.py
+++ b/solution.py
@@ -228,11 +228,15 @@
         return sum(parts[1:], parts[0])
 
     def forward(low_own, low_other):
-        product = jnp.dot(own, low_own, preferred_element_type=jnp.float32)
-        product = product + jnp.dot(other, low_other, preferred_element_type=jnp.float32)
-        product = product - center * (spread(low_own, own_offset) + spread(low_other, other_offset))
-        middle = product.shape[0] // 2
-        return product[:middle], product[middle:]
+        middle = group_rows * width // 2
+        shifted = center * (spread(low_own, own_offset) + spread(low_other, other_offset))
+
+        def part(rows):
+            product = jnp.dot(own[rows], low_own, preferred_element_type=jnp.float32)
+            product = product + jnp.dot(other[rows], low_other, preferred_element_type=jnp.float32)
+            return product - shifted[rows]
+
+        return part(slice(0, middle)), part(slice(middle, None))
 
     def backward(low):
         def part(tile, offset):
@@ -242,10 +246,11 @@
         return part(own, own_offset), part(other, other_offset)
 
     def sum_over(axis, bits, one, two):
-        for bit_one, bit_two in zip(bits, reversed(bits)):
-            from_one, from_two = lax.optimization_barrier(
-                (swap(one.astype(narrow), axis, bit_one), swap(two.astype(narrow), axis, bit_two))
-            )
+        for level, (bit_one, bit_two) in enumerate(zip(bits, reversed(bits))):
+            from_one = swap(one.astype(narrow), axis, bit_one)
+            from_two = swap(two.astype(narrow), axis, bit_two)
+            if level < len(bits) - 1:
+                from_one, from_two = lax.optimization_barrier((from_one, from_two))
             one, two = one + from_one.astype(jnp.float32), two + from_two.astype(jnp.float32)
         return one, two
 
@@ -273,10 +278,15 @@
     y4_own = scales[3] * image_own - carries[3] * y2_own
     y4_other = scales[3] * image_other - carries[3] * y2_other
 
-    mine = jnp.concatenate([y4_own, y4_other])
-    theirs = swap(jnp.concatenate([y4_other, y4_own]), "col", 1)
-    corner = exact_dot(mine, mine, ((0,), (0,)))
-    cross = exact_dot(theirs, jnp.where(mine_first, mine, theirs), ((0,), (0,)))
+    theirs_own = swap(y4_other, "col", 1)
+    theirs_other = swap(y4_own, "col", 1)
+
+    def product(left, right):
+        return exact_dot(left, right, ((0,), (0,)))
+
+    corner = product(y4_own, y4_own) + product(y4_other, y4_other)
+    cross = product(theirs_own, jnp.where(mine_first, y4_own, theirs_own))
+    cross = cross + product(theirs_other, jnp.where(mine_first, y4_other, theirs_other))
     rows = lax.broadcasted_iota(jnp.int32, (half, half), 0)
     lanes = lax.broadcasted_iota(jnp.int32, (half, half), 1)
     packed = jnp.where(mine_first | (rows >= lanes), cross, corner)
@@ -286,8 +296,8 @@
     partner = swap(total, "col", 1)
     orbital_count = piece_rows * row_count * col_count
     here = row_rank * piece_rows
-    mine = lax.dynamic_slice_in_dim(mine, here, piece_rows, 0)
-    theirs = lax.dynamic_slice_in_dim(theirs, here, piece_rows, 0)
+    mine = lax.dynamic_slice_in_dim(y4_own, here, piece_rows, 0)
+    theirs = lax.dynamic_slice_in_dim(theirs_own, here, piece_rows, 0)
     return orthonormal(total, partner, mine, theirs, mine_first, math.sqrt(orbital_count))
 
 

time: 97.5 us -> 100 us (1.026)
  starting transfers between devices: 28.1 us -> 32.1 us
  waiting for transfers between devices: 50.3 us -> 47.3 us
  matrix products: 5.68 us -> 6.69 us
    ppermute x27 -> x28, starting transfers between devices: 28.1 us -> 32.1 us  [swap(): return lax.ppermute(value, axis, [(i, i ^ distance) for i in range(count)])]
    ppermute x27 -> x28, waiting for transfers between devices: 50.3 us -> 47.3 us  [swap(): return lax.ppermute(value, axis, [(i, i ^ distance) for i in range(count)])]
    dot_general x4 -> x8, matrix products: 1.73 us -> 2.36 us  [the longest x4 1.18 us: part(): jnp.dot(other[rows], low_other, preferred_element_type=jnp.float32)]
    dot_general x2 -> x4, matrix products: 2.02 us -> 2.41 us  [exact_dot(): lax.dot_general(a, b, (dims, ((), ())), precision=lax.Precision.HIGHEST,...]
  transfers between devices with their start and end apart: 27 -> 28, of which waited for: 21 -> 20; matrix products, arithmetic and copies ran while one was open for 3% -> 6% of each run, Pallas kernels for 1% -> 1%
where the time goes in v8:
time: 100 us
  waiting for transfers between devices  47.3 us (47%)
  starting transfers between devices  32.1 us (32%)
  Pallas kernels  8.06 us (8%)
  matrix products  6.69 us (7%)
  other arithmetic  3.35 us (3%)
  local copies, waits for them, and re-layouts  2.22 us (2%)
    ppermute x28, waiting for transfers between devices, swap(): return lax.ppermute(value, axis, [(i, i ^ distance) for i in range(count)])  47.3 us
    ppermute x28, starting transfers between devices, swap(): return lax.ppermute(value, axis, [(i, i ^ distance) for i in range(count)])  32.1 us
    pallas_call x1, Pallas kernels, orthonormal(): pl.pallas_call(kernel, in_specs=[pl.BlockSpec(memory_space=pltpu.SMEM), v...  6.92 us
    dot_general x4, matrix products, exact_dot(): lax.dot_general(a, b, (dims, ((), ())), precision=lax.Precision.HIGHEST,...  2.41 us
    unnamed x6, local copies, waits for them, and re-layouts  2.09 us
  transfers between devices with their start and end apart: 28, of which 20 were waited for; matrix products, arithmetic and copies ran while one was open for 6% of the time, Pallas kernels for 1%

profile of v8, /device:TPU:0, one launch (start us, length us, event | category | flops | bytes accessed | tf_op | source)
XLA Modules:
  0.0 100.2 jit_solution(13492621104275691411)
XLA Ops:
  1.0 3.0 %collective-permute-start.3 = (bf16[128,256]{1,0:T(8,128)(2,1)S(1)}, bf16[128,256]{1,0:T(8,128)(2,1)S(1)}, u32[]{:S(2)}, u32[]{:S(2)}) collective-permute-start(bf16[128,256]{1,0:T(8,128)(2,1)S(1)} %convert_element_type.140), channel_id=1, source_target_pairs={{0,16},{8,24},{16,0},{24,8},{1,17},{9,25},{17,1},{25,9},{2,18},{10... | collective-permute-start | bytes 196616 | tf_op jit(solution)/shard_map/ppermute | solution.py:35
  13.2 2.1 %collective-permute-start.5 = (bf16[512,128]{1,0:T(8,128)(2,1)S(1)}, bf16[512,128]{1,0:T(8,128)(2,1)S(1)}, u32[]{:S(2)}, u32[]{:S(2)}) collective-permute-start(bf16[512,128]{1,0:T(8,128)(2,1)S(1)} %get-tuple-element.37), channel_id=1, source_target_pairs={{0,2},{1,3},{2,0},{3,1},{4,6},{5,7},{6,4},{7,5},{8,10},{9,11},{10,... | collective-permute-start | bytes 393224 | tf_op jit(solution)/shard_map/ppermute | solution.py:35
  15.6 2.6 %collective-permute-start.6 = (bf16[512,128]{1,0:T(8,128)(2,1)S(1)}, bf16[512,128]{1,0:T(8,128)(2,1)S(1)}, u32[]{:S(2)}, u32[]{:S(2)}) collective-permute-start(bf16[512,128]{1,0:T(8,128)(2,1)S(1)} %get-tuple-element.39), channel_id=1, source_target_pairs={{0,4},{1,5},{2,6},{3,7},{4,0},{5,1},{6,2},{7,3},{8,12},{9,13},{10,... | collective-permute-start | bytes 393224 | tf_op jit(solution)/shard_map/ppermute | solution.py:35
  19.3 5.6 %collective-permute-done.6 = bf16[512,128]{1,0:T(8,128)(2,1)S(1)} collective-permute-done((bf16[512,128]{1,0:T(8,128)(2,1)S(1)}, bf16[512,128]{1,0:T(8,128)(2,1)S(1)}, u32[]{:S(2)}, u32[]{:S(2)}) %collective-permute-start.6) | collective-permute-done | bytes 131104 | tf_op jit(solution)/shard_map/ppermute | solution.py:35
  25.1 3.0 %collective-permute-start.7 = (bf16[512,128]{1,0:T(8,128)(2,1)S(1)}, bf16[512,128]{1,0:T(8,128)(2,1)S(1)}, u32[]{:S(2)}, u32[]{:S(2)}) collective-permute-start(bf16[512,128]{1,0:T(8,128)(2,1)S(1)} %fusion.26), channel_id=1, source_target_pairs={{0,4},{1,5},{2,6},{3,7},{4,0},{5,1},{6,2},{7,3},{8,12},{9,13},{10,... | collective-permute-start | bytes 393224 | tf_op jit(solution)/shard_map/ppermute | solution.py:35
  28.1 3.5 %collective-permute-done.8 = bf16[512,128]{1,0:T(8,128)(2,1)S(1)} collective-permute-done((bf16[512,128]{1,0:T(8,128)(2,1)S(1)}, bf16[512,128]{1,0:T(8,128)(2,1)S(1)}, u32[]{:S(2)}, u32[]{:S(2)}) %collective-permute-start.8) | collective-permute-done | bytes 131104 | tf_op jit(solution)/shard_map/ppermute | solution.py:35
  31.7 1.8 %collective-permute-done.7 = bf16[512,128]{1,0:T(8,128)(2,1)S(1)} collective-permute-done((bf16[512,128]{1,0:T(8,128)(2,1)S(1)}, bf16[512,128]{1,0:T(8,128)(2,1)S(1)}, u32[]{:S(2)}, u32[]{:S(2)}) %collective-permute-start.7) | collective-permute-done | bytes 131104 | tf_op jit(solution)/shard_map/ppermute | solution.py:35
  34.2 1.6 %collective-permute-start.9 = (bf16[512,128]{1,0:T(8,128)(2,1)S(1)}, bf16[512,128]{1,0:T(8,128)(2,1)S(1)}, u32[]{:S(2)}, u32[]{:S(2)}) collective-permute-start(bf16[512,128]{1,0:T(8,128)(2,1)S(1)} %get-tuple-element.41), channel_id=1, source_target_pairs={{0,8},{8,0},{16,24},{24,16},{1,9},{9,1},{17,25},{25,17},{2,10},{10... | collective-permute-start | bytes 393224 | tf_op jit(solution)/shard_map/ppermute | solution.py:35
  36.2 1.6 %collective-permute-start.11 = (bf16[512,128]{1,0:T(8,128)(2,1)S(1)}, bf16[512,128]{1,0:T(8,128)(2,1)S(1)}, u32[]{:S(2)}, u32[]{:S(2)}) collective-permute-start(bf16[512,128]{1,0:T(8,128)(2,1)S(1)} %get-tuple-element.43), channel_id=1, source_target_pairs={{0,16},{8,24},{16,0},{24,8},{1,17},{9,25},{17,1},{25,9},{2,18},{10... | collective-permute-start | bytes 393224 | tf_op jit(solution)/shard_map/ppermute | solution.py:35
  39.2 2.5 %collective-permute-done.11 = bf16[512,128]{1,0:T(8,128)(2,1)S(1)} collective-permute-done((bf16[512,128]{1,0:T(8,128)(2,1)S(1)}, bf16[512,128]{1,0:T(8,128)(2,1)S(1)}, u32[]{:S(2)}, u32[]{:S(2)}) %collective-permute-start.11) | collective-permute-done | bytes 131104 | tf_op jit(solution)/shard_map/ppermute | solution.py:35
  41.8 1.6 %collective-permute-start.12 = (bf16[512,128]{1,0:T(8,128)(2,1)S(1)}, bf16[512,128]{1,0:T(8,128)(2,1)S(1)}, u32[]{:S(2)}, u32[]{:S(2)}) collective-permute-start(bf16[512,128]{1,0:T(8,128)(2,1)S(1)} %fusion.28), channel_id=1, source_target_pairs={{0,16},{8,24},{16,0},{24,8},{1,17},{9,25},{17,1},{25,9},{2,18},{10... | collective-permute-start | bytes 393224 | tf_op jit(solution)/shard_map/ppermute | solution.py:35
  44.0 2.8 %collective-permute-done.12 = bf16[512,128]{1,0:T(8,128)(2,1)S(1)} collective-permute-done((bf16[512,128]{1,0:T(8,128)(2,1)S(1)}, bf16[512,128]{1,0:T(8,128)(2,1)S(1)}, u32[]{:S(2)}, u32[]{:S(2)}) %collective-permute-start.12) | collective-permute-done | bytes 131104 | tf_op jit(solution)/shard_map/ppermute | solution.py:35
  46.9 1.5 %collective-permute-done.13 = bf16[512,128]{1,0:T(8,128)(2,1)S(1)} collective-permute-done((bf16[512,128]{1,0:T(8,128)(2,1)S(1)}, bf16[512,128]{1,0:T(8,128)(2,1)S(1)}, u32[]{:S(2)}, u32[]{:S(2)}) %collective-permute-start.13) | collective-permute-done | bytes 131104 | tf_op jit(solution)/shard_map/ppermute | solution.py:35
  49.8 3.3 %collective-permute-start.15 = (bf16[512,128]{1,0:T(8,128)(2,1)S(1)}, bf16[512,128]{1,0:T(8,128)(2,1)S(1)}, u32[]{:S(2)}, u32[]{:S(2)}) collective-permute-start(bf16[512,128]{1,0:T(8,128)(2,1)S(1)} %get-tuple-element.47), channel_id=1, source_target_pairs={{0,4},{1,5},{2,6},{3,7},{4,0},{5,1},{6,2},{7,3},{8,12},{9,13},{10,... | collective-permute-start | bytes 393224 | tf_op jit(solution)/shard_map/ppermute | solution.py:35
  53.1 4.7 %collective-permute-done.14 = bf16[512,128]{1,0:T(8,128)(2,1)S(1)} collective-permute-done((bf16[512,128]{1,0:T(8,128)(2,1)S(1)}, bf16[512,128]{1,0:T(8,128)(2,1)S(1)}, u32[]{:S(2)}, u32[]{:S(2)}) %collective-permute-start.14) | collective-permute-done | bytes 131104 | tf_op jit(solution)/shard_map/ppermute | solution.py:35
  57.8 2.3 %collective-permute-done.15 = bf16[512,128]{1,0:T(8,128)(2,1)S(1)} collective-permute-done((bf16[512,128]{1,0:T(8,128)(2,1)S(1)}, bf16[512,128]{1,0:T(8,128)(2,1)S(1)}, u32[]{:S(2)}, u32[]{:S(2)}) %collective-permute-start.15) | collective-permute-done | bytes 131104 | tf_op jit(solution)/shard_map/ppermute | solution.py:35
  60.3 2.6 %collective-permute-start.16 = (bf16[512,128]{1,0:T(8,128)(2,1)S(1)}, bf16[512,128]{1,0:T(8,128)(2,1)S(1)}, u32[]{:S(2)}, u32[]{:S(2)}) collective-permute-start(bf16[512,128]{1,0:T(8,128)(2,1)S(1)} %fusion.30), channel_id=1, source_target_pairs={{0,4},{1,5},{2,6},{3,7},{4,0},{5,1},{6,2},{7,3},{8,12},{9,13},{10,... | collective-permute-start | bytes 393224 | tf_op jit(solution)/shard_map/ppermute | solution.py:35
  63.0 3.7 %collective-permute-done.17 = bf16[512,128]{1,0:T(8,128)(2,1)S(1)} collective-permute-done((bf16[512,128]{1,0:T(8,128)(2,1)S(1)}, bf16[512,128]{1,0:T(8,128)(2,1)S(1)}, u32[]{:S(2)}, u32[]{:S(2)}) %collective-permute-start.17) | collective-permute-done | bytes 131104 | tf_op jit(solution)/shard_map/ppermute | solution.py:35
  69.1 3.3 %collective-permute-done.18 = bf16[512,128]{1,0:T(8,128)(2,1)S(1)} collective-permute-done((bf16[512,128]{1,0:T(8,128)(2,1)S(1)}, bf16[512,128]{1,0:T(8,128)(2,1)S(1)}, u32[]{:S(2)}, u32[]{:S(2)}) %collective-permute-start.18) | collective-permute-done | bytes 131104 | tf_op jit(solution)/shard_map/ppermute | solution.py:35
  75.7 3.0 %collective-permute-done.22 = bf16[512,128]{1,0:T(8,128)(2,1)S(1)} collective-permute-done((bf16[512,128]{1,0:T(8,128)(2,1)S(1)}, bf16[512,128]{1,0:T(8,128)(2,1)S(1)}, u32[]{:S(2)}, u32[]{:S(2)}) %collective-permute-start.22) | collective-permute-done | bytes 131104 | tf_op jit(solution)/shard_map/ppermute | solution.py:35
  82.2 2.1 %collective-permute-start.26 = (f32[136,128]{1,0:T(8,128)S(1)}, f32[136,128]{1,0:T(8,128)S(1)}, u32[]{:S(2)}, u32[]{:S(2)}) collective-permute-start(f32[136,128]{1,0:T(8,128)S(1)} %select_maximum_fusion), channel_id=1, source_target_pairs={{0,4},{1,5},{2,6},{3,7},{4,0},{5,1},{6,2},{7,3},{8,12},{9,13},{10,... | collective-permute-start | bytes 208904 | tf_op jit(solution)/shard_map/ppermute | solution.py:35
  84.3 1.8 %collective-permute-start.25 = (f32[136,128]{1,0:T(8,128)S(1)}, f32[136,128]{1,0:T(8,128)S(1)}, u32[]{:S(2)}, u32[]{:S(2)}) collective-permute-start(f32[136,128]{1,0:T(8,128)S(1)} %select_maximum_fusion), channel_id=1, source_target_pairs={{0,6},{1,7},{2,4},{3,5},{4,2},{5,3},{6,0},{7,1},{8,14},{9,15},{10,... | collective-permute-start | bytes 208904 | tf_op jit(solution)/shard_map/ppermute | solution.py:35
  86.1 5.0 %collective-permute-done.26 = f32[136,128]{1,0:T(8,128)S(1)} collective-permute-done((f32[136,128]{1,0:T(8,128)S(1)}, f32[136,128]{1,0:T(8,128)S(1)}, u32[]{:S(2)}, u32[]{:S(2)}) %collective-permute-start.26) | collective-permute-done | bytes 69664 | tf_op jit(solution)/shard_map/ppermute | solution.py:35
  93.3 6.9 %shard_map.38 = f32[128,256]{1,0:T(8,128)} custom-call(s32[1]{0:T(128)} %bitcast.first_ref, f32[136,128]{1,0:T(8,128)S(1)} %add_add_fusion.total_ref, f32[136,128]{1,0:T(8,128)S(1)} %collective-permute-done.27.partner_ref, f32[128,128]{1,0:T(8,128)S(1)} %constant_dynamic-slice_fusion.1.mine_ref, f32[128,128]{1,0:T(8,128)S(1)} %constant_dynamic-slice_fusion.theirs_ref), custom_call_target="tpu_custom_call" | custom-call | tf_op jit(solution)/shard_map/pallas_call | solution.py:171
  (95 shorter events, 27.6 us)
Async XLA Ops:
  1.0 9.4 %collective-permute-start.3 = (bf16[128,256]{1,0:T(8,128)(2,1)S(1)}, bf16[128,256]{1,0:T(8,128)(2,1)S(1)}, u32[]{:S(2)}, u32[]{:S(2)}) collective-permute-start(bf16[128,256]{1,0:T(8,128)(2,1)S(1)} %convert_element_type.140), channel_id=1, source_target_pairs={{0,16},{8,24},{16,0},{24,8},{1,17},{9,25},{17,1},{25,9},{2,18},{10... | collective-permute-start | bytes 196616 | tf_op jit(solution)/shard_map/ppermute | solution.py:35
  4.0 6.4 %collective-permute-start.2 = (bf16[128,256]{1,0:T(8,128)(2,1)S(1)}, bf16[128,256]{1,0:T(8,128)(2,1)S(1)}, u32[]{:S(2)}, u32[]{:S(2)}) collective-permute-start(bf16[128,256]{1,0:T(8,128)(2,1)S(1)} %convert_element_type.140), channel_id=1, source_target_pairs={{0,24},{8,16},{16,8},{24,0},{1,25},{9,17},{17,9},{25,1},{2,26},{10... | collective-permute-start | bytes 196616 | tf_op jit(solution)/shard_map/ppermute | solution.py:35
  5.4 5.0 %collective-permute-start.1 = (bf16[128,256]{1,0:T(8,128)(2,1)S(1)}, bf16[128,256]{1,0:T(8,128)(2,1)S(1)}, u32[]{:S(2)}, u32[]{:S(2)}) collective-permute-start(bf16[128,256]{1,0:T(8,128)(2,1)S(1)} %convert_element_type.140), channel_id=1, source_target_pairs={{0,8},{8,0},{16,24},{24,16},{1,9},{9,1},{17,25},{25,17},{2,10},{10... | collective-permute-start | bytes 196616 | tf_op jit(solution)/shard_map/ppermute | solution.py:35
  6.4 11.9 %collective-permute-start.10 = (f32[128,128]{1,0:T(8,128)S(1)}, f32[128,128]{1,0:T(8,128)S(1)}, u32[]{:S(2)}, u32[]{:S(2)}) collective-permute-start(f32[128,128]{1,0:T(8,128)S(1)} %get-tuple-element.32), channel_id=1, source_target_pairs={{0,1},{1,0},{2,3},{3,2},{4,5},{5,4},{6,7},{7,6},{8,9},{9,8},{10,11... | collective-permute-start | bytes 196616 | tf_op jit(solution)/shard_map/ppermute | solution.py:35
  9.8 3.1 %collective-permute-start = (bf16[1024,512]{1,0:T(8,128)(2,1)S(1)}, bf16[1024,512]{1,0:T(8,128)(2,1)S(1)}, u32[]{:S(2)}, u32[]{:S(2)}) collective-permute-start(bf16[1024,512]{1,0:T(8,128)(2,1)S(1)} %shard_map.37), channel_id=1, source_target_pairs={{0,1},{1,0},{2,3},{3,2},{4,5},{5,4},{6,7},{7,6},{8,9},{9,8},{10,11... | collective-permute-start | bytes 3145736 | tf_op jit(solution)/shard_map/ppermute | solution.py:35
  13.2 6.1 %collective-permute-start.5 = (bf16[512,128]{1,0:T(8,128)(2,1)S(1)}, bf16[512,128]{1,0:T(8,128)(2,1)S(1)}, u32[]{:S(2)}, u32[]{:S(2)}) collective-permute-start(bf16[512,128]{1,0:T(8,128)(2,1)S(1)} %get-tuple-element.37), channel_id=1, source_target_pairs={{0,2},{1,3},{2,0},{3,1},{4,6},{5,7},{6,4},{7,5},{8,10},{9,11},{10,... | collective-permute-start | bytes 393224 | tf_op jit(solution)/shard_map/ppermute | solution.py:35
  15.6 9.3 %collective-permute-start.6 = (bf16[512,128]{1,0:T(8,128)(2,1)S(1)}, bf16[512,128]{1,0:T(8,128)(2,1)S(1)}, u32[]{:S(2)}, u32[]{:S(2)}) collective-permute-start(bf16[512,128]{1,0:T(8,128)(2,1)S(1)} %get-tuple-element.39), channel_id=1, source_target_pairs={{0,4},{1,5},{2,6},{3,7},{4,0},{5,1},{6,2},{7,3},{8,12},{9,13},{10,... | collective-permute-start | bytes 393224 | tf_op jit(solution)/shard_map/ppermute | solution.py:35
  24.9 6.8 %collective-permute-start.8 = (bf16[512,128]{1,0:T(8,128)(2,1)S(1)}, bf16[512,128]{1,0:T(8,128)(2,1)S(1)}, u32[]{:S(2)}, u32[]{:S(2)}) collective-permute-start(bf16[512,128]{1,0:T(8,128)(2,1)S(1)} %fusion.27), channel_id=1, source_target_pairs={{0,2},{1,3},{2,0},{3,1},{4,6},{5,7},{6,4},{7,5},{8,10},{9,11},{10,... | collective-permute-start | bytes 393224 | tf_op jit(solution)/shard_map/ppermute | solution.py:35
  25.1 8.4 %collective-permute-start.7 = (bf16[512,128]{1,0:T(8,128)(2,1)S(1)}, bf16[512,128]{1,0:T(8,128)(2,1)S(1)}, u32[]{:S(2)}, u32[]{:S(2)}) collective-permute-start(bf16[512,128]{1,0:T(8,128)(2,1)S(1)} %fusion.26), channel_id=1, source_target_pairs={{0,4},{1,5},{2,6},{3,7},{4,0},{5,1},{6,2},{7,3},{8,12},{9,13},{10,... | collective-permute-start | bytes 393224 | tf_op jit(solution)/shard_map/ppermute | solution.py:35
  34.2 5.0 %collective-permute-start.9 = (bf16[512,128]{1,0:T(8,128)(2,1)S(1)}, bf16[512,128]{1,0:T(8,128)(2,1)S(1)}, u32[]{:S(2)}, u32[]{:S(2)}) collective-permute-start(bf16[512,128]{1,0:T(8,128)(2,1)S(1)} %get-tuple-element.41), channel_id=1, source_target_pairs={{0,8},{8,0},{16,24},{24,16},{1,9},{9,1},{17,25},{25,17},{2,10},{10... | collective-permute-start | bytes 393224 | tf_op jit(solution)/shard_map/ppermute | solution.py:35
  36.2 5.5 %collective-permute-start.11 = (bf16[512,128]{1,0:T(8,128)(2,1)S(1)}, bf16[512,128]{1,0:T(8,128)(2,1)S(1)}, u32[]{:S(2)}, u32[]{:S(2)}) collective-permute-start(bf16[512,128]{1,0:T(8,128)(2,1)S(1)} %get-tuple-element.43), channel_id=1, source_target_pairs={{0,16},{8,24},{16,0},{24,8},{1,17},{9,25},{17,1},{25,9},{2,18},{10... | collective-permute-start | bytes 393224 | tf_op jit(solution)/shard_map/ppermute | solution.py:35
  41.8 5.0 %collective-permute-start.12 = (bf16[512,128]{1,0:T(8,128)(2,1)S(1)}, bf16[512,128]{1,0:T(8,128)(2,1)S(1)}, u32[]{:S(2)}, u32[]{:S(2)}) collective-permute-start(bf16[512,128]{1,0:T(8,128)(2,1)S(1)} %fusion.28), channel_id=1, source_target_pairs={{0,16},{8,24},{16,0},{24,8},{1,17},{9,25},{17,1},{25,9},{2,18},{10... | collective-permute-start | bytes 393224 | tf_op jit(solution)/shard_map/ppermute | solution.py:35
  43.4 5.0 %collective-permute-start.13 = (bf16[512,128]{1,0:T(8,128)(2,1)S(1)}, bf16[512,128]{1,0:T(8,128)(2,1)S(1)}, u32[]{:S(2)}, u32[]{:S(2)}) collective-permute-start(bf16[512,128]{1,0:T(8,128)(2,1)S(1)} %fusion.29), channel_id=1, source_target_pairs={{0,8},{8,0},{16,24},{24,16},{1,9},{9,1},{17,25},{25,17},{2,10},{10... | collective-permute-start | bytes 393224 | tf_op jit(solution)/shard_map/ppermute | solution.py:35
  49.8 8.0 %collective-permute-start.14 = (bf16[512,128]{1,0:T(8,128)(2,1)S(1)}, bf16[512,128]{1,0:T(8,128)(2,1)S(1)}, u32[]{:S(2)}, u32[]{:S(2)}) collective-permute-start(bf16[512,128]{1,0:T(8,128)(2,1)S(1)} %get-tuple-element.45), channel_id=1, source_target_pairs={{0,2},{1,3},{2,0},{3,1},{4,6},{5,7},{6,4},{7,5},{8,10},{9,11},{10,... | collective-permute-start | bytes 393224 | tf_op jit(solution)/shard_map/ppermute | solution.py:35
  49.8 10.3 %collective-permute-start.15 = (bf16[512,128]{1,0:T(8,128)(2,1)S(1)}, bf16[512,128]{1,0:T(8,128)(2,1)S(1)}, u32[]{:S(2)}, u32[]{:S(2)}) collective-permute-start(bf16[512,128]{1,0:T(8,128)(2,1)S(1)} %get-tuple-element.47), channel_id=1, source_target_pairs={{0,4},{1,5},{2,6},{3,7},{4,0},{5,1},{6,2},{7,3},{8,12},{9,13},{10,... | collective-permute-start | bytes 393224 | tf_op jit(solution)/shard_map/ppermute | solution.py:35
  60.2 6.4 %collective-permute-start.17 = (bf16[512,128]{1,0:T(8,128)(2,1)S(1)}, bf16[512,128]{1,0:T(8,128)(2,1)S(1)}, u32[]{:S(2)}, u32[]{:S(2)}) collective-permute-start(bf16[512,128]{1,0:T(8,128)(2,1)S(1)} %fusion.31), channel_id=1, source_target_pairs={{0,2},{1,3},{2,0},{3,1},{4,6},{5,7},{6,4},{7,5},{8,10},{9,11},{10,... | collective-permute-start | bytes 393224 | tf_op jit(solution)/shard_map/ppermute | solution.py:35
  60.3 6.4 %collective-permute-start.16 = (bf16[512,128]{1,0:T(8,128)(2,1)S(1)}, bf16[512,128]{1,0:T(8,128)(2,1)S(1)}, u32[]{:S(2)}, u32[]{:S(2)}) collective-permute-start(bf16[512,128]{1,0:T(8,128)(2,1)S(1)} %fusion.30), channel_id=1, source_target_pairs={{0,4},{1,5},{2,6},{3,7},{4,0},{5,1},{6,2},{7,3},{8,12},{9,13},{10,... | collective-permute-start | bytes 393224 | tf_op jit(solution)/shard_map/ppermute | solution.py:35
  67.4 5.0 %collective-permute-start.18 = (bf16[512,128]{1,0:T(8,128)(2,1)S(1)}, bf16[512,128]{1,0:T(8,128)(2,1)S(1)}, u32[]{:S(2)}, u32[]{:S(2)}) collective-permute-start(bf16[512,128]{1,0:T(8,128)(2,1)S(1)} %get-tuple-element.49), channel_id=1, source_target_pairs={{0,8},{8,0},{16,24},{24,16},{1,9},{9,1},{17,25},{25,17},{2,10},{10... | collective-permute-start | bytes 393224 | tf_op jit(solution)/shard_map/ppermute | solution.py:35
  68.6 5.0 %collective-permute-start.19 = (bf16[512,128]{1,0:T(8,128)(2,1)S(1)}, bf16[512,128]{1,0:T(8,128)(2,1)S(1)}, u32[]{:S(2)}, u32[]{:S(2)}) collective-permute-start(bf16[512,128]{1,0:T(8,128)(2,1)S(1)} %get-tuple-element.51), channel_id=1, source_target_pairs={{0,16},{8,24},{16,0},{24,8},{1,17},{9,25},{17,1},{25,9},{2,18},{10... | collective-permute-start | bytes 393224 | tf_op jit(solution)/shard_map/ppermute | solution.py:35
  73.7 5.0 %collective-permute-start.22 = (bf16[512,128]{1,0:T(8,128)(2,1)S(1)}, bf16[512,128]{1,0:T(8,128)(2,1)S(1)}, u32[]{:S(2)}, u32[]{:S(2)}) collective-permute-start(bf16[512,128]{1,0:T(8,128)(2,1)S(1)} %fusion.33), channel_id=1, source_target_pairs={{0,16},{8,24},{16,0},{24,8},{1,17},{9,25},{17,1},{25,9},{2,18},{10... | collective-permute-start | bytes 393224 | tf_op jit(solution)/shard_map/ppermute | solution.py:35
  74.2 5.0 %collective-permute-start.20 = (bf16[512,128]{1,0:T(8,128)(2,1)S(1)}, bf16[512,128]{1,0:T(8,128)(2,1)S(1)}, u32[]{:S(2)}, u32[]{:S(2)}) collective-permute-start(bf16[512,128]{1,0:T(8,128)(2,1)S(1)} %fusion.32), channel_id=1, source_target_pairs={{0,8},{8,0},{16,24},{24,16},{1,9},{9,1},{17,25},{25,17},{2,10},{10... | collective-permute-start | bytes 393224 | tf_op jit(solution)/shard_map/ppermute | solution.py:35
  82.2 9.0 %collective-permute-start.26 = (f32[136,128]{1,0:T(8,128)S(1)}, f32[136,128]{1,0:T(8,128)S(1)}, u32[]{:S(2)}, u32[]{:S(2)}) collective-permute-start(f32[136,128]{1,0:T(8,128)S(1)} %select_maximum_fusion), channel_id=1, source_target_pairs={{0,4},{1,5},{2,6},{3,7},{4,0},{5,1},{6,2},{7,3},{8,12},{9,13},{10,... | collective-permute-start | bytes 208904 | tf_op jit(solution)/shard_map/ppermute | solution.py:35
  84.3 6.9 %collective-permute-start.25 = (f32[136,128]{1,0:T(8,128)S(1)}, f32[136,128]{1,0:T(8,128)S(1)}, u32[]{:S(2)}, u32[]{:S(2)}) collective-permute-start(f32[136,128]{1,0:T(8,128)S(1)} %select_maximum_fusion), channel_id=1, source_target_pairs={{0,6},{1,7},{2,4},{3,5},{4,2},{5,3},{6,0},{7,1},{8,14},{9,15},{10,... | collective-permute-start | bytes 208904 | tf_op jit(solution)/shard_map/ppermute | solution.py:35
  86.1 5.8 %collective-permute-start.24 = (f32[136,128]{1,0:T(8,128)S(1)}, f32[136,128]{1,0:T(8,128)S(1)}, u32[]{:S(2)}, u32[]{:S(2)}) collective-permute-start(f32[136,128]{1,0:T(8,128)S(1)} %select_maximum_fusion), channel_id=1, source_target_pairs={{0,2},{1,3},{2,0},{3,1},{4,6},{5,7},{6,4},{7,5},{8,10},{9,11},{10,... | collective-permute-start | bytes 208904 | tf_op jit(solution)/shard_map/ppermute | solution.py:35
  (7 other events, 19.5 us)

commit v9 on v7

--- a/solution.py
+++ b/solution.py
@@ -243,9 +243,15 @@
 
     def sum_over(axis, bits, one, two):
         for bit_one, bit_two in zip(bits, reversed(bits)):
-            from_one, from_two = lax.optimization_barrier(
-                (swap(one.astype(narrow), axis, bit_one), swap(two.astype(narrow), axis, bit_two))
-            )
+            sent = [(one.astype(narrow), bit_one), (two.astype(narrow), bit_two)]
+            if bit_two > bit_one:
+                from_two, from_one = lax.optimization_barrier(
+                    tuple(swap(value, axis, bit) for value, bit in reversed(sent))
+                )
+            else:
+                from_one, from_two = lax.optimization_barrier(
+                    tuple(swap(value, axis, bit) for value, bit in sent)
+                )
             one, two = one + from_one.astype(jnp.float32), two + from_two.astype(jnp.float32)
         return one, two
 

time: 97.5 us -> 97.7 us (level)
  starting transfers between devices: 28.1 us -> 34.2 us
  waiting for transfers between devices: 50.3 us -> 44.4 us
    ppermute x27, starting transfers between devices: 28.1 us -> 34.2 us  [swap(): return lax.ppermute(value, axis, [(i, i ^ distance) for i in range(count)])]
    ppermute x27, waiting for transfers between devices: 50.3 us -> 44.4 us  [swap(): return lax.ppermute(value, axis, [(i, i ^ distance) for i in range(count)])]
  transfers between devices with their start and end apart: 27 -> 27, of which waited for: 21 -> 21; matrix products, arithmetic and copies ran while one was open for 3% -> 2% of each run, Pallas kernels for 1% -> 1%
where the time goes in v9:
time: 97.7 us; the launch traced here: 97.5 us
  waiting for transfers between devices  44.4 us (45%)
  starting transfers between devices  34.2 us (35%)
  Pallas kernels  8.06 us (8%)
  matrix products  5.69 us (6%)
  other arithmetic  2.42 us (2%)
  local copies, waits for them, and re-layouts  2.29 us (2%)
    ppermute x27, waiting for transfers between devices, swap(): return lax.ppermute(value, axis, [(i, i ^ distance) for i in range(count)])  44.4 us
    ppermute x27, starting transfers between devices, swap(): return lax.ppermute(value, axis, [(i, i ^ distance) for i in range(count)])  34.2 us
    pallas_call x1, Pallas kernels, orthonormal(): pl.pallas_call(kernel, in_specs=[pl.BlockSpec(memory_space=pltpu.SMEM), v...  6.92 us
    unnamed x6, local copies, waits for them, and re-layouts  2.1 us
    dot_general x2, matrix products, exact_dot(): lax.dot_general(a, b, (dims, ((), ())), precision=lax.Precision.HIGHEST,...  2.02 us
  transfers between devices with their start and end apart: 27, of which 21 were waited for; matrix products, arithmetic and copies ran while one was open for 2% of the time, Pallas kernels for 1%

profile of v9, /device:TPU:0, one launch (start us, length us, event | category | flops | bytes accessed | tf_op | source)
XLA Modules:
  0.0 97.5 jit_solution(12840596470057668252)
XLA Ops:
  1.0 3.0 %collective-permute-start.3 = (bf16[128,256]{1,0:T(8,128)(2,1)S(1)}, bf16[128,256]{1,0:T(8,128)(2,1)S(1)}, u32[]{:S(2)}, u32[]{:S(2)}) collective-permute-start(bf16[128,256]{1,0:T(8,128)(2,1)S(1)} %convert_element_type.140), channel_id=1, source_target_pairs={{0,16},{8,24},{16,0},{24,8},{1,17},{9,25},{17,1},{25,9},{2,18},{10... | collective-permute-start | bytes 196616 | tf_op jit(solution)/shard_map/ppermute | solution.py:35
  12.2 3.1 %collective-permute-start.5 = (bf16[512,128]{1,0:T(8,128)(2,1)S(1)}, bf16[512,128]{1,0:T(8,128)(2,1)S(1)}, u32[]{:S(2)}, u32[]{:S(2)}) collective-permute-start(bf16[512,128]{1,0:T(8,128)(2,1)S(1)} %get-tuple-element.54), channel_id=1, source_target_pairs={{0,4},{1,5},{2,6},{3,7},{4,0},{5,1},{6,2},{7,3},{8,12},{9,13},{10,... | collective-permute-start | bytes 393224 | tf_op jit(solution)/shard_map/ppermute | solution.py:35
  15.3 1.6 %collective-permute-start.6 = (bf16[512,128]{1,0:T(8,128)(2,1)S(1)}, bf16[512,128]{1,0:T(8,128)(2,1)S(1)}, u32[]{:S(2)}, u32[]{:S(2)}) collective-permute-start(bf16[512,128]{1,0:T(8,128)(2,1)S(1)} %get-tuple-element.53), channel_id=1, source_target_pairs={{0,2},{1,3},{2,0},{3,1},{4,6},{5,7},{6,4},{7,5},{8,10},{9,11},{10,... | collective-permute-start | bytes 393224 | tf_op jit(solution)/shard_map/ppermute | solution.py:35
  17.0 5.0 %collective-permute-done.5 = bf16[512,128]{1,0:T(8,128)(2,1)S(1)} collective-permute-done((bf16[512,128]{1,0:T(8,128)(2,1)S(1)}, bf16[512,128]{1,0:T(8,128)(2,1)S(1)}, u32[]{:S(2)}, u32[]{:S(2)}) %collective-permute-start.5) | collective-permute-done | bytes 131104 | tf_op jit(solution)/shard_map/ppermute | solution.py:35
  23.7 2.4 %collective-permute-start.8 = (bf16[512,128]{1,0:T(8,128)(2,1)S(1)}, bf16[512,128]{1,0:T(8,128)(2,1)S(1)}, u32[]{:S(2)}, u32[]{:S(2)}) collective-permute-start(bf16[512,128]{1,0:T(8,128)(2,1)S(1)} %get-tuple-element.51), channel_id=1, source_target_pairs={{0,2},{1,3},{2,0},{3,1},{4,6},{5,7},{6,4},{7,5},{8,10},{9,11},{10,... | collective-permute-start | bytes 393224 | tf_op jit(solution)/shard_map/ppermute | solution.py:35
  26.4 4.5 %collective-permute-done.7 = bf16[512,128]{1,0:T(8,128)(2,1)S(1)} collective-permute-done((bf16[512,128]{1,0:T(8,128)(2,1)S(1)}, bf16[512,128]{1,0:T(8,128)(2,1)S(1)}, u32[]{:S(2)}, u32[]{:S(2)}) %collective-permute-start.7) | collective-permute-done | bytes 131104 | tf_op jit(solution)/shard_map/ppermute | solution.py:35
  32.1 1.6 %collective-permute-start.10 = (bf16[512,128]{1,0:T(8,128)(2,1)S(1)}, bf16[512,128]{1,0:T(8,128)(2,1)S(1)}, u32[]{:S(2)}, u32[]{:S(2)}) collective-permute-start(bf16[512,128]{1,0:T(8,128)(2,1)S(1)} %get-tuple-element.65), channel_id=1, source_target_pairs={{0,16},{8,24},{16,0},{24,8},{1,17},{9,25},{17,1},{25,9},{2,18},{10... | collective-permute-start | bytes 393224 | tf_op jit(solution)/shard_map/ppermute | solution.py:35
  33.7 1.5 %collective-permute-start.11 = (bf16[512,128]{1,0:T(8,128)(2,1)S(1)}, bf16[512,128]{1,0:T(8,128)(2,1)S(1)}, u32[]{:S(2)}, u32[]{:S(2)}) collective-permute-start(bf16[512,128]{1,0:T(8,128)(2,1)S(1)} %get-tuple-element.67), channel_id=1, source_target_pairs={{0,8},{8,0},{16,24},{24,16},{1,9},{9,1},{17,25},{25,17},{2,10},{10... | collective-permute-start | bytes 393224 | tf_op jit(solution)/shard_map/ppermute | solution.py:35
  35.2 1.9 %collective-permute-done.10 = bf16[512,128]{1,0:T(8,128)(2,1)S(1)} collective-permute-done((bf16[512,128]{1,0:T(8,128)(2,1)S(1)}, bf16[512,128]{1,0:T(8,128)(2,1)S(1)}, u32[]{:S(2)}, u32[]{:S(2)}) %collective-permute-start.10) | collective-permute-done | bytes 131104 | tf_op jit(solution)/shard_map/ppermute | solution.py:35
  37.2 1.5 %collective-permute-done.11 = bf16[512,128]{1,0:T(8,128)(2,1)S(1)} collective-permute-done((bf16[512,128]{1,0:T(8,128)(2,1)S(1)}, bf16[512,128]{1,0:T(8,128)(2,1)S(1)}, u32[]{:S(2)}, u32[]{:S(2)}) %collective-permute-start.11) | collective-permute-done | bytes 131104 | tf_op jit(solution)/shard_map/ppermute | solution.py:35
  39.3 1.6 %collective-permute-start.13 = (bf16[512,128]{1,0:T(8,128)(2,1)S(1)}, bf16[512,128]{1,0:T(8,128)(2,1)S(1)}, u32[]{:S(2)}, u32[]{:S(2)}) collective-permute-start(bf16[512,128]{1,0:T(8,128)(2,1)S(1)} %fusion.12), channel_id=1, source_target_pairs={{0,8},{8,0},{16,24},{24,16},{1,9},{9,1},{17,25},{25,17},{2,10},{10... | collective-permute-start | bytes 393224 | tf_op jit(solution)/shard_map/ppermute | solution.py:35
  40.9 2.9 %collective-permute-done.12 = bf16[512,128]{1,0:T(8,128)(2,1)S(1)} collective-permute-done((bf16[512,128]{1,0:T(8,128)(2,1)S(1)}, bf16[512,128]{1,0:T(8,128)(2,1)S(1)}, u32[]{:S(2)}, u32[]{:S(2)}) %collective-permute-start.12) | collective-permute-done | bytes 131104 | tf_op jit(solution)/shard_map/ppermute | solution.py:35
  45.4 1.8 %collective-permute-start.14 = (bf16[512,128]{1,0:T(8,128)(2,1)S(1)}, bf16[512,128]{1,0:T(8,128)(2,1)S(1)}, u32[]{:S(2)}, u32[]{:S(2)}) collective-permute-start(bf16[512,128]{1,0:T(8,128)(2,1)S(1)} %get-tuple-element.48), channel_id=1, source_target_pairs={{0,4},{1,5},{2,6},{3,7},{4,0},{5,1},{6,2},{7,3},{8,12},{9,13},{10,... | collective-permute-start | bytes 393224 | tf_op jit(solution)/shard_map/ppermute | solution.py:35
  47.2 1.8 %collective-permute-start.15 = (bf16[512,128]{1,0:T(8,128)(2,1)S(1)}, bf16[512,128]{1,0:T(8,128)(2,1)S(1)}, u32[]{:S(2)}, u32[]{:S(2)}) collective-permute-start(bf16[512,128]{1,0:T(8,128)(2,1)S(1)} %get-tuple-element.47), channel_id=1, source_target_pairs={{0,2},{1,3},{2,0},{3,1},{4,6},{5,7},{6,4},{7,5},{8,10},{9,11},{10,... | collective-permute-start | bytes 393224 | tf_op jit(solution)/shard_map/ppermute | solution.py:35
  49.0 6.6 %collective-permute-done.14 = bf16[512,128]{1,0:T(8,128)(2,1)S(1)} collective-permute-done((bf16[512,128]{1,0:T(8,128)(2,1)S(1)}, bf16[512,128]{1,0:T(8,128)(2,1)S(1)}, u32[]{:S(2)}, u32[]{:S(2)}) %collective-permute-start.14) | collective-permute-done | bytes 131104 | tf_op jit(solution)/shard_map/ppermute | solution.py:35
  55.8 3.2 %collective-permute-start.17 = (bf16[512,128]{1,0:T(8,128)(2,1)S(1)}, bf16[512,128]{1,0:T(8,128)(2,1)S(1)}, u32[]{:S(2)}, u32[]{:S(2)}) collective-permute-start(bf16[512,128]{1,0:T(8,128)(2,1)S(1)} %get-tuple-element.45), channel_id=1, source_target_pairs={{0,2},{1,3},{2,0},{3,1},{4,6},{5,7},{6,4},{7,5},{8,10},{9,11},{10,... | collective-permute-start | bytes 393224 | tf_op jit(solution)/shard_map/ppermute | solution.py:35
  58.9 3.9 %collective-permute-done.16 = bf16[512,128]{1,0:T(8,128)(2,1)S(1)} collective-permute-done((bf16[512,128]{1,0:T(8,128)(2,1)S(1)}, bf16[512,128]{1,0:T(8,128)(2,1)S(1)}, u32[]{:S(2)}, u32[]{:S(2)}) %collective-permute-start.16) | collective-permute-done | bytes 131104 | tf_op jit(solution)/shard_map/ppermute | solution.py:35
  65.8 1.5 %collective-permute-start.19 = (bf16[512,128]{1,0:T(8,128)(2,1)S(1)}, bf16[512,128]{1,0:T(8,128)(2,1)S(1)}, u32[]{:S(2)}, u32[]{:S(2)}) collective-permute-start(bf16[512,128]{1,0:T(8,128)(2,1)S(1)} %get-tuple-element.71), channel_id=1, source_target_pairs={{0,8},{8,0},{16,24},{24,16},{1,9},{9,1},{17,25},{25,17},{2,10},{10... | collective-permute-start | bytes 393224 | tf_op jit(solution)/shard_map/ppermute | solution.py:35
  67.3 2.2 %collective-permute-done.18 = bf16[512,128]{1,0:T(8,128)(2,1)S(1)} collective-permute-done((bf16[512,128]{1,0:T(8,128)(2,1)S(1)}, bf16[512,128]{1,0:T(8,128)(2,1)S(1)}, u32[]{:S(2)}, u32[]{:S(2)}) %collective-permute-start.18) | collective-permute-done | bytes 131104 | tf_op jit(solution)/shard_map/ppermute | solution.py:35
  71.7 1.5 %collective-permute-start.21 = (bf16[512,128]{1,0:T(8,128)(2,1)S(1)}, bf16[512,128]{1,0:T(8,128)(2,1)S(1)}, u32[]{:S(2)}, u32[]{:S(2)}) collective-permute-start(bf16[512,128]{1,0:T(8,128)(2,1)S(1)} %fusion.13), channel_id=1, source_target_pairs={{0,8},{8,0},{16,24},{24,16},{1,9},{9,1},{17,25},{25,17},{2,10},{10... | collective-permute-start | bytes 393224 | tf_op jit(solution)/shard_map/ppermute | solution.py:35
  73.2 2.6 %collective-permute-done.20 = bf16[512,128]{1,0:T(8,128)(2,1)S(1)} collective-permute-done((bf16[512,128]{1,0:T(8,128)(2,1)S(1)}, bf16[512,128]{1,0:T(8,128)(2,1)S(1)}, u32[]{:S(2)}, u32[]{:S(2)}) %collective-permute-start.20) | collective-permute-done | bytes 131104 | tf_op jit(solution)/shard_map/ppermute | solution.py:35
  80.4 2.6 %collective-permute-start.24 = (f32[136,128]{1,0:T(8,128)S(1)}, f32[136,128]{1,0:T(8,128)S(1)}, u32[]{:S(2)}, u32[]{:S(2)}) collective-permute-start(f32[136,128]{1,0:T(8,128)S(1)} %select_maximum_fusion), channel_id=1, source_target_pairs={{0,6},{1,7},{2,4},{3,5},{4,2},{5,3},{6,0},{7,1},{8,14},{9,15},{10,... | collective-permute-start | bytes 208904 | tf_op jit(solution)/shard_map/ppermute | solution.py:35
  83.6 4.8 %collective-permute-done.25 = f32[136,128]{1,0:T(8,128)S(1)} collective-permute-done((f32[136,128]{1,0:T(8,128)S(1)}, f32[136,128]{1,0:T(8,128)S(1)}, u32[]{:S(2)}, u32[]{:S(2)}) %collective-permute-start.25) | collective-permute-done | bytes 69664 | tf_op jit(solution)/shard_map/ppermute | solution.py:35
  90.6 6.9 %shard_map.38 = f32[128,256]{1,0:T(8,128)} custom-call(s32[1]{0:T(128)} %bitcast.first_ref, f32[136,128]{1,0:T(8,128)S(1)} %add_add_fusion.total_ref, f32[136,128]{1,0:T(8,128)S(1)} %collective-permute-done.26.partner_ref, f32[128,128]{1,0:T(8,128)S(1)} %fusion.23.mine_ref, f32[128,128]{1,0:T(8,128)S(1)} %constant_dynamic-slice_fusion.theirs_ref), custom_call_target="tpu_custom_call" | custom-call | tf_op jit(solution)/shard_map/pallas_call | solution.py:171
  (83 shorter events, 27.0 us)
Async XLA Ops:
  1.0 8.0 %collective-permute-start.3 = (bf16[128,256]{1,0:T(8,128)(2,1)S(1)}, bf16[128,256]{1,0:T(8,128)(2,1)S(1)}, u32[]{:S(2)}, u32[]{:S(2)}) collective-permute-start(bf16[128,256]{1,0:T(8,128)(2,1)S(1)} %convert_element_type.140), channel_id=1, source_target_pairs={{0,16},{8,24},{16,0},{24,8},{1,17},{9,25},{17,1},{25,9},{2,18},{10... | collective-permute-start | bytes 196616 | tf_op jit(solution)/shard_map/ppermute | solution.py:35
  4.0 5.7 %collective-permute-start.2 = (bf16[128,256]{1,0:T(8,128)(2,1)S(1)}, bf16[128,256]{1,0:T(8,128)(2,1)S(1)}, u32[]{:S(2)}, u32[]{:S(2)}) collective-permute-start(bf16[128,256]{1,0:T(8,128)(2,1)S(1)} %convert_element_type.140), channel_id=1, source_target_pairs={{0,24},{8,16},{16,8},{24,0},{1,25},{9,17},{17,9},{25,1},{2,26},{10... | collective-permute-start | bytes 196616 | tf_op jit(solution)/shard_map/ppermute | solution.py:35
  5.4 4.3 %collective-permute-start.1 = (bf16[128,256]{1,0:T(8,128)(2,1)S(1)}, bf16[128,256]{1,0:T(8,128)(2,1)S(1)}, u32[]{:S(2)}, u32[]{:S(2)}) collective-permute-start(bf16[128,256]{1,0:T(8,128)(2,1)S(1)} %convert_element_type.140), channel_id=1, source_target_pairs={{0,8},{8,0},{16,24},{24,16},{1,9},{9,1},{17,25},{25,17},{2,10},{10... | collective-permute-start | bytes 196616 | tf_op jit(solution)/shard_map/ppermute | solution.py:35
  8.8 3.0 %collective-permute-start = (bf16[1024,512]{1,0:T(8,128)(2,1)S(1)}, bf16[1024,512]{1,0:T(8,128)(2,1)S(1)}, u32[]{:S(2)}, u32[]{:S(2)}) collective-permute-start(bf16[1024,512]{1,0:T(8,128)(2,1)S(1)} %shard_map.37), channel_id=1, source_target_pairs={{0,1},{1,0},{2,3},{3,2},{4,5},{5,4},{6,7},{7,6},{8,9},{9,8},{10,11... | collective-permute-start | bytes 3145736 | tf_op jit(solution)/shard_map/ppermute | solution.py:35
  12.2 9.8 %collective-permute-start.5 = (bf16[512,128]{1,0:T(8,128)(2,1)S(1)}, bf16[512,128]{1,0:T(8,128)(2,1)S(1)}, u32[]{:S(2)}, u32[]{:S(2)}) collective-permute-start(bf16[512,128]{1,0:T(8,128)(2,1)S(1)} %get-tuple-element.54), channel_id=1, source_target_pairs={{0,4},{1,5},{2,6},{3,7},{4,0},{5,1},{6,2},{7,3},{8,12},{9,13},{10,... | collective-permute-start | bytes 393224 | tf_op jit(solution)/shard_map/ppermute | solution.py:35
  15.3 6.9 %collective-permute-start.6 = (bf16[512,128]{1,0:T(8,128)(2,1)S(1)}, bf16[512,128]{1,0:T(8,128)(2,1)S(1)}, u32[]{:S(2)}, u32[]{:S(2)}) collective-permute-start(bf16[512,128]{1,0:T(8,128)(2,1)S(1)} %get-tuple-element.53), channel_id=1, source_target_pairs={{0,2},{1,3},{2,0},{3,1},{4,6},{5,7},{6,4},{7,5},{8,10},{9,11},{10,... | collective-permute-start | bytes 393224 | tf_op jit(solution)/shard_map/ppermute | solution.py:35
  16.9 9.3 %collective-permute-start.9 = (f32[128,128]{1,0:T(8,128)S(1)}, f32[128,128]{1,0:T(8,128)S(1)}, u32[]{:S(2)}, u32[]{:S(2)}) collective-permute-start(f32[128,128]{1,0:T(8,128)S(1)} %get-tuple-element.59), channel_id=1, source_target_pairs={{0,1},{1,0},{2,3},{3,2},{4,5},{5,4},{6,7},{7,6},{8,9},{9,8},{10,11... | collective-permute-start | bytes 196616 | tf_op jit(solution)/shard_map/ppermute | solution.py:35
  22.3 8.6 %collective-permute-start.7 = (bf16[512,128]{1,0:T(8,128)(2,1)S(1)}, bf16[512,128]{1,0:T(8,128)(2,1)S(1)}, u32[]{:S(2)}, u32[]{:S(2)}) collective-permute-start(bf16[512,128]{1,0:T(8,128)(2,1)S(1)} %get-tuple-element.52), channel_id=1, source_target_pairs={{0,4},{1,5},{2,6},{3,7},{4,0},{5,1},{6,2},{7,3},{8,12},{9,13},{10,... | collective-permute-start | bytes 393224 | tf_op jit(solution)/shard_map/ppermute | solution.py:35
  23.7 7.3 %collective-permute-start.8 = (bf16[512,128]{1,0:T(8,128)(2,1)S(1)}, bf16[512,128]{1,0:T(8,128)(2,1)S(1)}, u32[]{:S(2)}, u32[]{:S(2)}) collective-permute-start(bf16[512,128]{1,0:T(8,128)(2,1)S(1)} %get-tuple-element.51), channel_id=1, source_target_pairs={{0,2},{1,3},{2,0},{3,1},{4,6},{5,7},{6,4},{7,5},{8,10},{9,11},{10,... | collective-permute-start | bytes 393224 | tf_op jit(solution)/shard_map/ppermute | solution.py:35
  32.1 5.0 %collective-permute-start.10 = (bf16[512,128]{1,0:T(8,128)(2,1)S(1)}, bf16[512,128]{1,0:T(8,128)(2,1)S(1)}, u32[]{:S(2)}, u32[]{:S(2)}) collective-permute-start(bf16[512,128]{1,0:T(8,128)(2,1)S(1)} %get-tuple-element.65), channel_id=1, source_target_pairs={{0,16},{8,24},{16,0},{24,8},{1,17},{9,25},{17,1},{25,9},{2,18},{10... | collective-permute-start | bytes 393224 | tf_op jit(solution)/shard_map/ppermute | solution.py:35
  33.7 5.0 %collective-permute-start.11 = (bf16[512,128]{1,0:T(8,128)(2,1)S(1)}, bf16[512,128]{1,0:T(8,128)(2,1)S(1)}, u32[]{:S(2)}, u32[]{:S(2)}) collective-permute-start(bf16[512,128]{1,0:T(8,128)(2,1)S(1)} %get-tuple-element.67), channel_id=1, source_target_pairs={{0,8},{8,0},{16,24},{24,16},{1,9},{9,1},{17,25},{25,17},{2,10},{10... | collective-permute-start | bytes 393224 | tf_op jit(solution)/shard_map/ppermute | solution.py:35
  38.7 5.0 %collective-permute-start.12 = (bf16[512,128]{1,0:T(8,128)(2,1)S(1)}, bf16[512,128]{1,0:T(8,128)(2,1)S(1)}, u32[]{:S(2)}, u32[]{:S(2)}) collective-permute-start(bf16[512,128]{1,0:T(8,128)(2,1)S(1)} %fusion.11), channel_id=1, source_target_pairs={{0,16},{8,24},{16,0},{24,8},{1,17},{9,25},{17,1},{25,9},{2,18},{10... | collective-permute-start | bytes 393224 | tf_op jit(solution)/shard_map/ppermute | solution.py:35
  39.3 5.0 %collective-permute-start.13 = (bf16[512,128]{1,0:T(8,128)(2,1)S(1)}, bf16[512,128]{1,0:T(8,128)(2,1)S(1)}, u32[]{:S(2)}, u32[]{:S(2)}) collective-permute-start(bf16[512,128]{1,0:T(8,128)(2,1)S(1)} %fusion.12), channel_id=1, source_target_pairs={{0,8},{8,0},{16,24},{24,16},{1,9},{9,1},{17,25},{25,17},{2,10},{10... | collective-permute-start | bytes 393224 | tf_op jit(solution)/shard_map/ppermute | solution.py:35
  45.4 10.2 %collective-permute-start.14 = (bf16[512,128]{1,0:T(8,128)(2,1)S(1)}, bf16[512,128]{1,0:T(8,128)(2,1)S(1)}, u32[]{:S(2)}, u32[]{:S(2)}) collective-permute-start(bf16[512,128]{1,0:T(8,128)(2,1)S(1)} %get-tuple-element.48), channel_id=1, source_target_pairs={{0,4},{1,5},{2,6},{3,7},{4,0},{5,1},{6,2},{7,3},{8,12},{9,13},{10,... | collective-permute-start | bytes 393224 | tf_op jit(solution)/shard_map/ppermute | solution.py:35
  47.2 8.4 %collective-permute-start.15 = (bf16[512,128]{1,0:T(8,128)(2,1)S(1)}, bf16[512,128]{1,0:T(8,128)(2,1)S(1)}, u32[]{:S(2)}, u32[]{:S(2)}) collective-permute-start(bf16[512,128]{1,0:T(8,128)(2,1)S(1)} %get-tuple-element.47), channel_id=1, source_target_pairs={{0,2},{1,3},{2,0},{3,1},{4,6},{5,7},{6,4},{7,5},{8,10},{9,11},{10,... | collective-permute-start | bytes 393224 | tf_op jit(solution)/shard_map/ppermute | solution.py:35
  55.7 7.1 %collective-permute-start.16 = (bf16[512,128]{1,0:T(8,128)(2,1)S(1)}, bf16[512,128]{1,0:T(8,128)(2,1)S(1)}, u32[]{:S(2)}, u32[]{:S(2)}) collective-permute-start(bf16[512,128]{1,0:T(8,128)(2,1)S(1)} %get-tuple-element.46), channel_id=1, source_target_pairs={{0,4},{1,5},{2,6},{3,7},{4,0},{5,1},{6,2},{7,3},{8,12},{9,13},{10,... | collective-permute-start | bytes 393224 | tf_op jit(solution)/shard_map/ppermute | solution.py:35
  55.8 7.5 %collective-permute-start.17 = (bf16[512,128]{1,0:T(8,128)(2,1)S(1)}, bf16[512,128]{1,0:T(8,128)(2,1)S(1)}, u32[]{:S(2)}, u32[]{:S(2)}) collective-permute-start(bf16[512,128]{1,0:T(8,128)(2,1)S(1)} %get-tuple-element.45), channel_id=1, source_target_pairs={{0,2},{1,3},{2,0},{3,1},{4,6},{5,7},{6,4},{7,5},{8,10},{9,11},{10,... | collective-permute-start | bytes 393224 | tf_op jit(solution)/shard_map/ppermute | solution.py:35
  64.5 5.0 %collective-permute-start.18 = (bf16[512,128]{1,0:T(8,128)(2,1)S(1)}, bf16[512,128]{1,0:T(8,128)(2,1)S(1)}, u32[]{:S(2)}, u32[]{:S(2)}) collective-permute-start(bf16[512,128]{1,0:T(8,128)(2,1)S(1)} %get-tuple-element.69), channel_id=1, source_target_pairs={{0,16},{8,24},{16,0},{24,8},{1,17},{9,25},{17,1},{25,9},{2,18},{10... | collective-permute-start | bytes 393224 | tf_op jit(solution)/shard_map/ppermute | solution.py:35
  65.8 5.0 %collective-permute-start.19 = (bf16[512,128]{1,0:T(8,128)(2,1)S(1)}, bf16[512,128]{1,0:T(8,128)(2,1)S(1)}, u32[]{:S(2)}, u32[]{:S(2)}) collective-permute-start(bf16[512,128]{1,0:T(8,128)(2,1)S(1)} %get-tuple-element.71), channel_id=1, source_target_pairs={{0,8},{8,0},{16,24},{24,16},{1,9},{9,1},{17,25},{25,17},{2,10},{10... | collective-permute-start | bytes 393224 | tf_op jit(solution)/shard_map/ppermute | solution.py:35
  70.8 5.0 %collective-permute-start.20 = (bf16[512,128]{1,0:T(8,128)(2,1)S(1)}, bf16[512,128]{1,0:T(8,128)(2,1)S(1)}, u32[]{:S(2)}, u32[]{:S(2)}) collective-permute-start(bf16[512,128]{1,0:T(8,128)(2,1)S(1)} %fusion.14), channel_id=1, source_target_pairs={{0,16},{8,24},{16,0},{24,8},{1,17},{9,25},{17,1},{25,9},{2,18},{10... | collective-permute-start | bytes 393224 | tf_op jit(solution)/shard_map/ppermute | solution.py:35
  71.7 5.0 %collective-permute-start.21 = (bf16[512,128]{1,0:T(8,128)(2,1)S(1)}, bf16[512,128]{1,0:T(8,128)(2,1)S(1)}, u32[]{:S(2)}, u32[]{:S(2)}) collective-permute-start(bf16[512,128]{1,0:T(8,128)(2,1)S(1)} %fusion.13), channel_id=1, source_target_pairs={{0,8},{8,0},{16,24},{24,16},{1,9},{9,1},{17,25},{25,17},{2,10},{10... | collective-permute-start | bytes 393224 | tf_op jit(solution)/shard_map/ppermute | solution.py:35
  80.0 8.4 %collective-permute-start.25 = (f32[136,128]{1,0:T(8,128)S(1)}, f32[136,128]{1,0:T(8,128)S(1)}, u32[]{:S(2)}, u32[]{:S(2)}) collective-permute-start(f32[136,128]{1,0:T(8,128)S(1)} %select_maximum_fusion), channel_id=1, source_target_pairs={{0,4},{1,5},{2,6},{3,7},{4,0},{5,1},{6,2},{7,3},{8,12},{9,13},{10,... | collective-permute-start | bytes 208904 | tf_op jit(solution)/shard_map/ppermute | solution.py:35
  80.4 7.9 %collective-permute-start.24 = (f32[136,128]{1,0:T(8,128)S(1)}, f32[136,128]{1,0:T(8,128)S(1)}, u32[]{:S(2)}, u32[]{:S(2)}) collective-permute-start(f32[136,128]{1,0:T(8,128)S(1)} %select_maximum_fusion), channel_id=1, source_target_pairs={{0,6},{1,7},{2,4},{3,5},{4,2},{5,3},{6,0},{7,1},{8,14},{9,15},{10,... | collective-permute-start | bytes 208904 | tf_op jit(solution)/shard_map/ppermute | solution.py:35
  83.0 6.2 %collective-permute-start.23 = (f32[136,128]{1,0:T(8,128)S(1)}, f32[136,128]{1,0:T(8,128)S(1)}, u32[]{:S(2)}, u32[]{:S(2)}) collective-permute-start(f32[136,128]{1,0:T(8,128)S(1)} %select_maximum_fusion), channel_id=1, source_target_pairs={{0,2},{1,3},{2,0},{3,1},{4,6},{5,7},{6,4},{7,5},{8,10},{9,11},{10,... | collective-permute-start | bytes 208904 | tf_op jit(solution)/shard_map/ppermute | solution.py:35
  (6 other events, 16.1 us)

commit v10 on v9

--- a/solution.py
+++ b/solution.py
@@ -202,13 +202,11 @@
 
     low_start = vectors.astype(narrow)
     arrived = {0: low_start, **{k: swap(low_start, "row", k) for k in partners(row_count)}}
-    low_own, sent = kept_and_sent(in_order(arrived, row_rank))
-    low_other = swap(sent, "col", 1)
+    low_group = in_order(arrived, row_rank)
     own_start, sent = kept_and_sent(vectors)
     other_start = swap(sent, "col", 1)
 
     own = densify(blocks, col_index, tile_blocks)
-    other = swap(own, "col", 1)
 
     first_row = row_rank * group_rows
     own_offset = first_row - col_rank * tile_blocks
@@ -223,18 +221,19 @@
         )
 
     def picked(low, offset):
-        value = low.astype(jnp.float32).reshape(segments, tile_rows, half)
+        value = low.astype(jnp.float32).reshape(segments, tile_rows, low.shape[1])
         parts = [jnp.where(offset == -k * tile_blocks, value[k], 0.0) for k in range(segments)]
         return sum(parts[1:], parts[0])
 
-    def forward(low_own, low_other):
-        product = jnp.dot(own, low_own, preferred_element_type=jnp.float32)
-        product = product + jnp.dot(other, low_other, preferred_element_type=jnp.float32)
-        product = product - center * (spread(low_own, own_offset) + spread(low_other, other_offset))
-        middle = product.shape[0] // 2
-        return product[:middle], product[middle:]
-
-    def backward(low):
+    def halves(value):
+        middle = value.shape[0] // 2
+        return value[:middle], value[middle:]
+
+    def part_of(tile, low, offset):
+        product = jnp.dot(tile, low, preferred_element_type=jnp.float32)
+        return product - center * spread(low, offset)
+
+    def backward(low, own, other):
         def part(tile, offset):
             product = lax.dot_general(tile, low, (((0,), (0,)), ((), ())), preferred_element_type=jnp.float32)
             return product - center * picked(low, offset)
@@ -259,10 +258,14 @@
         here = jnp.arange(row_count)[:, None, None] == row_rank
         return jnp.where(here, piece[None], 0.0).reshape(tile_rows, half)
 
-    y1_one, y1_two = [
-        scales[0] * image for image in sum_over("col", z_bits, *forward(low_own, low_other))
-    ]
-    part_own, part_other = backward(jnp.concatenate([y1_one.astype(narrow), y1_two.astype(narrow)]))
+    kept, sent = kept_and_sent(part_of(own, low_group, own_offset))
+    image = kept + swap(sent.astype(narrow), "col", 1).astype(jnp.float32)
+    y1_one, y1_two = [scales[0] * image for image in sum_over("col", z_bits, *halves(image))]
+    own, _ = lax.optimization_barrier((own, image))
+    other = swap(own, "col", 1)
+    part_own, part_other = backward(
+        jnp.concatenate([y1_one.astype(narrow), y1_two.astype(narrow)]), own, other
+    )
     y2_own, y2_other = sum_over(
         "row",
         row_bits,
@@ -270,17 +273,22 @@
         scales[1] * part_other - carries[1] * placed(other_start),
     )
     image_one, image_two = sum_over(
-        "col", z_bits, *forward(y2_own.astype(narrow), y2_other.astype(narrow))
+        "col",
+        z_bits,
+        *halves(
+            part_of(own, y2_own.astype(narrow), own_offset)
+            + part_of(other, y2_other.astype(narrow), other_offset)
+        ),
     )
     low_one = (scales[2] * image_one - carries[2] * y1_one).astype(narrow)
     low_two = (scales[2] * image_two - carries[2] * y1_two).astype(narrow)
-    part_own, part_other = backward(jnp.concatenate([low_one, low_two]))
+    part_own, part_other = backward(jnp.concatenate([low_one, low_two]), own, other)
     image_own, image_other = sum_over("row", row_bits, part_own, part_other)
     y4_own = scales[3] * image_own - carries[3] * y2_own
     y4_other = scales[3] * image_other - carries[3] * y2_other
 
     mine = jnp.concatenate([y4_own, y4_other])
-    theirs = swap(jnp.concatenate([y4_other, y4_own]), "col", 1)
+    theirs = swap(jnp.concatenate([y4_other, y4_own]).astype(narrow), "col", 1).astype(jnp.float32)
     corner = exact_dot(mine, mine, ((0,), (0,)))
     cross = exact_dot(theirs, jnp.where(mine_first, mine, theirs), ((0,), (0,)))
     rows = lax.broadcasted_iota(jnp.int32, (half, half), 0)

time: 97.7 us -> 98.4 us (level)
  other arithmetic: 2.42 us -> 3.95 us
  matrix products: 5.69 us -> 4.7 us
  transfers between devices with their start and end apart: 27 -> 27, of which waited for: 21 -> 22; matrix products, arithmetic and copies ran while one was open for 2% -> 4% of each run, Pallas kernels for 1% -> 1%
where the time goes in v10:
time: 98.4 us; the launch traced here: 98.2 us
  waiting for transfers between devices  44.7 us (45%)
  starting transfers between devices  34.2 us (35%)
  Pallas kernels  8.06 us (8%)
  matrix products  4.7 us (5%)
  other arithmetic  3.95 us (4%)
  local copies, waits for them, and re-layouts  2.29 us (2%)
    ppermute x27, waiting for transfers between devices, swap(): return lax.ppermute(value, axis, [(i, i ^ distance) for i in range(count)])  44.7 us
    ppermute x27, starting transfers between devices, swap(): return lax.ppermute(value, axis, [(i, i ^ distance) for i in range(count)])  34.2 us
    pallas_call x1, Pallas kernels, orthonormal(): pl.pallas_call(kernel, in_specs=[pl.BlockSpec(memory_space=pltpu.SMEM), v...  6.92 us
    unnamed x6, local copies, waits for them, and re-layouts  2.09 us
  transfers between devices with their start and end apart: 27, of which 22 were waited for; matrix products, arithmetic and copies ran while one was open for 4% of the time, Pallas kernels for 1%

profile of v10, /device:TPU:0, one launch (start us, length us, event | category | flops | bytes accessed | tf_op | source)
XLA Modules:
  0.0 98.2 jit_solution(16499769420288250721)
XLA Ops:
  0.9 3.0 %collective-permute-start = (bf16[128,256]{1,0:T(8,128)(2,1)S(1)}, bf16[128,256]{1,0:T(8,128)(2,1)S(1)}, u32[]{:S(2)}, u32[]{:S(2)}) collective-permute-start(bf16[128,256]{1,0:T(8,128)(2,1)S(1)} %convert_element_type.147), channel_id=1, source_target_pairs={{0,8},{8,0},{16,24},{24,16},{1,9},{9,1},{17,25},{25,17},{2,10},{10... | collective-permute-start | bytes 196616 | tf_op jit(solution)/shard_map/ppermute | solution.py:35
  10.7 1.5 %collective-permute-done.3 = bf16[1024,128]{1,0:T(8,128)(2,1)S(1)} collective-permute-done((bf16[1024,128]{1,0:T(8,128)(2,1)S(1)}, bf16[1024,128]{1,0:T(8,128)(2,1)S(1)}, u32[]{:S(2)}, u32[]{:S(2)}) %collective-permute-start.3) | collective-permute-done | bytes 262176 | tf_op jit(solution)/shard_map/ppermute | solution.py:35
  12.3 2.8 %collective-permute-start.5 = (bf16[512,128]{1,0:T(8,128)(2,1)S(1)}, bf16[512,128]{1,0:T(8,128)(2,1)S(1)}, u32[]{:S(2)}, u32[]{:S(2)}) collective-permute-start(bf16[512,128]{1,0:T(8,128)(2,1)S(1)} %get-tuple-element.58), channel_id=1, source_target_pairs={{0,4},{1,5},{2,6},{3,7},{4,0},{5,1},{6,2},{7,3},{8,12},{9,13},{10,... | collective-permute-start | bytes 393224 | tf_op jit(solution)/shard_map/ppermute | solution.py:35
  15.1 1.6 %collective-permute-start.6 = (bf16[512,128]{1,0:T(8,128)(2,1)S(1)}, bf16[512,128]{1,0:T(8,128)(2,1)S(1)}, u32[]{:S(2)}, u32[]{:S(2)}) collective-permute-start(bf16[512,128]{1,0:T(8,128)(2,1)S(1)} %get-tuple-element.57), channel_id=1, source_target_pairs={{0,2},{1,3},{2,0},{3,1},{4,6},{5,7},{6,4},{7,5},{8,10},{9,11},{10,... | collective-permute-start | bytes 393224 | tf_op jit(solution)/shard_map/ppermute | solution.py:35
  17.9 4.0 %collective-permute-done.5 = bf16[512,128]{1,0:T(8,128)(2,1)S(1)} collective-permute-done((bf16[512,128]{1,0:T(8,128)(2,1)S(1)}, bf16[512,128]{1,0:T(8,128)(2,1)S(1)}, u32[]{:S(2)}, u32[]{:S(2)}) %collective-permute-start.5) | collective-permute-done | bytes 131104 | tf_op jit(solution)/shard_map/ppermute | solution.py:35
  23.5 2.4 %collective-permute-start.8 = (bf16[512,128]{1,0:T(8,128)(2,1)S(1)}, bf16[512,128]{1,0:T(8,128)(2,1)S(1)}, u32[]{:S(2)}, u32[]{:S(2)}) collective-permute-start(bf16[512,128]{1,0:T(8,128)(2,1)S(1)} %get-tuple-element.55), channel_id=1, source_target_pairs={{0,2},{1,3},{2,0},{3,1},{4,6},{5,7},{6,4},{7,5},{8,10},{9,11},{10,... | collective-permute-start | bytes 393224 | tf_op jit(solution)/shard_map/ppermute | solution.py:35
  26.2 4.4 %collective-permute-done.7 = bf16[512,128]{1,0:T(8,128)(2,1)S(1)} collective-permute-done((bf16[512,128]{1,0:T(8,128)(2,1)S(1)}, bf16[512,128]{1,0:T(8,128)(2,1)S(1)}, u32[]{:S(2)}, u32[]{:S(2)}) %collective-permute-start.7) | collective-permute-done | bytes 131104 | tf_op jit(solution)/shard_map/ppermute | solution.py:35
  31.4 1.6 %collective-permute-start.11 = (bf16[512,128]{1,0:T(8,128)(2,1)S(1)}, bf16[512,128]{1,0:T(8,128)(2,1)S(1)}, u32[]{:S(2)}, u32[]{:S(2)}) collective-permute-start(bf16[512,128]{1,0:T(8,128)(2,1)S(1)} %get-tuple-element.71), channel_id=1, source_target_pairs={{0,8},{8,0},{16,24},{24,16},{1,9},{9,1},{17,25},{25,17},{2,10},{10... | collective-permute-start | bytes 393224 | tf_op jit(solution)/shard_map/ppermute | solution.py:35
  33.5 1.6 %collective-permute-start.10 = (bf16[512,128]{1,0:T(8,128)(2,1)S(1)}, bf16[512,128]{1,0:T(8,128)(2,1)S(1)}, u32[]{:S(2)}, u32[]{:S(2)}) collective-permute-start(bf16[512,128]{1,0:T(8,128)(2,1)S(1)} %get-tuple-element.69), channel_id=1, source_target_pairs={{0,16},{8,24},{16,0},{24,8},{1,17},{9,25},{17,1},{25,9},{2,18},{10... | collective-permute-start | bytes 393224 | tf_op jit(solution)/shard_map/ppermute | solution.py:35
  36.5 2.0 %collective-permute-done.10 = bf16[512,128]{1,0:T(8,128)(2,1)S(1)} collective-permute-done((bf16[512,128]{1,0:T(8,128)(2,1)S(1)}, bf16[512,128]{1,0:T(8,128)(2,1)S(1)}, u32[]{:S(2)}, u32[]{:S(2)}) %collective-permute-start.10) | collective-permute-done | bytes 131104 | tf_op jit(solution)/shard_map/ppermute | solution.py:35
  39.2 1.6 %collective-permute-start.12 = (bf16[512,128]{1,0:T(8,128)(2,1)S(1)}, bf16[512,128]{1,0:T(8,128)(2,1)S(1)}, u32[]{:S(2)}, u32[]{:S(2)}) collective-permute-start(bf16[512,128]{1,0:T(8,128)(2,1)S(1)} %fusion.10), channel_id=1, source_target_pairs={{0,16},{8,24},{16,0},{24,8},{1,17},{9,25},{17,1},{25,9},{2,18},{10... | collective-permute-start | bytes 393224 | tf_op jit(solution)/shard_map/ppermute | solution.py:35
  40.8 2.8 %collective-permute-done.13 = bf16[512,128]{1,0:T(8,128)(2,1)S(1)} collective-permute-done((bf16[512,128]{1,0:T(8,128)(2,1)S(1)}, bf16[512,128]{1,0:T(8,128)(2,1)S(1)}, u32[]{:S(2)}, u32[]{:S(2)}) %collective-permute-start.13) | collective-permute-done | bytes 131104 | tf_op jit(solution)/shard_map/ppermute | solution.py:35
  45.3 1.8 %collective-permute-start.14 = (bf16[512,128]{1,0:T(8,128)(2,1)S(1)}, bf16[512,128]{1,0:T(8,128)(2,1)S(1)}, u32[]{:S(2)}, u32[]{:S(2)}) collective-permute-start(bf16[512,128]{1,0:T(8,128)(2,1)S(1)} %get-tuple-element.52), channel_id=1, source_target_pairs={{0,4},{1,5},{2,6},{3,7},{4,0},{5,1},{6,2},{7,3},{8,12},{9,13},{10,... | collective-permute-start | bytes 393224 | tf_op jit(solution)/shard_map/ppermute | solution.py:35
  47.0 1.8 %collective-permute-start.15 = (bf16[512,128]{1,0:T(8,128)(2,1)S(1)}, bf16[512,128]{1,0:T(8,128)(2,1)S(1)}, u32[]{:S(2)}, u32[]{:S(2)}) collective-permute-start(bf16[512,128]{1,0:T(8,128)(2,1)S(1)} %get-tuple-element.51), channel_id=1, source_target_pairs={{0,2},{1,3},{2,0},{3,1},{4,6},{5,7},{6,4},{7,5},{8,10},{9,11},{10,... | collective-permute-start | bytes 393224 | tf_op jit(solution)/shard_map/ppermute | solution.py:35
  48.9 6.6 %collective-permute-done.14 = bf16[512,128]{1,0:T(8,128)(2,1)S(1)} collective-permute-done((bf16[512,128]{1,0:T(8,128)(2,1)S(1)}, bf16[512,128]{1,0:T(8,128)(2,1)S(1)}, u32[]{:S(2)}, u32[]{:S(2)}) %collective-permute-start.14) | collective-permute-done | bytes 131104 | tf_op jit(solution)/shard_map/ppermute | solution.py:35
  55.6 3.1 %collective-permute-start.17 = (bf16[512,128]{1,0:T(8,128)(2,1)S(1)}, bf16[512,128]{1,0:T(8,128)(2,1)S(1)}, u32[]{:S(2)}, u32[]{:S(2)}) collective-permute-start(bf16[512,128]{1,0:T(8,128)(2,1)S(1)} %get-tuple-element.49), channel_id=1, source_target_pairs={{0,2},{1,3},{2,0},{3,1},{4,6},{5,7},{6,4},{7,5},{8,10},{9,11},{10,... | collective-permute-start | bytes 393224 | tf_op jit(solution)/shard_map/ppermute | solution.py:35
  58.7 3.9 %collective-permute-done.16 = bf16[512,128]{1,0:T(8,128)(2,1)S(1)} collective-permute-done((bf16[512,128]{1,0:T(8,128)(2,1)S(1)}, bf16[512,128]{1,0:T(8,128)(2,1)S(1)}, u32[]{:S(2)}, u32[]{:S(2)}) %collective-permute-start.16) | collective-permute-done | bytes 131104 | tf_op jit(solution)/shard_map/ppermute | solution.py:35
  64.3 1.6 %collective-permute-start.18 = (bf16[512,128]{1,0:T(8,128)(2,1)S(1)}, bf16[512,128]{1,0:T(8,128)(2,1)S(1)}, u32[]{:S(2)}, u32[]{:S(2)}) collective-permute-start(bf16[512,128]{1,0:T(8,128)(2,1)S(1)} %get-tuple-element.73), channel_id=1, source_target_pairs={{0,16},{8,24},{16,0},{24,8},{1,17},{9,25},{17,1},{25,9},{2,18},{10... | collective-permute-start | bytes 393224 | tf_op jit(solution)/shard_map/ppermute | solution.py:35
  67.3 2.1 %collective-permute-done.18 = bf16[512,128]{1,0:T(8,128)(2,1)S(1)} collective-permute-done((bf16[512,128]{1,0:T(8,128)(2,1)S(1)}, bf16[512,128]{1,0:T(8,128)(2,1)S(1)}, u32[]{:S(2)}, u32[]{:S(2)}) %collective-permute-start.18) | collective-permute-done | bytes 131104 | tf_op jit(solution)/shard_map/ppermute | solution.py:35
  72.9 3.0 %collective-permute-done.21 = bf16[512,128]{1,0:T(8,128)(2,1)S(1)} collective-permute-done((bf16[512,128]{1,0:T(8,128)(2,1)S(1)}, bf16[512,128]{1,0:T(8,128)(2,1)S(1)}, u32[]{:S(2)}, u32[]{:S(2)}) %collective-permute-start.21) | collective-permute-done | bytes 131104 | tf_op jit(solution)/shard_map/ppermute | solution.py:35
  81.7 1.6 %collective-permute-start.25 = (f32[136,128]{1,0:T(8,128)S(1)}, f32[136,128]{1,0:T(8,128)S(1)}, u32[]{:S(2)}, u32[]{:S(2)}) collective-permute-start(f32[136,128]{1,0:T(8,128)S(1)} %select_maximum_fusion), channel_id=1, source_target_pairs={{0,4},{1,5},{2,6},{3,7},{4,0},{5,1},{6,2},{7,3},{8,12},{9,13},{10,... | collective-permute-start | bytes 208904 | tf_op jit(solution)/shard_map/ppermute | solution.py:35
  84.1 2.9 %collective-permute-done.24 = f32[136,128]{1,0:T(8,128)S(1)} collective-permute-done((f32[136,128]{1,0:T(8,128)S(1)}, f32[136,128]{1,0:T(8,128)S(1)}, u32[]{:S(2)}, u32[]{:S(2)}) %collective-permute-start.24) | collective-permute-done | bytes 69664 | tf_op jit(solution)/shard_map/ppermute | solution.py:35
  87.0 2.9 %collective-permute-done.25 = f32[136,128]{1,0:T(8,128)S(1)} collective-permute-done((f32[136,128]{1,0:T(8,128)S(1)}, f32[136,128]{1,0:T(8,128)S(1)}, u32[]{:S(2)}, u32[]{:S(2)}) %collective-permute-start.25) | collective-permute-done | bytes 69664 | tf_op jit(solution)/shard_map/ppermute | solution.py:35
  91.3 6.9 %shard_map.38 = f32[128,256]{1,0:T(8,128)} custom-call(s32[1]{0:T(128)} %bitcast.first_ref, f32[136,128]{1,0:T(8,128)S(1)} %add_add_fusion.total_ref, f32[136,128]{1,0:T(8,128)S(1)} %collective-permute-done.26.partner_ref, f32[128,128]{1,0:T(8,128)S(1)} %fusion.23.mine_ref, f32[128,128]{1,0:T(8,128)S(1)} %constant_dynamic-slice_fusion.theirs_ref), custom_call_target="tpu_custom_call" | custom-call | tf_op jit(solution)/shard_map/pallas_call | solution.py:171
  (81 shorter events, 30.4 us)
Async XLA Ops:
  0.9 8.7 %collective-permute-start = (bf16[128,256]{1,0:T(8,128)(2,1)S(1)}, bf16[128,256]{1,0:T(8,128)(2,1)S(1)}, u32[]{:S(2)}, u32[]{:S(2)}) collective-permute-start(bf16[128,256]{1,0:T(8,128)(2,1)S(1)} %convert_element_type.147), channel_id=1, source_target_pairs={{0,8},{8,0},{16,24},{24,16},{1,9},{9,1},{17,25},{25,17},{2,10},{10... | collective-permute-start | bytes 196616 | tf_op jit(solution)/shard_map/ppermute | solution.py:35
  3.9 5.7 %collective-permute-start.1 = (bf16[128,256]{1,0:T(8,128)(2,1)S(1)}, bf16[128,256]{1,0:T(8,128)(2,1)S(1)}, u32[]{:S(2)}, u32[]{:S(2)}) collective-permute-start(bf16[128,256]{1,0:T(8,128)(2,1)S(1)} %convert_element_type.147), channel_id=1, source_target_pairs={{0,24},{8,16},{16,8},{24,0},{1,25},{9,17},{17,9},{25,1},{2,26},{10... | collective-permute-start | bytes 196616 | tf_op jit(solution)/shard_map/ppermute | solution.py:35
  5.4 4.5 %collective-permute-start.2 = (bf16[128,256]{1,0:T(8,128)(2,1)S(1)}, bf16[128,256]{1,0:T(8,128)(2,1)S(1)}, u32[]{:S(2)}, u32[]{:S(2)}) collective-permute-start(bf16[128,256]{1,0:T(8,128)(2,1)S(1)} %convert_element_type.147), channel_id=1, source_target_pairs={{0,16},{8,24},{16,0},{24,8},{1,17},{9,25},{17,1},{25,9},{2,18},{10... | collective-permute-start | bytes 196616 | tf_op jit(solution)/shard_map/ppermute | solution.py:35
  12.3 9.5 %collective-permute-start.5 = (bf16[512,128]{1,0:T(8,128)(2,1)S(1)}, bf16[512,128]{1,0:T(8,128)(2,1)S(1)}, u32[]{:S(2)}, u32[]{:S(2)}) collective-permute-start(bf16[512,128]{1,0:T(8,128)(2,1)S(1)} %get-tuple-element.58), channel_id=1, source_target_pairs={{0,4},{1,5},{2,6},{3,7},{4,0},{5,1},{6,2},{7,3},{8,12},{9,13},{10,... | collective-permute-start | bytes 393224 | tf_op jit(solution)/shard_map/ppermute | solution.py:35
  15.1 6.9 %collective-permute-start.6 = (bf16[512,128]{1,0:T(8,128)(2,1)S(1)}, bf16[512,128]{1,0:T(8,128)(2,1)S(1)}, u32[]{:S(2)}, u32[]{:S(2)}) collective-permute-start(bf16[512,128]{1,0:T(8,128)(2,1)S(1)} %get-tuple-element.57), channel_id=1, source_target_pairs={{0,2},{1,3},{2,0},{3,1},{4,6},{5,7},{6,4},{7,5},{8,10},{9,11},{10,... | collective-permute-start | bytes 393224 | tf_op jit(solution)/shard_map/ppermute | solution.py:35
  17.4 8.7 %collective-permute-start.9 = (f32[128,128]{1,0:T(8,128)}, f32[128,128]{1,0:T(8,128)S(1)}, u32[]{:S(2)}, u32[]{:S(2)}) collective-permute-start(f32[128,128]{1,0:T(8,128)} %get-tuple-element.65), channel_id=1, source_target_pairs={{0,1},{1,0},{2,3},{3,2},{4,5},{5,4},{6,7},{7,6},{8,9},{9,8},{10,11... | collective-permute-start | bytes 196616 | tf_op jit(solution)/shard_map/ppermute | solution.py:35
  17.4 15.6 %collective-permute-start.4 = (bf16[1024,512]{1,0:T(8,128)(2,1)S(1)}, bf16[1024,512]{1,0:T(8,128)(2,1)S(1)}, u32[]{:S(2)}, u32[]{:S(2)}) collective-permute-start(bf16[1024,512]{1,0:T(8,128)(2,1)S(1)} %shard_map.37), channel_id=1, source_target_pairs={{0,1},{1,0},{2,3},{3,2},{4,5},{5,4},{6,7},{7,6},{8,9},{9,8},{10,11... | collective-permute-start | bytes 3145736 | tf_op jit(solution)/shard_map/ppermute | solution.py:35
  22.1 8.5 %collective-permute-start.7 = (bf16[512,128]{1,0:T(8,128)(2,1)S(1)}, bf16[512,128]{1,0:T(8,128)(2,1)S(1)}, u32[]{:S(2)}, u32[]{:S(2)}) collective-permute-start(bf16[512,128]{1,0:T(8,128)(2,1)S(1)} %get-tuple-element.56), channel_id=1, source_target_pairs={{0,4},{1,5},{2,6},{3,7},{4,0},{5,1},{6,2},{7,3},{8,12},{9,13},{10,... | collective-permute-start | bytes 393224 | tf_op jit(solution)/shard_map/ppermute | solution.py:35
  23.5 7.2 %collective-permute-start.8 = (bf16[512,128]{1,0:T(8,128)(2,1)S(1)}, bf16[512,128]{1,0:T(8,128)(2,1)S(1)}, u32[]{:S(2)}, u32[]{:S(2)}) collective-permute-start(bf16[512,128]{1,0:T(8,128)(2,1)S(1)} %get-tuple-element.55), channel_id=1, source_target_pairs={{0,2},{1,3},{2,0},{3,1},{4,6},{5,7},{6,4},{7,5},{8,10},{9,11},{10,... | collective-permute-start | bytes 393224 | tf_op jit(solution)/shard_map/ppermute | solution.py:35
  31.4 5.0 %collective-permute-start.11 = (bf16[512,128]{1,0:T(8,128)(2,1)S(1)}, bf16[512,128]{1,0:T(8,128)(2,1)S(1)}, u32[]{:S(2)}, u32[]{:S(2)}) collective-permute-start(bf16[512,128]{1,0:T(8,128)(2,1)S(1)} %get-tuple-element.71), channel_id=1, source_target_pairs={{0,8},{8,0},{16,24},{24,16},{1,9},{9,1},{17,25},{25,17},{2,10},{10... | collective-permute-start | bytes 393224 | tf_op jit(solution)/shard_map/ppermute | solution.py:35
  33.5 5.0 %collective-permute-start.10 = (bf16[512,128]{1,0:T(8,128)(2,1)S(1)}, bf16[512,128]{1,0:T(8,128)(2,1)S(1)}, u32[]{:S(2)}, u32[]{:S(2)}) collective-permute-start(bf16[512,128]{1,0:T(8,128)(2,1)S(1)} %get-tuple-element.69), channel_id=1, source_target_pairs={{0,16},{8,24},{16,0},{24,8},{1,17},{9,25},{17,1},{25,9},{2,18},{10... | collective-permute-start | bytes 393224 | tf_op jit(solution)/shard_map/ppermute | solution.py:35
  38.5 5.0 %collective-permute-start.13 = (bf16[512,128]{1,0:T(8,128)(2,1)S(1)}, bf16[512,128]{1,0:T(8,128)(2,1)S(1)}, u32[]{:S(2)}, u32[]{:S(2)}) collective-permute-start(bf16[512,128]{1,0:T(8,128)(2,1)S(1)} %fusion.11), channel_id=1, source_target_pairs={{0,8},{8,0},{16,24},{24,16},{1,9},{9,1},{17,25},{25,17},{2,10},{10... | collective-permute-start | bytes 393224 | tf_op jit(solution)/shard_map/ppermute | solution.py:35
  39.2 5.0 %collective-permute-start.12 = (bf16[512,128]{1,0:T(8,128)(2,1)S(1)}, bf16[512,128]{1,0:T(8,128)(2,1)S(1)}, u32[]{:S(2)}, u32[]{:S(2)}) collective-permute-start(bf16[512,128]{1,0:T(8,128)(2,1)S(1)} %fusion.10), channel_id=1, source_target_pairs={{0,16},{8,24},{16,0},{24,8},{1,17},{9,25},{17,1},{25,9},{2,18},{10... | collective-permute-start | bytes 393224 | tf_op jit(solution)/shard_map/ppermute | solution.py:35
  45.3 10.2 %collective-permute-start.14 = (bf16[512,128]{1,0:T(8,128)(2,1)S(1)}, bf16[512,128]{1,0:T(8,128)(2,1)S(1)}, u32[]{:S(2)}, u32[]{:S(2)}) collective-permute-start(bf16[512,128]{1,0:T(8,128)(2,1)S(1)} %get-tuple-element.52), channel_id=1, source_target_pairs={{0,4},{1,5},{2,6},{3,7},{4,0},{5,1},{6,2},{7,3},{8,12},{9,13},{10,... | collective-permute-start | bytes 393224 | tf_op jit(solution)/shard_map/ppermute | solution.py:35
  47.0 8.4 %collective-permute-start.15 = (bf16[512,128]{1,0:T(8,128)(2,1)S(1)}, bf16[512,128]{1,0:T(8,128)(2,1)S(1)}, u32[]{:S(2)}, u32[]{:S(2)}) collective-permute-start(bf16[512,128]{1,0:T(8,128)(2,1)S(1)} %get-tuple-element.51), channel_id=1, source_target_pairs={{0,2},{1,3},{2,0},{3,1},{4,6},{5,7},{6,4},{7,5},{8,10},{9,11},{10,... | collective-permute-start | bytes 393224 | tf_op jit(solution)/shard_map/ppermute | solution.py:35
  55.5 7.1 %collective-permute-start.16 = (bf16[512,128]{1,0:T(8,128)(2,1)S(1)}, bf16[512,128]{1,0:T(8,128)(2,1)S(1)}, u32[]{:S(2)}, u32[]{:S(2)}) collective-permute-start(bf16[512,128]{1,0:T(8,128)(2,1)S(1)} %get-tuple-element.50), channel_id=1, source_target_pairs={{0,4},{1,5},{2,6},{3,7},{4,0},{5,1},{6,2},{7,3},{8,12},{9,13},{10,... | collective-permute-start | bytes 393224 | tf_op jit(solution)/shard_map/ppermute | solution.py:35
  55.6 7.5 %collective-permute-start.17 = (bf16[512,128]{1,0:T(8,128)(2,1)S(1)}, bf16[512,128]{1,0:T(8,128)(2,1)S(1)}, u32[]{:S(2)}, u32[]{:S(2)}) collective-permute-start(bf16[512,128]{1,0:T(8,128)(2,1)S(1)} %get-tuple-element.49), channel_id=1, source_target_pairs={{0,2},{1,3},{2,0},{3,1},{4,6},{5,7},{6,4},{7,5},{8,10},{9,11},{10,... | collective-permute-start | bytes 393224 | tf_op jit(solution)/shard_map/ppermute | solution.py:35
  64.3 5.1 %collective-permute-start.18 = (bf16[512,128]{1,0:T(8,128)(2,1)S(1)}, bf16[512,128]{1,0:T(8,128)(2,1)S(1)}, u32[]{:S(2)}, u32[]{:S(2)}) collective-permute-start(bf16[512,128]{1,0:T(8,128)(2,1)S(1)} %get-tuple-element.73), channel_id=1, source_target_pairs={{0,16},{8,24},{16,0},{24,8},{1,17},{9,25},{17,1},{25,9},{2,18},{10... | collective-permute-start | bytes 393224 | tf_op jit(solution)/shard_map/ppermute | solution.py:35
  65.9 5.0 %collective-permute-start.19 = (bf16[512,128]{1,0:T(8,128)(2,1)S(1)}, bf16[512,128]{1,0:T(8,128)(2,1)S(1)}, u32[]{:S(2)}, u32[]{:S(2)}) collective-permute-start(bf16[512,128]{1,0:T(8,128)(2,1)S(1)} %get-tuple-element.75), channel_id=1, source_target_pairs={{0,8},{8,0},{16,24},{24,16},{1,9},{9,1},{17,25},{25,17},{2,10},{10... | collective-permute-start | bytes 393224 | tf_op jit(solution)/shard_map/ppermute | solution.py:35
  70.9 5.0 %collective-permute-start.21 = (bf16[512,128]{1,0:T(8,128)(2,1)S(1)}, bf16[512,128]{1,0:T(8,128)(2,1)S(1)}, u32[]{:S(2)}, u32[]{:S(2)}) collective-permute-start(bf16[512,128]{1,0:T(8,128)(2,1)S(1)} %fusion.12), channel_id=1, source_target_pairs={{0,8},{8,0},{16,24},{24,16},{1,9},{9,1},{17,25},{25,17},{2,10},{10... | collective-permute-start | bytes 393224 | tf_op jit(solution)/shard_map/ppermute | solution.py:35
  72.4 5.0 %collective-permute-start.20 = (bf16[512,128]{1,0:T(8,128)(2,1)S(1)}, bf16[512,128]{1,0:T(8,128)(2,1)S(1)}, u32[]{:S(2)}, u32[]{:S(2)}) collective-permute-start(bf16[512,128]{1,0:T(8,128)(2,1)S(1)} %fusion.13), channel_id=1, source_target_pairs={{0,16},{8,24},{16,0},{24,8},{1,17},{9,25},{17,1},{25,9},{2,18},{10... | collective-permute-start | bytes 393224 | tf_op jit(solution)/shard_map/ppermute | solution.py:35
  79.7 4.4 %collective-permute-start.23 = (f32[136,128]{1,0:T(8,128)S(1)}, f32[136,128]{1,0:T(8,128)S(1)}, u32[]{:S(2)}, u32[]{:S(2)}) collective-permute-start(f32[136,128]{1,0:T(8,128)S(1)} %select_maximum_fusion), channel_id=1, source_target_pairs={{0,2},{1,3},{2,0},{3,1},{4,6},{5,7},{6,4},{7,5},{8,10},{9,11},{10,... | collective-permute-start | bytes 208904 | tf_op jit(solution)/shard_map/ppermute | solution.py:35
  80.4 6.6 %collective-permute-start.24 = (f32[136,128]{1,0:T(8,128)S(1)}, f32[136,128]{1,0:T(8,128)S(1)}, u32[]{:S(2)}, u32[]{:S(2)}) collective-permute-start(f32[136,128]{1,0:T(8,128)S(1)} %select_maximum_fusion), channel_id=1, source_target_pairs={{0,6},{1,7},{2,4},{3,5},{4,2},{5,3},{6,0},{7,1},{8,14},{9,15},{10,... | collective-permute-start | bytes 208904 | tf_op jit(solution)/shard_map/ppermute | solution.py:35
  81.7 8.2 %collective-permute-start.25 = (f32[136,128]{1,0:T(8,128)S(1)}, f32[136,128]{1,0:T(8,128)S(1)}, u32[]{:S(2)}, u32[]{:S(2)}) collective-permute-start(f32[136,128]{1,0:T(8,128)S(1)} %select_maximum_fusion), channel_id=1, source_target_pairs={{0,4},{1,5},{2,6},{3,7},{4,0},{5,1},{6,2},{7,3},{8,12},{9,13},{10,... | collective-permute-start | bytes 208904 | tf_op jit(solution)/shard_map/ppermute | solution.py:35
  (6 other events, 12.8 us)

commit v11 on v10

--- a/solution.py
+++ b/solution.py
@@ -200,7 +200,7 @@
         left, right = value[:, :half], value[:, half:]
         return jnp.where(mine_first, left, right), jnp.where(mine_first, right, left)
 
-    low_start = vectors.astype(narrow)
+    low_start = lax.optimization_barrier(vectors.astype(narrow))
     arrived = {0: low_start, **{k: swap(low_start, "row", k) for k in partners(row_count)}}
     low_group = in_order(arrived, row_rank)
     own_start, sent = kept_and_sent(vectors)
@@ -296,7 +296,8 @@
     packed = jnp.where(mine_first | (rows >= lanes), cross, corner)
     diagonal = jnp.sum(jnp.where(rows == lanes, corner, 0.0), axis=0, keepdims=True)
     total = jnp.concatenate([packed, jnp.pad(diagonal, ((0, 7), (0, 0)))])
-    total = sum([swap(total, "col", 2 * k) for k in partners(z_count)], total)
+    far_to_near = [*range(2, z_count), 1]
+    total = sum(lax.optimization_barrier([swap(total, "col", 2 * k) for k in far_to_near]), total)
     partner = swap(total, "col", 1)
     orbital_count = piece_rows * row_count * col_count
     here = row_rank * piece_rows

time: 98.4 us -> 96.7 us (0.983)
  starting transfers between devices: 34.2 us -> 32.7 us
    ppermute x27, starting transfers between devices: 34.2 us -> 32.7 us  [swap(): return lax.ppermute(value, axis, [(i, i ^ distance) for i in range(count)])]
  transfers between devices with their start and end apart: 27 -> 27, of which waited for: 22 -> 22; matrix products, arithmetic and copies ran while one was open for 4% -> 3% of each run, Pallas kernels for 1% -> 1%
where the time goes in v11:
time: 96.7 us; the launch traced here: 96.5 us
  waiting for transfers between devices  45.4 us (47%)
  starting transfers between devices  32.7 us (34%)
  Pallas kernels  8.06 us (8%)
  matrix products  4.7 us (5%)
  other arithmetic  3.03 us (3%)
  local copies, waits for them, and re-layouts  2.29 us (2%)
    ppermute x27, waiting for transfers between devices, swap(): return lax.ppermute(value, axis, [(i, i ^ distance) for i in range(count)])  45.4 us
    ppermute x27, starting transfers between devices, swap(): return lax.ppermute(value, axis, [(i, i ^ distance) for i in range(count)])  32.7 us
    pallas_call x1, Pallas kernels, orthonormal(): pl.pallas_call(kernel, in_specs=[pl.BlockSpec(memory_space=pltpu.SMEM), v...  6.92 us
    unnamed x6, local copies, waits for them, and re-layouts  2.1 us
  transfers between devices with their start and end apart: 27, of which 22 were waited for; matrix products, arithmetic and copies ran while one was open for 3% of the time, Pallas kernels for 1%

profile of v11, /device:TPU:0, one launch (start us, length us, event | category | flops | bytes accessed | tf_op | source)
XLA Modules:
  0.0 96.5 jit_solution(11312072123595873557)
XLA Ops:
  0.9 3.0 %collective-permute-start = (bf16[128,256]{1,0:T(8,128)(2,1)S(1)}, bf16[128,256]{1,0:T(8,128)(2,1)S(1)}, u32[]{:S(2)}, u32[]{:S(2)}) collective-permute-start(bf16[128,256]{1,0:T(8,128)(2,1)S(1)} %convert_element_type.147), channel_id=1, source_target_pairs={{0,8},{8,0},{16,24},{24,16},{1,9},{9,1},{17,25},{25,17},{2,10},{10... | collective-permute-start | bytes 196616 | tf_op jit(solution)/shard_map/ppermute | solution.py:35
  3.9 1.5 %collective-permute-start.1 = (bf16[128,256]{1,0:T(8,128)(2,1)S(1)}, bf16[128,256]{1,0:T(8,128)(2,1)S(1)}, u32[]{:S(2)}, u32[]{:S(2)}) collective-permute-start(bf16[128,256]{1,0:T(8,128)(2,1)S(1)} %convert_element_type.147), channel_id=1, source_target_pairs={{0,24},{8,16},{16,8},{24,0},{1,25},{9,17},{17,9},{25,1},{2,26},{10... | collective-permute-start | bytes 196616 | tf_op jit(solution)/shard_map/ppermute | solution.py:35
  5.5 1.4 %copy-done = bf16[8,6,128,128]{3,2,1,0:T(8,128)(2,1)S(1)} copy-done((bf16[8,6,128,128]{3,2,1,0:T(8,128)(2,1)S(1)}, bf16[8,6,128,128]{3,2,1,0:T(8,128)(2,1)}, u32[]{:S(2)}) %copy-start) | copy-done | bytes 1572888
  10.7 1.5 %collective-permute-done.3 = bf16[1024,128]{1,0:T(8,128)(2,1)S(1)} collective-permute-done((bf16[1024,128]{1,0:T(8,128)(2,1)S(1)}, bf16[1024,128]{1,0:T(8,128)(2,1)S(1)}, u32[]{:S(2)}, u32[]{:S(2)}) %collective-permute-start.3) | collective-permute-done | bytes 262176 | tf_op jit(solution)/shard_map/ppermute | solution.py:35
  12.3 2.6 %collective-permute-start.5 = (bf16[512,128]{1,0:T(8,128)(2,1)S(1)}, bf16[512,128]{1,0:T(8,128)(2,1)S(1)}, u32[]{:S(2)}, u32[]{:S(2)}) collective-permute-start(bf16[512,128]{1,0:T(8,128)(2,1)S(1)} %get-tuple-element.64), channel_id=1, source_target_pairs={{0,4},{1,5},{2,6},{3,7},{4,0},{5,1},{6,2},{7,3},{8,12},{9,13},{10,... | collective-permute-start | bytes 393224 | tf_op jit(solution)/shard_map/ppermute | solution.py:35
  15.0 1.6 %collective-permute-start.6 = (bf16[512,128]{1,0:T(8,128)(2,1)S(1)}, bf16[512,128]{1,0:T(8,128)(2,1)S(1)}, u32[]{:S(2)}, u32[]{:S(2)}) collective-permute-start(bf16[512,128]{1,0:T(8,128)(2,1)S(1)} %get-tuple-element.63), channel_id=1, source_target_pairs={{0,2},{1,3},{2,0},{3,1},{4,6},{5,7},{6,4},{7,5},{8,10},{9,11},{10,... | collective-permute-start | bytes 393224 | tf_op jit(solution)/shard_map/ppermute | solution.py:35
  17.7 4.0 %collective-permute-done.5 = bf16[512,128]{1,0:T(8,128)(2,1)S(1)} collective-permute-done((bf16[512,128]{1,0:T(8,128)(2,1)S(1)}, bf16[512,128]{1,0:T(8,128)(2,1)S(1)}, u32[]{:S(2)}, u32[]{:S(2)}) %collective-permute-start.5) | collective-permute-done | bytes 131104 | tf_op jit(solution)/shard_map/ppermute | solution.py:35
  22.0 1.4 %collective-permute-start.7 = (bf16[512,128]{1,0:T(8,128)(2,1)S(1)}, bf16[512,128]{1,0:T(8,128)(2,1)S(1)}, u32[]{:S(2)}, u32[]{:S(2)}) collective-permute-start(bf16[512,128]{1,0:T(8,128)(2,1)S(1)} %get-tuple-element.62), channel_id=1, source_target_pairs={{0,4},{1,5},{2,6},{3,7},{4,0},{5,1},{6,2},{7,3},{8,12},{9,13},{10,... | collective-permute-start | bytes 393224 | tf_op jit(solution)/shard_map/ppermute | solution.py:35
  23.4 2.4 %collective-permute-start.8 = (bf16[512,128]{1,0:T(8,128)(2,1)S(1)}, bf16[512,128]{1,0:T(8,128)(2,1)S(1)}, u32[]{:S(2)}, u32[]{:S(2)}) collective-permute-start(bf16[512,128]{1,0:T(8,128)(2,1)S(1)} %get-tuple-element.61), channel_id=1, source_target_pairs={{0,2},{1,3},{2,0},{3,1},{4,6},{5,7},{6,4},{7,5},{8,10},{9,11},{10,... | collective-permute-start | bytes 393224 | tf_op jit(solution)/shard_map/ppermute | solution.py:35
  26.0 4.4 %collective-permute-done.7 = bf16[512,128]{1,0:T(8,128)(2,1)S(1)} collective-permute-done((bf16[512,128]{1,0:T(8,128)(2,1)S(1)}, bf16[512,128]{1,0:T(8,128)(2,1)S(1)}, u32[]{:S(2)}, u32[]{:S(2)}) %collective-permute-start.7) | collective-permute-done | bytes 131104 | tf_op jit(solution)/shard_map/ppermute | solution.py:35
  34.1 2.1 %collective-permute-done.11 = bf16[512,128]{1,0:T(8,128)(2,1)S(1)} collective-permute-done((bf16[512,128]{1,0:T(8,128)(2,1)S(1)}, bf16[512,128]{1,0:T(8,128)(2,1)S(1)}, u32[]{:S(2)}, u32[]{:S(2)}) %collective-permute-start.11) | collective-permute-done | bytes 131104 | tf_op jit(solution)/shard_map/ppermute | solution.py:35
  36.3 1.8 %collective-permute-done.10 = bf16[512,128]{1,0:T(8,128)(2,1)S(1)} collective-permute-done((bf16[512,128]{1,0:T(8,128)(2,1)S(1)}, bf16[512,128]{1,0:T(8,128)(2,1)S(1)}, u32[]{:S(2)}, u32[]{:S(2)}) %collective-permute-start.10) | collective-permute-done | bytes 131104 | tf_op jit(solution)/shard_map/ppermute | solution.py:35
  40.0 3.1 %collective-permute-done.13 = bf16[512,128]{1,0:T(8,128)(2,1)S(1)} collective-permute-done((bf16[512,128]{1,0:T(8,128)(2,1)S(1)}, bf16[512,128]{1,0:T(8,128)(2,1)S(1)}, u32[]{:S(2)}, u32[]{:S(2)}) %collective-permute-start.13) | collective-permute-done | bytes 131104 | tf_op jit(solution)/shard_map/ppermute | solution.py:35
  45.1 1.8 %collective-permute-start.14 = (bf16[512,128]{1,0:T(8,128)(2,1)S(1)}, bf16[512,128]{1,0:T(8,128)(2,1)S(1)}, u32[]{:S(2)}, u32[]{:S(2)}) collective-permute-start(bf16[512,128]{1,0:T(8,128)(2,1)S(1)} %get-tuple-element.58), channel_id=1, source_target_pairs={{0,4},{1,5},{2,6},{3,7},{4,0},{5,1},{6,2},{7,3},{8,12},{9,13},{10,... | collective-permute-start | bytes 393224 | tf_op jit(solution)/shard_map/ppermute | solution.py:35
  46.9 1.8 %collective-permute-start.15 = (bf16[512,128]{1,0:T(8,128)(2,1)S(1)}, bf16[512,128]{1,0:T(8,128)(2,1)S(1)}, u32[]{:S(2)}, u32[]{:S(2)}) collective-permute-start(bf16[512,128]{1,0:T(8,128)(2,1)S(1)} %get-tuple-element.57), channel_id=1, source_target_pairs={{0,2},{1,3},{2,0},{3,1},{4,6},{5,7},{6,4},{7,5},{8,10},{9,11},{10,... | collective-permute-start | bytes 393224 | tf_op jit(solution)/shard_map/ppermute | solution.py:35
  48.7 6.6 %collective-permute-done.14 = bf16[512,128]{1,0:T(8,128)(2,1)S(1)} collective-permute-done((bf16[512,128]{1,0:T(8,128)(2,1)S(1)}, bf16[512,128]{1,0:T(8,128)(2,1)S(1)}, u32[]{:S(2)}, u32[]{:S(2)}) %collective-permute-start.14) | collective-permute-done | bytes 131104 | tf_op jit(solution)/shard_map/ppermute | solution.py:35
  55.4 3.1 %collective-permute-start.17 = (bf16[512,128]{1,0:T(8,128)(2,1)S(1)}, bf16[512,128]{1,0:T(8,128)(2,1)S(1)}, u32[]{:S(2)}, u32[]{:S(2)}) collective-permute-start(bf16[512,128]{1,0:T(8,128)(2,1)S(1)} %get-tuple-element.55), channel_id=1, source_target_pairs={{0,2},{1,3},{2,0},{3,1},{4,6},{5,7},{6,4},{7,5},{8,10},{9,11},{10,... | collective-permute-start | bytes 393224 | tf_op jit(solution)/shard_map/ppermute | solution.py:35
  58.5 3.9 %collective-permute-done.16 = bf16[512,128]{1,0:T(8,128)(2,1)S(1)} collective-permute-done((bf16[512,128]{1,0:T(8,128)(2,1)S(1)}, bf16[512,128]{1,0:T(8,128)(2,1)S(1)}, u32[]{:S(2)}, u32[]{:S(2)}) %collective-permute-start.16) | collective-permute-done | bytes 131104 | tf_op jit(solution)/shard_map/ppermute | solution.py:35
  66.4 2.7 %collective-permute-done.18 = bf16[512,128]{1,0:T(8,128)(2,1)S(1)} collective-permute-done((bf16[512,128]{1,0:T(8,128)(2,1)S(1)}, bf16[512,128]{1,0:T(8,128)(2,1)S(1)}, u32[]{:S(2)}, u32[]{:S(2)}) %collective-permute-start.18) | collective-permute-done | bytes 131104 | tf_op jit(solution)/shard_map/ppermute | solution.py:35
  72.6 2.6 %collective-permute-done.21 = bf16[512,128]{1,0:T(8,128)(2,1)S(1)} collective-permute-done((bf16[512,128]{1,0:T(8,128)(2,1)S(1)}, bf16[512,128]{1,0:T(8,128)(2,1)S(1)}, u32[]{:S(2)}, u32[]{:S(2)}) %collective-permute-start.21) | collective-permute-done | bytes 131104 | tf_op jit(solution)/shard_map/ppermute | solution.py:35
  75.2 1.4 %collective-permute-done.20 = bf16[512,128]{1,0:T(8,128)(2,1)S(1)} collective-permute-done((bf16[512,128]{1,0:T(8,128)(2,1)S(1)}, bf16[512,128]{1,0:T(8,128)(2,1)S(1)}, u32[]{:S(2)}, u32[]{:S(2)}) %collective-permute-start.20) | collective-permute-done | bytes 131104 | tf_op jit(solution)/shard_map/ppermute | solution.py:35
  79.4 2.6 %collective-permute-start.24 = (f32[136,128]{1,0:T(8,128)S(1)}, f32[136,128]{1,0:T(8,128)S(1)}, u32[]{:S(2)}, u32[]{:S(2)}) collective-permute-start(f32[136,128]{1,0:T(8,128)S(1)} %select_maximum_fusion), channel_id=1, source_target_pairs={{0,6},{1,7},{2,4},{3,5},{4,2},{5,3},{6,0},{7,1},{8,14},{9,15},{10,... | collective-permute-start | bytes 208904 | tf_op jit(solution)/shard_map/ppermute | solution.py:35
  82.6 4.7 %collective-permute-done.23 = f32[136,128]{1,0:T(8,128)S(1)} collective-permute-done((f32[136,128]{1,0:T(8,128)S(1)}, f32[136,128]{1,0:T(8,128)S(1)}, u32[]{:S(2)}, u32[]{:S(2)}) %collective-permute-start.23) | collective-permute-done | bytes 69664 | tf_op jit(solution)/shard_map/ppermute | solution.py:35
  89.6 6.9 %shard_map.38 = f32[128,256]{1,0:T(8,128)} custom-call(s32[1]{0:T(128)} %bitcast.first_ref, f32[136,128]{1,0:T(8,128)S(1)} %add_add_fusion.total_ref, f32[136,128]{1,0:T(8,128)S(1)} %collective-permute-done.26.partner_ref, f32[128,128]{1,0:T(8,128)S(1)} %fusion.23.mine_ref, f32[128,128]{1,0:T(8,128)S(1)} %constant_dynamic-slice_fusion.theirs_ref), custom_call_target="tpu_custom_call" | custom-call | tf_op jit(solution)/shard_map/pallas_call | solution.py:171
  (80 shorter events, 27.1 us)
Async XLA Ops:
  0.9 7.8 %collective-permute-start = (bf16[128,256]{1,0:T(8,128)(2,1)S(1)}, bf16[128,256]{1,0:T(8,128)(2,1)S(1)}, u32[]{:S(2)}, u32[]{:S(2)}) collective-permute-start(bf16[128,256]{1,0:T(8,128)(2,1)S(1)} %convert_element_type.147), channel_id=1, source_target_pairs={{0,8},{8,0},{16,24},{24,16},{1,9},{9,1},{17,25},{25,17},{2,10},{10... | collective-permute-start | bytes 196616 | tf_op jit(solution)/shard_map/ppermute | solution.py:35
  3.9 5.2 %collective-permute-start.1 = (bf16[128,256]{1,0:T(8,128)(2,1)S(1)}, bf16[128,256]{1,0:T(8,128)(2,1)S(1)}, u32[]{:S(2)}, u32[]{:S(2)}) collective-permute-start(bf16[128,256]{1,0:T(8,128)(2,1)S(1)} %convert_element_type.147), channel_id=1, source_target_pairs={{0,24},{8,16},{16,8},{24,0},{1,25},{9,17},{17,9},{25,1},{2,26},{10... | collective-permute-start | bytes 196616 | tf_op jit(solution)/shard_map/ppermute | solution.py:35
  5.4 4.5 %collective-permute-start.2 = (bf16[128,256]{1,0:T(8,128)(2,1)S(1)}, bf16[128,256]{1,0:T(8,128)(2,1)S(1)}, u32[]{:S(2)}, u32[]{:S(2)}) collective-permute-start(bf16[128,256]{1,0:T(8,128)(2,1)S(1)} %convert_element_type.147), channel_id=1, source_target_pairs={{0,16},{8,24},{16,0},{24,8},{1,17},{9,25},{17,1},{25,9},{2,18},{10... | collective-permute-start | bytes 196616 | tf_op jit(solution)/shard_map/ppermute | solution.py:35
  12.3 9.4 %collective-permute-start.5 = (bf16[512,128]{1,0:T(8,128)(2,1)S(1)}, bf16[512,128]{1,0:T(8,128)(2,1)S(1)}, u32[]{:S(2)}, u32[]{:S(2)}) collective-permute-start(bf16[512,128]{1,0:T(8,128)(2,1)S(1)} %get-tuple-element.64), channel_id=1, source_target_pairs={{0,4},{1,5},{2,6},{3,7},{4,0},{5,1},{6,2},{7,3},{8,12},{9,13},{10,... | collective-permute-start | bytes 393224 | tf_op jit(solution)/shard_map/ppermute | solution.py:35
  15.0 7.0 %collective-permute-start.6 = (bf16[512,128]{1,0:T(8,128)(2,1)S(1)}, bf16[512,128]{1,0:T(8,128)(2,1)S(1)}, u32[]{:S(2)}, u32[]{:S(2)}) collective-permute-start(bf16[512,128]{1,0:T(8,128)(2,1)S(1)} %get-tuple-element.63), channel_id=1, source_target_pairs={{0,2},{1,3},{2,0},{3,1},{4,6},{5,7},{6,4},{7,5},{8,10},{9,11},{10,... | collective-permute-start | bytes 393224 | tf_op jit(solution)/shard_map/ppermute | solution.py:35
  17.2 8.7 %collective-permute-start.9 = (f32[128,128]{1,0:T(8,128)}, f32[128,128]{1,0:T(8,128)S(1)}, u32[]{:S(2)}, u32[]{:S(2)}) collective-permute-start(f32[128,128]{1,0:T(8,128)} %get-tuple-element.71), channel_id=1, source_target_pairs={{0,1},{1,0},{2,3},{3,2},{4,5},{5,4},{6,7},{7,6},{8,9},{9,8},{10,11... | collective-permute-start | bytes 196616 | tf_op jit(solution)/shard_map/ppermute | solution.py:35
  17.2 15.4 %collective-permute-start.4 = (bf16[1024,512]{1,0:T(8,128)(2,1)S(1)}, bf16[1024,512]{1,0:T(8,128)(2,1)S(1)}, u32[]{:S(2)}, u32[]{:S(2)}) collective-permute-start(bf16[1024,512]{1,0:T(8,128)(2,1)S(1)} %shard_map.37), channel_id=1, source_target_pairs={{0,1},{1,0},{2,3},{3,2},{4,5},{5,4},{6,7},{7,6},{8,9},{9,8},{10,11... | collective-permute-start | bytes 3145736 | tf_op jit(solution)/shard_map/ppermute | solution.py:35
  22.0 8.5 %collective-permute-start.7 = (bf16[512,128]{1,0:T(8,128)(2,1)S(1)}, bf16[512,128]{1,0:T(8,128)(2,1)S(1)}, u32[]{:S(2)}, u32[]{:S(2)}) collective-permute-start(bf16[512,128]{1,0:T(8,128)(2,1)S(1)} %get-tuple-element.62), channel_id=1, source_target_pairs={{0,4},{1,5},{2,6},{3,7},{4,0},{5,1},{6,2},{7,3},{8,12},{9,13},{10,... | collective-permute-start | bytes 393224 | tf_op jit(solution)/shard_map/ppermute | solution.py:35
  23.4 7.3 %collective-permute-start.8 = (bf16[512,128]{1,0:T(8,128)(2,1)S(1)}, bf16[512,128]{1,0:T(8,128)(2,1)S(1)}, u32[]{:S(2)}, u32[]{:S(2)}) collective-permute-start(bf16[512,128]{1,0:T(8,128)(2,1)S(1)} %get-tuple-element.61), channel_id=1, source_target_pairs={{0,2},{1,3},{2,0},{3,1},{4,6},{5,7},{6,4},{7,5},{8,10},{9,11},{10,... | collective-permute-start | bytes 393224 | tf_op jit(solution)/shard_map/ppermute | solution.py:35
  31.3 5.0 %collective-permute-start.11 = (bf16[512,128]{1,0:T(8,128)(2,1)S(1)}, bf16[512,128]{1,0:T(8,128)(2,1)S(1)}, u32[]{:S(2)}, u32[]{:S(2)}) collective-permute-start(bf16[512,128]{1,0:T(8,128)(2,1)S(1)} %get-tuple-element.77), channel_id=1, source_target_pairs={{0,8},{8,0},{16,24},{24,16},{1,9},{9,1},{17,25},{25,17},{2,10},{10... | collective-permute-start | bytes 393224 | tf_op jit(solution)/shard_map/ppermute | solution.py:35
  33.0 5.0 %collective-permute-start.10 = (bf16[512,128]{1,0:T(8,128)(2,1)S(1)}, bf16[512,128]{1,0:T(8,128)(2,1)S(1)}, u32[]{:S(2)}, u32[]{:S(2)}) collective-permute-start(bf16[512,128]{1,0:T(8,128)(2,1)S(1)} %get-tuple-element.75), channel_id=1, source_target_pairs={{0,16},{8,24},{16,0},{24,8},{1,17},{9,25},{17,1},{25,9},{2,18},{10... | collective-permute-start | bytes 393224 | tf_op jit(solution)/shard_map/ppermute | solution.py:35
  38.1 5.0 %collective-permute-start.13 = (bf16[512,128]{1,0:T(8,128)(2,1)S(1)}, bf16[512,128]{1,0:T(8,128)(2,1)S(1)}, u32[]{:S(2)}, u32[]{:S(2)}) collective-permute-start(bf16[512,128]{1,0:T(8,128)(2,1)S(1)} %fusion.11), channel_id=1, source_target_pairs={{0,8},{8,0},{16,24},{24,16},{1,9},{9,1},{17,25},{25,17},{2,10},{10... | collective-permute-start | bytes 393224 | tf_op jit(solution)/shard_map/ppermute | solution.py:35
  39.0 5.0 %collective-permute-start.12 = (bf16[512,128]{1,0:T(8,128)(2,1)S(1)}, bf16[512,128]{1,0:T(8,128)(2,1)S(1)}, u32[]{:S(2)}, u32[]{:S(2)}) collective-permute-start(bf16[512,128]{1,0:T(8,128)(2,1)S(1)} %fusion.10), channel_id=1, source_target_pairs={{0,16},{8,24},{16,0},{24,8},{1,17},{9,25},{17,1},{25,9},{2,18},{10... | collective-permute-start | bytes 393224 | tf_op jit(solution)/shard_map/ppermute | solution.py:35
  45.1 10.2 %collective-permute-start.14 = (bf16[512,128]{1,0:T(8,128)(2,1)S(1)}, bf16[512,128]{1,0:T(8,128)(2,1)S(1)}, u32[]{:S(2)}, u32[]{:S(2)}) collective-permute-start(bf16[512,128]{1,0:T(8,128)(2,1)S(1)} %get-tuple-element.58), channel_id=1, source_target_pairs={{0,4},{1,5},{2,6},{3,7},{4,0},{5,1},{6,2},{7,3},{8,12},{9,13},{10,... | collective-permute-start | bytes 393224 | tf_op jit(solution)/shard_map/ppermute | solution.py:35
  46.9 8.4 %collective-permute-start.15 = (bf16[512,128]{1,0:T(8,128)(2,1)S(1)}, bf16[512,128]{1,0:T(8,128)(2,1)S(1)}, u32[]{:S(2)}, u32[]{:S(2)}) collective-permute-start(bf16[512,128]{1,0:T(8,128)(2,1)S(1)} %get-tuple-element.57), channel_id=1, source_target_pairs={{0,2},{1,3},{2,0},{3,1},{4,6},{5,7},{6,4},{7,5},{8,10},{9,11},{10,... | collective-permute-start | bytes 393224 | tf_op jit(solution)/shard_map/ppermute | solution.py:35
  55.3 7.1 %collective-permute-start.16 = (bf16[512,128]{1,0:T(8,128)(2,1)S(1)}, bf16[512,128]{1,0:T(8,128)(2,1)S(1)}, u32[]{:S(2)}, u32[]{:S(2)}) collective-permute-start(bf16[512,128]{1,0:T(8,128)(2,1)S(1)} %get-tuple-element.56), channel_id=1, source_target_pairs={{0,4},{1,5},{2,6},{3,7},{4,0},{5,1},{6,2},{7,3},{8,12},{9,13},{10,... | collective-permute-start | bytes 393224 | tf_op jit(solution)/shard_map/ppermute | solution.py:35
  55.4 7.4 %collective-permute-start.17 = (bf16[512,128]{1,0:T(8,128)(2,1)S(1)}, bf16[512,128]{1,0:T(8,128)(2,1)S(1)}, u32[]{:S(2)}, u32[]{:S(2)}) collective-permute-start(bf16[512,128]{1,0:T(8,128)(2,1)S(1)} %get-tuple-element.55), channel_id=1, source_target_pairs={{0,2},{1,3},{2,0},{3,1},{4,6},{5,7},{6,4},{7,5},{8,10},{9,11},{10,... | collective-permute-start | bytes 393224 | tf_op jit(solution)/shard_map/ppermute | solution.py:35
  64.1 5.0 %collective-permute-start.18 = (bf16[512,128]{1,0:T(8,128)(2,1)S(1)}, bf16[512,128]{1,0:T(8,128)(2,1)S(1)}, u32[]{:S(2)}, u32[]{:S(2)}) collective-permute-start(bf16[512,128]{1,0:T(8,128)(2,1)S(1)} %get-tuple-element.79), channel_id=1, source_target_pairs={{0,16},{8,24},{16,0},{24,8},{1,17},{9,25},{17,1},{25,9},{2,18},{10... | collective-permute-start | bytes 393224 | tf_op jit(solution)/shard_map/ppermute | solution.py:35
  65.1 5.0 %collective-permute-start.19 = (bf16[512,128]{1,0:T(8,128)(2,1)S(1)}, bf16[512,128]{1,0:T(8,128)(2,1)S(1)}, u32[]{:S(2)}, u32[]{:S(2)}) collective-permute-start(bf16[512,128]{1,0:T(8,128)(2,1)S(1)} %get-tuple-element.81), channel_id=1, source_target_pairs={{0,8},{8,0},{16,24},{24,16},{1,9},{9,1},{17,25},{25,17},{2,10},{10... | collective-permute-start | bytes 393224 | tf_op jit(solution)/shard_map/ppermute | solution.py:35
  70.1 5.0 %collective-permute-start.21 = (bf16[512,128]{1,0:T(8,128)(2,1)S(1)}, bf16[512,128]{1,0:T(8,128)(2,1)S(1)}, u32[]{:S(2)}, u32[]{:S(2)}) collective-permute-start(bf16[512,128]{1,0:T(8,128)(2,1)S(1)} %fusion.12), channel_id=1, source_target_pairs={{0,8},{8,0},{16,24},{24,16},{1,9},{9,1},{17,25},{25,17},{2,10},{10... | collective-permute-start | bytes 393224 | tf_op jit(solution)/shard_map/ppermute | solution.py:35
  71.5 5.0 %collective-permute-start.20 = (bf16[512,128]{1,0:T(8,128)(2,1)S(1)}, bf16[512,128]{1,0:T(8,128)(2,1)S(1)}, u32[]{:S(2)}, u32[]{:S(2)}) collective-permute-start(bf16[512,128]{1,0:T(8,128)(2,1)S(1)} %fusion.13), channel_id=1, source_target_pairs={{0,16},{8,24},{16,0},{24,8},{1,17},{9,25},{17,1},{25,9},{2,18},{10... | collective-permute-start | bytes 393224 | tf_op jit(solution)/shard_map/ppermute | solution.py:35
  78.9 8.4 %collective-permute-start.23 = (f32[136,128]{1,0:T(8,128)S(1)}, f32[136,128]{1,0:T(8,128)S(1)}, u32[]{:S(2)}, u32[]{:S(2)}) collective-permute-start(f32[136,128]{1,0:T(8,128)S(1)} %select_maximum_fusion), channel_id=1, source_target_pairs={{0,4},{1,5},{2,6},{3,7},{4,0},{5,1},{6,2},{7,3},{8,12},{9,13},{10,... | collective-permute-start | bytes 208904 | tf_op jit(solution)/shard_map/ppermute | solution.py:35
  79.4 7.9 %collective-permute-start.24 = (f32[136,128]{1,0:T(8,128)S(1)}, f32[136,128]{1,0:T(8,128)S(1)}, u32[]{:S(2)}, u32[]{:S(2)}) collective-permute-start(f32[136,128]{1,0:T(8,128)S(1)} %select_maximum_fusion), channel_id=1, source_target_pairs={{0,6},{1,7},{2,4},{3,5},{4,2},{5,3},{6,0},{7,1},{8,14},{9,15},{10,... | collective-permute-start | bytes 208904 | tf_op jit(solution)/shard_map/ppermute | solution.py:35
  82.0 6.2 %collective-permute-start.25 = (f32[136,128]{1,0:T(8,128)S(1)}, f32[136,128]{1,0:T(8,128)S(1)}, u32[]{:S(2)}, u32[]{:S(2)}) collective-permute-start(f32[136,128]{1,0:T(8,128)S(1)} %select_maximum_fusion), channel_id=1, source_target_pairs={{0,2},{1,3},{2,0},{3,1},{4,6},{5,7},{6,4},{7,5},{8,10},{9,11},{10,... | collective-permute-start | bytes 208904 | tf_op jit(solution)/shard_map/ppermute | solution.py:35
  (6 other events, 12.6 us)

commit v12 on v11

--- a/solution.py
+++ b/solution.py
@@ -59,7 +59,7 @@
 def densify(blocks, col_index, tile_blocks):
     group_rows, slots, width, _ = blocks.shape
     slots = min(slots, tile_blocks)
-    step = max(group_rows // 2, 1)
+    step = group_rows
 
     def kernel(index_ref, blocks_ref, tile_ref):
         nothing = jnp.zeros((width, width), blocks.dtype)
@@ -242,15 +242,10 @@
 
     def sum_over(axis, bits, one, two):
         for bit_one, bit_two in zip(bits, reversed(bits)):
-            sent = [(one.astype(narrow), bit_one), (two.astype(narrow), bit_two)]
-            if bit_two > bit_one:
-                from_two, from_one = lax.optimization_barrier(
-                    tuple(swap(value, axis, bit) for value, bit in reversed(sent))
-                )
-            else:
-                from_one, from_two = lax.optimization_barrier(
-                    tuple(swap(value, axis, bit) for value, bit in sent)
-                )
+            from_one = swap(one.astype(narrow), axis, bit_one)
+            from_two = swap(two.astype(narrow), axis, bit_two)
+            if axis == "col" or bit_one != bits[-1]:
+                from_one, from_two = lax.optimization_barrier((from_one, from_two))
             one, two = one + from_one.astype(jnp.float32), two + from_two.astype(jnp.float32)
         return one, two
 
@@ -296,7 +291,7 @@
     packed = jnp.where(mine_first | (rows >= lanes), cross, corner)
     diagonal = jnp.sum(jnp.where(rows == lanes, corner, 0.0), axis=0, keepdims=True)
     total = jnp.concatenate([packed, jnp.pad(diagonal, ((0, 7), (0, 0)))])
-    far_to_near = [*range(2, z_count), 1]
+    far_to_near = range(z_count - 1, 0, -1)
     total = sum(lax.optimization_barrier([swap(total, "col", 2 * k) for k in far_to_near]), total)
     partner = swap(total, "col", 1)
     orbital_count = piece_rows * row_count * col_count

time: 96.7 us -> 94.6 us (0.978)
  starting transfers between devices: 32.7 us -> 31.3 us
    ppermute x27, starting transfers between devices: 32.7 us -> 31.3 us  [swap(): return lax.ppermute(value, axis, [(i, i ^ distance) for i in range(count)])]
  transfers between devices with their start and end apart: 27 -> 27, of which waited for: 22 -> 20; matrix products, arithmetic and copies ran while one was open for 3% -> 4% of each run, Pallas kernels for 1% -> 1%
where the time goes in v12:
time: 94.6 us; the launch traced here: 94.4 us
  waiting for transfers between devices  44.8 us (47%)
  starting transfers between devices  31.3 us (33%)
  Pallas kernels  7.99 us (8%)
  matrix products  4.71 us (5%)
  other arithmetic  3.03 us (3%)
  local copies, waits for them, and re-layouts  2.29 us (2%)
    ppermute x27, waiting for transfers between devices, swap(): return lax.ppermute(value, axis, [(i, i ^ distance) for i in range(count)])  44.8 us
    ppermute x27, starting transfers between devices, swap(): return lax.ppermute(value, axis, [(i, i ^ distance) for i in range(count)])  31.3 us
    pallas_call x1, Pallas kernels, orthonormal(): pl.pallas_call(kernel, in_specs=[pl.BlockSpec(memory_space=pltpu.SMEM), v...  6.92 us
    unnamed x6, local copies, waits for them, and re-layouts  2.1 us
    dot_general x4, matrix products, part(): lax.dot_general(tile, low, (((0,), (0,)), ((), ())), preferred_element_ty...  1.91 us
  transfers between devices with their start and end apart: 27, of which 20 were waited for; matrix products, arithmetic and copies ran while one was open for 4% of the time, Pallas kernels for 1%

profile of v12, /device:TPU:0, one launch (start us, length us, event | category | flops | bytes accessed | tf_op | source)
XLA Modules:
  0.0 94.4 jit_solution(4140177082439401769)
XLA Ops:
  0.9 3.0 %collective-permute-start.2 = (bf16[128,256]{1,0:T(8,128)(2,1)S(1)}, bf16[128,256]{1,0:T(8,128)(2,1)S(1)}, u32[]{:S(2)}, u32[]{:S(2)}) collective-permute-start(bf16[128,256]{1,0:T(8,128)(2,1)S(1)} %convert_element_type.147), channel_id=1, source_target_pairs={{0,16},{8,24},{16,0},{24,8},{1,17},{9,25},{17,1},{25,9},{2,18},{10... | collective-permute-start | bytes 196616 | tf_op jit(solution)/shard_map/ppermute | solution.py:35
  10.4 1.5 %collective-permute-done.3 = bf16[1024,128]{1,0:T(8,128)(2,1)S(1)} collective-permute-done((bf16[1024,128]{1,0:T(8,128)(2,1)S(1)}, bf16[1024,128]{1,0:T(8,128)(2,1)S(1)}, u32[]{:S(2)}, u32[]{:S(2)}) %collective-permute-start.3) | collective-permute-done | bytes 262176 | tf_op jit(solution)/shard_map/ppermute | solution.py:35
  12.0 1.6 %collective-permute-start.5 = (bf16[512,128]{1,0:T(8,128)(2,1)S(1)}, bf16[512,128]{1,0:T(8,128)(2,1)S(1)}, u32[]{:S(2)}, u32[]{:S(2)}) collective-permute-start(bf16[512,128]{1,0:T(8,128)(2,1)S(1)} %get-tuple-element.56), channel_id=1, source_target_pairs={{0,2},{1,3},{2,0},{3,1},{4,6},{5,7},{6,4},{7,5},{8,10},{9,11},{10,... | collective-permute-start | bytes 393224 | tf_op jit(solution)/shard_map/ppermute | solution.py:35
  13.7 2.6 %collective-permute-start.6 = (bf16[512,128]{1,0:T(8,128)(2,1)S(1)}, bf16[512,128]{1,0:T(8,128)(2,1)S(1)}, u32[]{:S(2)}, u32[]{:S(2)}) collective-permute-start(bf16[512,128]{1,0:T(8,128)(2,1)S(1)} %get-tuple-element.55), channel_id=1, source_target_pairs={{0,4},{1,5},{2,6},{3,7},{4,0},{5,1},{6,2},{7,3},{8,12},{9,13},{10,... | collective-permute-start | bytes 393224 | tf_op jit(solution)/shard_map/ppermute | solution.py:35
  17.4 2.6 %collective-permute-done.5 = bf16[512,128]{1,0:T(8,128)(2,1)S(1)} collective-permute-done((bf16[512,128]{1,0:T(8,128)(2,1)S(1)}, bf16[512,128]{1,0:T(8,128)(2,1)S(1)}, u32[]{:S(2)}, u32[]{:S(2)}) %collective-permute-start.5) | collective-permute-done | bytes 131104 | tf_op jit(solution)/shard_map/ppermute | solution.py:35
  20.0 2.7 %collective-permute-done.6 = bf16[512,128]{1,0:T(8,128)(2,1)S(1)} collective-permute-done((bf16[512,128]{1,0:T(8,128)(2,1)S(1)}, bf16[512,128]{1,0:T(8,128)(2,1)S(1)}, u32[]{:S(2)}, u32[]{:S(2)}) %collective-permute-start.6) | collective-permute-done | bytes 131104 | tf_op jit(solution)/shard_map/ppermute | solution.py:35
  23.1 2.7 %collective-permute-start.8 = (bf16[512,128]{1,0:T(8,128)(2,1)S(1)}, bf16[512,128]{1,0:T(8,128)(2,1)S(1)}, u32[]{:S(2)}, u32[]{:S(2)}) collective-permute-start(bf16[512,128]{1,0:T(8,128)(2,1)S(1)} %get-tuple-element.53), channel_id=1, source_target_pairs={{0,2},{1,3},{2,0},{3,1},{4,6},{5,7},{6,4},{7,5},{8,10},{9,11},{10,... | collective-permute-start | bytes 393224 | tf_op jit(solution)/shard_map/ppermute | solution.py:35
  26.1 4.0 %collective-permute-done.7 = bf16[512,128]{1,0:T(8,128)(2,1)S(1)} collective-permute-done((bf16[512,128]{1,0:T(8,128)(2,1)S(1)}, bf16[512,128]{1,0:T(8,128)(2,1)S(1)}, u32[]{:S(2)}, u32[]{:S(2)}) %collective-permute-start.7) | collective-permute-done | bytes 131104 | tf_op jit(solution)/shard_map/ppermute | solution.py:35
  32.3 1.6 %collective-permute-start.11 = (bf16[512,128]{1,0:T(8,128)(2,1)S(1)}, bf16[512,128]{1,0:T(8,128)(2,1)S(1)}, u32[]{:S(2)}, u32[]{:S(2)}) collective-permute-start(bf16[512,128]{1,0:T(8,128)(2,1)S(1)} %get-tuple-element.69), channel_id=1, source_target_pairs={{0,16},{8,24},{16,0},{24,8},{1,17},{9,25},{17,1},{25,9},{2,18},{10... | collective-permute-start | bytes 393224 | tf_op jit(solution)/shard_map/ppermute | solution.py:35
  33.9 2.1 %collective-permute-done.9 = bf16[512,128]{1,0:T(8,128)(2,1)S(1)} collective-permute-done((bf16[512,128]{1,0:T(8,128)(2,1)S(1)}, bf16[512,128]{1,0:T(8,128)(2,1)S(1)}, u32[]{:S(2)}, u32[]{:S(2)}) %collective-permute-start.9) | collective-permute-done | bytes 131104 | tf_op jit(solution)/shard_map/ppermute | solution.py:35
  36.0 2.3 %collective-permute-done.11 = bf16[512,128]{1,0:T(8,128)(2,1)S(1)} collective-permute-done((bf16[512,128]{1,0:T(8,128)(2,1)S(1)}, bf16[512,128]{1,0:T(8,128)(2,1)S(1)}, u32[]{:S(2)}, u32[]{:S(2)}) %collective-permute-start.11) | collective-permute-done | bytes 131104 | tf_op jit(solution)/shard_map/ppermute | solution.py:35
  39.5 1.6 %collective-permute-start.12 = (bf16[512,128]{1,0:T(8,128)(2,1)S(1)}, bf16[512,128]{1,0:T(8,128)(2,1)S(1)}, u32[]{:S(2)}, u32[]{:S(2)}) collective-permute-start(bf16[512,128]{1,0:T(8,128)(2,1)S(1)} %fusion.10), channel_id=1, source_target_pairs={{0,16},{8,24},{16,0},{24,8},{1,17},{9,25},{17,1},{25,9},{2,18},{10... | collective-permute-start | bytes 393224 | tf_op jit(solution)/shard_map/ppermute | solution.py:35
  41.1 2.2 %collective-permute-done.13 = bf16[512,128]{1,0:T(8,128)(2,1)S(1)} collective-permute-done((bf16[512,128]{1,0:T(8,128)(2,1)S(1)}, bf16[512,128]{1,0:T(8,128)(2,1)S(1)}, u32[]{:S(2)}, u32[]{:S(2)}) %collective-permute-start.13) | collective-permute-done | bytes 131104 | tf_op jit(solution)/shard_map/ppermute | solution.py:35
  45.6 2.6 %collective-permute-start.15 = (bf16[512,128]{1,0:T(8,128)(2,1)S(1)}, bf16[512,128]{1,0:T(8,128)(2,1)S(1)}, u32[]{:S(2)}, u32[]{:S(2)}) collective-permute-start(bf16[512,128]{1,0:T(8,128)(2,1)S(1)} %get-tuple-element.49), channel_id=1, source_target_pairs={{0,4},{1,5},{2,6},{3,7},{4,0},{5,1},{6,2},{7,3},{8,12},{9,13},{10,... | collective-permute-start | bytes 393224 | tf_op jit(solution)/shard_map/ppermute | solution.py:35
  48.2 3.6 %collective-permute-done.14 = bf16[512,128]{1,0:T(8,128)(2,1)S(1)} collective-permute-done((bf16[512,128]{1,0:T(8,128)(2,1)S(1)}, bf16[512,128]{1,0:T(8,128)(2,1)S(1)}, u32[]{:S(2)}, u32[]{:S(2)}) %collective-permute-start.14) | collective-permute-done | bytes 131104 | tf_op jit(solution)/shard_map/ppermute | solution.py:35
  51.8 2.8 %collective-permute-done.15 = bf16[512,128]{1,0:T(8,128)(2,1)S(1)} collective-permute-done((bf16[512,128]{1,0:T(8,128)(2,1)S(1)}, bf16[512,128]{1,0:T(8,128)(2,1)S(1)}, u32[]{:S(2)}, u32[]{:S(2)}) %collective-permute-start.15) | collective-permute-done | bytes 131104 | tf_op jit(solution)/shard_map/ppermute | solution.py:35
  55.6 6.3 %collective-permute-done.16 = bf16[512,128]{1,0:T(8,128)(2,1)S(1)} collective-permute-done((bf16[512,128]{1,0:T(8,128)(2,1)S(1)}, bf16[512,128]{1,0:T(8,128)(2,1)S(1)}, u32[]{:S(2)}, u32[]{:S(2)}) %collective-permute-start.16) | collective-permute-done | bytes 131104 | tf_op jit(solution)/shard_map/ppermute | solution.py:35
  64.2 1.6 %collective-permute-start.19 = (bf16[512,128]{1,0:T(8,128)(2,1)S(1)}, bf16[512,128]{1,0:T(8,128)(2,1)S(1)}, u32[]{:S(2)}, u32[]{:S(2)}) collective-permute-start(bf16[512,128]{1,0:T(8,128)(2,1)S(1)} %get-tuple-element.73), channel_id=1, source_target_pairs={{0,16},{8,24},{16,0},{24,8},{1,17},{9,25},{17,1},{25,9},{2,18},{10... | collective-permute-start | bytes 393224 | tf_op jit(solution)/shard_map/ppermute | solution.py:35
  65.8 1.9 %collective-permute-done.18 = bf16[512,128]{1,0:T(8,128)(2,1)S(1)} collective-permute-done((bf16[512,128]{1,0:T(8,128)(2,1)S(1)}, bf16[512,128]{1,0:T(8,128)(2,1)S(1)}, u32[]{:S(2)}, u32[]{:S(2)}) %collective-permute-start.18) | collective-permute-done | bytes 131104 | tf_op jit(solution)/shard_map/ppermute | solution.py:35
  70.4 1.6 %collective-permute-start.21 = (bf16[512,128]{1,0:T(8,128)(2,1)S(1)}, bf16[512,128]{1,0:T(8,128)(2,1)S(1)}, u32[]{:S(2)}, u32[]{:S(2)}) collective-permute-start(bf16[512,128]{1,0:T(8,128)(2,1)S(1)} %fusion.13), channel_id=1, source_target_pairs={{0,16},{8,24},{16,0},{24,8},{1,17},{9,25},{17,1},{25,9},{2,18},{10... | collective-permute-start | bytes 393224 | tf_op jit(solution)/shard_map/ppermute | solution.py:35
  72.0 2.3 %collective-permute-done.20 = bf16[512,128]{1,0:T(8,128)(2,1)S(1)} collective-permute-done((bf16[512,128]{1,0:T(8,128)(2,1)S(1)}, bf16[512,128]{1,0:T(8,128)(2,1)S(1)}, u32[]{:S(2)}, u32[]{:S(2)}) %collective-permute-start.20) | collective-permute-done | bytes 131104 | tf_op jit(solution)/shard_map/ppermute | solution.py:35
  79.2 2.9 %collective-permute-start.25 = (f32[136,128]{1,0:T(8,128)S(1)}, f32[136,128]{1,0:T(8,128)S(1)}, u32[]{:S(2)}, u32[]{:S(2)}) collective-permute-start(f32[136,128]{1,0:T(8,128)S(1)} %select_maximum_fusion), channel_id=1, source_target_pairs={{0,2},{1,3},{2,0},{3,1},{4,6},{5,7},{6,4},{7,5},{8,10},{9,11},{10,... | collective-permute-start | bytes 208904 | tf_op jit(solution)/shard_map/ppermute | solution.py:35
  82.2 2.4 %collective-permute-done.23 = f32[136,128]{1,0:T(8,128)S(1)} collective-permute-done((f32[136,128]{1,0:T(8,128)S(1)}, f32[136,128]{1,0:T(8,128)S(1)}, u32[]{:S(2)}, u32[]{:S(2)}) %collective-permute-start.23) | collective-permute-done | bytes 69664 | tf_op jit(solution)/shard_map/ppermute | solution.py:35
  87.5 6.9 %shard_map.38 = f32[128,256]{1,0:T(8,128)} custom-call(s32[1]{0:T(128)} %bitcast.first_ref, f32[136,128]{1,0:T(8,128)S(1)} %add_add_fusion.total_ref, f32[136,128]{1,0:T(8,128)S(1)} %collective-permute-done.26.partner_ref, f32[128,128]{1,0:T(8,128)S(1)} %fusion.23.mine_ref, f32[128,128]{1,0:T(8,128)S(1)} %constant_dynamic-slice_fusion.theirs_ref), custom_call_target="tpu_custom_call" | custom-call | tf_op jit(solution)/shard_map/pallas_call | solution.py:171
  (81 shorter events, 28.6 us)
Async XLA Ops:
  0.9 7.8 %collective-permute-start.2 = (bf16[128,256]{1,0:T(8,128)(2,1)S(1)}, bf16[128,256]{1,0:T(8,128)(2,1)S(1)}, u32[]{:S(2)}, u32[]{:S(2)}) collective-permute-start(bf16[128,256]{1,0:T(8,128)(2,1)S(1)} %convert_element_type.147), channel_id=1, source_target_pairs={{0,16},{8,24},{16,0},{24,8},{1,17},{9,25},{17,1},{25,9},{2,18},{10... | collective-permute-start | bytes 196616 | tf_op jit(solution)/shard_map/ppermute | solution.py:35
  3.9 5.7 %collective-permute-start.1 = (bf16[128,256]{1,0:T(8,128)(2,1)S(1)}, bf16[128,256]{1,0:T(8,128)(2,1)S(1)}, u32[]{:S(2)}, u32[]{:S(2)}) collective-permute-start(bf16[128,256]{1,0:T(8,128)(2,1)S(1)} %convert_element_type.147), channel_id=1, source_target_pairs={{0,24},{8,16},{16,8},{24,0},{1,25},{9,17},{17,9},{25,1},{2,26},{10... | collective-permute-start | bytes 196616 | tf_op jit(solution)/shard_map/ppermute | solution.py:35
  5.4 4.3 %collective-permute-start = (bf16[128,256]{1,0:T(8,128)(2,1)S(1)}, bf16[128,256]{1,0:T(8,128)(2,1)S(1)}, u32[]{:S(2)}, u32[]{:S(2)}) collective-permute-start(bf16[128,256]{1,0:T(8,128)(2,1)S(1)} %convert_element_type.147), channel_id=1, source_target_pairs={{0,8},{8,0},{16,24},{24,16},{1,9},{9,1},{17,25},{25,17},{2,10},{10... | collective-permute-start | bytes 196616 | tf_op jit(solution)/shard_map/ppermute | solution.py:35
  12.0 8.0 %collective-permute-start.5 = (bf16[512,128]{1,0:T(8,128)(2,1)S(1)}, bf16[512,128]{1,0:T(8,128)(2,1)S(1)}, u32[]{:S(2)}, u32[]{:S(2)}) collective-permute-start(bf16[512,128]{1,0:T(8,128)(2,1)S(1)} %get-tuple-element.56), channel_id=1, source_target_pairs={{0,2},{1,3},{2,0},{3,1},{4,6},{5,7},{6,4},{7,5},{8,10},{9,11},{10,... | collective-permute-start | bytes 393224 | tf_op jit(solution)/shard_map/ppermute | solution.py:35
  13.7 9.0 %collective-permute-start.6 = (bf16[512,128]{1,0:T(8,128)(2,1)S(1)}, bf16[512,128]{1,0:T(8,128)(2,1)S(1)}, u32[]{:S(2)}, u32[]{:S(2)}) collective-permute-start(bf16[512,128]{1,0:T(8,128)(2,1)S(1)} %get-tuple-element.55), channel_id=1, source_target_pairs={{0,4},{1,5},{2,6},{3,7},{4,0},{5,1},{6,2},{7,3},{8,12},{9,13},{10,... | collective-permute-start | bytes 393224 | tf_op jit(solution)/shard_map/ppermute | solution.py:35
  16.9 9.0 %collective-permute-start.10 = (f32[128,128]{1,0:T(8,128)}, f32[128,128]{1,0:T(8,128)S(1)}, u32[]{:S(2)}, u32[]{:S(2)}) collective-permute-start(f32[128,128]{1,0:T(8,128)} %get-tuple-element.64), channel_id=1, source_target_pairs={{0,1},{1,0},{2,3},{3,2},{4,5},{5,4},{6,7},{7,6},{8,9},{9,8},{10,11... | collective-permute-start | bytes 196616 | tf_op jit(solution)/shard_map/ppermute | solution.py:35
  16.9 14.9 %collective-permute-start.4 = (bf16[1024,512]{1,0:T(8,128)(2,1)S(1)}, bf16[1024,512]{1,0:T(8,128)(2,1)S(1)}, u32[]{:S(2)}, u32[]{:S(2)}) collective-permute-start(bf16[1024,512]{1,0:T(8,128)(2,1)S(1)} %shard_map.37), channel_id=1, source_target_pairs={{0,1},{1,0},{2,3},{3,2},{4,5},{5,4},{6,7},{7,6},{8,9},{9,8},{10,11... | collective-permute-start | bytes 3145736 | tf_op jit(solution)/shard_map/ppermute | solution.py:35
  22.7 7.3 %collective-permute-start.7 = (bf16[512,128]{1,0:T(8,128)(2,1)S(1)}, bf16[512,128]{1,0:T(8,128)(2,1)S(1)}, u32[]{:S(2)}, u32[]{:S(2)}) collective-permute-start(bf16[512,128]{1,0:T(8,128)(2,1)S(1)} %get-tuple-element.54), channel_id=1, source_target_pairs={{0,4},{1,5},{2,6},{3,7},{4,0},{5,1},{6,2},{7,3},{8,12},{9,13},{10,... | collective-permute-start | bytes 393224 | tf_op jit(solution)/shard_map/ppermute | solution.py:35
  23.1 7.0 %collective-permute-start.8 = (bf16[512,128]{1,0:T(8,128)(2,1)S(1)}, bf16[512,128]{1,0:T(8,128)(2,1)S(1)}, u32[]{:S(2)}, u32[]{:S(2)}) collective-permute-start(bf16[512,128]{1,0:T(8,128)(2,1)S(1)} %get-tuple-element.53), channel_id=1, source_target_pairs={{0,2},{1,3},{2,0},{3,1},{4,6},{5,7},{6,4},{7,5},{8,10},{9,11},{10,... | collective-permute-start | bytes 393224 | tf_op jit(solution)/shard_map/ppermute | solution.py:35
  30.8 5.2 %collective-permute-start.9 = (bf16[512,128]{1,0:T(8,128)(2,1)S(1)}, bf16[512,128]{1,0:T(8,128)(2,1)S(1)}, u32[]{:S(2)}, u32[]{:S(2)}) collective-permute-start(bf16[512,128]{1,0:T(8,128)(2,1)S(1)} %get-tuple-element.67), channel_id=1, source_target_pairs={{0,8},{8,0},{16,24},{24,16},{1,9},{9,1},{17,25},{25,17},{2,10},{10... | collective-permute-start | bytes 393224 | tf_op jit(solution)/shard_map/ppermute | solution.py:35
  32.3 5.9 %collective-permute-start.11 = (bf16[512,128]{1,0:T(8,128)(2,1)S(1)}, bf16[512,128]{1,0:T(8,128)(2,1)S(1)}, u32[]{:S(2)}, u32[]{:S(2)}) collective-permute-start(bf16[512,128]{1,0:T(8,128)(2,1)S(1)} %get-tuple-element.69), channel_id=1, source_target_pairs={{0,16},{8,24},{16,0},{24,8},{1,17},{9,25},{17,1},{25,9},{2,18},{10... | collective-permute-start | bytes 393224 | tf_op jit(solution)/shard_map/ppermute | solution.py:35
  38.3 5.0 %collective-permute-start.13 = (bf16[512,128]{1,0:T(8,128)(2,1)S(1)}, bf16[512,128]{1,0:T(8,128)(2,1)S(1)}, u32[]{:S(2)}, u32[]{:S(2)}) collective-permute-start(bf16[512,128]{1,0:T(8,128)(2,1)S(1)} %fusion.11), channel_id=1, source_target_pairs={{0,8},{8,0},{16,24},{24,16},{1,9},{9,1},{17,25},{25,17},{2,10},{10... | collective-permute-start | bytes 393224 | tf_op jit(solution)/shard_map/ppermute | solution.py:35
  39.5 5.0 %collective-permute-start.12 = (bf16[512,128]{1,0:T(8,128)(2,1)S(1)}, bf16[512,128]{1,0:T(8,128)(2,1)S(1)}, u32[]{:S(2)}, u32[]{:S(2)}) collective-permute-start(bf16[512,128]{1,0:T(8,128)(2,1)S(1)} %fusion.10), channel_id=1, source_target_pairs={{0,16},{8,24},{16,0},{24,8},{1,17},{9,25},{17,1},{25,9},{2,18},{10... | collective-permute-start | bytes 393224 | tf_op jit(solution)/shard_map/ppermute | solution.py:35
  45.6 6.3 %collective-permute-start.14 = (bf16[512,128]{1,0:T(8,128)(2,1)S(1)}, bf16[512,128]{1,0:T(8,128)(2,1)S(1)}, u32[]{:S(2)}, u32[]{:S(2)}) collective-permute-start(bf16[512,128]{1,0:T(8,128)(2,1)S(1)} %get-tuple-element.50), channel_id=1, source_target_pairs={{0,2},{1,3},{2,0},{3,1},{4,6},{5,7},{6,4},{7,5},{8,10},{9,11},{10,... | collective-permute-start | bytes 393224 | tf_op jit(solution)/shard_map/ppermute | solution.py:35
  45.6 9.0 %collective-permute-start.15 = (bf16[512,128]{1,0:T(8,128)(2,1)S(1)}, bf16[512,128]{1,0:T(8,128)(2,1)S(1)}, u32[]{:S(2)}, u32[]{:S(2)}) collective-permute-start(bf16[512,128]{1,0:T(8,128)(2,1)S(1)} %get-tuple-element.49), channel_id=1, source_target_pairs={{0,4},{1,5},{2,6},{3,7},{4,0},{5,1},{6,2},{7,3},{8,12},{9,13},{10,... | collective-permute-start | bytes 393224 | tf_op jit(solution)/shard_map/ppermute | solution.py:35
  54.7 7.2 %collective-permute-start.16 = (bf16[512,128]{1,0:T(8,128)(2,1)S(1)}, bf16[512,128]{1,0:T(8,128)(2,1)S(1)}, u32[]{:S(2)}, u32[]{:S(2)}) collective-permute-start(bf16[512,128]{1,0:T(8,128)(2,1)S(1)} %get-tuple-element.48), channel_id=1, source_target_pairs={{0,4},{1,5},{2,6},{3,7},{4,0},{5,1},{6,2},{7,3},{8,12},{9,13},{10,... | collective-permute-start | bytes 393224 | tf_op jit(solution)/shard_map/ppermute | solution.py:35
  55.6 6.4 %collective-permute-start.17 = (bf16[512,128]{1,0:T(8,128)(2,1)S(1)}, bf16[512,128]{1,0:T(8,128)(2,1)S(1)}, u32[]{:S(2)}, u32[]{:S(2)}) collective-permute-start(bf16[512,128]{1,0:T(8,128)(2,1)S(1)} %get-tuple-element.47), channel_id=1, source_target_pairs={{0,2},{1,3},{2,0},{3,1},{4,6},{5,7},{6,4},{7,5},{8,10},{9,11},{10,... | collective-permute-start | bytes 393224 | tf_op jit(solution)/shard_map/ppermute | solution.py:35
  62.7 5.0 %collective-permute-start.18 = (bf16[512,128]{1,0:T(8,128)(2,1)S(1)}, bf16[512,128]{1,0:T(8,128)(2,1)S(1)}, u32[]{:S(2)}, u32[]{:S(2)}) collective-permute-start(bf16[512,128]{1,0:T(8,128)(2,1)S(1)} %get-tuple-element.71), channel_id=1, source_target_pairs={{0,8},{8,0},{16,24},{24,16},{1,9},{9,1},{17,25},{25,17},{2,10},{10... | collective-permute-start | bytes 393224 | tf_op jit(solution)/shard_map/ppermute | solution.py:35
  64.2 5.0 %collective-permute-start.19 = (bf16[512,128]{1,0:T(8,128)(2,1)S(1)}, bf16[512,128]{1,0:T(8,128)(2,1)S(1)}, u32[]{:S(2)}, u32[]{:S(2)}) collective-permute-start(bf16[512,128]{1,0:T(8,128)(2,1)S(1)} %get-tuple-element.73), channel_id=1, source_target_pairs={{0,16},{8,24},{16,0},{24,8},{1,17},{9,25},{17,1},{25,9},{2,18},{10... | collective-permute-start | bytes 393224 | tf_op jit(solution)/shard_map/ppermute | solution.py:35
  69.3 5.0 %collective-permute-start.20 = (bf16[512,128]{1,0:T(8,128)(2,1)S(1)}, bf16[512,128]{1,0:T(8,128)(2,1)S(1)}, u32[]{:S(2)}, u32[]{:S(2)}) collective-permute-start(bf16[512,128]{1,0:T(8,128)(2,1)S(1)} %fusion.12), channel_id=1, source_target_pairs={{0,8},{8,0},{16,24},{24,16},{1,9},{9,1},{17,25},{25,17},{2,10},{10... | collective-permute-start | bytes 393224 | tf_op jit(solution)/shard_map/ppermute | solution.py:35
  70.4 5.0 %collective-permute-start.21 = (bf16[512,128]{1,0:T(8,128)(2,1)S(1)}, bf16[512,128]{1,0:T(8,128)(2,1)S(1)}, u32[]{:S(2)}, u32[]{:S(2)}) collective-permute-start(bf16[512,128]{1,0:T(8,128)(2,1)S(1)} %fusion.13), channel_id=1, source_target_pairs={{0,16},{8,24},{16,0},{24,8},{1,17},{9,25},{17,1},{25,9},{2,18},{10... | collective-permute-start | bytes 393224 | tf_op jit(solution)/shard_map/ppermute | solution.py:35
  77.7 6.9 %collective-permute-start.23 = (f32[136,128]{1,0:T(8,128)S(1)}, f32[136,128]{1,0:T(8,128)S(1)}, u32[]{:S(2)}, u32[]{:S(2)}) collective-permute-start(f32[136,128]{1,0:T(8,128)S(1)} %select_maximum_fusion), channel_id=1, source_target_pairs={{0,6},{1,7},{2,4},{3,5},{4,2},{5,3},{6,0},{7,1},{8,14},{9,15},{10,... | collective-permute-start | bytes 208904 | tf_op jit(solution)/shard_map/ppermute | solution.py:35
  78.3 7.8 %collective-permute-start.24 = (f32[136,128]{1,0:T(8,128)S(1)}, f32[136,128]{1,0:T(8,128)S(1)}, u32[]{:S(2)}, u32[]{:S(2)}) collective-permute-start(f32[136,128]{1,0:T(8,128)S(1)} %select_maximum_fusion), channel_id=1, source_target_pairs={{0,4},{1,5},{2,6},{3,7},{4,0},{5,1},{6,2},{7,3},{8,12},{9,13},{10,... | collective-permute-start | bytes 208904 | tf_op jit(solution)/shard_map/ppermute | solution.py:35
  79.2 6.9 %collective-permute-start.25 = (f32[136,128]{1,0:T(8,128)S(1)}, f32[136,128]{1,0:T(8,128)S(1)}, u32[]{:S(2)}, u32[]{:S(2)}) collective-permute-start(f32[136,128]{1,0:T(8,128)S(1)} %select_maximum_fusion), channel_id=1, source_target_pairs={{0,2},{1,3},{2,0},{3,1},{4,6},{5,7},{6,4},{7,5},{8,10},{9,11},{10,... | collective-permute-start | bytes 208904 | tf_op jit(solution)/shard_map/ppermute | solution.py:35
  (6 other events, 12.6 us)

commit v13 on v12

--- a/solution.py
+++ b/solution.py
@@ -64,7 +64,7 @@
     def kernel(index_ref, blocks_ref, tile_ref):
         nothing = jnp.zeros((width, width), blocks.dtype)
         for inner in range(step):
-            places = [index_ref[pl.program_id(0) * step + inner, slot] for slot in range(slots)]
+            places = [index_ref[inner, slot] for slot in range(slots)]
             places = [jnp.where(place >= 0, lax.rem(place, tile_blocks), -1) for place in places]
             for column in range(tile_blocks):
                 value = nothing
@@ -74,12 +74,8 @@
 
     return pl.pallas_call(
         kernel,
-        grid_spec=pltpu.PrefetchScalarGridSpec(
-            num_scalar_prefetch=1,
-            grid=(group_rows // step,),
-            in_specs=[pl.BlockSpec((step, slots, width, width), lambda i, index: (i, 0, 0, 0))],
-            out_specs=pl.BlockSpec((step * width, tile_blocks * width), lambda i, index: (i, 0)),
-        ),
+        in_specs=[pl.BlockSpec(memory_space=pltpu.SMEM), pl.BlockSpec(memory_space=pltpu.VMEM)],
+        out_specs=pl.BlockSpec(memory_space=pltpu.VMEM),
         out_shape=jax.ShapeDtypeStruct((group_rows * width, tile_blocks * width), blocks.dtype),
         compiler_params=pltpu.CompilerParams(vmem_limit_bytes=24 << 20),
     )(col_index, blocks)

time: 94.6 us -> 94.6 us (level)
  no operation moved by 1% of the time
where the time goes in v13:
time: 94.6 us; the launch traced here: 94.4 us
  waiting for transfers between devices  44.9 us (47%)
  starting transfers between devices  31.3 us (33%)
  Pallas kernels  7.91 us (8%)
  matrix products  4.71 us (5%)
  other arithmetic  3.03 us (3%)
  local copies, waits for them, and re-layouts  2.29 us (2%)
    ppermute x27, waiting for transfers between devices, swap(): return lax.ppermute(value, axis, [(i, i ^ distance) for i in range(count)])  44.9 us
    ppermute x27, starting transfers between devices, swap(): return lax.ppermute(value, axis, [(i, i ^ distance) for i in range(count)])  31.3 us
    pallas_call x1, Pallas kernels, orthonormal(): pl.pallas_call(kernel, in_specs=[pl.BlockSpec(memory_space=pltpu.SMEM), v...  6.92 us
    unnamed x6, local copies, waits for them, and re-layouts  2.1 us
    dot_general x4, matrix products, part(): lax.dot_general(tile, low, (((0,), (0,)), ((), ())), preferred_element_ty...  1.91 us
  transfers between devices with their start and end apart: 27, of which 20 were waited for; matrix products, arithmetic and copies ran while one was open for 4% of the time, Pallas kernels for 1%

profile of v13, /device:TPU:0, one launch (start us, length us, event | category | flops | bytes accessed | tf_op | source)
XLA Modules:
  0.0 94.4 jit_solution(11155339536926811624)
XLA Ops:
  0.9 3.0 %collective-permute-start.2 = (bf16[128,256]{1,0:T(8,128)(2,1)S(1)}, bf16[128,256]{1,0:T(8,128)(2,1)S(1)}, u32[]{:S(2)}, u32[]{:S(2)}) collective-permute-start(bf16[128,256]{1,0:T(8,128)(2,1)S(1)} %convert_element_type.147), channel_id=1, source_target_pairs={{0,16},{8,24},{16,0},{24,8},{1,17},{9,25},{17,1},{25,9},{2,18},{10... | collective-permute-start | bytes 196616 | tf_op jit(solution)/shard_map/ppermute | solution.py:35
  10.4 1.5 %collective-permute-done.3 = bf16[1024,128]{1,0:T(8,128)(2,1)S(1)} collective-permute-done((bf16[1024,128]{1,0:T(8,128)(2,1)S(1)}, bf16[1024,128]{1,0:T(8,128)(2,1)S(1)}, u32[]{:S(2)}, u32[]{:S(2)}) %collective-permute-start.3) | collective-permute-done | bytes 262176 | tf_op jit(solution)/shard_map/ppermute | solution.py:35
  12.0 1.6 %collective-permute-start.5 = (bf16[512,128]{1,0:T(8,128)(2,1)S(1)}, bf16[512,128]{1,0:T(8,128)(2,1)S(1)}, u32[]{:S(2)}, u32[]{:S(2)}) collective-permute-start(bf16[512,128]{1,0:T(8,128)(2,1)S(1)} %get-tuple-element.56), channel_id=1, source_target_pairs={{0,2},{1,3},{2,0},{3,1},{4,6},{5,7},{6,4},{7,5},{8,10},{9,11},{10,... | collective-permute-start | bytes 393224 | tf_op jit(solution)/shard_map/ppermute | solution.py:35
  13.7 2.6 %collective-permute-start.6 = (bf16[512,128]{1,0:T(8,128)(2,1)S(1)}, bf16[512,128]{1,0:T(8,128)(2,1)S(1)}, u32[]{:S(2)}, u32[]{:S(2)}) collective-permute-start(bf16[512,128]{1,0:T(8,128)(2,1)S(1)} %get-tuple-element.55), channel_id=1, source_target_pairs={{0,4},{1,5},{2,6},{3,7},{4,0},{5,1},{6,2},{7,3},{8,12},{9,13},{10,... | collective-permute-start | bytes 393224 | tf_op jit(solution)/shard_map/ppermute | solution.py:35
  17.4 2.6 %collective-permute-done.5 = bf16[512,128]{1,0:T(8,128)(2,1)S(1)} collective-permute-done((bf16[512,128]{1,0:T(8,128)(2,1)S(1)}, bf16[512,128]{1,0:T(8,128)(2,1)S(1)}, u32[]{:S(2)}, u32[]{:S(2)}) %collective-permute-start.5) | collective-permute-done | bytes 131104 | tf_op jit(solution)/shard_map/ppermute | solution.py:35
  20.0 2.7 %collective-permute-done.6 = bf16[512,128]{1,0:T(8,128)(2,1)S(1)} collective-permute-done((bf16[512,128]{1,0:T(8,128)(2,1)S(1)}, bf16[512,128]{1,0:T(8,128)(2,1)S(1)}, u32[]{:S(2)}, u32[]{:S(2)}) %collective-permute-start.6) | collective-permute-done | bytes 131104 | tf_op jit(solution)/shard_map/ppermute | solution.py:35
  23.1 2.7 %collective-permute-start.8 = (bf16[512,128]{1,0:T(8,128)(2,1)S(1)}, bf16[512,128]{1,0:T(8,128)(2,1)S(1)}, u32[]{:S(2)}, u32[]{:S(2)}) collective-permute-start(bf16[512,128]{1,0:T(8,128)(2,1)S(1)} %get-tuple-element.53), channel_id=1, source_target_pairs={{0,2},{1,3},{2,0},{3,1},{4,6},{5,7},{6,4},{7,5},{8,10},{9,11},{10,... | collective-permute-start | bytes 393224 | tf_op jit(solution)/shard_map/ppermute | solution.py:35
  26.1 4.0 %collective-permute-done.7 = bf16[512,128]{1,0:T(8,128)(2,1)S(1)} collective-permute-done((bf16[512,128]{1,0:T(8,128)(2,1)S(1)}, bf16[512,128]{1,0:T(8,128)(2,1)S(1)}, u32[]{:S(2)}, u32[]{:S(2)}) %collective-permute-start.7) | collective-permute-done | bytes 131104 | tf_op jit(solution)/shard_map/ppermute | solution.py:35
  32.3 1.5 %collective-permute-start.11 = (bf16[512,128]{1,0:T(8,128)(2,1)S(1)}, bf16[512,128]{1,0:T(8,128)(2,1)S(1)}, u32[]{:S(2)}, u32[]{:S(2)}) collective-permute-start(bf16[512,128]{1,0:T(8,128)(2,1)S(1)} %get-tuple-element.69), channel_id=1, source_target_pairs={{0,16},{8,24},{16,0},{24,8},{1,17},{9,25},{17,1},{25,9},{2,18},{10... | collective-permute-start | bytes 393224 | tf_op jit(solution)/shard_map/ppermute | solution.py:35
  33.8 2.2 %collective-permute-done.9 = bf16[512,128]{1,0:T(8,128)(2,1)S(1)} collective-permute-done((bf16[512,128]{1,0:T(8,128)(2,1)S(1)}, bf16[512,128]{1,0:T(8,128)(2,1)S(1)}, u32[]{:S(2)}, u32[]{:S(2)}) %collective-permute-start.9) | collective-permute-done | bytes 131104 | tf_op jit(solution)/shard_map/ppermute | solution.py:35
  36.0 2.2 %collective-permute-done.11 = bf16[512,128]{1,0:T(8,128)(2,1)S(1)} collective-permute-done((bf16[512,128]{1,0:T(8,128)(2,1)S(1)}, bf16[512,128]{1,0:T(8,128)(2,1)S(1)}, u32[]{:S(2)}, u32[]{:S(2)}) %collective-permute-start.11) | collective-permute-done | bytes 131104 | tf_op jit(solution)/shard_map/ppermute | solution.py:35
  39.5 1.7 %collective-permute-start.12 = (bf16[512,128]{1,0:T(8,128)(2,1)S(1)}, bf16[512,128]{1,0:T(8,128)(2,1)S(1)}, u32[]{:S(2)}, u32[]{:S(2)}) collective-permute-start(bf16[512,128]{1,0:T(8,128)(2,1)S(1)} %fusion.10), channel_id=1, source_target_pairs={{0,16},{8,24},{16,0},{24,8},{1,17},{9,25},{17,1},{25,9},{2,18},{10... | collective-permute-start | bytes 393224 | tf_op jit(solution)/shard_map/ppermute | solution.py:35
  41.2 2.1 %collective-permute-done.13 = bf16[512,128]{1,0:T(8,128)(2,1)S(1)} collective-permute-done((bf16[512,128]{1,0:T(8,128)(2,1)S(1)}, bf16[512,128]{1,0:T(8,128)(2,1)S(1)}, u32[]{:S(2)}, u32[]{:S(2)}) %collective-permute-start.13) | collective-permute-done | bytes 131104 | tf_op jit(solution)/shard_map/ppermute | solution.py:35
  45.7 2.5 %collective-permute-start.15 = (bf16[512,128]{1,0:T(8,128)(2,1)S(1)}, bf16[512,128]{1,0:T(8,128)(2,1)S(1)}, u32[]{:S(2)}, u32[]{:S(2)}) collective-permute-start(bf16[512,128]{1,0:T(8,128)(2,1)S(1)} %get-tuple-element.49), channel_id=1, source_target_pairs={{0,4},{1,5},{2,6},{3,7},{4,0},{5,1},{6,2},{7,3},{8,12},{9,13},{10,... | collective-permute-start | bytes 393224 | tf_op jit(solution)/shard_map/ppermute | solution.py:35
  48.2 3.6 %collective-permute-done.14 = bf16[512,128]{1,0:T(8,128)(2,1)S(1)} collective-permute-done((bf16[512,128]{1,0:T(8,128)(2,1)S(1)}, bf16[512,128]{1,0:T(8,128)(2,1)S(1)}, u32[]{:S(2)}, u32[]{:S(2)}) %collective-permute-start.14) | collective-permute-done | bytes 131104 | tf_op jit(solution)/shard_map/ppermute | solution.py:35
  51.8 2.8 %collective-permute-done.15 = bf16[512,128]{1,0:T(8,128)(2,1)S(1)} collective-permute-done((bf16[512,128]{1,0:T(8,128)(2,1)S(1)}, bf16[512,128]{1,0:T(8,128)(2,1)S(1)}, u32[]{:S(2)}, u32[]{:S(2)}) %collective-permute-start.15) | collective-permute-done | bytes 131104 | tf_op jit(solution)/shard_map/ppermute | solution.py:35
  55.6 6.3 %collective-permute-done.16 = bf16[512,128]{1,0:T(8,128)(2,1)S(1)} collective-permute-done((bf16[512,128]{1,0:T(8,128)(2,1)S(1)}, bf16[512,128]{1,0:T(8,128)(2,1)S(1)}, u32[]{:S(2)}, u32[]{:S(2)}) %collective-permute-start.16) | collective-permute-done | bytes 131104 | tf_op jit(solution)/shard_map/ppermute | solution.py:35
  64.2 1.5 %collective-permute-start.19 = (bf16[512,128]{1,0:T(8,128)(2,1)S(1)}, bf16[512,128]{1,0:T(8,128)(2,1)S(1)}, u32[]{:S(2)}, u32[]{:S(2)}) collective-permute-start(bf16[512,128]{1,0:T(8,128)(2,1)S(1)} %get-tuple-element.73), channel_id=1, source_target_pairs={{0,16},{8,24},{16,0},{24,8},{1,17},{9,25},{17,1},{25,9},{2,18},{10... | collective-permute-start | bytes 393224 | tf_op jit(solution)/shard_map/ppermute | solution.py:35
  65.7 2.0 %collective-permute-done.18 = bf16[512,128]{1,0:T(8,128)(2,1)S(1)} collective-permute-done((bf16[512,128]{1,0:T(8,128)(2,1)S(1)}, bf16[512,128]{1,0:T(8,128)(2,1)S(1)}, u32[]{:S(2)}, u32[]{:S(2)}) %collective-permute-start.18) | collective-permute-done | bytes 131104 | tf_op jit(solution)/shard_map/ppermute | solution.py:35
  70.4 1.6 %collective-permute-start.21 = (bf16[512,128]{1,0:T(8,128)(2,1)S(1)}, bf16[512,128]{1,0:T(8,128)(2,1)S(1)}, u32[]{:S(2)}, u32[]{:S(2)}) collective-permute-start(bf16[512,128]{1,0:T(8,128)(2,1)S(1)} %fusion.13), channel_id=1, source_target_pairs={{0,16},{8,24},{16,0},{24,8},{1,17},{9,25},{17,1},{25,9},{2,18},{10... | collective-permute-start | bytes 393224 | tf_op jit(solution)/shard_map/ppermute | solution.py:35
  72.0 2.3 %collective-permute-done.20 = bf16[512,128]{1,0:T(8,128)(2,1)S(1)} collective-permute-done((bf16[512,128]{1,0:T(8,128)(2,1)S(1)}, bf16[512,128]{1,0:T(8,128)(2,1)S(1)}, u32[]{:S(2)}, u32[]{:S(2)}) %collective-permute-start.20) | collective-permute-done | bytes 131104 | tf_op jit(solution)/shard_map/ppermute | solution.py:35
  79.2 2.9 %collective-permute-start.25 = (f32[136,128]{1,0:T(8,128)S(1)}, f32[136,128]{1,0:T(8,128)S(1)}, u32[]{:S(2)}, u32[]{:S(2)}) collective-permute-start(f32[136,128]{1,0:T(8,128)S(1)} %select_maximum_fusion), channel_id=1, source_target_pairs={{0,2},{1,3},{2,0},{3,1},{4,6},{5,7},{6,4},{7,5},{8,10},{9,11},{10,... | collective-permute-start | bytes 208904 | tf_op jit(solution)/shard_map/ppermute | solution.py:35
  82.2 2.4 %collective-permute-done.23 = f32[136,128]{1,0:T(8,128)S(1)} collective-permute-done((f32[136,128]{1,0:T(8,128)S(1)}, f32[136,128]{1,0:T(8,128)S(1)}, u32[]{:S(2)}, u32[]{:S(2)}) %collective-permute-start.23) | collective-permute-done | bytes 69664 | tf_op jit(solution)/shard_map/ppermute | solution.py:35
  87.5 6.9 %shard_map.38 = f32[128,256]{1,0:T(8,128)} custom-call(s32[1]{0:T(128)} %bitcast.first_ref, f32[136,128]{1,0:T(8,128)S(1)} %add_add_fusion.total_ref, f32[136,128]{1,0:T(8,128)S(1)} %collective-permute-done.26.partner_ref, f32[128,128]{1,0:T(8,128)S(1)} %fusion.23.mine_ref, f32[128,128]{1,0:T(8,128)S(1)} %constant_dynamic-slice_fusion.theirs_ref), custom_call_target="tpu_custom_call" | custom-call | tf_op jit(solution)/shard_map/pallas_call | solution.py:167
  (81 shorter events, 28.7 us)
Async XLA Ops:
  0.9 7.7 %collective-permute-start.2 = (bf16[128,256]{1,0:T(8,128)(2,1)S(1)}, bf16[128,256]{1,0:T(8,128)(2,1)S(1)}, u32[]{:S(2)}, u32[]{:S(2)}) collective-permute-start(bf16[128,256]{1,0:T(8,128)(2,1)S(1)} %convert_element_type.147), channel_id=1, source_target_pairs={{0,16},{8,24},{16,0},{24,8},{1,17},{9,25},{17,1},{25,9},{2,18},{10... | collective-permute-start | bytes 196616 | tf_op jit(solution)/shard_map/ppermute | solution.py:35
  3.9 5.7 %collective-permute-start.1 = (bf16[128,256]{1,0:T(8,128)(2,1)S(1)}, bf16[128,256]{1,0:T(8,128)(2,1)S(1)}, u32[]{:S(2)}, u32[]{:S(2)}) collective-permute-start(bf16[128,256]{1,0:T(8,128)(2,1)S(1)} %convert_element_type.147), channel_id=1, source_target_pairs={{0,24},{8,16},{16,8},{24,0},{1,25},{9,17},{17,9},{25,1},{2,26},{10... | collective-permute-start | bytes 196616 | tf_op jit(solution)/shard_map/ppermute | solution.py:35
  5.4 4.3 %collective-permute-start = (bf16[128,256]{1,0:T(8,128)(2,1)S(1)}, bf16[128,256]{1,0:T(8,128)(2,1)S(1)}, u32[]{:S(2)}, u32[]{:S(2)}) collective-permute-start(bf16[128,256]{1,0:T(8,128)(2,1)S(1)} %convert_element_type.147), channel_id=1, source_target_pairs={{0,8},{8,0},{16,24},{24,16},{1,9},{9,1},{17,25},{25,17},{2,10},{10... | collective-permute-start | bytes 196616 | tf_op jit(solution)/shard_map/ppermute | solution.py:35
  12.0 8.0 %collective-permute-start.5 = (bf16[512,128]{1,0:T(8,128)(2,1)S(1)}, bf16[512,128]{1,0:T(8,128)(2,1)S(1)}, u32[]{:S(2)}, u32[]{:S(2)}) collective-permute-start(bf16[512,128]{1,0:T(8,128)(2,1)S(1)} %get-tuple-element.56), channel_id=1, source_target_pairs={{0,2},{1,3},{2,0},{3,1},{4,6},{5,7},{6,4},{7,5},{8,10},{9,11},{10,... | collective-permute-start | bytes 393224 | tf_op jit(solution)/shard_map/ppermute | solution.py:35
  13.7 9.0 %collective-permute-start.6 = (bf16[512,128]{1,0:T(8,128)(2,1)S(1)}, bf16[512,128]{1,0:T(8,128)(2,1)S(1)}, u32[]{:S(2)}, u32[]{:S(2)}) collective-permute-start(bf16[512,128]{1,0:T(8,128)(2,1)S(1)} %get-tuple-element.55), channel_id=1, source_target_pairs={{0,4},{1,5},{2,6},{3,7},{4,0},{5,1},{6,2},{7,3},{8,12},{9,13},{10,... | collective-permute-start | bytes 393224 | tf_op jit(solution)/shard_map/ppermute | solution.py:35
  16.9 9.0 %collective-permute-start.10 = (f32[128,128]{1,0:T(8,128)}, f32[128,128]{1,0:T(8,128)S(1)}, u32[]{:S(2)}, u32[]{:S(2)}) collective-permute-start(f32[128,128]{1,0:T(8,128)} %get-tuple-element.64), channel_id=1, source_target_pairs={{0,1},{1,0},{2,3},{3,2},{4,5},{5,4},{6,7},{7,6},{8,9},{9,8},{10,11... | collective-permute-start | bytes 196616 | tf_op jit(solution)/shard_map/ppermute | solution.py:35
  16.9 14.9 %collective-permute-start.4 = (bf16[1024,512]{1,0:T(8,128)(2,1)S(1)}, bf16[1024,512]{1,0:T(8,128)(2,1)S(1)}, u32[]{:S(2)}, u32[]{:S(2)}) collective-permute-start(bf16[1024,512]{1,0:T(8,128)(2,1)S(1)} %shard_map.37), channel_id=1, source_target_pairs={{0,1},{1,0},{2,3},{3,2},{4,5},{5,4},{6,7},{7,6},{8,9},{9,8},{10,11... | collective-permute-start | bytes 3145736 | tf_op jit(solution)/shard_map/ppermute | solution.py:35
  22.7 7.3 %collective-permute-start.7 = (bf16[512,128]{1,0:T(8,128)(2,1)S(1)}, bf16[512,128]{1,0:T(8,128)(2,1)S(1)}, u32[]{:S(2)}, u32[]{:S(2)}) collective-permute-start(bf16[512,128]{1,0:T(8,128)(2,1)S(1)} %get-tuple-element.54), channel_id=1, source_target_pairs={{0,4},{1,5},{2,6},{3,7},{4,0},{5,1},{6,2},{7,3},{8,12},{9,13},{10,... | collective-permute-start | bytes 393224 | tf_op jit(solution)/shard_map/ppermute | solution.py:35
  23.1 7.0 %collective-permute-start.8 = (bf16[512,128]{1,0:T(8,128)(2,1)S(1)}, bf16[512,128]{1,0:T(8,128)(2,1)S(1)}, u32[]{:S(2)}, u32[]{:S(2)}) collective-permute-start(bf16[512,128]{1,0:T(8,128)(2,1)S(1)} %get-tuple-element.53), channel_id=1, source_target_pairs={{0,2},{1,3},{2,0},{3,1},{4,6},{5,7},{6,4},{7,5},{8,10},{9,11},{10,... | collective-permute-start | bytes 393224 | tf_op jit(solution)/shard_map/ppermute | solution.py:35
  30.8 5.2 %collective-permute-start.9 = (bf16[512,128]{1,0:T(8,128)(2,1)S(1)}, bf16[512,128]{1,0:T(8,128)(2,1)S(1)}, u32[]{:S(2)}, u32[]{:S(2)}) collective-permute-start(bf16[512,128]{1,0:T(8,128)(2,1)S(1)} %get-tuple-element.67), channel_id=1, source_target_pairs={{0,8},{8,0},{16,24},{24,16},{1,9},{9,1},{17,25},{25,17},{2,10},{10... | collective-permute-start | bytes 393224 | tf_op jit(solution)/shard_map/ppermute | solution.py:35
  32.3 5.9 %collective-permute-start.11 = (bf16[512,128]{1,0:T(8,128)(2,1)S(1)}, bf16[512,128]{1,0:T(8,128)(2,1)S(1)}, u32[]{:S(2)}, u32[]{:S(2)}) collective-permute-start(bf16[512,128]{1,0:T(8,128)(2,1)S(1)} %get-tuple-element.69), channel_id=1, source_target_pairs={{0,16},{8,24},{16,0},{24,8},{1,17},{9,25},{17,1},{25,9},{2,18},{10... | collective-permute-start | bytes 393224 | tf_op jit(solution)/shard_map/ppermute | solution.py:35
  38.2 5.0 %collective-permute-start.13 = (bf16[512,128]{1,0:T(8,128)(2,1)S(1)}, bf16[512,128]{1,0:T(8,128)(2,1)S(1)}, u32[]{:S(2)}, u32[]{:S(2)}) collective-permute-start(bf16[512,128]{1,0:T(8,128)(2,1)S(1)} %fusion.11), channel_id=1, source_target_pairs={{0,8},{8,0},{16,24},{24,16},{1,9},{9,1},{17,25},{25,17},{2,10},{10... | collective-permute-start | bytes 393224 | tf_op jit(solution)/shard_map/ppermute | solution.py:35
  39.5 5.0 %collective-permute-start.12 = (bf16[512,128]{1,0:T(8,128)(2,1)S(1)}, bf16[512,128]{1,0:T(8,128)(2,1)S(1)}, u32[]{:S(2)}, u32[]{:S(2)}) collective-permute-start(bf16[512,128]{1,0:T(8,128)(2,1)S(1)} %fusion.10), channel_id=1, source_target_pairs={{0,16},{8,24},{16,0},{24,8},{1,17},{9,25},{17,1},{25,9},{2,18},{10... | collective-permute-start | bytes 393224 | tf_op jit(solution)/shard_map/ppermute | solution.py:35
  45.6 6.3 %collective-permute-start.14 = (bf16[512,128]{1,0:T(8,128)(2,1)S(1)}, bf16[512,128]{1,0:T(8,128)(2,1)S(1)}, u32[]{:S(2)}, u32[]{:S(2)}) collective-permute-start(bf16[512,128]{1,0:T(8,128)(2,1)S(1)} %get-tuple-element.50), channel_id=1, source_target_pairs={{0,2},{1,3},{2,0},{3,1},{4,6},{5,7},{6,4},{7,5},{8,10},{9,11},{10,... | collective-permute-start | bytes 393224 | tf_op jit(solution)/shard_map/ppermute | solution.py:35
  45.7 9.0 %collective-permute-start.15 = (bf16[512,128]{1,0:T(8,128)(2,1)S(1)}, bf16[512,128]{1,0:T(8,128)(2,1)S(1)}, u32[]{:S(2)}, u32[]{:S(2)}) collective-permute-start(bf16[512,128]{1,0:T(8,128)(2,1)S(1)} %get-tuple-element.49), channel_id=1, source_target_pairs={{0,4},{1,5},{2,6},{3,7},{4,0},{5,1},{6,2},{7,3},{8,12},{9,13},{10,... | collective-permute-start | bytes 393224 | tf_op jit(solution)/shard_map/ppermute | solution.py:35
  54.7 7.2 %collective-permute-start.16 = (bf16[512,128]{1,0:T(8,128)(2,1)S(1)}, bf16[512,128]{1,0:T(8,128)(2,1)S(1)}, u32[]{:S(2)}, u32[]{:S(2)}) collective-permute-start(bf16[512,128]{1,0:T(8,128)(2,1)S(1)} %get-tuple-element.48), channel_id=1, source_target_pairs={{0,4},{1,5},{2,6},{3,7},{4,0},{5,1},{6,2},{7,3},{8,12},{9,13},{10,... | collective-permute-start | bytes 393224 | tf_op jit(solution)/shard_map/ppermute | solution.py:35
  55.6 6.4 %collective-permute-start.17 = (bf16[512,128]{1,0:T(8,128)(2,1)S(1)}, bf16[512,128]{1,0:T(8,128)(2,1)S(1)}, u32[]{:S(2)}, u32[]{:S(2)}) collective-permute-start(bf16[512,128]{1,0:T(8,128)(2,1)S(1)} %get-tuple-element.47), channel_id=1, source_target_pairs={{0,2},{1,3},{2,0},{3,1},{4,6},{5,7},{6,4},{7,5},{8,10},{9,11},{10,... | collective-permute-start | bytes 393224 | tf_op jit(solution)/shard_map/ppermute | solution.py:35
  62.7 5.0 %collective-permute-start.18 = (bf16[512,128]{1,0:T(8,128)(2,1)S(1)}, bf16[512,128]{1,0:T(8,128)(2,1)S(1)}, u32[]{:S(2)}, u32[]{:S(2)}) collective-permute-start(bf16[512,128]{1,0:T(8,128)(2,1)S(1)} %get-tuple-element.71), channel_id=1, source_target_pairs={{0,8},{8,0},{16,24},{24,16},{1,9},{9,1},{17,25},{25,17},{2,10},{10... | collective-permute-start | bytes 393224 | tf_op jit(solution)/shard_map/ppermute | solution.py:35
  64.2 5.0 %collective-permute-start.19 = (bf16[512,128]{1,0:T(8,128)(2,1)S(1)}, bf16[512,128]{1,0:T(8,128)(2,1)S(1)}, u32[]{:S(2)}, u32[]{:S(2)}) collective-permute-start(bf16[512,128]{1,0:T(8,128)(2,1)S(1)} %get-tuple-element.73), channel_id=1, source_target_pairs={{0,16},{8,24},{16,0},{24,8},{1,17},{9,25},{17,1},{25,9},{2,18},{10... | collective-permute-start | bytes 393224 | tf_op jit(solution)/shard_map/ppermute | solution.py:35
  69.3 5.0 %collective-permute-start.20 = (bf16[512,128]{1,0:T(8,128)(2,1)S(1)}, bf16[512,128]{1,0:T(8,128)(2,1)S(1)}, u32[]{:S(2)}, u32[]{:S(2)}) collective-permute-start(bf16[512,128]{1,0:T(8,128)(2,1)S(1)} %fusion.12), channel_id=1, source_target_pairs={{0,8},{8,0},{16,24},{24,16},{1,9},{9,1},{17,25},{25,17},{2,10},{10... | collective-permute-start | bytes 393224 | tf_op jit(solution)/shard_map/ppermute | solution.py:35
  70.4 5.0 %collective-permute-start.21 = (bf16[512,128]{1,0:T(8,128)(2,1)S(1)}, bf16[512,128]{1,0:T(8,128)(2,1)S(1)}, u32[]{:S(2)}, u32[]{:S(2)}) collective-permute-start(bf16[512,128]{1,0:T(8,128)(2,1)S(1)} %fusion.13), channel_id=1, source_target_pairs={{0,16},{8,24},{16,0},{24,8},{1,17},{9,25},{17,1},{25,9},{2,18},{10... | collective-permute-start | bytes 393224 | tf_op jit(solution)/shard_map/ppermute | solution.py:35
  77.7 6.9 %collective-permute-start.23 = (f32[136,128]{1,0:T(8,128)S(1)}, f32[136,128]{1,0:T(8,128)S(1)}, u32[]{:S(2)}, u32[]{:S(2)}) collective-permute-start(f32[136,128]{1,0:T(8,128)S(1)} %select_maximum_fusion), channel_id=1, source_target_pairs={{0,6},{1,7},{2,4},{3,5},{4,2},{5,3},{6,0},{7,1},{8,14},{9,15},{10,... | collective-permute-start | bytes 208904 | tf_op jit(solution)/shard_map/ppermute | solution.py:35
  78.3 7.8 %collective-permute-start.24 = (f32[136,128]{1,0:T(8,128)S(1)}, f32[136,128]{1,0:T(8,128)S(1)}, u32[]{:S(2)}, u32[]{:S(2)}) collective-permute-start(f32[136,128]{1,0:T(8,128)S(1)} %select_maximum_fusion), channel_id=1, source_target_pairs={{0,4},{1,5},{2,6},{3,7},{4,0},{5,1},{6,2},{7,3},{8,12},{9,13},{10,... | collective-permute-start | bytes 208904 | tf_op jit(solution)/shard_map/ppermute | solution.py:35
  79.2 6.9 %collective-permute-start.25 = (f32[136,128]{1,0:T(8,128)S(1)}, f32[136,128]{1,0:T(8,128)S(1)}, u32[]{:S(2)}, u32[]{:S(2)}) collective-permute-start(f32[136,128]{1,0:T(8,128)S(1)} %select_maximum_fusion), channel_id=1, source_target_pairs={{0,2},{1,3},{2,0},{3,1},{4,6},{5,7},{6,4},{7,5},{8,10},{9,11},{10,... | collective-permute-start | bytes 208904 | tf_op jit(solution)/shard_map/ppermute | solution.py:35
  (6 other events, 12.6 us)

commit v14 on v13

--- a/solution.py
+++ b/solution.py
@@ -105,23 +105,32 @@
         x = jnp.where(block, jnp.where(lane - first == sub, 1.0, 0.0), head)
         z = x
         pivots = jnp.ones_like(x)
-        inverses = jnp.ones_like(x)
-        for p in range(tall):
-            pivot = columns[p][p : p + 1, :]
-            inverse = 1.0 / pivot
-            masked = jnp.where(sub == p, 0.0, columns[p])
-            others = masked * inverse
-            below = jnp.where(sub > p, others, 0.0)
-            for q in range(p + 1, tall):
-                if q == p + 1:
-                    columns[q] = columns[q] - (masked * columns[q][p : p + 1, :]) * inverse
+        straight = jnp.zeros_like(x)
+        crossed = jnp.zeros_like(x)
+        for p in range(0, tall, 2):
+            s = p + 1
+            here, after = sub == p, sub == s
+            a, b, c = columns[p][p : p + 1, :], columns[p][s : s + 1, :], columns[s][s : s + 1, :]
+            inverse = 1.0 / (a * c - b * b)
+            ratio = b / a
+            from_p = jnp.where(here | after, 0.0, columns[p] * c - columns[s] * b)
+            from_s = jnp.where(here | after, 0.0, columns[s] * a - columns[p] * b)
+            by_p, by_s = from_p * inverse, from_s * inverse
+            for q in range(p + 2, tall):
+                row_p, row_s = columns[q][p : p + 1, :], columns[q][s : s + 1, :]
+                if q < p + 4:
+                    columns[q] = columns[q] - (from_p * row_p + from_s * row_s) * inverse
                 else:
-                    columns[q] = columns[q] - others * columns[q][p : p + 1, :]
-            x = x - below * x[p : p + 1, :]
-            z = z - others * z[p : p + 1, :]
-            pivots = jnp.where(sub == p, pivot, pivots)
-            inverses = jnp.where(sub == p, inverse, inverses)
-        z = z * inverses
+                    columns[q] = columns[q] - by_p * row_p - by_s * row_s
+            x_p, x_s = x[p : p + 1, :], x[s : s + 1, :]
+            below = sub > s
+            x = x - jnp.where(below, by_p, jnp.where(after, ratio, 0.0)) * x_p - jnp.where(below, by_s, 0.0) * x_s
+            z = z - by_p * z[p : p + 1, :] - by_s * z[s : s + 1, :]
+            pivots = jnp.where(here, a, jnp.where(after, c - b * ratio, pivots))
+            straight = jnp.where(here, c * inverse, jnp.where(after, a * inverse, straight))
+            crossed = jnp.where(here | after, b * inverse, crossed)
+        turned = jnp.where(sub % 2 == 0, pltpu.roll(z, tall - 1, 0), pltpu.roll(z, 1, 0))
+        z = z * straight - turned * crossed
         if number + 1 < len(groups):
             following = groups[number + 1]
             terms = [following[:, first + p : first + p + 1] * z[p : p + 1, :] for p in range(tall)]

time: 94.6 us -> 94.6 us (level)
  no operation moved by 1% of the time
where the time goes in v14:
time: 94.6 us; the launch traced here: 94.4 us
  waiting for transfers between devices  44.9 us (47%)
  starting transfers between devices  31.3 us (33%)
  Pallas kernels  7.89 us (8%)
  matrix products  4.71 us (5%)
  other arithmetic  3.03 us (3%)
  local copies, waits for them, and re-layouts  2.29 us (2%)
    ppermute x27, waiting for transfers between devices, swap(): return lax.ppermute(value, axis, [(i, i ^ distance) for i in range(count)])  44.9 us
    ppermute x27, starting transfers between devices, swap(): return lax.ppermute(value, axis, [(i, i ^ distance) for i in range(count)])  31.3 us
    pallas_call x1, Pallas kernels, orthonormal(): pl.pallas_call(kernel, in_specs=[pl.BlockSpec(memory_space=pltpu.SMEM), v...  6.91 us
    unnamed x6, local copies, waits for them, and re-layouts  2.1 us
    dot_general x4, matrix products, part(): lax.dot_general(tile, low, (((0,), (0,)), ((), ())), preferred_element_ty...  1.91 us
  transfers between devices with their start and end apart: 27, of which 20 were waited for; matrix products, arithmetic and copies ran while one was open for 4% of the time, Pallas kernels for 1%

profile of v14, /device:TPU:0, one launch (start us, length us, event | category | flops | bytes accessed | tf_op | source)
XLA Modules:
  0.0 94.4 jit_solution(13784331530711023901)
XLA Ops:
  0.9 3.0 %collective-permute-start.2 = (bf16[128,256]{1,0:T(8,128)(2,1)S(1)}, bf16[128,256]{1,0:T(8,128)(2,1)S(1)}, u32[]{:S(2)}, u32[]{:S(2)}) collective-permute-start(bf16[128,256]{1,0:T(8,128)(2,1)S(1)} %convert_element_type.147), channel_id=1, source_target_pairs={{0,16},{8,24},{16,0},{24,8},{1,17},{9,25},{17,1},{25,9},{2,18},{10... | collective-permute-start | bytes 196616 | tf_op jit(solution)/shard_map/ppermute | solution.py:35
  10.4 1.5 %collective-permute-done.3 = bf16[1024,128]{1,0:T(8,128)(2,1)S(1)} collective-permute-done((bf16[1024,128]{1,0:T(8,128)(2,1)S(1)}, bf16[1024,128]{1,0:T(8,128)(2,1)S(1)}, u32[]{:S(2)}, u32[]{:S(2)}) %collective-permute-start.3) | collective-permute-done | bytes 262176 | tf_op jit(solution)/shard_map/ppermute | solution.py:35
  12.0 1.6 %collective-permute-start.5 = (bf16[512,128]{1,0:T(8,128)(2,1)S(1)}, bf16[512,128]{1,0:T(8,128)(2,1)S(1)}, u32[]{:S(2)}, u32[]{:S(2)}) collective-permute-start(bf16[512,128]{1,0:T(8,128)(2,1)S(1)} %get-tuple-element.56), channel_id=1, source_target_pairs={{0,2},{1,3},{2,0},{3,1},{4,6},{5,7},{6,4},{7,5},{8,10},{9,11},{10,... | collective-permute-start | bytes 393224 | tf_op jit(solution)/shard_map/ppermute | solution.py:35
  13.7 2.6 %collective-permute-start.6 = (bf16[512,128]{1,0:T(8,128)(2,1)S(1)}, bf16[512,128]{1,0:T(8,128)(2,1)S(1)}, u32[]{:S(2)}, u32[]{:S(2)}) collective-permute-start(bf16[512,128]{1,0:T(8,128)(2,1)S(1)} %get-tuple-element.55), channel_id=1, source_target_pairs={{0,4},{1,5},{2,6},{3,7},{4,0},{5,1},{6,2},{7,3},{8,12},{9,13},{10,... | collective-permute-start | bytes 393224 | tf_op jit(solution)/shard_map/ppermute | solution.py:35
  17.4 2.6 %collective-permute-done.5 = bf16[512,128]{1,0:T(8,128)(2,1)S(1)} collective-permute-done((bf16[512,128]{1,0:T(8,128)(2,1)S(1)}, bf16[512,128]{1,0:T(8,128)(2,1)S(1)}, u32[]{:S(2)}, u32[]{:S(2)}) %collective-permute-start.5) | collective-permute-done | bytes 131104 | tf_op jit(solution)/shard_map/ppermute | solution.py:35
  20.0 2.7 %collective-permute-done.6 = bf16[512,128]{1,0:T(8,128)(2,1)S(1)} collective-permute-done((bf16[512,128]{1,0:T(8,128)(2,1)S(1)}, bf16[512,128]{1,0:T(8,128)(2,1)S(1)}, u32[]{:S(2)}, u32[]{:S(2)}) %collective-permute-start.6) | collective-permute-done | bytes 131104 | tf_op jit(solution)/shard_map/ppermute | solution.py:35
  23.1 2.7 %collective-permute-start.8 = (bf16[512,128]{1,0:T(8,128)(2,1)S(1)}, bf16[512,128]{1,0:T(8,128)(2,1)S(1)}, u32[]{:S(2)}, u32[]{:S(2)}) collective-permute-start(bf16[512,128]{1,0:T(8,128)(2,1)S(1)} %get-tuple-element.53), channel_id=1, source_target_pairs={{0,2},{1,3},{2,0},{3,1},{4,6},{5,7},{6,4},{7,5},{8,10},{9,11},{10,... | collective-permute-start | bytes 393224 | tf_op jit(solution)/shard_map/ppermute | solution.py:35
  26.1 4.0 %collective-permute-done.7 = bf16[512,128]{1,0:T(8,128)(2,1)S(1)} collective-permute-done((bf16[512,128]{1,0:T(8,128)(2,1)S(1)}, bf16[512,128]{1,0:T(8,128)(2,1)S(1)}, u32[]{:S(2)}, u32[]{:S(2)}) %collective-permute-start.7) | collective-permute-done | bytes 131104 | tf_op jit(solution)/shard_map/ppermute | solution.py:35
  32.3 1.5 %collective-permute-start.11 = (bf16[512,128]{1,0:T(8,128)(2,1)S(1)}, bf16[512,128]{1,0:T(8,128)(2,1)S(1)}, u32[]{:S(2)}, u32[]{:S(2)}) collective-permute-start(bf16[512,128]{1,0:T(8,128)(2,1)S(1)} %get-tuple-element.69), channel_id=1, source_target_pairs={{0,16},{8,24},{16,0},{24,8},{1,17},{9,25},{17,1},{25,9},{2,18},{10... | collective-permute-start | bytes 393224 | tf_op jit(solution)/shard_map/ppermute | solution.py:35
  33.8 2.2 %collective-permute-done.9 = bf16[512,128]{1,0:T(8,128)(2,1)S(1)} collective-permute-done((bf16[512,128]{1,0:T(8,128)(2,1)S(1)}, bf16[512,128]{1,0:T(8,128)(2,1)S(1)}, u32[]{:S(2)}, u32[]{:S(2)}) %collective-permute-start.9) | collective-permute-done | bytes 131104 | tf_op jit(solution)/shard_map/ppermute | solution.py:35
  36.0 2.2 %collective-permute-done.11 = bf16[512,128]{1,0:T(8,128)(2,1)S(1)} collective-permute-done((bf16[512,128]{1,0:T(8,128)(2,1)S(1)}, bf16[512,128]{1,0:T(8,128)(2,1)S(1)}, u32[]{:S(2)}, u32[]{:S(2)}) %collective-permute-start.11) | collective-permute-done | bytes 131104 | tf_op jit(solution)/shard_map/ppermute | solution.py:35
  39.5 1.7 %collective-permute-start.12 = (bf16[512,128]{1,0:T(8,128)(2,1)S(1)}, bf16[512,128]{1,0:T(8,128)(2,1)S(1)}, u32[]{:S(2)}, u32[]{:S(2)}) collective-permute-start(bf16[512,128]{1,0:T(8,128)(2,1)S(1)} %fusion.10), channel_id=1, source_target_pairs={{0,16},{8,24},{16,0},{24,8},{1,17},{9,25},{17,1},{25,9},{2,18},{10... | collective-permute-start | bytes 393224 | tf_op jit(solution)/shard_map/ppermute | solution.py:35
  41.2 2.1 %collective-permute-done.13 = bf16[512,128]{1,0:T(8,128)(2,1)S(1)} collective-permute-done((bf16[512,128]{1,0:T(8,128)(2,1)S(1)}, bf16[512,128]{1,0:T(8,128)(2,1)S(1)}, u32[]{:S(2)}, u32[]{:S(2)}) %collective-permute-start.13) | collective-permute-done | bytes 131104 | tf_op jit(solution)/shard_map/ppermute | solution.py:35
  45.7 2.5 %collective-permute-start.15 = (bf16[512,128]{1,0:T(8,128)(2,1)S(1)}, bf16[512,128]{1,0:T(8,128)(2,1)S(1)}, u32[]{:S(2)}, u32[]{:S(2)}) collective-permute-start(bf16[512,128]{1,0:T(8,128)(2,1)S(1)} %get-tuple-element.49), channel_id=1, source_target_pairs={{0,4},{1,5},{2,6},{3,7},{4,0},{5,1},{6,2},{7,3},{8,12},{9,13},{10,... | collective-permute-start | bytes 393224 | tf_op jit(solution)/shard_map/ppermute | solution.py:35
  48.2 3.6 %collective-permute-done.14 = bf16[512,128]{1,0:T(8,128)(2,1)S(1)} collective-permute-done((bf16[512,128]{1,0:T(8,128)(2,1)S(1)}, bf16[512,128]{1,0:T(8,128)(2,1)S(1)}, u32[]{:S(2)}, u32[]{:S(2)}) %collective-permute-start.14) | collective-permute-done | bytes 131104 | tf_op jit(solution)/shard_map/ppermute | solution.py:35
  51.8 2.8 %collective-permute-done.15 = bf16[512,128]{1,0:T(8,128)(2,1)S(1)} collective-permute-done((bf16[512,128]{1,0:T(8,128)(2,1)S(1)}, bf16[512,128]{1,0:T(8,128)(2,1)S(1)}, u32[]{:S(2)}, u32[]{:S(2)}) %collective-permute-start.15) | collective-permute-done | bytes 131104 | tf_op jit(solution)/shard_map/ppermute | solution.py:35
  55.6 6.3 %collective-permute-done.16 = bf16[512,128]{1,0:T(8,128)(2,1)S(1)} collective-permute-done((bf16[512,128]{1,0:T(8,128)(2,1)S(1)}, bf16[512,128]{1,0:T(8,128)(2,1)S(1)}, u32[]{:S(2)}, u32[]{:S(2)}) %collective-permute-start.16) | collective-permute-done | bytes 131104 | tf_op jit(solution)/shard_map/ppermute | solution.py:35
  64.2 1.5 %collective-permute-start.19 = (bf16[512,128]{1,0:T(8,128)(2,1)S(1)}, bf16[512,128]{1,0:T(8,128)(2,1)S(1)}, u32[]{:S(2)}, u32[]{:S(2)}) collective-permute-start(bf16[512,128]{1,0:T(8,128)(2,1)S(1)} %get-tuple-element.73), channel_id=1, source_target_pairs={{0,16},{8,24},{16,0},{24,8},{1,17},{9,25},{17,1},{25,9},{2,18},{10... | collective-permute-start | bytes 393224 | tf_op jit(solution)/shard_map/ppermute | solution.py:35
  65.7 2.0 %collective-permute-done.18 = bf16[512,128]{1,0:T(8,128)(2,1)S(1)} collective-permute-done((bf16[512,128]{1,0:T(8,128)(2,1)S(1)}, bf16[512,128]{1,0:T(8,128)(2,1)S(1)}, u32[]{:S(2)}, u32[]{:S(2)}) %collective-permute-start.18) | collective-permute-done | bytes 131104 | tf_op jit(solution)/shard_map/ppermute | solution.py:35
  70.4 1.6 %collective-permute-start.21 = (bf16[512,128]{1,0:T(8,128)(2,1)S(1)}, bf16[512,128]{1,0:T(8,128)(2,1)S(1)}, u32[]{:S(2)}, u32[]{:S(2)}) collective-permute-start(bf16[512,128]{1,0:T(8,128)(2,1)S(1)} %fusion.13), channel_id=1, source_target_pairs={{0,16},{8,24},{16,0},{24,8},{1,17},{9,25},{17,1},{25,9},{2,18},{10... | collective-permute-start | bytes 393224 | tf_op jit(solution)/shard_map/ppermute | solution.py:35
  72.0 2.3 %collective-permute-done.20 = bf16[512,128]{1,0:T(8,128)(2,1)S(1)} collective-permute-done((bf16[512,128]{1,0:T(8,128)(2,1)S(1)}, bf16[512,128]{1,0:T(8,128)(2,1)S(1)}, u32[]{:S(2)}, u32[]{:S(2)}) %collective-permute-start.20) | collective-permute-done | bytes 131104 | tf_op jit(solution)/shard_map/ppermute | solution.py:35
  79.2 2.9 %collective-permute-start.25 = (f32[136,128]{1,0:T(8,128)S(1)}, f32[136,128]{1,0:T(8,128)S(1)}, u32[]{:S(2)}, u32[]{:S(2)}) collective-permute-start(f32[136,128]{1,0:T(8,128)S(1)} %select_maximum_fusion), channel_id=1, source_target_pairs={{0,2},{1,3},{2,0},{3,1},{4,6},{5,7},{6,4},{7,5},{8,10},{9,11},{10,... | collective-permute-start | bytes 208904 | tf_op jit(solution)/shard_map/ppermute | solution.py:35
  82.2 2.4 %collective-permute-done.23 = f32[136,128]{1,0:T(8,128)S(1)} collective-permute-done((f32[136,128]{1,0:T(8,128)S(1)}, f32[136,128]{1,0:T(8,128)S(1)}, u32[]{:S(2)}, u32[]{:S(2)}) %collective-permute-start.23) | collective-permute-done | bytes 69664 | tf_op jit(solution)/shard_map/ppermute | solution.py:35
  87.5 6.9 %shard_map.38 = f32[128,256]{1,0:T(8,128)} custom-call(s32[1]{0:T(128)} %bitcast.first_ref, f32[136,128]{1,0:T(8,128)S(1)} %add_add_fusion.total_ref, f32[136,128]{1,0:T(8,128)S(1)} %collective-permute-done.26.partner_ref, f32[128,128]{1,0:T(8,128)S(1)} %fusion.23.mine_ref, f32[128,128]{1,0:T(8,128)S(1)} %constant_dynamic-slice_fusion.theirs_ref), custom_call_target="tpu_custom_call" | custom-call | tf_op jit(solution)/shard_map/pallas_call | solution.py:176
  (81 shorter events, 28.7 us)
Async XLA Ops:
  0.9 7.7 %collective-permute-start.2 = (bf16[128,256]{1,0:T(8,128)(2,1)S(1)}, bf16[128,256]{1,0:T(8,128)(2,1)S(1)}, u32[]{:S(2)}, u32[]{:S(2)}) collective-permute-start(bf16[128,256]{1,0:T(8,128)(2,1)S(1)} %convert_element_type.147), channel_id=1, source_target_pairs={{0,16},{8,24},{16,0},{24,8},{1,17},{9,25},{17,1},{25,9},{2,18},{10... | collective-permute-start | bytes 196616 | tf_op jit(solution)/shard_map/ppermute | solution.py:35
  3.9 5.7 %collective-permute-start.1 = (bf16[128,256]{1,0:T(8,128)(2,1)S(1)}, bf16[128,256]{1,0:T(8,128)(2,1)S(1)}, u32[]{:S(2)}, u32[]{:S(2)}) collective-permute-start(bf16[128,256]{1,0:T(8,128)(2,1)S(1)} %convert_element_type.147), channel_id=1, source_target_pairs={{0,24},{8,16},{16,8},{24,0},{1,25},{9,17},{17,9},{25,1},{2,26},{10... | collective-permute-start | bytes 196616 | tf_op jit(solution)/shard_map/ppermute | solution.py:35
  5.4 4.3 %collective-permute-start = (bf16[128,256]{1,0:T(8,128)(2,1)S(1)}, bf16[128,256]{1,0:T(8,128)(2,1)S(1)}, u32[]{:S(2)}, u32[]{:S(2)}) collective-permute-start(bf16[128,256]{1,0:T(8,128)(2,1)S(1)} %convert_element_type.147), channel_id=1, source_target_pairs={{0,8},{8,0},{16,24},{24,16},{1,9},{9,1},{17,25},{25,17},{2,10},{10... | collective-permute-start | bytes 196616 | tf_op jit(solution)/shard_map/ppermute | solution.py:35
  12.0 8.0 %collective-permute-start.5 = (bf16[512,128]{1,0:T(8,128)(2,1)S(1)}, bf16[512,128]{1,0:T(8,128)(2,1)S(1)}, u32[]{:S(2)}, u32[]{:S(2)}) collective-permute-start(bf16[512,128]{1,0:T(8,128)(2,1)S(1)} %get-tuple-element.56), channel_id=1, source_target_pairs={{0,2},{1,3},{2,0},{3,1},{4,6},{5,7},{6,4},{7,5},{8,10},{9,11},{10,... | collective-permute-start | bytes 393224 | tf_op jit(solution)/shard_map/ppermute | solution.py:35
  13.7 9.0 %collective-permute-start.6 = (bf16[512,128]{1,0:T(8,128)(2,1)S(1)}, bf16[512,128]{1,0:T(8,128)(2,1)S(1)}, u32[]{:S(2)}, u32[]{:S(2)}) collective-permute-start(bf16[512,128]{1,0:T(8,128)(2,1)S(1)} %get-tuple-element.55), channel_id=1, source_target_pairs={{0,4},{1,5},{2,6},{3,7},{4,0},{5,1},{6,2},{7,3},{8,12},{9,13},{10,... | collective-permute-start | bytes 393224 | tf_op jit(solution)/shard_map/ppermute | solution.py:35
  16.9 9.0 %collective-permute-start.10 = (f32[128,128]{1,0:T(8,128)}, f32[128,128]{1,0:T(8,128)S(1)}, u32[]{:S(2)}, u32[]{:S(2)}) collective-permute-start(f32[128,128]{1,0:T(8,128)} %get-tuple-element.64), channel_id=1, source_target_pairs={{0,1},{1,0},{2,3},{3,2},{4,5},{5,4},{6,7},{7,6},{8,9},{9,8},{10,11... | collective-permute-start | bytes 196616 | tf_op jit(solution)/shard_map/ppermute | solution.py:35
  16.9 14.9 %collective-permute-start.4 = (bf16[1024,512]{1,0:T(8,128)(2,1)S(1)}, bf16[1024,512]{1,0:T(8,128)(2,1)S(1)}, u32[]{:S(2)}, u32[]{:S(2)}) collective-permute-start(bf16[1024,512]{1,0:T(8,128)(2,1)S(1)} %shard_map.37), channel_id=1, source_target_pairs={{0,1},{1,0},{2,3},{3,2},{4,5},{5,4},{6,7},{7,6},{8,9},{9,8},{10,11... | collective-permute-start | bytes 3145736 | tf_op jit(solution)/shard_map/ppermute | solution.py:35
  22.7 7.3 %collective-permute-start.7 = (bf16[512,128]{1,0:T(8,128)(2,1)S(1)}, bf16[512,128]{1,0:T(8,128)(2,1)S(1)}, u32[]{:S(2)}, u32[]{:S(2)}) collective-permute-start(bf16[512,128]{1,0:T(8,128)(2,1)S(1)} %get-tuple-element.54), channel_id=1, source_target_pairs={{0,4},{1,5},{2,6},{3,7},{4,0},{5,1},{6,2},{7,3},{8,12},{9,13},{10,... | collective-permute-start | bytes 393224 | tf_op jit(solution)/shard_map/ppermute | solution.py:35
  23.1 7.0 %collective-permute-start.8 = (bf16[512,128]{1,0:T(8,128)(2,1)S(1)}, bf16[512,128]{1,0:T(8,128)(2,1)S(1)}, u32[]{:S(2)}, u32[]{:S(2)}) collective-permute-start(bf16[512,128]{1,0:T(8,128)(2,1)S(1)} %get-tuple-element.53), channel_id=1, source_target_pairs={{0,2},{1,3},{2,0},{3,1},{4,6},{5,7},{6,4},{7,5},{8,10},{9,11},{10,... | collective-permute-start | bytes 393224 | tf_op jit(solution)/shard_map/ppermute | solution.py:35
  30.8 5.2 %collective-permute-start.9 = (bf16[512,128]{1,0:T(8,128)(2,1)S(1)}, bf16[512,128]{1,0:T(8,128)(2,1)S(1)}, u32[]{:S(2)}, u32[]{:S(2)}) collective-permute-start(bf16[512,128]{1,0:T(8,128)(2,1)S(1)} %get-tuple-element.67), channel_id=1, source_target_pairs={{0,8},{8,0},{16,24},{24,16},{1,9},{9,1},{17,25},{25,17},{2,10},{10... | collective-permute-start | bytes 393224 | tf_op jit(solution)/shard_map/ppermute | solution.py:35
  32.3 5.9 %collective-permute-start.11 = (bf16[512,128]{1,0:T(8,128)(2,1)S(1)}, bf16[512,128]{1,0:T(8,128)(2,1)S(1)}, u32[]{:S(2)}, u32[]{:S(2)}) collective-permute-start(bf16[512,128]{1,0:T(8,128)(2,1)S(1)} %get-tuple-element.69), channel_id=1, source_target_pairs={{0,16},{8,24},{16,0},{24,8},{1,17},{9,25},{17,1},{25,9},{2,18},{10... | collective-permute-start | bytes 393224 | tf_op jit(solution)/shard_map/ppermute | solution.py:35
  38.2 5.0 %collective-permute-start.13 = (bf16[512,128]{1,0:T(8,128)(2,1)S(1)}, bf16[512,128]{1,0:T(8,128)(2,1)S(1)}, u32[]{:S(2)}, u32[]{:S(2)}) collective-permute-start(bf16[512,128]{1,0:T(8,128)(2,1)S(1)} %fusion.11), channel_id=1, source_target_pairs={{0,8},{8,0},{16,24},{24,16},{1,9},{9,1},{17,25},{25,17},{2,10},{10... | collective-permute-start | bytes 393224 | tf_op jit(solution)/shard_map/ppermute | solution.py:35
  39.5 5.0 %collective-permute-start.12 = (bf16[512,128]{1,0:T(8,128)(2,1)S(1)}, bf16[512,128]{1,0:T(8,128)(2,1)S(1)}, u32[]{:S(2)}, u32[]{:S(2)}) collective-permute-start(bf16[512,128]{1,0:T(8,128)(2,1)S(1)} %fusion.10), channel_id=1, source_target_pairs={{0,16},{8,24},{16,0},{24,8},{1,17},{9,25},{17,1},{25,9},{2,18},{10... | collective-permute-start | bytes 393224 | tf_op jit(solution)/shard_map/ppermute | solution.py:35
  45.6 6.3 %collective-permute-start.14 = (bf16[512,128]{1,0:T(8,128)(2,1)S(1)}, bf16[512,128]{1,0:T(8,128)(2,1)S(1)}, u32[]{:S(2)}, u32[]{:S(2)}) collective-permute-start(bf16[512,128]{1,0:T(8,128)(2,1)S(1)} %get-tuple-element.50), channel_id=1, source_target_pairs={{0,2},{1,3},{2,0},{3,1},{4,6},{5,7},{6,4},{7,5},{8,10},{9,11},{10,... | collective-permute-start | bytes 393224 | tf_op jit(solution)/shard_map/ppermute | solution.py:35
  45.7 9.0 %collective-permute-start.15 = (bf16[512,128]{1,0:T(8,128)(2,1)S(1)}, bf16[512,128]{1,0:T(8,128)(2,1)S(1)}, u32[]{:S(2)}, u32[]{:S(2)}) collective-permute-start(bf16[512,128]{1,0:T(8,128)(2,1)S(1)} %get-tuple-element.49), channel_id=1, source_target_pairs={{0,4},{1,5},{2,6},{3,7},{4,0},{5,1},{6,2},{7,3},{8,12},{9,13},{10,... | collective-permute-start | bytes 393224 | tf_op jit(solution)/shard_map/ppermute | solution.py:35
  54.7 7.2 %collective-permute-start.16 = (bf16[512,128]{1,0:T(8,128)(2,1)S(1)}, bf16[512,128]{1,0:T(8,128)(2,1)S(1)}, u32[]{:S(2)}, u32[]{:S(2)}) collective-permute-start(bf16[512,128]{1,0:T(8,128)(2,1)S(1)} %get-tuple-element.48), channel_id=1, source_target_pairs={{0,4},{1,5},{2,6},{3,7},{4,0},{5,1},{6,2},{7,3},{8,12},{9,13},{10,... | collective-permute-start | bytes 393224 | tf_op jit(solution)/shard_map/ppermute | solution.py:35
  55.6 6.4 %collective-permute-start.17 = (bf16[512,128]{1,0:T(8,128)(2,1)S(1)}, bf16[512,128]{1,0:T(8,128)(2,1)S(1)}, u32[]{:S(2)}, u32[]{:S(2)}) collective-permute-start(bf16[512,128]{1,0:T(8,128)(2,1)S(1)} %get-tuple-element.47), channel_id=1, source_target_pairs={{0,2},{1,3},{2,0},{3,1},{4,6},{5,7},{6,4},{7,5},{8,10},{9,11},{10,... | collective-permute-start | bytes 393224 | tf_op jit(solution)/shard_map/ppermute | solution.py:35
  62.7 5.0 %collective-permute-start.18 = (bf16[512,128]{1,0:T(8,128)(2,1)S(1)}, bf16[512,128]{1,0:T(8,128)(2,1)S(1)}, u32[]{:S(2)}, u32[]{:S(2)}) collective-permute-start(bf16[512,128]{1,0:T(8,128)(2,1)S(1)} %get-tuple-element.71), channel_id=1, source_target_pairs={{0,8},{8,0},{16,24},{24,16},{1,9},{9,1},{17,25},{25,17},{2,10},{10... | collective-permute-start | bytes 393224 | tf_op jit(solution)/shard_map/ppermute | solution.py:35
  64.2 5.0 %collective-permute-start.19 = (bf16[512,128]{1,0:T(8,128)(2,1)S(1)}, bf16[512,128]{1,0:T(8,128)(2,1)S(1)}, u32[]{:S(2)}, u32[]{:S(2)}) collective-permute-start(bf16[512,128]{1,0:T(8,128)(2,1)S(1)} %get-tuple-element.73), channel_id=1, source_target_pairs={{0,16},{8,24},{16,0},{24,8},{1,17},{9,25},{17,1},{25,9},{2,18},{10... | collective-permute-start | bytes 393224 | tf_op jit(solution)/shard_map/ppermute | solution.py:35
  69.3 5.0 %collective-permute-start.20 = (bf16[512,128]{1,0:T(8,128)(2,1)S(1)}, bf16[512,128]{1,0:T(8,128)(2,1)S(1)}, u32[]{:S(2)}, u32[]{:S(2)}) collective-permute-start(bf16[512,128]{1,0:T(8,128)(2,1)S(1)} %fusion.12), channel_id=1, source_target_pairs={{0,8},{8,0},{16,24},{24,16},{1,9},{9,1},{17,25},{25,17},{2,10},{10... | collective-permute-start | bytes 393224 | tf_op jit(solution)/shard_map/ppermute | solution.py:35
  70.4 5.0 %collective-permute-start.21 = (bf16[512,128]{1,0:T(8,128)(2,1)S(1)}, bf16[512,128]{1,0:T(8,128)(2,1)S(1)}, u32[]{:S(2)}, u32[]{:S(2)}) collective-permute-start(bf16[512,128]{1,0:T(8,128)(2,1)S(1)} %fusion.13), channel_id=1, source_target_pairs={{0,16},{8,24},{16,0},{24,8},{1,17},{9,25},{17,1},{25,9},{2,18},{10... | collective-permute-start | bytes 393224 | tf_op jit(solution)/shard_map/ppermute | solution.py:35
  77.7 6.9 %collective-permute-start.23 = (f32[136,128]{1,0:T(8,128)S(1)}, f32[136,128]{1,0:T(8,128)S(1)}, u32[]{:S(2)}, u32[]{:S(2)}) collective-permute-start(f32[136,128]{1,0:T(8,128)S(1)} %select_maximum_fusion), channel_id=1, source_target_pairs={{0,6},{1,7},{2,4},{3,5},{4,2},{5,3},{6,0},{7,1},{8,14},{9,15},{10,... | collective-permute-start | bytes 208904 | tf_op jit(solution)/shard_map/ppermute | solution.py:35
  78.3 7.8 %collective-permute-start.24 = (f32[136,128]{1,0:T(8,128)S(1)}, f32[136,128]{1,0:T(8,128)S(1)}, u32[]{:S(2)}, u32[]{:S(2)}) collective-permute-start(f32[136,128]{1,0:T(8,128)S(1)} %select_maximum_fusion), channel_id=1, source_target_pairs={{0,4},{1,5},{2,6},{3,7},{4,0},{5,1},{6,2},{7,3},{8,12},{9,13},{10,... | collective-permute-start | bytes 208904 | tf_op jit(solution)/shard_map/ppermute | solution.py:35
  79.2 6.9 %collective-permute-start.25 = (f32[136,128]{1,0:T(8,128)S(1)}, f32[136,128]{1,0:T(8,128)S(1)}, u32[]{:S(2)}, u32[]{:S(2)}) collective-permute-start(f32[136,128]{1,0:T(8,128)S(1)} %select_maximum_fusion), channel_id=1, source_target_pairs={{0,2},{1,3},{2,0},{3,1},{4,6},{5,7},{6,4},{7,5},{8,10},{9,11},{10,... | collective-permute-start | bytes 208904 | tf_op jit(solution)/shard_map/ppermute | solution.py:35
  (6 other events, 12.6 us)
